TPU v7x, 32 devices: a whole 2x2x4 slice. The times are simulated.
32 devices in a mesh: group: 2 (over y), resp: 4 (over z), tensor: 4 (over x, core).
Axes of the slice: x: 2, y: 2, z: 4, core: 2. Of those that a mesh axis runs over, the one named last changes fastest.
Arguments:
- queries: bfloat16 [8, 512, 8192], P(('group', 'resp'), None, 'tensor'), parts along dimension 0, may hold values from -50 to 50
- resp_keys: bfloat16 [8, 512, 1024], P(('group', 'resp'), None, 'tensor'), parts along dimension 0, may hold values from -6 to 6
- resp_values: bfloat16 [8, 512, 1024], P(('group', 'resp'), None, 'tensor'), parts along dimension 0, may hold values from -6 to 6
- prompt_keys: bfloat16 [4096, 1024], P(('group', 'resp', 'tensor')), parts along dimension 0, may hold values from -7 to 7
- prompt_values: bfloat16 [4096, 1024], P(('group', 'resp', 'tensor')), parts along dimension 0, may hold values from -6 to 6
- out_grad: bfloat16 [8, 512, 8192], P(('group', 'resp'), None, 'tensor'), parts along dimension 0, may hold values from -6 to 6
- lengths: int32 [8], P(('group', 'resp')), parts along dimension 0, may hold values from 1 to 512, 1280 in all
Outputs:
- attended: bfloat16 [8, 512, 8192], P(('group', 'resp'), None, 'tensor'), parts along dimension 0
- query_grad: bfloat16 [8, 512, 8192], P(('group', 'resp'), None, 'tensor'), parts along dimension 0
- resp_key_grad: bfloat16 [8, 512, 1024], P(('group', 'resp'), None, 'tensor'), parts along dimension 0
- resp_value_grad: bfloat16 [8, 512, 1024], P(('group', 'resp'), None, 'tensor'), parts along dimension 0
- prompt_key_grad: float32 [4096, 1024], P(('group', 'resp', 'tensor')), parts along dimension 0
- prompt_value_grad: float32 [4096, 1024], P(('group', 'resp', 'tensor')), parts along dimension 0
There are 2 independent parts, one for each index of `group`. A program takes and returns all parts, laid end to end along the dimension named above; each array names one. Nothing has to cross between parts.
Inputs may be any that keep to these rules, and one draw needn't show every extreme that they name: For each prompt group separately, its 4 lengths sum to 1280, and one of them is exactly 512; the table lists the groups one after another.
All inputs are finite; a program needn't handle non-finite values.
Results may differ from a plain program's by a relative error of at most 0.012.
The roundings to bfloat16 on the way count: a program that leaves them out, or rounds other values in their place, can miss the bound.
Values may be sent and summed in bfloat16 or wider, within the bound.
No kernel may reach another device: no remote copies, remote signals or barrier semaphores. Data moves between devices by JAX's collectives and lax.ppermute only.
A program may use at most 64 MiB of HBM per device.

v0:
```python
import jax
import jax.numpy as jnp
from jax import lax
from jax.sharding import PartitionSpec as P

HD = 128


def head_slice(array, index, column, width):
    picked = lax.dynamic_index_in_dim(array, index, 0, keepdims=False)
    return lax.dynamic_slice_in_dim(picked, column, width, 1)


def add_block(running, term, where_at):
    current = lax.dynamic_slice(running, where_at, term.shape)
    return lax.dynamic_update_slice(running, current + term, where_at)


def per_device(queries, resp_keys, resp_values, prompt_keys, prompt_values, out_grad, lengths):
    member_count, seq_len, query_width = queries.shape
    pair_width = resp_keys.shape[2]
    query_heads = query_width // HD
    heads_per = query_heads // (pair_width // HD)
    block_count = member_count * query_heads
    factor = HD ** (-0.5)
    every_keys, every_values = (
        lax.all_gather(prompt_keys, ("resp", "tensor"), axis=0, tiled=True),
        lax.all_gather(prompt_values, ("resp", "tensor"), axis=0, tiled=True),
    )
    offset = lax.axis_index("tensor") * pair_width
    cache_keys = lax.dynamic_slice_in_dim(every_keys, offset, pair_width, 1)
    cache_values = lax.dynamic_slice_in_dim(every_values, offset, pair_width, 1)
    prompt_rows = cache_keys.shape[0]
    positions = jnp.arange(seq_len, dtype=jnp.int32)
    causal = positions[None, :] <= positions[:, None]

    def block_inputs(block_index):
        member = block_index // query_heads
        head_index = block_index % query_heads
        column = head_index // heads_per * HD
        query_rows = head_slice(queries, member, head_index * HD, HD)
        grad_rows = head_slice(out_grad, member, head_index * HD, HD)
        resp_length = lax.dynamic_index_in_dim(lengths, member, 0, keepdims=False)
        live_rows = (positions < resp_length)[:, None]
        live_grad = jnp.where(live_rows, grad_rows, jnp.zeros_like(grad_rows))
        return (member, head_index, column, query_rows, live_grad, live_rows, resp_length)

    def main_step(block_index, state_tuple):
        (
            attended,
            query_grad,
            key_running,
            value_running,
            prompt_key_running,
            prompt_value_running,
            row_tops,
            row_totals,
            row_deltas,
        ) = state_tuple
        member, head_index, column, query_rows, live_grad, live_rows, resp_length = block_inputs(
            block_index
        )
        key_prompt = lax.dynamic_slice_in_dim(cache_keys, column, HD, 1)
        value_prompt = lax.dynamic_slice_in_dim(cache_values, column, HD, 1)
        key_resp = head_slice(resp_keys, member, column, HD)
        value_resp = head_slice(resp_values, member, column, HD)
        allowed = causal & (positions[None, :] < resp_length)
        score_prompt = (
            jnp.einsum("qd,kd->qk", query_rows, key_prompt, preferred_element_type=jnp.float32)
            * factor
        )
        score_resp = jnp.where(
            allowed,
            jnp.einsum("qd,kd->qk", query_rows, key_resp, preferred_element_type=jnp.float32)
            * factor,
            -jnp.inf,
        )
        row_top = jnp.maximum(jnp.max(score_prompt, 1), jnp.max(score_resp, 1))
        exp_prompt = jnp.exp(score_prompt - row_top[:, None])
        exp_resp = jnp.exp(score_resp - row_top[:, None])
        row_total = jnp.sum(exp_prompt, 1) + jnp.sum(exp_resp, 1)
        frac_prompt = exp_prompt / row_total[:, None]
        frac_resp = exp_resp / row_total[:, None]
        weight_prompt = frac_prompt.astype(jnp.bfloat16)
        weight_resp = frac_resp.astype(jnp.bfloat16)
        mixture = jnp.dot(
            weight_prompt, value_prompt, preferred_element_type=jnp.float32
        ) + jnp.dot(weight_resp, value_resp, preferred_element_type=jnp.float32)
        out_block = jnp.where(live_rows, mixture, 0.0).astype(jnp.bfloat16)
        row_delta = jnp.sum(
            live_grad.astype(jnp.float32) * lax.optimization_barrier(out_block).astype(jnp.float32),
            1,
        )
        dprob_prompt = jnp.einsum(
            "qd,kd->qk", live_grad, value_prompt, preferred_element_type=jnp.float32
        )
        dprob_resp = jnp.einsum(
            "qd,kd->qk", live_grad, value_resp, preferred_element_type=jnp.float32
        )
        sgrad_prompt = (frac_prompt * (dprob_prompt - row_delta[:, None])).astype(jnp.bfloat16)
        sgrad_resp = (frac_resp * (dprob_resp - row_delta[:, None])).astype(jnp.bfloat16)
        block_qgrad = (
            factor
            * (
                jnp.dot(sgrad_prompt, key_prompt, preferred_element_type=jnp.float32)
                + jnp.dot(sgrad_resp, key_resp, preferred_element_type=jnp.float32)
            )
        ).astype(jnp.bfloat16)
        key_term = factor * jnp.einsum(
            "qk,qd->kd", sgrad_resp, query_rows, preferred_element_type=jnp.float32
        )
        value_term = jnp.einsum(
            "qk,qd->kd", weight_resp, live_grad, preferred_element_type=jnp.float32
        )
        attended = lax.dynamic_update_slice(attended, out_block[None], (member, 0, head_index * HD))
        query_grad = lax.dynamic_update_slice(
            query_grad, block_qgrad[None], (member, 0, head_index * HD)
        )
        key_running = add_block(key_running, key_term[None], (member, 0, column))
        value_running = add_block(value_running, value_term[None], (member, 0, column))
        prompt_key_term = factor * jnp.einsum(
            "qk,qd->kd", sgrad_prompt, query_rows, preferred_element_type=jnp.float32
        )
        prompt_value_term = jnp.einsum(
            "qk,qd->kd", weight_prompt, live_grad, preferred_element_type=jnp.float32
        )
        prompt_key_running = add_block(prompt_key_running, prompt_key_term, (0, column))
        prompt_value_running = add_block(prompt_value_running, prompt_value_term, (0, column))
        return (
            attended,
            query_grad,
            key_running,
            value_running,
            prompt_key_running,
            prompt_value_running,
            row_tops,
            row_totals,
            row_deltas,
        )

    prompt_start = jnp.zeros((prompt_rows, pair_width), jnp.float32)
    stats_start = jnp.zeros((0,), jnp.float32)
    start_state = (
        jnp.zeros_like(queries),
        jnp.zeros_like(queries),
        jnp.zeros(resp_keys.shape, jnp.float32),
        jnp.zeros(resp_keys.shape, jnp.float32),
        prompt_start,
        prompt_start,
        stats_start,
        stats_start,
        stats_start,
    )
    final_state = lax.fori_loop(0, block_count, main_step, start_state)
    (
        attended,
        query_grad,
        key_running,
        value_running,
        prompt_key_running,
        prompt_value_running,
        row_tops,
        row_totals,
        row_deltas,
    ) = final_state
    key_sum, value_sum = (
        lax.psum_scatter(prompt_key_running, "resp", scatter_dimension=0, tiled=True),
        lax.psum_scatter(prompt_value_running, "resp", scatter_dimension=0, tiled=True),
    )
    key_grad, value_grad = (
        lax.all_to_all(key_sum, "tensor", split_axis=0, concat_axis=1, tiled=True),
        lax.all_to_all(value_sum, "tensor", split_axis=0, concat_axis=1, tiled=True),
    )
    return (
        attended,
        query_grad,
        key_running.astype(jnp.bfloat16),
        value_running.astype(jnp.bfloat16),
        key_grad,
        value_grad,
    )


def solution(mesh):
    placed = (
        P(("group", "resp"), None, "tensor"),
        P(("group", "resp"), None, "tensor"),
        P(("group", "resp"), None, "tensor"),
        P(("group", "resp", "tensor"), None),
        P(("group", "resp", "tensor"), None),
        P(("group", "resp"), None, "tensor"),
        P(("group", "resp")),
    )
    return jax.shard_map(
        per_device,
        mesh=mesh,
        in_specs=placed,
        out_specs=(
            P(("group", "resp"), None, "tensor"),
            P(("group", "resp"), None, "tensor"),
            P(("group", "resp"), None, "tensor"),
            P(("group", "resp"), None, "tensor"),
            P(("group", "resp", "tensor"), None),
            P(("group", "resp", "tensor"), None),
        ),
        check_vma=False,
    )
```

profile of v0, /device:TPU:0, one launch (start us, length us, event | category | flops | bytes accessed | tf_op | source)
XLA Modules:
  0.0 559.2 jit_solution(14396727909907717286)
XLA Ops:
  8.7 54.8 %all-gather.3.cloned.1.call-done = bf16[2048,1024]{1,0:T(8,128)(2,1)} async-done(((bf16[128,1024]{1,0:T(8,128)(2,1)}), bf16[2048,1024]{1,0:T(8,128)(2,1)}) %all-gather.3.cloned.1.call-update) | async-done | bytes 4194320 | tf_op jit(solution)/shard_map/all_gather | solution.py:27
  64.7 50.0 %all-gather.5.cloned.1.call-done = bf16[2048,1024]{1,0:T(8,128)(2,1)} async-done(((bf16[128,1024]{1,0:T(8,128)(2,1)}), bf16[2048,1024]{1,0:T(8,128)(2,1)}) %all-gather.5.cloned.1.call-update) | async-done | bytes 4194320 | tf_op jit(solution)/shard_map/all_gather | solution.py:28
  114.7 2.3 constant_dynamic-slice_fusion
  123.4 326.4 %while.26 = (s32[]{:T(128)}, bf16[1,512,2048]{2,1,0:T(8,128)(2,1)}, bf16[1,512,2048]{2,1,0:T(8,128)(2,1)}, f32[1,512,256]{2,1,0:T(8,128)}, f32[1,512,256]{2,1,0:...) while((s32[]{:T(128)}, bf16[1,512,2048]{2,1,0:T(8,128)(2,1)}, ...), condition=%wide.region_6.7_spmd.clone, body=%wide.region_0.6_spmd.clone.sunk | while | flops 2033581056 | bytes 83544896 | solution.py:154
  125.3 1.7 multiply_reduce_fusion.4
  136.5 1.9 multiply_convert_fusion.2
  138.5 1.8 fusion.128
  141.0 1.8 fusion.127
  156.9 1.9 multiply_convert_fusion.2
  158.8 1.8 fusion.128
  161.4 1.8 fusion.127
  177.3 1.9 multiply_convert_fusion.2
  179.2 1.8 fusion.128
  181.8 1.8 fusion.127
  197.7 1.9 multiply_convert_fusion.2
  199.6 1.8 fusion.128
  202.2 1.8 fusion.127
  218.1 1.9 multiply_convert_fusion.2
  220.0 1.8 fusion.128
  222.6 1.8 fusion.127
  238.5 1.9 multiply_convert_fusion.2
  240.4 1.8 fusion.128
  242.9 1.8 fusion.127
  258.9 1.9 multiply_convert_fusion.2
  260.8 1.8 fusion.128
  263.3 1.8 fusion.127
  279.2 1.9 multiply_convert_fusion.2
  281.2 1.8 fusion.128
  283.7 1.8 fusion.127
  299.6 1.9 multiply_convert_fusion.2
  301.6 1.8 fusion.128
  304.1 1.8 fusion.127
  308.8 1.7 multiply_reduce_fusion.4
  320.1 1.9 multiply_convert_fusion.2
  322.0 1.8 fusion.128
  324.5 1.8 fusion.127
  329.2 1.7 multiply_reduce_fusion.4
  340.5 1.9 multiply_convert_fusion.2
  342.4 1.8 fusion.128
  344.9 1.8 fusion.127
  349.6 1.7 multiply_reduce_fusion.4
  360.9 1.9 multiply_convert_fusion.2
  362.8 1.8 fusion.128
  365.3 1.8 fusion.127
  370.0 1.7 multiply_reduce_fusion.4
  381.3 1.9 multiply_convert_fusion.2
  383.2 1.8 fusion.128
  385.8 1.8 fusion.127
  390.5 1.7 multiply_reduce_fusion.4
  401.7 1.9 multiply_convert_fusion.2
  403.6 1.8 fusion.128
  406.2 1.8 fusion.127
  410.9 1.7 multiply_reduce_fusion.4
  422.1 1.9 multiply_convert_fusion.2
  424.0 1.8 fusion.128
  426.6 1.8 fusion.127
  442.5 1.9 multiply_convert_fusion.2
  444.4 1.8 fusion.128
  447.0 1.8 fusion.127
  451.7 41.9 %reduce-scatter.3.cloned.1.call-done = f32[512,256]{1,0:T(8,128)} async-done(((f32[2048,256]{1,0:T(8,128)}), f32[512,256]{1,0:T(8,128)}) %reduce-scatter.3.cloned.1.call-update) | async-done | bytes 524304 | tf_op jit(solution)/shard_map/reduce_scatter | solution.py:167
  493.7 3.5 all-to-all-start
  497.2 42.0 %reduce-scatter.5.cloned.1.call-done = f32[512,256]{1,0:T(8,128)} async-done(((f32[2048,256]{1,0:T(8,128)}), f32[512,256]{1,0:T(8,128)}) %reduce-scatter.5.cloned.1.call-update) | async-done | bytes 524304 | tf_op jit(solution)/shard_map/reduce_scatter | solution.py:168
  539.1 3.5 all-to-all-start.1
  545.3 6.1 %all-to-all-done.1 = f32[4,128,256]{2,1,0:T(8,128)S(1)} async-done(((f32[4,128,256]{2,1,0:T(8,128)}), f32[4,128,256]{2,1,0:T(8,128)S(1)}, u32[]{:S(2)}, u32[]{:S(2)}) %all-to-all-start.1) | async-done | bytes 524320 | tf_op jit(solution)/shard_map/all_to_all | solution.py:172
  (535 shorter events, 239.4 us)
Async XLA Ops:
  7.2 56.3 %all-gather.3.cloned.1.call-start = ((), (), s32[]{:S(2)}) async-start(), calls=%async_computation.4 | async-start | bytes 4456448 | tf_op jit(solution)/shard_map/all_gather | solution.py:27
  7.9 106.8 %all-gather.5.cloned.1.call-start = ((), (), s32[]{:S(2)}) async-start(), calls=%async_computation.5 | async-start | bytes 4456448 | tf_op jit(solution)/shard_map/all_gather | solution.py:28
  8.6 485.0 %reduce-scatter.3.cloned.1.call-start = ((), (), s32[]{:S(2)}) async-start(), calls=%async_computation.6 | async-start | bytes 2621440 | tf_op jit(solution)/shard_map/reduce_scatter | solution.py:167
  121.8 1.6 copy-start.10
  133.9 1.4 copy-start.4
  136.5 1.9 copy-start.5
  136.5 1.9 copy-start.1
  140.3 2.5 copy-start.2
  154.3 1.4 copy-start.4
  156.9 1.9 copy-start.5
  156.9 1.9 copy-start.1
  160.7 2.5 copy-start.2
  174.7 1.4 copy-start.4
  177.3 1.9 copy-start.5
  177.3 1.9 copy-start.1
  181.1 2.5 copy-start.2
  195.0 1.4 copy-start.4
  197.7 1.9 copy-start.5
  197.7 1.9 copy-start.1
  201.4 2.5 copy-start.2
  215.4 1.4 copy-start.4
  218.1 1.9 copy-start.5
  218.1 1.9 copy-start.1
  221.8 2.5 copy-start.2
  238.5 1.9 copy-start.5
  238.5 1.9 copy-start.1
  242.2 2.5 copy-start.2
  258.8 1.9 copy-start.5
  258.9 1.9 copy-start.1
  262.6 2.5 copy-start.2
  276.6 1.4 copy-start.4
  279.2 1.9 copy-start.5
  279.2 1.9 copy-start.1
  283.0 2.5 copy-start.2
  297.0 1.4 copy-start.4
  299.6 1.9 copy-start.5
  299.6 1.9 copy-start.1
  303.4 2.5 copy-start.2
  320.0 1.9 copy-start.5
  320.0 1.9 copy-start.1
  323.8 2.5 copy-start.2
  340.4 1.9 copy-start.5
  340.5 1.9 copy-start.1
  344.2 2.5 copy-start.2
  360.9 1.9 copy-start.5
  360.9 1.9 copy-start.1
  364.6 2.5 copy-start.2
  381.3 1.9 copy-start.5
  381.3 1.9 copy-start.1
  385.0 2.5 copy-start.2
  401.7 1.9 copy-start.5
  401.7 1.9 copy-start.1
  405.4 2.5 copy-start.2
  422.1 1.9 copy-start.5
  422.1 1.9 copy-start.1
  425.8 2.5 copy-start.2
  442.5 1.9 copy-start.5
  442.5 1.9 copy-start.1
  446.3 2.5 copy-start.2
  451.2 88.0 %reduce-scatter.5.cloned.1.call-start = ((), (), s32[]{:S(2)}) async-start(), calls=%async_computation.7 | async-start | bytes 2621440 | tf_op jit(solution)/shard_map/reduce_scatter | solution.py:168
  451.2 91.4 %copy-start.6 = (f32[1,512,256]{2,1,0:T(8,128)S(1)}, f32[1,512,256]{2,1,0:T(8,128)}, u32[]{:S(2)}) copy-start(f32[1,512,256]{2,1,0:T(8,128)} %get-tuple-element.390) | copy-start | bytes 1572868
  451.2 92.1 %copy-start.9 = (f32[1,512,256]{2,1,0:T(8,128)S(1)}, f32[1,512,256]{2,1,0:T(8,128)}, u32[]{:S(2)}) copy-start(f32[1,512,256]{2,1,0:T(8,128)} %get-tuple-element.391) | copy-start | bytes 1572868
  493.7 45.5 %all-to-all-start = ((f32[4,128,256]{2,1,0:T(8,128)}), f32[4,128,256]{2,1,0:T(8,128)S(1)}, u32[]{:S(2)}, u32[]{:S(2)}) async-start(f32[4,128,256]{2,1,0:T(8,128)} %bitcast.115), calls=%async_computation.1 | async-start | bytes 1048576 | tf_op jit(solution)/shard_map/all_to_all | solution.py:171
  539.1 12.3 %all-to-all-start.1 = ((f32[4,128,256]{2,1,0:T(8,128)}), f32[4,128,256]{2,1,0:T(8,128)S(1)}, u32[]{:S(2)}, u32[]{:S(2)}) async-start(f32[4,128,256]{2,1,0:T(8,128)} %bitcast.114), calls=%async_computation.3 | async-start | bytes 1048576 | tf_op jit(solution)/shard_map/all_to_all | solution.py:172
  (74 other events, 89.4 us)
Sparse Core Ops, SparseCore 0:
  10.2 53.2 all-gather.2
  65.6 49.0 all-gather.4
  451.3 42.3 reduce-scatter.2
  495.9 43.1 reduce-scatter.4
where the time goes:
time: 564 us; the launch traced here: 559 us
  matrix products  254 us (45%)
  waiting for transfers between devices  197 us (35%)
  other arithmetic  59.7 us (11%)
  local copies, waits for them, and re-layouts  25.6 us (5%)
  between operations  13.8 us (2%)
  starting transfers between devices  7.09 us (1%)
    all_gather x1, waiting for transfers between devices, per_device(): lax.all_gather(prompt_keys, ('resp', 'tensor'), axis=0, tiled=True)  54.8 us
    all_gather x1, waiting for transfers between devices, per_device(): lax.all_gather(prompt_values, ('resp', 'tensor'), axis=0, tiled=True)  50 us
    reduce_scatter x1, waiting for transfers between devices, per_device(): lax.psum_scatter(prompt_value_running, 'resp', scatter_dimension=0, tiled...  42 us
    reduce_scatter x1, waiting for transfers between devices, per_device(): lax.psum_scatter(prompt_key_running, 'resp', scatter_dimension=0, tiled=T...  41.9 us
    dot_general x16, matrix products, main_step(): jnp.einsum('qd,kd->qk', live_grad, value_prompt, preferred_element_type=j...  30.3 us
    dot_general x16, matrix products, main_step(): jnp.einsum('qk,qd->kd', weight_prompt, live_grad, preferred_element_type=...  29 us
    dot_general x16, matrix products, main_step(): jnp.einsum('qk,qd->kd', sgrad_prompt, query_rows, preferred_element_type=...  28.2 us
    dot_general x16, matrix products, main_step(): jnp.einsum('qd,kd->qk', query_rows, key_prompt, preferred_element_type=jn...  27.2 us
  transfers between devices with their start and end apart: 6, of which 5 were waited for; matrix products, arithmetic and copies ran while one was open for 1% of the time, Pallas kernels for 0%

commit v1 on v0

v1 whole, which is shorter than its diff:
```python
import functools
import math

import jax
import jax.numpy as jnp
from jax import lax
from jax.experimental import pallas as pl
from jax.experimental.pallas import tpu as pltpu
from jax.sharding import PartitionSpec as P

HD = 128
BF16 = jnp.bfloat16
F32 = jnp.float32


def dot(a, b):
    return jnp.dot(a, b, preferred_element_type=F32)


def attention_kernel(
    parts,
    heads_per,
    len_ref,
    q_ref,
    g_ref,
    cache_ref,
    kr_ref,
    vr_ref,
    *rest,
):
    (
        out_ref,
        dq_ref,
        dkr_ref,
        dvr_ref,
        dcache_ref,
        keys,
        values,
        keys_t,
        values_t,
        exps,
        dprobs,
        weights,
        dk_sum,
        dv_sum,
        tops,
        sums,
    ) = rest[-16:]
    rows = q_ref.shape[0]
    part_rows = cache_ref.shape[2]
    prompt_rows = parts * part_rows
    chunk = rows
    prompt_chunks = prompt_rows // chunk
    chunks = prompt_chunks + 1
    factor = HD ** (-0.5)
    factor2 = factor * math.log2(math.e)
    length = len_ref[0]
    step = pl.program_id(0)

    @pl.when(step == 0)
    def _():
        for p in range(parts):
            at = pl.ds(p * part_rows, part_rows)
            keys[at, :] = cache_ref[p, 0]
            values[at, :] = cache_ref[p, 1]
            keys_t[:, at] = cache_ref[p, 0].astype(F32).T.astype(BF16)
            values_t[:, at] = cache_ref[p, 1].astype(F32).T.astype(BF16)
        at = pl.ds(prompt_rows, rows)
        keys[at, :] = kr_ref[...]
        values[at, :] = vr_ref[...]
        keys_t[:, at] = kr_ref[...].astype(F32).T.astype(BF16)
        values_t[:, at] = vr_ref[...].astype(F32).T.astype(BF16)
        dk_sum[...] = jnp.zeros_like(dk_sum)
        dv_sum[...] = jnp.zeros_like(dv_sum)

    live_rows = lax.broadcasted_iota(jnp.int32, (rows, HD), 0) < length
    live_grad = jnp.where(live_rows, g_ref[...].astype(F32), 0.0)
    grad = live_grad.astype(BF16)
    grad_t32 = live_grad.T
    grad_t = grad_t32.astype(BF16)
    query = q_ref[...]
    query_t = query.astype(F32).T.astype(BF16)

    def first(c, masked):
        at = pl.ds(pl.multiple_of(c * chunk, chunk), chunk)
        score = dot(keys[at, :], query_t)
        if masked:
            j = lax.broadcasted_iota(jnp.int32, (chunk, rows), 0)
            i = lax.broadcasted_iota(jnp.int32, (chunk, rows), 1)
            score = jnp.where((j <= i) & (j < length), score, -jnp.inf)
        top = jnp.max(score, axis=0, keepdims=True) * factor2
        exp = jnp.exp2(score * factor2 - top)
        exps[at, :] = exp
        tops[pl.ds(c, 1), :] = top
        sums[pl.ds(c, 1), :] = jnp.sum(exp, axis=0, keepdims=True)
        dprobs[at, :] = dot(values[at, :], grad_t)

    def first_step(c, carry):
        first(c, False)
        return carry

    lax.fori_loop(0, prompt_chunks, first_step, 0)
    first(prompt_chunks, True)

    top = jnp.max(tops[:chunks, :], axis=0, keepdims=True)
    scale = jnp.exp2(tops[:chunks, :] - top)
    total = jnp.sum(scale * sums[:chunks, :], axis=0, keepdims=True)
    sums[:chunks, :] = scale / total

    def second_step(c, mixture):
        at = pl.ds(pl.multiple_of(c * chunk, chunk), chunk)
        weight = (exps[at, :] * sums[pl.ds(c, 1), :]).astype(BF16)
        weights[at, :] = weight
        return mixture + dot(values_t[:, at], weight)

    mixture = lax.fori_loop(0, chunks, second_step, jnp.zeros((HD, rows), F32))
    live_lanes = lax.broadcasted_iota(jnp.int32, (HD, rows), 1) < length
    attended = jnp.where(live_lanes, mixture, 0.0).astype(BF16).astype(F32)
    out_ref[...] = attended.T.astype(BF16)
    delta = jnp.sum(grad_t32 * attended, axis=0, keepdims=True)

    def third_step(c, dquery):
        at = pl.ds(pl.multiple_of(c * chunk, chunk), chunk)
        frac = exps[at, :] * sums[pl.ds(c, 1), :]
        sgrad = (frac * (dprobs[at, :] - delta)).astype(BF16)
        dk_sum[at, :] += dot(sgrad, query)
        dv_sum[at, :] += dot(weights[at, :], grad)
        return dquery + dot(keys_t[:, at], sgrad)

    dquery = lax.fori_loop(0, chunks, third_step, jnp.zeros((HD, rows), F32))
    dq_ref[...] = (factor * dquery).T.astype(BF16)

    @pl.when(step == heads_per - 1)
    def _():
        for p in range(parts):
            at = pl.ds(p * part_rows, part_rows)
            dcache_ref[p, 0] = (factor * dk_sum[at, :]).astype(BF16)
            dcache_ref[p, 1] = dv_sum[at, :].astype(BF16)
        at = pl.ds(prompt_rows, rows)
        dkr_ref[...] = (factor * dk_sum[at, :]).astype(BF16)
        dvr_ref[...] = dv_sum[at, :].astype(BF16)


def attend(pair, heads_per, lengths, queries, out_grad, cache, resp_keys, resp_values, earlier):
    rows, query_width = queries.shape
    parts = cache.shape[0]
    prompt_rows = parts * cache.shape[2]
    total_rows = prompt_rows + rows
    head_block = pl.BlockSpec((rows, HD), lambda s: (0, pair * heads_per + s))
    pair_block = pl.BlockSpec((rows, HD), lambda s: (0, pair))
    cache_block = pl.BlockSpec(cache.shape, lambda s: (0, 0, 0, 0))
    chunk_rows = -(-(prompt_rows // rows + 1) // 8) * 8
    in_specs = [
        pl.BlockSpec(memory_space=pltpu.SMEM),
        head_block,
        head_block,
        cache_block,
        pair_block,
        pair_block,
    ] + [pl.BlockSpec(memory_space=pl.ANY)] * len(earlier)
    aliases = {6 + i: i for i in range(len(earlier))}
    return pl.pallas_call(
        functools.partial(attention_kernel, parts, heads_per),
        grid=(heads_per,),
        in_specs=in_specs,
        out_specs=[head_block, head_block, pair_block, pair_block, cache_block],
        out_shape=[
            jax.ShapeDtypeStruct(queries.shape, BF16),
            jax.ShapeDtypeStruct(queries.shape, BF16),
            jax.ShapeDtypeStruct(resp_keys.shape, BF16),
            jax.ShapeDtypeStruct(resp_keys.shape, BF16),
            jax.ShapeDtypeStruct(cache.shape, BF16),
        ],
        scratch_shapes=[
            pltpu.VMEM((total_rows, HD), BF16),
            pltpu.VMEM((total_rows, HD), BF16),
            pltpu.VMEM((HD, total_rows), BF16),
            pltpu.VMEM((HD, total_rows), BF16),
            pltpu.VMEM((total_rows, rows), F32),
            pltpu.VMEM((total_rows, rows), F32),
            pltpu.VMEM((total_rows, rows), BF16),
            pltpu.VMEM((total_rows, HD), F32),
            pltpu.VMEM((total_rows, HD), F32),
            pltpu.VMEM((chunk_rows, rows), F32),
            pltpu.VMEM((chunk_rows, rows), F32),
        ],
        input_output_aliases=aliases,
        cost_estimate=pl.CostEstimate(
            flops=12 * heads_per * rows * total_rows * HD,
            bytes_accessed=8 * heads_per * rows * HD,
            transcendentals=heads_per * rows * total_rows,
        ),
        compiler_params=pltpu.CompilerParams(vmem_limit_bytes=48 * 1024 * 1024),
        name=f"attend_pair_{pair}",
    )(lengths, queries, out_grad, cache, resp_keys, resp_values, *earlier)


def per_device(queries, resp_keys, resp_values, prompt_keys, prompt_values, out_grad, lengths):
    _, seq_len, query_width = queries.shape
    pair_width = resp_keys.shape[2]
    pairs = pair_width // HD
    heads_per = query_width // pair_width
    queries, out_grad, resp_keys, resp_values = (
        a[0] for a in (queries, out_grad, resp_keys, resp_values)
    )
    own = jnp.stack([prompt_keys, prompt_values])
    own = lax.all_to_all(own, "tensor", split_axis=2, concat_axis=1, tiled=True)
    caches = [
        lax.all_gather(own[:, :, p * HD : (p + 1) * HD], "resp", axis=0) for p in range(pairs)
    ]
    earlier = ()
    sums = []
    for p in range(pairs):
        *earlier, dcache = attend(
            p, heads_per, lengths, queries, out_grad, caches[p], resp_keys, resp_values, earlier
        )
        sums.append(lax.psum_scatter(dcache, "resp", scatter_dimension=0))
    sums = jnp.concatenate(sums, axis=2)
    sums = lax.all_to_all(sums, "tensor", split_axis=1, concat_axis=2, tiled=True).astype(F32)
    return (*(a[None] for a in earlier), sums[0], sums[1])


def solution(mesh):
    rows = P(("group", "resp"), None, "tensor")
    prompt = P(("group", "resp", "tensor"), None)
    return jax.shard_map(
        per_device,
        mesh=mesh,
        in_specs=(rows, rows, rows, prompt, prompt, rows, P(("group", "resp"))),
        out_specs=(rows, rows, rows, rows, prompt, prompt),
        check_vma=False,
    )
```

time: 564 us -> 260 us (0.46)
  matrix products: 254 us -> 0 us
  Pallas kernels: 0 us -> 126 us
  waiting for transfers between devices: 197 us -> 83 us
  other arithmetic: 59.7 us -> 2.53 us
  blocking collectives: 0 us -> 24.5 us
  local copies, waits for them, and re-layouts: 25.6 us -> 8.87 us
  starting transfers between devices: 7.09 us -> 0.16 us
    dot_general x192 -> x0, matrix products: 254 us -> none  [the longest x16 30.3 us: main_step(): jnp.einsum('qd,kd->qk', live_grad, value_prompt, preferred_element_type=j...]
    pallas_call x0 -> x2, Pallas kernels: none -> 126 us  [attend(): pl.pallas_call(functools.partial(attention_kernel, parts, heads_per), gri...]
    all_gather x2, waiting for transfers between devices: 105 us -> 27.4 us  [per_device(): lax.all_gather(own[:, :, p * HD:(p + 1) * HD], 'resp', axis=0)]
    reduce_sum x48 -> x0, other arithmetic: 34.5 us -> none  [the longest x16 18.2 us: main_step(): jnp.sum(live_grad.astype(jnp.float32) * lax.optimization_barrier(out_bloc...]
    reduce_scatter x2, waiting for transfers between devices: 83.9 us -> 54.3 us  [per_device(): sums.append(lax.psum_scatter(dcache, 'resp', scatter_dimension=0))]
    all_to_all x0 -> x2, blocking collectives: none -> 24.5 us  [the longest x1 13.1 us: per_device(): own = lax.all_to_all(own, 'tensor', split_axis=2, concat_axis=1, tiled=True)]
    div x16 -> x0, other arithmetic: 13.2 us -> none  [main_step(): frac_prompt = exp_prompt / row_total[:, None]]
    while x256 -> x0, local copies, waits for them, and re-layouts: 11.9 us -> none
  transfers between devices with their start and end apart: 6 -> 4, of which waited for: 5 -> 3; matrix products, arithmetic and copies ran while one was open for 1% -> 0% of each run, Pallas kernels for 0% -> 24%
where the time goes in v1:
time: 260 us; the launch traced here: 259 us
  Pallas kernels  126 us (48%)
  waiting for transfers between devices  83 us (32%)
  blocking collectives  24.5 us (9%)
  between operations  14.5 us (6%)
  local copies, waits for them, and re-layouts  8.87 us (3%)
    pallas_call x2, Pallas kernels, attend(): pl.pallas_call(functools.partial(attention_kernel, parts, heads_per), gri...  126 us
    reduce_scatter x2, waiting for transfers between devices, per_device(): sums.append(lax.psum_scatter(dcache, 'resp', scatter_dimension=0))  54.3 us
    all_gather x2, waiting for transfers between devices, per_device(): lax.all_gather(own[:, :, p * HD:(p + 1) * HD], 'resp', axis=0)  27.4 us
    all_to_all x1, blocking collectives, per_device(): own = lax.all_to_all(own, 'tensor', split_axis=2, concat_axis=1, tiled=True)  13.1 us
    all_to_all x1, blocking collectives, per_device(): lax.all_to_all(sums, 'tensor', split_axis=1, concat_axis=2, tiled=True)  11.4 us
  transfers between devices with their start and end apart: 4, of which 3 were waited for; matrix products, arithmetic and copies ran while one was open for 0% of the time, Pallas kernels for 24%

profile of v1, /device:TPU:0, one launch (start us, length us, event | category | flops | bytes accessed | tf_op | source)
XLA Modules:
  0.0 259.4 jit_solution(14328010420867920040)
XLA Ops:
  7.2 0.0 all-gather.7.cloned.1.call-start
  7.2 1.1 pad_maximum_fusion
  8.3 0.4 copy.26
  8.7 0.0 copy-start
  8.7 0.0 copy-start.3
  8.7 0.0 copy-start.4
  8.8 13.1 %all_to_all.27 = bf16[2,128,1024]{1,0,2:T(2,128)(2,1)} all-to-all(bf16[2,128,1024]{1,0,2:T(2,128)(2,1)S(1)} %copy.26), channel_id=1, replica_groups=mesh['group'=2,'resp'=4,'tensor'=4] {'tensor'}, dimensions={2} | all-to-all | bytes 1048576 | tf_op jit(solution)/shard_map/all_to_all | solution.py:207
  21.8 1.3 copy.27
  23.2 0.9 fusion.1
  24.0 0.0 all-gather.7.cloned.1.call-update
  24.1 0.0 all-gather.5.cloned.1.call-start
  24.1 0.7 all-gather.5.cloned.1.call-update
  24.8 0.0 reduce-scatter.5.cloned.1.call-start
  25.5 27.4 %all-gather.7.cloned.1.call-done = bf16[8,512,128]{2,1,0:T(8,128)(2,1)} async-done(((bf16[2,512,128]{2,1,0:T(8,128)(2,1)}), bf16[8,512,128]{2,1,0:T(8,128)(2,1)}) %all-gather.7.cloned.1.call-update) | async-done | bytes 1048592 | tf_op jit(solution)/shard_map/all_gather | solution.py:209
  52.9 0.0 copy-done
  52.9 0.0 copy-done.3
  52.9 0.0 copy-done.4
  52.9 0.0 copy-start.1
  52.9 1.2 copy-done.1
  54.1 62.9 %attend_pair_0.1 = (bf16[512,2048]{1,0:T(8,128)(2,1)}, bf16[512,2048]{1,0:T(8,128)(2,1)}, bf16[512,256]{1,0:T(8,128)(2,1)}, bf16[512,256]{1,0:T(8,128)(2,1)}, bf16[4,2,512,128]{3,2,1,0:T(8,128)(2,1)}) custom-call(s32[1]{0:T(128)S(6)} %copy.37.len_ref, bf16[512,2048]{1,0:T(8,128)(2,1)S(1)} %bitcast.28, bf16[512,2048]{1,0:T(8,128)(2,1)} %bitcast.47, ...), custom_call_target="tpu_custom_call" | custom-call | flops 16106127360 | bytes 4194304 | tf_op jit(solution)/shard_map/attend_pair_0/pallas_call | solution.py:162
  117.0 0.0 all-gather.5.cloned.1.call-done
  117.1 0.0 copy-start.2
  117.1 1.2 copy-done.2
  118.3 63.0 %attend_pair_1.1 = (bf16[512,2048]{1,0:T(8,128)(2,1)}, bf16[512,2048]{1,0:T(8,128)(2,1)}, bf16[512,256]{1,0:T(8,128)(2,1)}, bf16[512,256]{1,0:T(8,128)(2,1)}, bf16[4,2,512,128]{3,2,1,0:T(8,128)(2,1)}) custom-call(s32[1]{0:T(128)S(6)} %copy.37.len_ref, ...), custom_call_target="tpu_custom_call", output_to_operand_aliasing={{0}: (6, {}), {1}: (7, {}), {2}: (8, {}), {3}: (9, {})} | custom-call | flops 16106127360 | bytes 4194304 | tf_op jit(solution)/shard_map/attend_pair_1/pallas_call | solution.py:162
  181.2 0.0 reduce-scatter.5.cloned.1.call-update
  181.3 0.0 reduce-scatter.3.cloned.1.call-start
  181.3 0.5 reduce-scatter.3.cloned.1.call-update
  181.9 26.2 %reduce-scatter.5.cloned.1.call-done = bf16[1,2,512,128]{3,2,1,0:T(8,128)(2,1)} async-done(((bf16[4,2,512,128]{3,2,1,0:T(8,128)(2,1)}), bf16[1,2,512,128]{3,2,1,0:T(8,128)(2,1)}) %reduce-scatter.5.cloned.1.call-update) | async-done | bytes 262160 | tf_op jit(solution)/shard_map/reduce_scatter | solution.py:217
  208.1 28.1 %reduce-scatter.3.cloned.1.call-done = bf16[1,2,512,128]{3,2,1,0:T(8,128)(2,1)} async-done(((bf16[4,2,512,128]{3,2,1,0:T(8,128)(2,1)}), bf16[1,2,512,128]{3,2,1,0:T(8,128)(2,1)}) %reduce-scatter.3.cloned.1.call-update) | async-done | bytes 262160 | tf_op jit(solution)/shard_map/reduce_scatter | solution.py:217
  236.1 1.1 pad_maximum_fusion.1
  237.2 0.5 copy.28
  237.8 11.4 %all_to_all.28 = bf16[2,512,256]{2,0,1:T(2,128)(2,1)S(1)} all-to-all(bf16[2,512,256]{2,0,1:T(2,128)(2,1)S(1)} %copy.28), channel_id=1, replica_groups=mesh['group'=2,'resp'=4,'tensor'=4] {'tensor'}, dimensions={1} | all-to-all | bytes 1048576 | tf_op jit(solution)/shard_map/all_to_all | solution.py:219
  249.2 0.4 convert_bitcast_fusion
  249.5 0.8 fusion
  250.4 0.3 copy.30
  250.7 0.9 copy.32
  251.6 0.3 copy.29
  251.9 0.9 copy.31
Async XLA Ops:
  7.2 45.7 %all-gather.7.cloned.1.call-start = ((), (), s32[]{:S(2)}) async-start(), calls=%async_computation.7 | async-start | bytes 1310720 | tf_op jit(solution)/shard_map/all_gather | solution.py:209
  8.7 44.2 %copy-start = (bf16[1,512,2048]{2,1,0:T(8,128)(2,1)S(1)}, bf16[1,512,2048]{2,1,0:T(8,128)(2,1)}, u32[]{:S(2)}) copy-start(bf16[1,512,2048]{2,1,0:T(8,128)(2,1)} %param.7) | copy-start | bytes 6291460
  8.7 44.2 %copy-start.3 = (bf16[1,512,256]{2,1,0:T(8,128)(2,1)S(1)}, bf16[1,512,256]{2,1,0:T(8,128)(2,1)}, u32[]{:S(2)}) copy-start(bf16[1,512,256]{2,1,0:T(8,128)(2,1)} %param.8) | copy-start | bytes 786436
  8.7 44.2 %copy-start.4 = (bf16[1,512,256]{2,1,0:T(8,128)(2,1)S(1)}, bf16[1,512,256]{2,1,0:T(8,128)(2,1)}, u32[]{:S(2)}) copy-start(bf16[1,512,256]{2,1,0:T(8,128)(2,1)} %param.9) | copy-start | bytes 786436
  24.1 93.0 %all-gather.5.cloned.1.call-start = ((), (), s32[]{:S(2)}) async-start(), calls=%async_computation.6 | async-start | bytes 1310720 | tf_op jit(solution)/shard_map/all_gather | solution.py:209
  24.8 183.3 %reduce-scatter.5.cloned.1.call-start = ((), (), s32[]{:S(2)}) async-start(), calls=%async_computation.5 | async-start | bytes 1310720 | tf_op jit(solution)/shard_map/reduce_scatter | solution.py:217
  52.9 1.2 copy-start.1
  117.1 1.2 copy-start.2
  181.3 54.9 %reduce-scatter.3.cloned.1.call-start = ((), (), s32[]{:S(2)}) async-start(), calls=%async_computation.4 | async-start | bytes 1310720 | tf_op jit(solution)/shard_map/reduce_scatter | solution.py:217
Sparse Core Ops, SparseCore 0:
  24.2 28.6 all-gather.6
  55.0 27.3 all-gather.4
  181.4 26.6 reduce-scatter.4
  210.3 25.7 reduce-scatter.2

commit v2 on v1

v2 whole, which is shorter than its diff:
```python
import functools
import math

import jax
import jax.numpy as jnp
from jax import lax
from jax.experimental import pallas as pl
from jax.experimental.pallas import tpu as pltpu
from jax.sharding import PartitionSpec as P

HD = 128
SUB = 128
LOWEST = -1e30
BF16 = jnp.bfloat16
F32 = jnp.float32


def dot(a, b):
    return jnp.dot(a, b, preferred_element_type=F32)


def attention_kernel(
    parts,
    heads_per,
    len_ref,
    q_ref,
    g_ref,
    cache_ref,
    kr_ref,
    vr_ref,
    *rest,
):
    (
        out_ref,
        dq_ref,
        dkr_ref,
        dvr_ref,
        dcache_ref,
        keys,
        values,
        keys_t,
        values_t,
        query,
        query_t,
        grad,
        grad_t,
        exps_even,
        exps_odd,
        fracs,
        deltas,
        dk_sum,
        dv_sum,
        dq_sum,
        tops,
        sums,
    ) = rest[-22:]
    rows = q_ref.shape[0]
    part_rows = cache_ref.shape[2]
    prompt_rows = parts * part_rows
    chunk = rows
    blocks = chunk // SUB
    prompt_chunks = prompt_rows // chunk
    chunks = prompt_chunks + 1
    stats = chunks * blocks
    factor = HD ** (-0.5)
    factor2 = factor * math.log2(math.e)
    length = len_ref[0]
    step = pl.program_id(0)
    slots = (exps_even, exps_odd)

    @pl.when(step == 0)
    def _():
        for p in range(parts):
            at = pl.ds(p * part_rows, part_rows)
            keys[at, :] = cache_ref[p, 0]
            values[at, :] = cache_ref[p, 1]
            keys_t[:, at] = cache_ref[p, 0].astype(F32).T.astype(BF16)
            values_t[:, at] = cache_ref[p, 1].astype(F32).T.astype(BF16)
        at = pl.ds(prompt_rows, rows)
        keys[at, :] = kr_ref[...]
        values[at, :] = vr_ref[...]
        keys_t[:, at] = kr_ref[...].astype(F32).T.astype(BF16)
        values_t[:, at] = vr_ref[...].astype(F32).T.astype(BF16)
        dk_sum[...] = jnp.zeros_like(dk_sum)
        dv_sum[...] = jnp.zeros_like(dv_sum)

    def rows_at(c):
        return pl.ds(pl.multiple_of(c * chunk, chunk), chunk)

    def score_part(now, c, masked):
        score = dot(keys[rows_at(c), :], query_t[now])
        if masked:
            j = lax.broadcasted_iota(jnp.int32, (chunk, rows), 0)
            i = lax.broadcasted_iota(jnp.int32, (chunk, rows), 1)
            score = jnp.where((j <= i) & (j < length), score, -jnp.inf)
        for u in range(blocks):
            block = score[u * SUB : (u + 1) * SUB, :]
            top = jnp.max(block, axis=0, keepdims=True)
            top = jnp.maximum(top, LOWEST) * factor2
            exp = jnp.exp2(block * factor2 - top)
            slots[now][pl.ds(pl.multiple_of(c * chunk + u * SUB, SUB), SUB), :] = exp
            tops[pl.ds(c * blocks + u, 1), :] = top
            sums[pl.ds(c * blocks + u, 1), :] = jnp.sum(exp, axis=0, keepdims=True)

    def scaled(slot, c, u):
        at = pl.ds(pl.multiple_of(c * chunk + u * SUB, SUB), SUB)
        return slots[slot][at, :] * fracs[slot, pl.ds(c * blocks + u, 1), :]

    def grad_part(before, c):
        at = rows_at(c)
        dprob = dot(values[at, :], grad_t[before])
        delta = deltas[before]
        weight, sgrad = [], []
        for u in range(blocks):
            frac = scaled(before, c, u)
            weight.append(frac.astype(BF16))
            sgrad.append((frac * (dprob[u * SUB : (u + 1) * SUB, :] - delta)).astype(BF16))
        weight, sgrad = jnp.concatenate(weight, 0), jnp.concatenate(sgrad, 0)
        dv_sum[at, :] += dot(weight, grad[before])
        dk_sum[at, :] += dot(sgrad, query[before])
        dq_sum[...] += dot(keys_t[:, at], sgrad)

    def run(now, with_score, with_grad):
        def body(c, carry, masked=False):
            if with_score:
                score_part(now, c, masked)
            if with_grad:
                grad_part(1 - now, c)
            return carry

        if with_grad:
            dq_sum[...] = jnp.zeros_like(dq_sum)
        lax.fori_loop(0, prompt_chunks, body, 0)
        body(prompt_chunks, 0, True)
        if with_grad:
            dq_ref[...] = (factor * dq_sum[...]).T.astype(BF16)

    def prepare(now):
        live_rows = lax.broadcasted_iota(jnp.int32, (rows, HD), 0) < length
        live_grad = jnp.where(live_rows, g_ref[...].astype(F32), 0.0)
        grad[now] = live_grad.astype(BF16)
        grad_t[now] = live_grad.T.astype(BF16)
        query[now] = q_ref[...]
        query_t[now] = q_ref[...].astype(F32).T.astype(BF16)

    def finish(now):
        top = jnp.max(tops[:stats, :], axis=0, keepdims=True)
        scale = jnp.exp2(tops[:stats, :] - top)
        total = jnp.sum(scale * sums[:stats, :], axis=0, keepdims=True)
        fracs[now, :stats, :] = scale / total

        mixture = jnp.zeros((HD, rows), F32)
        for c in range(chunks):
            weight = jnp.concatenate(
                [scaled(now, c, u).astype(BF16) for u in range(blocks)], 0
            )
            mixture = mixture + dot(values_t[:, c * chunk : (c + 1) * chunk], weight)
        live_lanes = lax.broadcasted_iota(jnp.int32, (HD, rows), 1) < length
        attended = jnp.where(live_lanes, mixture, 0.0).astype(BF16).astype(F32)
        out_ref[...] = attended.T.astype(BF16)
        deltas[now] = jnp.sum(grad_t[now].astype(F32) * attended, axis=0, keepdims=True)

    @pl.when(step == 0)
    def _():
        prepare(0)
        run(0, True, False)
        finish(0)

    for now in range(2):
        @pl.when((step > 0) & (step < heads_per) & (lax.rem(step, 2) == now))
        def _():
            prepare(now)
            run(now, True, True)
            finish(now)

    @pl.when(step == heads_per)
    def _():
        run(heads_per % 2, False, True)

    @pl.when(step == heads_per)
    def _():
        for p in range(parts):
            at = pl.ds(p * part_rows, part_rows)
            dcache_ref[p, 0] = (factor * dk_sum[at, :]).astype(BF16)
            dcache_ref[p, 1] = dv_sum[at, :].astype(BF16)
        at = pl.ds(prompt_rows, rows)
        dkr_ref[...] = (factor * dk_sum[at, :]).astype(BF16)
        dvr_ref[...] = dv_sum[at, :].astype(BF16)


def attend(pair, heads_per, lengths, queries, out_grad, cache, resp_keys, resp_values, earlier):
    rows, query_width = queries.shape
    parts = cache.shape[0]
    prompt_rows = parts * cache.shape[2]
    total_rows = prompt_rows + rows
    first, last = pair * heads_per, (pair + 1) * heads_per - 1
    head_block = pl.BlockSpec((rows, HD), lambda s: (0, jnp.minimum(first + s, last)))
    late_block = pl.BlockSpec((rows, HD), lambda s: (0, jnp.maximum(first + s - 1, first)))
    pair_block = pl.BlockSpec((rows, HD), lambda s: (0, pair))
    cache_block = pl.BlockSpec(cache.shape, lambda s: (0, 0, 0, 0))
    stats = -(-total_rows // SUB // 8) * 8
    in_specs = [
        pl.BlockSpec(memory_space=pltpu.SMEM),
        head_block,
        head_block,
        cache_block,
        pair_block,
        pair_block,
    ] + [pl.BlockSpec(memory_space=pl.ANY)] * len(earlier)
    aliases = {6 + i: i for i in range(len(earlier))}
    return pl.pallas_call(
        functools.partial(attention_kernel, parts, heads_per),
        grid=(heads_per + 1,),
        in_specs=in_specs,
        out_specs=[head_block, late_block, pair_block, pair_block, cache_block],
        out_shape=[
            jax.ShapeDtypeStruct(queries.shape, BF16),
            jax.ShapeDtypeStruct(queries.shape, BF16),
            jax.ShapeDtypeStruct(resp_keys.shape, BF16),
            jax.ShapeDtypeStruct(resp_keys.shape, BF16),
            jax.ShapeDtypeStruct(cache.shape, BF16),
        ],
        scratch_shapes=[
            pltpu.VMEM((total_rows, HD), BF16),
            pltpu.VMEM((total_rows, HD), BF16),
            pltpu.VMEM((HD, total_rows), BF16),
            pltpu.VMEM((HD, total_rows), BF16),
            pltpu.VMEM((2, rows, HD), BF16),
            pltpu.VMEM((2, HD, rows), BF16),
            pltpu.VMEM((2, rows, HD), BF16),
            pltpu.VMEM((2, HD, rows), BF16),
            pltpu.VMEM((total_rows, rows), F32),
            pltpu.VMEM((total_rows, rows), F32),
            pltpu.VMEM((2, stats, rows), F32),
            pltpu.VMEM((2, 1, rows), F32),
            pltpu.VMEM((total_rows, HD), F32),
            pltpu.VMEM((total_rows, HD), F32),
            pltpu.VMEM((HD, rows), F32),
            pltpu.VMEM((stats, rows), F32),
            pltpu.VMEM((stats, rows), F32),
        ],
        input_output_aliases=aliases,
        cost_estimate=pl.CostEstimate(
            flops=12 * heads_per * rows * total_rows * HD,
            bytes_accessed=8 * heads_per * rows * HD,
            transcendentals=heads_per * rows * total_rows,
        ),
        compiler_params=pltpu.CompilerParams(vmem_limit_bytes=48 * 1024 * 1024),
        name=f"attend_pair_{pair}",
    )(lengths, queries, out_grad, cache, resp_keys, resp_values, *earlier)


def whole_block(shape):
    return pl.BlockSpec(shape, lambda: (0,) * len(shape))


def cut_kernel(width, k_ref, v_ref, *outs):
    me = lax.axis_index("tensor")
    for i, out in enumerate(outs):
        columns = pl.ds(pl.multiple_of((me ^ i) * width, width), width)
        out[0] = k_ref[:, columns]
        out[1] = v_ref[:, columns]


def cut(prompt_keys, prompt_values, width):
    rows, columns = prompt_keys.shape
    count = columns // width
    return pl.pallas_call(
        functools.partial(cut_kernel, width),
        in_specs=[whole_block((rows, columns))] * 2,
        out_specs=[whole_block((2, rows, width))] * count,
        out_shape=[jax.ShapeDtypeStruct((2, rows, width), BF16)] * count,
        name="cut",
    )(prompt_keys, prompt_values)


def line_up_kernel(ins, *refs):
    ins, outs = refs[:ins], refs[ins:]
    for i, block in enumerate(ins):
        rows = block.shape[1]
        for p, out in enumerate(outs):
            out[:, i * rows : (i + 1) * rows, :] = block[:, :, p * HD : (p + 1) * HD]


def line_up(blocks):
    _, rows, width = blocks[0].shape
    shape = (2, rows * len(blocks), HD)
    return pl.pallas_call(
        functools.partial(line_up_kernel, len(blocks)),
        in_specs=[whole_block(blocks[0].shape)] * len(blocks),
        out_specs=[whole_block(shape)] * (width // HD),
        out_shape=[jax.ShapeDtypeStruct(shape, BF16)] * (width // HD),
        name="line_up",
    )(*blocks)


def split_kernel(ins, *refs):
    ins, outs = refs[:ins], refs[ins:]
    for p, block in enumerate(ins):
        for i, out in enumerate(outs):
            rows = out.shape[1]
            out[:, :, p * HD : (p + 1) * HD] = block[:, i * rows : (i + 1) * rows, :]


def split(sums, rows):
    count = sums[0].shape[1] // rows
    shape = (2, rows, HD * len(sums))
    return pl.pallas_call(
        functools.partial(split_kernel, len(sums)),
        in_specs=[whole_block(sums[0].shape)] * len(sums),
        out_specs=[whole_block(shape)] * count,
        out_shape=[jax.ShapeDtypeStruct(shape, BF16)] * count,
        name="split",
    )(*sums)


def place_kernel(*refs):
    *ins, dk_ref, dv_ref = refs
    me = lax.axis_index("tensor")
    for i, block in enumerate(ins):
        width = block.shape[2]
        columns = pl.ds(pl.multiple_of((me ^ i) * width, width), width)
        dk_ref[:, columns] = block[0].astype(F32)
        dv_ref[:, columns] = block[1].astype(F32)


def place(blocks):
    _, rows, width = blocks[0].shape
    shape = (rows, width * len(blocks))
    return pl.pallas_call(
        place_kernel,
        in_specs=[whole_block(blocks[0].shape)] * len(blocks),
        out_specs=[whole_block(shape)] * 2,
        out_shape=[jax.ShapeDtypeStruct(shape, F32)] * 2,
        name="place",
    )(*blocks)


def exchange(blocks):
    count = len(blocks)
    return [blocks[0]] + [
        lax.ppermute(blocks[i], "tensor", [(j, j ^ i) for j in range(count)])
        for i in range(1, count)
    ]


def per_device(queries, resp_keys, resp_values, prompt_keys, prompt_values, out_grad, lengths):
    _, seq_len, query_width = queries.shape
    pair_width = resp_keys.shape[2]
    pairs = pair_width // HD
    heads_per = query_width // pair_width
    queries, out_grad, resp_keys, resp_values = (
        a[0] for a in (queries, out_grad, resp_keys, resp_values)
    )
    own = line_up(exchange(cut(prompt_keys, prompt_values, pair_width)))
    caches = [lax.all_gather(own[p], "resp", axis=0) for p in range(pairs)]
    earlier = ()
    sums = []
    for p in range(pairs):
        *earlier, dcache = attend(
            p, heads_per, lengths, queries, out_grad, caches[p], resp_keys, resp_values, earlier
        )
        if sums:
            dcache, sums[-1] = lax.optimization_barrier((dcache, sums[-1]))
        sums.append(lax.psum_scatter(dcache, "resp", scatter_dimension=0))
    key_grad, value_grad = place(exchange(split(sums, prompt_keys.shape[0])))
    return (*(a[None] for a in earlier), key_grad, value_grad)


def solution(mesh):
    rows = P(("group", "resp"), None, "tensor")
    prompt = P(("group", "resp", "tensor"), None)
    return jax.shard_map(
        per_device,
        mesh=mesh,
        in_specs=(rows, rows, rows, prompt, prompt, rows, P(("group", "resp"))),
        out_specs=(rows, rows, rows, rows, prompt, prompt),
        check_vma=False,
    )
```

time: 260 us -> 206 us (0.79)
  blocking collectives: 24.5 us -> 0 us
  Pallas kernels: 126 us -> 110 us
  waiting for transfers between devices: 83 us -> 69.1 us
  starting transfers between devices: 0.16 us -> 5.29 us
    reduce_scatter x2, waiting for transfers between devices: 54.3 us -> 26.8 us  [per_device(): sums.append(lax.psum_scatter(dcache, 'resp', scatter_dimension=0))]
    all_to_all x2 -> x0, blocking collectives: 24.5 us -> none  [the longest x1 13.1 us: per_device(): own = lax.all_to_all(own, 'tensor', split_axis=2, concat_axis=1, tiled=True)]
    pallas_call x2, Pallas kernels: 126 us -> 102 us  [attend(): pl.pallas_call(functools.partial(attention_kernel, parts, heads_per), gri...]
    ppermute x0 -> x6, waiting for transfers between devices: none -> 13.5 us  [exchange(): lax.ppermute(blocks[i], 'tensor', [(j, j ^ i) for j in range(count)])]
    pallas_call x0 -> x4, Pallas kernels: none -> 7.89 us  [the longest x1 2.13 us: place(): pl.pallas_call(place_kernel, in_specs=[whole_block(blocks[0].shape)] * le...]
    ppermute x0 -> x6, starting transfers between devices: none -> 4.95 us  [exchange(): lax.ppermute(blocks[i], 'tensor', [(j, j ^ i) for j in range(count)])]
    unnamed x12 -> x28, local copies, waits for them, and re-layouts: 4.24 us -> 7.27 us
  transfers between devices with their start and end apart: 4 -> 10, of which waited for: 3 -> 6; matrix products, arithmetic and copies ran while one was open for 0% -> 0% of each run, Pallas kernels for 24% -> 50%
where the time goes in v2:
time: 206 us
  Pallas kernels  110 us (53%)
  waiting for transfers between devices  69.1 us (34%)
  between operations  14.5 us (7%)
  local copies, waits for them, and re-layouts  7.27 us (4%)
  starting transfers between devices  5.29 us (3%)
    pallas_call x2, Pallas kernels, attend(): pl.pallas_call(functools.partial(attention_kernel, parts, heads_per), gri...  102 us
    all_gather x2, waiting for transfers between devices, per_device(): caches = [lax.all_gather(own[p], 'resp', axis=0) for p in range(pairs)]  28 us
    reduce_scatter x2, waiting for transfers between devices, per_device(): sums.append(lax.psum_scatter(dcache, 'resp', scatter_dimension=0))  26.8 us
    ppermute x6, waiting for transfers between devices, exchange(): lax.ppermute(blocks[i], 'tensor', [(j, j ^ i) for j in range(count)])  13.5 us
    unnamed x28, local copies, waits for them, and re-layouts  7.27 us
    ppermute x6, starting transfers between devices, exchange(): lax.ppermute(blocks[i], 'tensor', [(j, j ^ i) for j in range(count)])  4.95 us
  transfers between devices with their start and end apart: 10, of which 6 were waited for; matrix products, arithmetic and copies ran while one was open for 0% of the time, Pallas kernels for 50%

profile of v2, /device:TPU:0, one launch (start us, length us, event | category | flops | bytes accessed | tf_op | source)
XLA Modules:
  0.0 206.0 jit_solution(17688267787394575110)
XLA Ops:
  7.2 0.0 all-gather.7.cloned.1.call-start
  7.2 1.9 cut.1
  9.1 0.5 collective-permute-start
  9.5 2.5 %collective-permute-start.1 = (bf16[2,128,256]{2,1,0:T(8,128)(2,1)}, bf16[2,128,256]{2,1,0:T(8,128)(2,1)S(1)}, u32[]{:S(2)}, u32[]{:S(2)}) collective-permute-start(bf16[2,128,256]{2,1,0:T(8,128)(2,1)} %get-tuple-element.32), channel_id=1, source_target_pairs={{0,2},{1,3},{2,0},{3,1},{4,6},{5,7},{6,4},{7,5},{8,10},{9,11},{10,... | collective-permute-start | bytes 393224 | tf_op jit(solution)/shard_map/ppermute | solution.py:342
  12.0 0.1 collective-permute-start.2
  12.2 0.0 collective-permute-done.refs_1_
  12.2 0.0 copy-start.8
  12.2 4.4 %collective-permute-done.1.refs_2_ = bf16[2,128,256]{2,1,0:T(8,128)(2,1)S(1)} collective-permute-done((bf16[2,128,256]{2,1,0:T(8,128)(2,1)}, bf16[2,128,256]{2,1,0:T(8,128)(2,1)S(1)}, u32[]{:S(2)}, u32[]{:S(2)}) %collective-permute-start.1) | collective-permute-done | bytes 131104 | tf_op jit(solution)/shard_map/ppermute | solution.py:342
  16.6 0.0 copy-start.10
  16.6 2.4 %collective-permute-done.2.refs_3_ = bf16[2,128,256]{2,1,0:T(8,128)(2,1)S(1)} collective-permute-done((bf16[2,128,256]{2,1,0:T(8,128)(2,1)}, bf16[2,128,256]{2,1,0:T(8,128)(2,1)S(1)}, u32[]{:S(2)}, u32[]{:S(2)}) %collective-permute-start.2) | collective-permute-done | bytes 131104 | tf_op jit(solution)/shard_map/ppermute | solution.py:342
  19.0 0.0 copy-start.12
  19.0 0.0 copy-done.8
  19.0 0.0 copy-done.10
  19.0 0.6 copy-done.12
  19.7 2.0 line_up.1
  21.7 0.0 all-gather.7.cloned.1.call-update
  21.7 0.0 all-gather.5.cloned.1.call-start
  21.7 0.7 all-gather.5.cloned.1.call-update
  22.4 0.0 reduce-scatter.3.cloned.1.call-start
  23.1 28.0 %all-gather.7.cloned.1.call-done = bf16[8,512,128]{2,1,0:T(8,128)(2,1)} async-done(((bf16[2,512,128]{2,1,0:T(8,128)(2,1)}), bf16[8,512,128]{2,1,0:T(8,128)(2,1)}) %all-gather.7.cloned.1.call-update) | async-done | bytes 1048592 | tf_op jit(solution)/shard_map/all_gather | solution.py:356
  51.1 0.0 copy-start
  51.1 1.6 copy-done
  52.7 0.0 copy-start.3
  52.7 1.2 copy-done.3
  53.9 0.0 copy-start.4
  53.9 0.9 copy-done.4
  54.9 0.0 copy-start.6
  54.9 0.9 copy-done.6
  55.8 0.0 copy-start.1
  55.8 0.0 copy-start.5
  55.8 0.0 copy-start.7
  55.8 51.1 %attend_pair_0.1 = (bf16[512,2048]{1,0:T(8,128)(2,1)}, bf16[512,2048]{1,0:T(8,128)(2,1)}, bf16[512,256]{1,0:T(8,128)(2,1)}, bf16[512,256]{1,0:T(8,128)(2,1)}, bf16[4,2,512,128]{3,2,1,0:T(8,128)(2,1)}) custom-call(s32[1]{0:T(128)S(6)} %copy.21.len_ref, bf16[512,2048]{1,0:T(8,128)(2,1)S(1)} %bitcast.12, bf16[512,2048]{1,0:T(8,128)(2,1)} %bitcast.22, ...), custom_call_target="tpu_custom_call" | custom-call | flops 16106127360 | bytes 4194304 | tf_op jit(solution)/shard_map/attend_pair_0/pallas_call | solution.py:211
  106.9 0.0 reduce-scatter.3.cloned.1.call-update
  107.0 0.2 reduce-scatter.5.cloned.1.call-start
  107.2 0.0 all-gather.5.cloned.1.call-done
  107.2 0.0 copy-done.1
  107.2 0.0 copy-done.5
  107.2 0.0 copy-done.7
  107.2 0.0 copy-start.2
  107.2 1.2 copy-done.2
  108.5 50.9 %attend_pair_1.1 = (bf16[512,2048]{1,0:T(8,128)(2,1)}, bf16[512,2048]{1,0:T(8,128)(2,1)}, bf16[512,256]{1,0:T(8,128)(2,1)}, bf16[512,256]{1,0:T(8,128)(2,1)}, bf16[4,2,512,128]{3,2,1,0:T(8,128)(2,1)}) custom-call(s32[1]{0:T(128)S(6)} %copy.21.len_ref, ...), custom_call_target="tpu_custom_call", output_to_operand_aliasing={{0}: (6, {}), {1}: (7, {}), {2}: (8, {}), {3}: (9, {})} | custom-call | flops 16106127360 | bytes 4194304 | tf_op jit(solution)/shard_map/attend_pair_1/pallas_call | solution.py:211
  159.4 0.0 reduce-scatter.3.cloned.1.call-done
  159.4 0.0 reduce-scatter.5.cloned.1.call-update
  159.4 26.8 %reduce-scatter.5.cloned.1.call-done = bf16[1,2,512,128]{3,2,1,0:T(8,128)(2,1)} async-done(((bf16[4,2,512,128]{3,2,1,0:T(8,128)(2,1)}), bf16[1,2,512,128]{3,2,1,0:T(8,128)(2,1)}) %reduce-scatter.5.cloned.1.call-update) | async-done | bytes 262160 | tf_op jit(solution)/shard_map/reduce_scatter | solution.py:365
  186.2 1.9 split.1
  188.1 0.0 collective-permute-start.3
  188.1 1.5 collective-permute-start.4
  189.6 0.4 collective-permute-start.5
  190.0 0.0 collective-permute-done.3.refs_1_
  190.0 0.0 copy-start.9
  190.0 4.6 %collective-permute-done.4.refs_2_ = bf16[2,128,256]{2,1,0:T(8,128)(2,1)S(1)} collective-permute-done((bf16[2,128,256]{2,1,0:T(8,128)(2,1)}, bf16[2,128,256]{2,1,0:T(8,128)(2,1)S(1)}, u32[]{:S(2)}, u32[]{:S(2)}) %collective-permute-start.4) | collective-permute-done | bytes 131104 | tf_op jit(solution)/shard_map/ppermute | solution.py:342
  194.6 0.0 copy-start.11
  194.6 2.0 collective-permute-done.5.refs_3_
  196.7 0.0 copy-start.13
  196.7 0.0 copy-done.9
  196.7 0.0 copy-done.11
  196.7 0.7 copy-done.13
  197.3 2.1 %place.1 = (f32[128,1024]{1,0:T(8,128)}, f32[128,1024]{1,0:T(8,128)}) custom-call(bf16[2,128,256]{2,1,0:T(8,128)(2,1)} %get-tuple-element.48.refs_0_, bf16[2,128,256]{2,1,0:T(8,128)(2,1)} %copy-done.9, bf16[2,128,256]{2,1,0:T(8,128)(2,1)} %copy-done.11, bf16[2,128,256]{2,1,0:T(8,128)(2,1)} %copy-done.13), custom_call_target="tpu_custom_call" | custom-call | tf_op jit(solution)/shard_map/place/pallas_call | solution.py:330
Async XLA Ops:
  7.2 43.9 %all-gather.7.cloned.1.call-start = ((), (), s32[]{:S(2)}) async-start(), calls=%async_computation.5 | async-start | bytes 1310720 | tf_op jit(solution)/shard_map/all_gather | solution.py:356
  9.1 3.1 %collective-permute-start = (bf16[2,128,256]{2,1,0:T(8,128)(2,1)}, bf16[2,128,256]{2,1,0:T(8,128)(2,1)S(1)}, u32[]{:S(2)}, u32[]{:S(2)}) collective-permute-start(bf16[2,128,256]{2,1,0:T(8,128)(2,1)} %get-tuple-element.31), channel_id=1, source_target_pairs={{0,1},{1,0},{2,3},{3,2},{4,5},{5,4},{6,7},{7,6},{8,9},{9,8},{10,11... | collective-permute-start | bytes 393224 | tf_op jit(solution)/shard_map/ppermute | solution.py:342
  9.5 7.0 %collective-permute-start.1 = (bf16[2,128,256]{2,1,0:T(8,128)(2,1)}, bf16[2,128,256]{2,1,0:T(8,128)(2,1)S(1)}, u32[]{:S(2)}, u32[]{:S(2)}) collective-permute-start(bf16[2,128,256]{2,1,0:T(8,128)(2,1)} %get-tuple-element.32), channel_id=1, source_target_pairs={{0,2},{1,3},{2,0},{3,1},{4,6},{5,7},{6,4},{7,5},{8,10},{9,11},{10,... | collective-permute-start | bytes 393224 | tf_op jit(solution)/shard_map/ppermute | solution.py:342
  12.0 7.0 %collective-permute-start.2 = (bf16[2,128,256]{2,1,0:T(8,128)(2,1)}, bf16[2,128,256]{2,1,0:T(8,128)(2,1)S(1)}, u32[]{:S(2)}, u32[]{:S(2)}) collective-permute-start(bf16[2,128,256]{2,1,0:T(8,128)(2,1)} %get-tuple-element.33), channel_id=1, source_target_pairs={{0,3},{1,2},{2,1},{3,0},{4,7},{5,6},{6,5},{7,4},{8,11},{9,10},{10,... | collective-permute-start | bytes 393224 | tf_op jit(solution)/shard_map/ppermute | solution.py:342
  12.2 6.9 %copy-start.8 = (bf16[2,128,256]{2,1,0:T(8,128)(2,1)}, bf16[2,128,256]{2,1,0:T(8,128)(2,1)S(1)}, u32[]{:S(2)}) copy-start(bf16[2,128,256]{2,1,0:T(8,128)(2,1)S(1)} %collective-permute-done.refs_1_) | copy-start | bytes 393220
  16.6 2.4 %copy-start.10 = (bf16[2,128,256]{2,1,0:T(8,128)(2,1)}, bf16[2,128,256]{2,1,0:T(8,128)(2,1)S(1)}, u32[]{:S(2)}) copy-start(bf16[2,128,256]{2,1,0:T(8,128)(2,1)S(1)} %collective-permute-done.1.refs_2_) | copy-start | bytes 393220
  19.0 0.7 copy-start.12
  21.7 85.5 %all-gather.5.cloned.1.call-start = ((), (), s32[]{:S(2)}) async-start(), calls=%async_computation.4 | async-start | bytes 1310720 | tf_op jit(solution)/shard_map/all_gather | solution.py:356
  22.4 137.0 %reduce-scatter.3.cloned.1.call-start = ((), (), s32[]{:S(2)}) async-start(), calls=%async_computation.2 | async-start | bytes 1310720 | tf_op jit(solution)/shard_map/reduce_scatter | solution.py:365
  51.1 1.6 copy-start
  52.7 1.2 copy-start.3
  53.9 0.9 copy-start.4
  54.9 0.9 copy-start.6
  55.8 51.4 %copy-start.1 = (bf16[1,512,2048]{2,1,0:T(8,128)(2,1)S(1)}, bf16[1,512,2048]{2,1,0:T(8,128)(2,1)}, u32[]{:S(2)}) copy-start(bf16[1,512,2048]{2,1,0:T(8,128)(2,1)} %param.7) | copy-start | bytes 6291460
  55.8 51.4 %copy-start.5 = (bf16[1,512,256]{2,1,0:T(8,128)(2,1)S(1)}, bf16[1,512,256]{2,1,0:T(8,128)(2,1)}, u32[]{:S(2)}) copy-start(bf16[1,512,256]{2,1,0:T(8,128)(2,1)} %param.8) | copy-start | bytes 786436
  55.8 51.4 %copy-start.7 = (bf16[1,512,256]{2,1,0:T(8,128)(2,1)S(1)}, bf16[1,512,256]{2,1,0:T(8,128)(2,1)}, u32[]{:S(2)}) copy-start(bf16[1,512,256]{2,1,0:T(8,128)(2,1)} %param.9) | copy-start | bytes 786436
  107.0 79.3 %reduce-scatter.5.cloned.1.call-start = ((), (), s32[]{:S(2)}) async-start(), calls=%async_computation.3 | async-start | bytes 1310720 | tf_op jit(solution)/shard_map/reduce_scatter | solution.py:365
  107.2 1.2 copy-start.2
  188.1 1.9 collective-permute-start.3
  188.1 6.5 %collective-permute-start.4 = (bf16[2,128,256]{2,1,0:T(8,128)(2,1)}, bf16[2,128,256]{2,1,0:T(8,128)(2,1)S(1)}, u32[]{:S(2)}, u32[]{:S(2)}) collective-permute-start(bf16[2,128,256]{2,1,0:T(8,128)(2,1)} %get-tuple-element.50), channel_id=1, source_target_pairs={{0,2},{1,3},{2,0},{3,1},{4,6},{5,7},{6,4},{7,5},{8,10},{9,11},{10,... | collective-permute-start | bytes 393224 | tf_op jit(solution)/shard_map/ppermute | solution.py:342
  189.6 7.1 %collective-permute-start.5 = (bf16[2,128,256]{2,1,0:T(8,128)(2,1)}, bf16[2,128,256]{2,1,0:T(8,128)(2,1)S(1)}, u32[]{:S(2)}, u32[]{:S(2)}) collective-permute-start(bf16[2,128,256]{2,1,0:T(8,128)(2,1)} %get-tuple-element.51), channel_id=1, source_target_pairs={{0,3},{1,2},{2,1},{3,0},{4,7},{5,6},{6,5},{7,4},{8,11},{9,10},{10,... | collective-permute-start | bytes 393224 | tf_op jit(solution)/shard_map/ppermute | solution.py:342
  190.0 6.7 %copy-start.9 = (bf16[2,128,256]{2,1,0:T(8,128)(2,1)}, bf16[2,128,256]{2,1,0:T(8,128)(2,1)S(1)}, u32[]{:S(2)}) copy-start(bf16[2,128,256]{2,1,0:T(8,128)(2,1)S(1)} %collective-permute-done.3.refs_1_) | copy-start | bytes 393220
  194.6 2.0 copy-start.11
  196.7 0.7 copy-start.13
Sparse Core Ops, SparseCore 0:
  21.8 29.2 all-gather.6
  53.2 27.4 all-gather.4
  107.1 26.6 reduce-scatter.2
  159.6 26.6 reduce-scatter.4

commit v3 on v2

--- a/solution.py
+++ b/solution.py
@@ -46,27 +46,36 @@
         grad_t,
         exps_even,
         exps_odd,
+        weights_even,
+        weights_odd,
+        sgrads,
+        score_even,
+        score_odd,
+        dprob_even,
+        dprob_odd,
         fracs,
         deltas,
         dk_sum,
         dv_sum,
-        dq_sum,
         tops,
         sums,
-    ) = rest[-22:]
+    ) = rest[-28:]
     rows = q_ref.shape[0]
     part_rows = cache_ref.shape[2]
     prompt_rows = parts * part_rows
-    chunk = rows
-    blocks = chunk // SUB
-    prompt_chunks = prompt_rows // chunk
-    chunks = prompt_chunks + 1
-    stats = chunks * blocks
+    total_rows = prompt_rows + rows
+    half = rows // 2
+    pieces = [(at, rows, 0) for at in range(0, prompt_rows, rows)]
+    pieces += [(prompt_rows, half, 0), (prompt_rows + half, half, half)]
+    count = len(pieces)
     factor = HD ** (-0.5)
     factor2 = factor * math.log2(math.e)
     length = len_ref[0]
     step = pl.program_id(0)
-    slots = (exps_even, exps_odd)
+    exps = (exps_even, exps_odd)
+    weights = (weights_even, weights_odd)
+    scores = (score_even, score_odd)
+    dprobs = (dprob_even, dprob_odd)
 
     @pl.when(step == 0)
     def _():
@@ -74,66 +83,91 @@
             at = pl.ds(p * part_rows, part_rows)
             keys[at, :] = cache_ref[p, 0]
             values[at, :] = cache_ref[p, 1]
-            keys_t[:, at] = cache_ref[p, 0].astype(F32).T.astype(BF16)
-            values_t[:, at] = cache_ref[p, 1].astype(F32).T.astype(BF16)
+            keys_t[:, at] = cache_ref[p, 0].T
+            values_t[:, at] = cache_ref[p, 1].T
         at = pl.ds(prompt_rows, rows)
         keys[at, :] = kr_ref[...]
         values[at, :] = vr_ref[...]
-        keys_t[:, at] = kr_ref[...].astype(F32).T.astype(BF16)
-        values_t[:, at] = vr_ref[...].astype(F32).T.astype(BF16)
+        keys_t[:, at] = kr_ref[...].T
+        values_t[:, at] = vr_ref[...].T
         dk_sum[...] = jnp.zeros_like(dk_sum)
         dv_sum[...] = jnp.zeros_like(dv_sum)
-
-    def rows_at(c):
-        return pl.ds(pl.multiple_of(c * chunk, chunk), chunk)
-
-    def score_part(now, c, masked):
-        score = dot(keys[rows_at(c), :], query_t[now])
-        if masked:
-            j = lax.broadcasted_iota(jnp.int32, (chunk, rows), 0)
-            i = lax.broadcasted_iota(jnp.int32, (chunk, rows), 1)
-            score = jnp.where((j <= i) & (j < length), score, -jnp.inf)
-        for u in range(blocks):
-            block = score[u * SUB : (u + 1) * SUB, :]
-            top = jnp.max(block, axis=0, keepdims=True)
-            top = jnp.maximum(top, LOWEST) * factor2
-            exp = jnp.exp2(block * factor2 - top)
-            slots[now][pl.ds(pl.multiple_of(c * chunk + u * SUB, SUB), SUB), :] = exp
-            tops[pl.ds(c * blocks + u, 1), :] = top
-            sums[pl.ds(c * blocks + u, 1), :] = jnp.sum(exp, axis=0, keepdims=True)
-
-    def scaled(slot, c, u):
-        at = pl.ds(pl.multiple_of(c * chunk + u * SUB, SUB), SUB)
-        return slots[slot][at, :] * fracs[slot, pl.ds(c * blocks + u, 1), :]
-
-    def grad_part(before, c):
-        at = rows_at(c)
-        dprob = dot(values[at, :], grad_t[before])
-        delta = deltas[before]
-        weight, sgrad = [], []
-        for u in range(blocks):
-            frac = scaled(before, c, u)
-            weight.append(frac.astype(BF16))
-            sgrad.append((frac * (dprob[u * SUB : (u + 1) * SUB, :] - delta)).astype(BF16))
-        weight, sgrad = jnp.concatenate(weight, 0), jnp.concatenate(sgrad, 0)
-        dv_sum[at, :] += dot(weight, grad[before])
-        dk_sum[at, :] += dot(sgrad, query[before])
-        dq_sum[...] += dot(keys_t[:, at], sgrad)
+        tops[...] = jnp.full_like(tops, LOWEST)
+        sums[...] = jnp.zeros_like(sums)
+        for ref in (*weights, sgrads):
+            ref[prompt_rows + half :, :half] = jnp.zeros((half, half), BF16)
+
+    def blocks(piece):
+        at, size, row = pieces[piece]
+        for u in range(0, size, SUB):
+            for r in range(0, rows - row, SUB):
+                yield u, r, slice(at + u, at + u + SUB), slice(row + r, row + r + SUB)
+
+    def stat(block_at):
+        return slice(block_at.start // SUB * 8, block_at.start // SUB * 8 + 8)
+
+    def score_product(now, piece):
+        at, size, row = pieces[piece]
+        scores[piece % 2][:size, : rows - row] = dot(
+            keys[at : at + size, :], query_t[now, :, row:]
+        )
+
+    def score_chain(now, piece):
+        for u, r, key_at, row_at in blocks(piece):
+            block = scores[piece % 2][u : u + SUB, r : r + SUB]
+            if key_at.start >= prompt_rows:
+                j = lax.broadcasted_iota(jnp.int32, (SUB, SUB), 0) + key_at.start - prompt_rows
+                i = lax.broadcasted_iota(jnp.int32, (SUB, SUB), 1) + row_at.start
+                block = jnp.where((j <= i) & (j < length), block, -jnp.inf)
+            block = block.reshape(SUB // 8, 8, SUB) * factor2
+            top = jnp.maximum(jnp.max(block, axis=0), LOWEST)
+            exp = jnp.exp2(block - top[None])
+            exps[now][key_at, row_at] = exp.reshape(SUB, SUB)
+            tops[stat(key_at), row_at] = top
+            sums[stat(key_at), row_at] = jnp.sum(exp, axis=0)
+
+    def frac(slot, key_at, row_at):
+        block = exps[slot][key_at, row_at].reshape(SUB // 8, 8, SUB)
+        return block * fracs[slot, stat(key_at), row_at][None]
+
+    def dprob_product(before, piece):
+        at, size, row = pieces[piece]
+        dprobs[piece % 2][:size, : rows - row] = dot(
+            values[at : at + size, :], grad_t[before, :, row:]
+        )
+
+    def grad_chain(before, piece):
+        for u, r, key_at, row_at in blocks(piece):
+            dprob = dprobs[piece % 2][u : u + SUB, r : r + SUB].reshape(SUB // 8, 8, SUB)
+            sgrad = frac(before, key_at, row_at) * (dprob - deltas[before, :, row_at][None])
+            sgrads[key_at, row_at] = sgrad.reshape(SUB, SUB).astype(BF16)
+
+    def grad_products(before, piece):
+        at, size, row = pieces[piece]
+        key_at = slice(at, at + size)
+        dv_sum[key_at, :] += dot(weights[before][key_at, row:], grad[before, row:, :])
+        dk_sum[key_at, :] += dot(sgrads[key_at, row:], query[before, row:, :])
 
     def run(now, with_score, with_grad):
-        def body(c, carry, masked=False):
-            if with_score:
-                score_part(now, c, masked)
-            if with_grad:
-                grad_part(1 - now, c)
-            return carry
-
+        before = 1 - now
+        for stage in range(-1, count + 1):
+            if stage + 1 < count:
+                if with_score:
+                    score_product(now, stage + 1)
+                if with_grad:
+                    dprob_product(before, stage + 1)
+            if 0 <= stage < count:
+                if with_score:
+                    score_chain(now, stage)
+                if with_grad:
+                    grad_chain(before, stage)
+            if stage >= 1 and with_grad:
+                grad_products(before, stage - 1)
         if with_grad:
-            dq_sum[...] = jnp.zeros_like(dq_sum)
-        lax.fori_loop(0, prompt_chunks, body, 0)
-        body(prompt_chunks, 0, True)
-        if with_grad:
-            dq_ref[...] = (factor * dq_sum[...]).T.astype(BF16)
+            dquery = dot(keys_t[...], sgrads[...])
+            dq_ref[...] = (factor * dquery).T.astype(BF16)
+        if with_score:
+            finish(now)
 
     def prepare(now):
         live_rows = lax.broadcasted_iota(jnp.int32, (rows, HD), 0) < length
@@ -141,44 +175,38 @@
         grad[now] = live_grad.astype(BF16)
         grad_t[now] = live_grad.T.astype(BF16)
         query[now] = q_ref[...]
-        query_t[now] = q_ref[...].astype(F32).T.astype(BF16)
+        query_t[now] = q_ref[...].T
 
     def finish(now):
-        top = jnp.max(tops[:stats, :], axis=0, keepdims=True)
-        scale = jnp.exp2(tops[:stats, :] - top)
-        total = jnp.sum(scale * sums[:stats, :], axis=0, keepdims=True)
-        fracs[now, :stats, :] = scale / total
-
-        mixture = jnp.zeros((HD, rows), F32)
-        for c in range(chunks):
-            weight = jnp.concatenate(
-                [scaled(now, c, u).astype(BF16) for u in range(blocks)], 0
-            )
-            mixture = mixture + dot(values_t[:, c * chunk : (c + 1) * chunk], weight)
+        top = jnp.max(tops[...], axis=0, keepdims=True)
+        scale = jnp.exp2(tops[...] - top)
+        total = jnp.sum(scale * sums[...], axis=0, keepdims=True)
+        fracs[now] = scale * (1.0 / total)
+        for piece in range(count):
+            for _, _, key_at, row_at in blocks(piece):
+                weight = frac(now, key_at, row_at).reshape(SUB, SUB)
+                weights[now][key_at, row_at] = weight.astype(BF16)
+        mixture = dot(values_t[...], weights[now][...])
         live_lanes = lax.broadcasted_iota(jnp.int32, (HD, rows), 1) < length
         attended = jnp.where(live_lanes, mixture, 0.0).astype(BF16).astype(F32)
         out_ref[...] = attended.T.astype(BF16)
-        deltas[now] = jnp.sum(grad_t[now].astype(F32) * attended, axis=0, keepdims=True)
+        delta = jnp.sum(grad_t[now].astype(F32) * attended, axis=0, keepdims=True)
+        deltas[now] = jnp.broadcast_to(delta, (8, rows))
 
     @pl.when(step == 0)
     def _():
         prepare(0)
         run(0, True, False)
-        finish(0)
 
     for now in range(2):
         @pl.when((step > 0) & (step < heads_per) & (lax.rem(step, 2) == now))
         def _():
             prepare(now)
             run(now, True, True)
-            finish(now)
 
     @pl.when(step == heads_per)
     def _():
         run(heads_per % 2, False, True)
-
-    @pl.when(step == heads_per)
-    def _():
         for p in range(parts):
             at = pl.ds(p * part_rows, part_rows)
             dcache_ref[p, 0] = (factor * dk_sum[at, :]).astype(BF16)
@@ -198,7 +226,7 @@
     late_block = pl.BlockSpec((rows, HD), lambda s: (0, jnp.maximum(first + s - 1, first)))
     pair_block = pl.BlockSpec((rows, HD), lambda s: (0, pair))
     cache_block = pl.BlockSpec(cache.shape, lambda s: (0, 0, 0, 0))
-    stats = -(-total_rows // SUB // 8) * 8
+    stats = total_rows // SUB * 8
     in_specs = [
         pl.BlockSpec(memory_space=pltpu.SMEM),
         head_block,
@@ -231,11 +259,17 @@
             pltpu.VMEM((2, HD, rows), BF16),
             pltpu.VMEM((total_rows, rows), F32),
             pltpu.VMEM((total_rows, rows), F32),
+            pltpu.VMEM((total_rows, rows), BF16),
+            pltpu.VMEM((total_rows, rows), BF16),
+            pltpu.VMEM((total_rows, rows), BF16),
+            pltpu.VMEM((rows, rows), F32),
+            pltpu.VMEM((rows, rows), F32),
+            pltpu.VMEM((rows, rows), F32),
+            pltpu.VMEM((rows, rows), F32),
             pltpu.VMEM((2, stats, rows), F32),
-            pltpu.VMEM((2, 1, rows), F32),
+            pltpu.VMEM((2, 8, rows), F32),
             pltpu.VMEM((total_rows, HD), F32),
             pltpu.VMEM((total_rows, HD), F32),
-            pltpu.VMEM((HD, rows), F32),
             pltpu.VMEM((stats, rows), F32),
             pltpu.VMEM((stats, rows), F32),
         ],

time: 206 us -> 182 us (0.88)
  Pallas kernels: 110 us -> 85.9 us
    pallas_call x2, Pallas kernels: 102 us -> 78 us  [attend(): pl.pallas_call(functools.partial(attention_kernel, parts, heads_per), gri...]
  transfers between devices with their start and end apart: 10 -> 10, of which waited for: 6 -> 6; matrix products, arithmetic and copies ran while one was open for 0% -> 0% of each run, Pallas kernels for 50% -> 43%
where the time goes in v3:
time: 182 us
  Pallas kernels  85.9 us (47%)
  waiting for transfers between devices  69.1 us (38%)
  between operations  14.5 us (8%)
  local copies, waits for them, and re-layouts  7.27 us (4%)
  starting transfers between devices  5.11 us (3%)
    pallas_call x2, Pallas kernels, attend(): pl.pallas_call(functools.partial(attention_kernel, parts, heads_per), gri...  78 us
    all_gather x2, waiting for transfers between devices, per_device(): caches = [lax.all_gather(own[p], 'resp', axis=0) for p in range(pairs)]  28 us
    reduce_scatter x2, waiting for transfers between devices, per_device(): sums.append(lax.psum_scatter(dcache, 'resp', scatter_dimension=0))  26.8 us
    ppermute x6, waiting for transfers between devices, exchange(): lax.ppermute(blocks[i], 'tensor', [(j, j ^ i) for j in range(count)])  13.5 us
    unnamed x28, local copies, waits for them, and re-layouts  7.27 us
    ppermute x6, starting transfers between devices, exchange(): lax.ppermute(blocks[i], 'tensor', [(j, j ^ i) for j in range(count)])  4.95 us
  transfers between devices with their start and end apart: 10, of which 6 were waited for; matrix products, arithmetic and copies ran while one was open for 0% of the time, Pallas kernels for 43%

profile of v3, /device:TPU:0, one launch (start us, length us, event | category | flops | bytes accessed | tf_op | source)
XLA Modules:
  0.0 181.8 jit_solution(17631500492977801280)
XLA Ops:
  7.2 0.0 all-gather.7.cloned.1.call-start
  7.2 1.9 %cut.1 = (bf16[2,128,256]{2,1,0:T(8,128)(2,1)}, bf16[2,128,256]{2,1,0:T(8,128)(2,1)}, bf16[2,128,256]{2,1,0:T(8,128)(2,1)}, bf16[2,128,256]{2,1,0:T(8,128)(2,1)}) custom-call(bf16[128,1024]{1,0:T(8,128)(2,1)} %k_ref.1, bf16[128,1024]{1,0:T(8,128)(2,1)} %v_ref.1), custom_call_target="tpu_custom_call" | custom-call | tf_op jit(solution)/shard_map/cut/pallas_call | solution.py:302
  9.1 0.5 collective-permute-start
  9.5 2.5 %collective-permute-start.1 = (bf16[2,128,256]{2,1,0:T(8,128)(2,1)}, bf16[2,128,256]{2,1,0:T(8,128)(2,1)S(1)}, u32[]{:S(2)}, u32[]{:S(2)}) collective-permute-start(bf16[2,128,256]{2,1,0:T(8,128)(2,1)} %get-tuple-element.32), channel_id=1, source_target_pairs={{0,2},{1,3},{2,0},{3,1},{4,6},{5,7},{6,4},{7,5},{8,10},{9,11},{10,... | collective-permute-start | bytes 393224 | tf_op jit(solution)/shard_map/ppermute | solution.py:376
  12.0 0.1 collective-permute-start.2
  12.2 0.0 collective-permute-done.refs_1_
  12.2 0.0 copy-start.8
  12.2 4.4 %collective-permute-done.1.refs_2_ = bf16[2,128,256]{2,1,0:T(8,128)(2,1)S(1)} collective-permute-done((bf16[2,128,256]{2,1,0:T(8,128)(2,1)}, bf16[2,128,256]{2,1,0:T(8,128)(2,1)S(1)}, u32[]{:S(2)}, u32[]{:S(2)}) %collective-permute-start.1) | collective-permute-done | bytes 131104 | tf_op jit(solution)/shard_map/ppermute | solution.py:376
  16.6 0.0 copy-start.10
  16.6 2.4 %collective-permute-done.2.refs_3_ = bf16[2,128,256]{2,1,0:T(8,128)(2,1)S(1)} collective-permute-done((bf16[2,128,256]{2,1,0:T(8,128)(2,1)}, bf16[2,128,256]{2,1,0:T(8,128)(2,1)S(1)}, u32[]{:S(2)}, u32[]{:S(2)}) %collective-permute-start.2) | collective-permute-done | bytes 131104 | tf_op jit(solution)/shard_map/ppermute | solution.py:376
  19.0 0.0 copy-start.12
  19.0 0.0 copy-done.8
  19.0 0.0 copy-done.10
  19.0 0.6 copy-done.12
  19.7 2.0 %line_up.1 = (bf16[2,512,128]{2,1,0:T(8,128)(2,1)}, bf16[2,512,128]{2,1,0:T(8,128)(2,1)}) custom-call(bf16[2,128,256]{2,1,0:T(8,128)(2,1)} %get-tuple-element.30.refs_0_, bf16[2,128,256]{2,1,0:T(8,128)(2,1)} %copy-done.8, bf16[2,128,256]{2,1,0:T(8,128)(2,1)} %copy-done.10, bf16[2,128,256]{2,1,0:T(8,128)(2,1)} %copy-done.12), custom_call_target="tpu_custom_call" | custom-call | tf_op jit(solution)/shard_map/line_up/pallas_call | solution.py:322
  21.7 0.0 all-gather.7.cloned.1.call-update
  21.7 0.0 all-gather.5.cloned.1.call-start
  21.7 0.7 all-gather.5.cloned.1.call-update
  22.4 0.0 reduce-scatter.3.cloned.1.call-start
  23.1 28.0 %all-gather.7.cloned.1.call-done = bf16[8,512,128]{2,1,0:T(8,128)(2,1)} async-done(((bf16[2,512,128]{2,1,0:T(8,128)(2,1)}), bf16[8,512,128]{2,1,0:T(8,128)(2,1)}) %all-gather.7.cloned.1.call-update) | async-done | bytes 1048592 | tf_op jit(solution)/shard_map/all_gather | solution.py:390
  51.1 0.0 copy-start
  51.1 1.6 copy-done
  52.7 0.0 copy-start.3
  52.7 1.2 copy-done.3
  53.9 0.0 copy-start.4
  53.9 0.9 copy-done.4
  54.9 0.0 copy-start.6
  54.9 0.9 copy-done.6
  55.8 0.0 copy-start.1
  55.8 0.0 copy-start.5
  55.8 0.0 copy-start.7
  55.8 39.1 %attend_pair_0.1 = (bf16[512,2048]{1,0:T(8,128)(2,1)}, bf16[512,2048]{1,0:T(8,128)(2,1)}, bf16[512,256]{1,0:T(8,128)(2,1)}, bf16[512,256]{1,0:T(8,128)(2,1)}, bf16[4,2,512,128]{3,2,1,0:T(8,128)(2,1)}) custom-call(s32[1]{0:T(128)S(6)} %copy.21.len_ref, bf16[512,2048]{1,0:T(8,128)(2,1)S(1)} %bitcast.12, bf16[512,2048]{1,0:T(8,128)(2,1)} %bitcast.22, ...), custom_call_target="tpu_custom_call" | custom-call | flops 16106127360 | bytes 4194304 | tf_op jit(solution)/shard_map/attend_pair_0/pallas_call | solution.py:239
  94.9 0.0 reduce-scatter.3.cloned.1.call-update
  94.9 0.0 reduce-scatter.5.cloned.1.call-start
  95.0 0.0 all-gather.5.cloned.1.call-done
  95.0 0.0 copy-done.1
  95.0 0.0 copy-done.5
  95.0 0.0 copy-done.7
  95.0 0.0 copy-start.2
  95.1 1.2 copy-done.2
  96.3 38.9 %attend_pair_1.1 = (bf16[512,2048]{1,0:T(8,128)(2,1)}, bf16[512,2048]{1,0:T(8,128)(2,1)}, bf16[512,256]{1,0:T(8,128)(2,1)}, bf16[512,256]{1,0:T(8,128)(2,1)}, bf16[4,2,512,128]{3,2,1,0:T(8,128)(2,1)}) custom-call(s32[1]{0:T(128)S(6)} %copy.21.len_ref, ...), custom_call_target="tpu_custom_call", output_to_operand_aliasing={{0}: (6, {}), {1}: (7, {}), {2}: (8, {}), {3}: (9, {})} | custom-call | flops 16106127360 | bytes 4194304 | tf_op jit(solution)/shard_map/attend_pair_1/pallas_call | solution.py:239
  135.2 0.0 reduce-scatter.3.cloned.1.call-done
  135.2 0.0 reduce-scatter.5.cloned.1.call-update
  135.2 26.8 %reduce-scatter.5.cloned.1.call-done = bf16[1,2,512,128]{3,2,1,0:T(8,128)(2,1)} async-done(((bf16[4,2,512,128]{3,2,1,0:T(8,128)(2,1)}), bf16[1,2,512,128]{3,2,1,0:T(8,128)(2,1)}) %reduce-scatter.5.cloned.1.call-update) | async-done | bytes 262160 | tf_op jit(solution)/shard_map/reduce_scatter | solution.py:399
  162.0 1.9 %split.1 = (bf16[2,128,256]{2,1,0:T(8,128)(2,1)}, bf16[2,128,256]{2,1,0:T(8,128)(2,1)}, bf16[2,128,256]{2,1,0:T(8,128)(2,1)}, bf16[2,128,256]{2,1,0:T(8,128)(2,1)}) custom-call(bf16[2,512,128]{2,1,0:T(8,128)(2,1)} %bitcast.20, bf16[2,512,128]{2,1,0:T(8,128)(2,1)} %bitcast.21), custom_call_target="tpu_custom_call" | custom-call | tf_op jit(solution)/shard_map/split/pallas_call | solution.py:342
  163.9 0.0 collective-permute-start.3
  163.9 1.5 collective-permute-start.4
  165.4 0.4 collective-permute-start.5
  165.8 0.0 collective-permute-done.3.refs_1_
  165.8 0.0 copy-start.9
  165.8 4.6 %collective-permute-done.4.refs_2_ = bf16[2,128,256]{2,1,0:T(8,128)(2,1)S(1)} collective-permute-done((bf16[2,128,256]{2,1,0:T(8,128)(2,1)}, bf16[2,128,256]{2,1,0:T(8,128)(2,1)S(1)}, u32[]{:S(2)}, u32[]{:S(2)}) %collective-permute-start.4) | collective-permute-done | bytes 131104 | tf_op jit(solution)/shard_map/ppermute | solution.py:376
  170.4 0.0 copy-start.11
  170.4 2.0 %collective-permute-done.5.refs_3_ = bf16[2,128,256]{2,1,0:T(8,128)(2,1)S(1)} collective-permute-done((bf16[2,128,256]{2,1,0:T(8,128)(2,1)}, bf16[2,128,256]{2,1,0:T(8,128)(2,1)S(1)}, u32[]{:S(2)}, u32[]{:S(2)}) %collective-permute-start.5) | collective-permute-done | bytes 131104 | tf_op jit(solution)/shard_map/ppermute | solution.py:376
  172.5 0.0 copy-start.13
  172.5 0.0 copy-done.9
  172.5 0.0 copy-done.11
  172.5 0.7 copy-done.13
  173.1 2.1 %place.1 = (f32[128,1024]{1,0:T(8,128)}, f32[128,1024]{1,0:T(8,128)}) custom-call(bf16[2,128,256]{2,1,0:T(8,128)(2,1)} %get-tuple-element.48.refs_0_, bf16[2,128,256]{2,1,0:T(8,128)(2,1)} %copy-done.9, bf16[2,128,256]{2,1,0:T(8,128)(2,1)} %copy-done.11, bf16[2,128,256]{2,1,0:T(8,128)(2,1)} %copy-done.13), custom_call_target="tpu_custom_call" | custom-call | tf_op jit(solution)/shard_map/place/pallas_call | solution.py:364
Async XLA Ops:
  7.2 43.9 %all-gather.7.cloned.1.call-start = ((), (), s32[]{:S(2)}) async-start(), calls=%async_computation.5 | async-start | bytes 1310720 | tf_op jit(solution)/shard_map/all_gather | solution.py:390
  9.1 3.1 %collective-permute-start = (bf16[2,128,256]{2,1,0:T(8,128)(2,1)}, bf16[2,128,256]{2,1,0:T(8,128)(2,1)S(1)}, u32[]{:S(2)}, u32[]{:S(2)}) collective-permute-start(bf16[2,128,256]{2,1,0:T(8,128)(2,1)} %get-tuple-element.31), channel_id=1, source_target_pairs={{0,1},{1,0},{2,3},{3,2},{4,5},{5,4},{6,7},{7,6},{8,9},{9,8},{10,11... | collective-permute-start | bytes 393224 | tf_op jit(solution)/shard_map/ppermute | solution.py:376
  9.5 7.0 %collective-permute-start.1 = (bf16[2,128,256]{2,1,0:T(8,128)(2,1)}, bf16[2,128,256]{2,1,0:T(8,128)(2,1)S(1)}, u32[]{:S(2)}, u32[]{:S(2)}) collective-permute-start(bf16[2,128,256]{2,1,0:T(8,128)(2,1)} %get-tuple-element.32), channel_id=1, source_target_pairs={{0,2},{1,3},{2,0},{3,1},{4,6},{5,7},{6,4},{7,5},{8,10},{9,11},{10,... | collective-permute-start | bytes 393224 | tf_op jit(solution)/shard_map/ppermute | solution.py:376
  12.0 7.0 %collective-permute-start.2 = (bf16[2,128,256]{2,1,0:T(8,128)(2,1)}, bf16[2,128,256]{2,1,0:T(8,128)(2,1)S(1)}, u32[]{:S(2)}, u32[]{:S(2)}) collective-permute-start(bf16[2,128,256]{2,1,0:T(8,128)(2,1)} %get-tuple-element.33), channel_id=1, source_target_pairs={{0,3},{1,2},{2,1},{3,0},{4,7},{5,6},{6,5},{7,4},{8,11},{9,10},{10,... | collective-permute-start | bytes 393224 | tf_op jit(solution)/shard_map/ppermute | solution.py:376
  12.2 6.9 %copy-start.8 = (bf16[2,128,256]{2,1,0:T(8,128)(2,1)}, bf16[2,128,256]{2,1,0:T(8,128)(2,1)S(1)}, u32[]{:S(2)}) copy-start(bf16[2,128,256]{2,1,0:T(8,128)(2,1)S(1)} %collective-permute-done.refs_1_) | copy-start | bytes 393220
  16.6 2.4 %copy-start.10 = (bf16[2,128,256]{2,1,0:T(8,128)(2,1)}, bf16[2,128,256]{2,1,0:T(8,128)(2,1)S(1)}, u32[]{:S(2)}) copy-start(bf16[2,128,256]{2,1,0:T(8,128)(2,1)S(1)} %collective-permute-done.1.refs_2_) | copy-start | bytes 393220
  19.0 0.7 copy-start.12
  21.7 73.3 %all-gather.5.cloned.1.call-start = ((), (), s32[]{:S(2)}) async-start(), calls=%async_computation.4 | async-start | bytes 1310720 | tf_op jit(solution)/shard_map/all_gather | solution.py:390
  22.4 112.8 %reduce-scatter.3.cloned.1.call-start = ((), (), s32[]{:S(2)}) async-start(), calls=%async_computation.2 | async-start | bytes 1310720 | tf_op jit(solution)/shard_map/reduce_scatter | solution.py:399
  51.1 1.6 copy-start
  52.7 1.2 copy-start.3
  53.9 0.9 copy-start.4
  54.9 0.9 copy-start.6
  55.8 39.2 %copy-start.1 = (bf16[1,512,2048]{2,1,0:T(8,128)(2,1)S(1)}, bf16[1,512,2048]{2,1,0:T(8,128)(2,1)}, u32[]{:S(2)}) copy-start(bf16[1,512,2048]{2,1,0:T(8,128)(2,1)} %param.7) | copy-start | bytes 6291460
  55.8 39.2 %copy-start.5 = (bf16[1,512,256]{2,1,0:T(8,128)(2,1)S(1)}, bf16[1,512,256]{2,1,0:T(8,128)(2,1)}, u32[]{:S(2)}) copy-start(bf16[1,512,256]{2,1,0:T(8,128)(2,1)} %param.8) | copy-start | bytes 786436
  55.8 39.2 %copy-start.7 = (bf16[1,512,256]{2,1,0:T(8,128)(2,1)S(1)}, bf16[1,512,256]{2,1,0:T(8,128)(2,1)}, u32[]{:S(2)}) copy-start(bf16[1,512,256]{2,1,0:T(8,128)(2,1)} %param.9) | copy-start | bytes 786436
  94.9 67.1 %reduce-scatter.5.cloned.1.call-start = ((), (), s32[]{:S(2)}) async-start(), calls=%async_computation.3 | async-start | bytes 1310720 | tf_op jit(solution)/shard_map/reduce_scatter | solution.py:399
  95.0 1.2 copy-start.2
  163.9 1.9 %collective-permute-start.3 = (bf16[2,128,256]{2,1,0:T(8,128)(2,1)}, bf16[2,128,256]{2,1,0:T(8,128)(2,1)S(1)}, u32[]{:S(2)}, u32[]{:S(2)}) collective-permute-start(bf16[2,128,256]{2,1,0:T(8,128)(2,1)} %get-tuple-element.49), channel_id=1, source_target_pairs={{0,1},{1,0},{2,3},{3,2},{4,5},{5,4},{6,7},{7,6},{8,9},{9,8},{10,11... | collective-permute-start | bytes 393224 | tf_op jit(solution)/shard_map/ppermute | solution.py:376
  163.9 6.5 %collective-permute-start.4 = (bf16[2,128,256]{2,1,0:T(8,128)(2,1)}, bf16[2,128,256]{2,1,0:T(8,128)(2,1)S(1)}, u32[]{:S(2)}, u32[]{:S(2)}) collective-permute-start(bf16[2,128,256]{2,1,0:T(8,128)(2,1)} %get-tuple-element.50), channel_id=1, source_target_pairs={{0,2},{1,3},{2,0},{3,1},{4,6},{5,7},{6,4},{7,5},{8,10},{9,11},{10,... | collective-permute-start | bytes 393224 | tf_op jit(solution)/shard_map/ppermute | solution.py:376
  165.4 7.1 %collective-permute-start.5 = (bf16[2,128,256]{2,1,0:T(8,128)(2,1)}, bf16[2,128,256]{2,1,0:T(8,128)(2,1)S(1)}, u32[]{:S(2)}, u32[]{:S(2)}) collective-permute-start(bf16[2,128,256]{2,1,0:T(8,128)(2,1)} %get-tuple-element.51), channel_id=1, source_target_pairs={{0,3},{1,2},{2,1},{3,0},{4,7},{5,6},{6,5},{7,4},{8,11},{9,10},{10,... | collective-permute-start | bytes 393224 | tf_op jit(solution)/shard_map/ppermute | solution.py:376
  165.8 6.7 %copy-start.9 = (bf16[2,128,256]{2,1,0:T(8,128)(2,1)}, bf16[2,128,256]{2,1,0:T(8,128)(2,1)S(1)}, u32[]{:S(2)}) copy-start(bf16[2,128,256]{2,1,0:T(8,128)(2,1)S(1)} %collective-permute-done.3.refs_1_) | copy-start | bytes 393220
  170.4 2.0 %copy-start.11 = (bf16[2,128,256]{2,1,0:T(8,128)(2,1)}, bf16[2,128,256]{2,1,0:T(8,128)(2,1)S(1)}, u32[]{:S(2)}) copy-start(bf16[2,128,256]{2,1,0:T(8,128)(2,1)S(1)} %collective-permute-done.4.refs_2_) | copy-start | bytes 393220
  172.5 0.7 copy-start.13
Sparse Core Ops, SparseCore 0:
  21.8 29.2 all-gather.6
  53.2 27.4 all-gather.4
  95.1 26.6 reduce-scatter.2
  135.4 26.6 reduce-scatter.4

commit v4 on v3

--- a/solution.py
+++ b/solution.py
@@ -20,22 +20,20 @@
 
 
 def attention_kernel(
-    parts,
+    layout,
     heads_per,
+    earlier,
     len_ref,
     q_ref,
     g_ref,
-    cache_ref,
     kr_ref,
     vr_ref,
     *rest,
 ):
+    caches, rest = rest[: layout.caches], rest[layout.caches + earlier :]
+    out_ref, dq_ref, dkr_ref, dvr_ref, *rest = rest
+    dcaches, rest = rest[: layout.dcaches], rest[layout.dcaches :]
     (
-        out_ref,
-        dq_ref,
-        dkr_ref,
-        dvr_ref,
-        dcache_ref,
         keys,
         values,
         keys_t,
@@ -59,10 +57,9 @@
         dv_sum,
         tops,
         sums,
-    ) = rest[-28:]
+    ) = rest
     rows = q_ref.shape[0]
-    part_rows = cache_ref.shape[2]
-    prompt_rows = parts * part_rows
+    prompt_rows = layout.prompt_rows
     total_rows = prompt_rows + rows
     half = rows // 2
     pieces = [(at, rows, 0) for at in range(0, prompt_rows, rows)]
@@ -79,12 +76,13 @@
 
     @pl.when(step == 0)
     def _():
-        for p in range(parts):
-            at = pl.ds(p * part_rows, part_rows)
-            keys[at, :] = cache_ref[p, 0]
-            values[at, :] = cache_ref[p, 1]
-            keys_t[:, at] = cache_ref[p, 0].T
-            values_t[:, at] = cache_ref[p, 1].T
+        for at, key_block, value_block in layout.load(caches):
+            keys[at, :] = key_block
+            values[at, :] = value_block
+        for at in range(0, prompt_rows, rows):
+            at = pl.ds(at, rows)
+            keys_t[:, at] = keys[at, :].T
+            values_t[:, at] = values[at, :].T
         at = pl.ds(prompt_rows, rows)
         keys[at, :] = kr_ref[...]
         values[at, :] = vr_ref[...]
@@ -207,46 +205,105 @@
     @pl.when(step == heads_per)
     def _():
         run(heads_per % 2, False, True)
-        for p in range(parts):
-            at = pl.ds(p * part_rows, part_rows)
-            dcache_ref[p, 0] = (factor * dk_sum[at, :]).astype(BF16)
-            dcache_ref[p, 1] = dv_sum[at, :].astype(BF16)
+        layout.store(dcaches, dk_sum, dv_sum, factor)
         at = pl.ds(prompt_rows, rows)
         dkr_ref[...] = (factor * dk_sum[at, :]).astype(BF16)
         dvr_ref[...] = dv_sum[at, :].astype(BF16)
 
 
-def attend(pair, heads_per, lengths, queries, out_grad, cache, resp_keys, resp_values, earlier):
+class Gathered:
+    def __init__(self, members, ranks, own_rows):
+        self.members, self.ranks, self.own_rows = members, ranks, own_rows
+        self.part_rows = ranks * own_rows
+        self.prompt_rows = members * self.part_rows
+        self.caches = 1
+        self.dcaches = members * ranks
+
+    def cache_shapes(self):
+        return [(self.members, 2, self.part_rows, HD)]
+
+    def dcache_shapes(self):
+        return [(2, self.own_rows, HD)] * self.dcaches
+
+    def load(self, caches):
+        for m in range(self.members):
+            at = pl.ds(m * self.part_rows, self.part_rows)
+            yield at, caches[0][m, 0], caches[0][m, 1]
+
+    def store(self, dcaches, dk_sum, dv_sum, factor):
+        me = lax.axis_index("resp")
+        for shift in range(self.members):
+            part = lax.rem(me + shift, self.members) * self.part_rows
+            for i in range(self.ranks):
+                at = pl.multiple_of(part + i * self.own_rows, self.own_rows)
+                at = pl.ds(at, self.own_rows)
+                ref = dcaches[shift * self.ranks + i]
+                ref[0] = (factor * dk_sum[at, :]).astype(BF16)
+                ref[1] = dv_sum[at, :].astype(BF16)
+
+
+class Scattered(Gathered):
+    def __init__(self, members, ranks, own_rows):
+        super().__init__(members, ranks, own_rows)
+        self.caches, self.dcaches = self.dcaches, self.caches
+
+    def cache_shapes(self):
+        return [(2, self.own_rows, HD)] * self.caches
+
+    def dcache_shapes(self):
+        return [(self.members, 2, self.part_rows, HD)]
+
+    def load(self, caches):
+        for i, ref in enumerate(caches):
+            yield pl.ds(i * self.own_rows, self.own_rows), ref[0], ref[1]
+
+    def store(self, dcaches, dk_sum, dv_sum, factor):
+        me = lax.axis_index("resp")
+        for shift in range(self.members):
+            part = lax.rem(me - shift + self.members, self.members)
+            at = pl.ds(shift * self.part_rows, self.part_rows)
+            dcaches[0][part, 0] = (factor * dk_sum[at, :]).astype(BF16)
+            dcaches[0][part, 1] = dv_sum[at, :].astype(BF16)
+
+
+def attend(
+    layout, pair, heads_per, lengths, queries, out_grad, caches, resp_keys, resp_values, earlier
+):
     rows, query_width = queries.shape
-    parts = cache.shape[0]
-    prompt_rows = parts * cache.shape[2]
-    total_rows = prompt_rows + rows
+    total_rows = layout.prompt_rows + rows
     first, last = pair * heads_per, (pair + 1) * heads_per - 1
     head_block = pl.BlockSpec((rows, HD), lambda s: (0, jnp.minimum(first + s, last)))
     late_block = pl.BlockSpec((rows, HD), lambda s: (0, jnp.maximum(first + s - 1, first)))
     pair_block = pl.BlockSpec((rows, HD), lambda s: (0, pair))
-    cache_block = pl.BlockSpec(cache.shape, lambda s: (0, 0, 0, 0))
+    cache_blocks = [
+        pl.BlockSpec(shape, lambda s, rank=len(shape): (0,) * rank)
+        for shape in layout.cache_shapes()
+    ]
+    dcache_blocks = [
+        pl.BlockSpec(shape, lambda s, rank=len(shape): (0,) * rank)
+        for shape in layout.dcache_shapes()
+    ]
     stats = total_rows // SUB * 8
     in_specs = [
         pl.BlockSpec(memory_space=pltpu.SMEM),
         head_block,
         head_block,
-        cache_block,
         pair_block,
         pair_block,
+        *cache_blocks,
     ] + [pl.BlockSpec(memory_space=pl.ANY)] * len(earlier)
-    aliases = {6 + i: i for i in range(len(earlier))}
+    aliases = {5 + layout.caches + i: i for i in range(len(earlier))}
     return pl.pallas_call(
-        functools.partial(attention_kernel, parts, heads_per),
+        functools.partial(attention_kernel, layout, heads_per, len(earlier)),
         grid=(heads_per + 1,),
         in_specs=in_specs,
-        out_specs=[head_block, late_block, pair_block, pair_block, cache_block],
+        out_specs=[head_block, late_block, pair_block, pair_block, *dcache_blocks],
         out_shape=[
             jax.ShapeDtypeStruct(queries.shape, BF16),
             jax.ShapeDtypeStruct(queries.shape, BF16),
             jax.ShapeDtypeStruct(resp_keys.shape, BF16),
             jax.ShapeDtypeStruct(resp_keys.shape, BF16),
-            jax.ShapeDtypeStruct(cache.shape, BF16),
+            *[jax.ShapeDtypeStruct(shape, BF16) for shape in layout.dcache_shapes()],
         ],
         scratch_shapes=[
             pltpu.VMEM((total_rows, HD), BF16),
@@ -279,90 +336,57 @@
             bytes_accessed=8 * heads_per * rows * HD,
             transcendentals=heads_per * rows * total_rows,
         ),
-        compiler_params=pltpu.CompilerParams(vmem_limit_bytes=48 * 1024 * 1024),
+        compiler_params=pltpu.CompilerParams(vmem_limit_bytes=60 * 1024 * 1024),
         name=f"attend_pair_{pair}",
-    )(lengths, queries, out_grad, cache, resp_keys, resp_values, *earlier)
+    )(lengths, queries, out_grad, resp_keys, resp_values, *caches, *earlier)
 
 
 def whole_block(shape):
     return pl.BlockSpec(shape, lambda: (0,) * len(shape))
 
 
-def cut_kernel(width, k_ref, v_ref, *outs):
+def cut_kernel(pairs, k_ref, v_ref, *outs):
     me = lax.axis_index("tensor")
-    for i, out in enumerate(outs):
-        columns = pl.ds(pl.multiple_of((me ^ i) * width, width), width)
-        out[0] = k_ref[:, columns]
-        out[1] = v_ref[:, columns]
-
-
-def cut(prompt_keys, prompt_values, width):
+    ranks = len(outs) // pairs
+    for p in range(pairs):
+        for i in range(ranks):
+            columns = pl.ds(pl.multiple_of(((me ^ i) * pairs + p) * HD, HD), HD)
+            outs[p * ranks + i][0] = k_ref[:, columns]
+            outs[p * ranks + i][1] = v_ref[:, columns]
+
+
+def cut(prompt_keys, prompt_values, pairs):
     rows, columns = prompt_keys.shape
-    count = columns // width
-    return pl.pallas_call(
-        functools.partial(cut_kernel, width),
+    count = columns // HD
+    blocks = pl.pallas_call(
+        functools.partial(cut_kernel, pairs),
         in_specs=[whole_block((rows, columns))] * 2,
-        out_specs=[whole_block((2, rows, width))] * count,
-        out_shape=[jax.ShapeDtypeStruct((2, rows, width), BF16)] * count,
+        out_specs=[whole_block((2, rows, HD))] * count,
+        out_shape=[jax.ShapeDtypeStruct((2, rows, HD), BF16)] * count,
         name="cut",
     )(prompt_keys, prompt_values)
-
-
-def line_up_kernel(ins, *refs):
-    ins, outs = refs[:ins], refs[ins:]
-    for i, block in enumerate(ins):
-        rows = block.shape[1]
-        for p, out in enumerate(outs):
-            out[:, i * rows : (i + 1) * rows, :] = block[:, :, p * HD : (p + 1) * HD]
-
-
-def line_up(blocks):
-    _, rows, width = blocks[0].shape
-    shape = (2, rows * len(blocks), HD)
-    return pl.pallas_call(
-        functools.partial(line_up_kernel, len(blocks)),
-        in_specs=[whole_block(blocks[0].shape)] * len(blocks),
-        out_specs=[whole_block(shape)] * (width // HD),
-        out_shape=[jax.ShapeDtypeStruct(shape, BF16)] * (width // HD),
-        name="line_up",
-    )(*blocks)
-
-
-def split_kernel(ins, *refs):
-    ins, outs = refs[:ins], refs[ins:]
-    for p, block in enumerate(ins):
-        for i, out in enumerate(outs):
-            rows = out.shape[1]
-            out[:, :, p * HD : (p + 1) * HD] = block[:, i * rows : (i + 1) * rows, :]
-
-
-def split(sums, rows):
-    count = sums[0].shape[1] // rows
-    shape = (2, rows, HD * len(sums))
-    return pl.pallas_call(
-        functools.partial(split_kernel, len(sums)),
-        in_specs=[whole_block(sums[0].shape)] * len(sums),
-        out_specs=[whole_block(shape)] * count,
-        out_shape=[jax.ShapeDtypeStruct(shape, BF16)] * count,
-        name="split",
-    )(*sums)
-
-
-def place_kernel(*refs):
+    return [blocks[p * count // pairs : (p + 1) * count // pairs] for p in range(pairs)]
+
+
+def place_kernel(members, pairs, *refs):
     *ins, dk_ref, dv_ref = refs
     me = lax.axis_index("tensor")
-    for i, block in enumerate(ins):
-        width = block.shape[2]
-        columns = pl.ds(pl.multiple_of((me ^ i) * width, width), width)
-        dk_ref[:, columns] = block[0].astype(F32)
-        dv_ref[:, columns] = block[1].astype(F32)
-
-
-def place(blocks):
-    _, rows, width = blocks[0].shape
-    shape = (rows, width * len(blocks))
+    ranks = dk_ref.shape[1] // HD // pairs
+    for i in range(ranks):
+        at = 0
+        for p, count in enumerate(members):
+            columns = pl.ds(pl.multiple_of(((me ^ i) * pairs + p) * HD, HD), HD)
+            blocks = [ins[at + m * ranks + i] for m in range(count)]
+            at += count * ranks
+            dk_ref[:, columns] = sum(block[0].astype(F32) for block in blocks)
+            dv_ref[:, columns] = sum(block[1].astype(F32) for block in blocks)
+
+
+def place(blocks, members, pairs, columns):
+    _, rows, _ = blocks[0].shape
+    shape = (rows, columns)
     return pl.pallas_call(
-        place_kernel,
+        functools.partial(place_kernel, members, pairs),
         in_specs=[whole_block(blocks[0].shape)] * len(blocks),
         out_specs=[whole_block(shape)] * 2,
         out_shape=[jax.ShapeDtypeStruct(shape, F32)] * 2,
@@ -370,7 +394,7 @@
     )(*blocks)
 
 
-def exchange(blocks):
+def swap(blocks):
     count = len(blocks)
     return [blocks[0]] + [
         lax.ppermute(blocks[i], "tensor", [(j, j ^ i) for j in range(count)])
@@ -378,26 +402,78 @@
     ]
 
 
-def per_device(queries, resp_keys, resp_values, prompt_keys, prompt_values, out_grad, lengths):
-    _, seq_len, query_width = queries.shape
+def send(block, members, ranks, shift, i):
+    if shift == 0 and i == 0:
+        return block
+    pairs = [
+        (m * ranks + j, (m + shift) % members * ranks + (j ^ i))
+        for m in range(members)
+        for j in range(ranks)
+    ]
+    return lax.ppermute(block, ("resp", "tensor"), pairs)
+
+
+def cut_rows(block, count):
+    rows = block.shape[1] // count
+    return [block[:, i * rows : (i + 1) * rows] for i in range(count)]
+
+
+def per_device(
+    members, ranks, queries, resp_keys, resp_values, prompt_keys, prompt_values, out_grad, lengths
+):
+    query_width = queries.shape[2]
     pair_width = resp_keys.shape[2]
     pairs = pair_width // HD
     heads_per = query_width // pair_width
+    own_rows, columns = prompt_keys.shape
     queries, out_grad, resp_keys, resp_values = (
         a[0] for a in (queries, out_grad, resp_keys, resp_values)
     )
-    own = line_up(exchange(cut(prompt_keys, prompt_values, pair_width)))
-    caches = [lax.all_gather(own[p], "resp", axis=0) for p in range(pairs)]
+    cuts = cut(prompt_keys, prompt_values, pairs)
+    kinds = [Scattered(members, ranks, own_rows)]
+    kinds += [Gathered(members, ranks, own_rows) for _ in range(pairs - 1)]
+    caches = [
+        [send(cuts[0][i], members, ranks, shift, i) for shift in range(members) for i in range(ranks)]
+    ]
+    for p in range(1, pairs):
+        own = jnp.concatenate(swap(cuts[p]), axis=1)
+        own, caches[0] = lax.optimization_barrier((own, caches[0]))
+        caches.append([lax.all_gather(own, "resp", axis=0)])
     earlier = ()
-    sums = []
+    total = None
+    blocks, counts = [], []
     for p in range(pairs):
-        *earlier, dcache = attend(
-            p, heads_per, lengths, queries, out_grad, caches[p], resp_keys, resp_values, earlier
+        results = attend(
+            kinds[p],
+            p,
+            heads_per,
+            lengths,
+            queries,
+            out_grad,
+            caches[p],
+            resp_keys,
+            resp_values,
+            earlier,
         )
-        if sums:
-            dcache, sums[-1] = lax.optimization_barrier((dcache, sums[-1]))
-        sums.append(lax.psum_scatter(dcache, "resp", scatter_dimension=0))
-    key_grad, value_grad = place(exchange(split(sums, prompt_keys.shape[0])))
+        earlier, dcaches = results[:4], results[4:]
+        if total is not None:
+            dcaches, total = lax.optimization_barrier((dcaches, total))
+            blocks += swap(cut_rows(total, ranks))
+            counts.append(1)
+            total = None
+        if isinstance(kinds[p], Scattered):
+            total = lax.psum_scatter(dcaches[0], "resp", scatter_dimension=0)
+        else:
+            blocks += [
+                send(dcaches[shift * ranks + i], members, ranks, shift, i)
+                for shift in range(members)
+                for i in range(ranks)
+            ]
+            counts.append(members)
+    if total is not None:
+        blocks += swap(cut_rows(total, ranks))
+        counts.append(1)
+    key_grad, value_grad = place(blocks, counts, pairs, columns)
     return (*(a[None] for a in earlier), key_grad, value_grad)
 
 
@@ -405,7 +481,7 @@
     rows = P(("group", "resp"), None, "tensor")
     prompt = P(("group", "resp", "tensor"), None)
     return jax.shard_map(
-        per_device,
+        functools.partial(per_device, mesh.shape["resp"], mesh.shape["tensor"]),
         mesh=mesh,
         in_specs=(rows, rows, rows, prompt, prompt, rows, P(("group", "resp"))),
         out_specs=(rows, rows, rows, rows, prompt, prompt),

time: 182 us -> 169 us (0.929)
  waiting for transfers between devices: 69.1 us -> 16.7 us
  starting transfers between devices: 5.11 us -> 48.1 us
  local copies, waits for them, and re-layouts: 7.27 us -> 2.18 us
    ppermute x6 -> x36, starting transfers between devices: 4.95 us -> 48 us  [the longest x30 43.1 us: send(): return lax.ppermute(block, ('resp', 'tensor'), pairs)]
    all_gather x2 -> x1, waiting for transfers between devices: 28 us -> 0.02 us  [per_device(): caches.append([lax.all_gather(own, 'resp', axis=0)])]
    reduce_scatter x2 -> x1, waiting for transfers between devices: 26.8 us -> 0.02 us  [per_device(): total = lax.psum_scatter(dcaches[0], 'resp', scatter_dimension=0)]
    unnamed x28 -> x66, local copies, waits for them, and re-layouts: 7.27 us -> 0.59 us
    ppermute x6 -> x36, waiting for transfers between devices: 13.5 us -> 16.6 us  [the longest x30 14.9 us: send(): return lax.ppermute(block, ('resp', 'tensor'), pairs)]
    pallas_call x6 -> x4, Pallas kernels: 85.9 us -> 84.3 us  [the longest x2 79.9 us: attend(): pl.pallas_call(functools.partial(attention_kernel, layout, heads_per, len...]
  transfers between devices with their start and end apart: 10 -> 38, of which waited for: 6 -> 10; matrix products, arithmetic and copies ran while one was open for 0% -> 1% of each run, Pallas kernels for 43% -> 48%
where the time goes in v4:
time: 169 us; the launch traced here: 168 us
  Pallas kernels  84.3 us (50%)
  starting transfers between devices  48.1 us (28%)
  waiting for transfers between devices  16.7 us (10%)
  between operations  15.1 us (9%)
  local copies, waits for them, and re-layouts  2.18 us (1%)
    pallas_call x2, Pallas kernels, attend(): pl.pallas_call(functools.partial(attention_kernel, layout, heads_per, len...  79.9 us
    ppermute x30, starting transfers between devices, send(): return lax.ppermute(block, ('resp', 'tensor'), pairs)  43.1 us
    ppermute x30, waiting for transfers between devices, send(): return lax.ppermute(block, ('resp', 'tensor'), pairs)  14.9 us
    ppermute x6, starting transfers between devices, swap(): lax.ppermute(blocks[i], 'tensor', [(j, j ^ i) for j in range(count)])  4.95 us
  transfers between devices with their start and end apart: 38, of which 10 were waited for; matrix products, arithmetic and copies ran while one was open for 1% of the time, Pallas kernels for 48%

profile of v4, /device:TPU:0, one launch (start us, length us, event | category | flops | bytes accessed | tf_op | source)
XLA Modules:
  0.0 167.9 jit_solution(8253809149815513891)
XLA Ops:
  7.2 0.0 all-gather.3.cloned.1.call-start
  7.2 1.9 %cut.1 = (bf16[2,128,128]{2,1,0:T(8,128)(2,1)}, bf16[2,128,128]{2,1,0:T(8,128)(2,1)}, bf16[2,128,128]{2,1,0:T(8,128)(2,1)}, bf16[2,128,128]{2,1,0:T(8,128)(2,1)}...) custom-call(bf16[128,1024]{1,0:T(8,128)(2,1)} %k_ref.1, ...), custom_call_target="tpu_custom_call" | custom-call | tf_op jit(solution)/shard_map/cut/pallas_call | solution.py:361
  9.1 0.5 collective-permute-start
  9.6 2.5 %collective-permute-start.1 = (bf16[2,128,128]{2,1,0:T(8,128)(2,1)}, bf16[2,128,128]{2,1,0:T(8,128)(2,1)S(1)}, u32[]{:S(2)}, u32[]{:S(2)}) collective-permute-start(bf16[2,128,128]{2,1,0:T(8,128)(2,1)} %get-tuple-element.77), channel_id=1, source_target_pairs={{0,2},{1,3},{2,0},{3,1},{4,6},{5,7},{6,4},{7,5},{8,10},{9,11},{10,... | collective-permute-start | bytes 196616 | tf_op jit(solution)/shard_map/ppermute | solution.py:400
  12.1 0.1 collective-permute-start.2
  12.2 3.8 %collective-permute-start.14 = (bf16[2,128,128]{2,1,0:T(8,128)(2,1)}, bf16[2,128,128]{2,1,0:T(8,128)(2,1)S(1)}, u32[]{:S(2)}, u32[]{:S(2)}) collective-permute-start(bf16[2,128,128]{2,1,0:T(8,128)(2,1)} %get-tuple-element.84.rest_0_), channel_id=1, source_target_pairs={{0,12},{1,13},{2,14},{3,15},{4,0},{5,1},{6,2},{7,3},{8,4},{9,5},{1... | collective-permute-start | bytes 196616 | tf_op jit(solution)/shard_map/ppermute | solution.py:413
  16.1 0.0 collective-permute-start.10
  16.1 0.0 collective-permute-done
  16.1 1.0 collective-permute-start.6
  17.1 0.0 collective-permute-done.1
  17.1 2.2 %collective-permute-start.15 = (bf16[2,128,128]{2,1,0:T(8,128)(2,1)}, bf16[2,128,128]{2,1,0:T(8,128)(2,1)S(1)}, u32[]{:S(2)}, u32[]{:S(2)}) collective-permute-start(bf16[2,128,128]{2,1,0:T(8,128)(2,1)} %get-tuple-element.80), channel_id=1, source_target_pairs={{0,13},{1,12},{2,15},{3,14},{4,1},{5,0},{6,3},{7,2},{8,5},{9,4},{1... | collective-permute-start | bytes 196616 | tf_op jit(solution)/shard_map/ppermute | solution.py:413
  19.3 0.0 collective-permute-done.2
  19.3 1.5 collective-permute-start.11
  20.7 0.0 collective-permute-done.14.rest_12_
  20.8 3.2 %collective-permute-done.10.rest_8_ = bf16[2,128,128]{2,1,0:T(8,128)(2,1)S(1)} collective-permute-done((bf16[2,128,128]{2,1,0:T(8,128)(2,1)}, bf16[2,128,128]{2,1,0:T(8,128)(2,1)S(1)}, u32[]{:S(2)}, u32[]{:S(2)}) %collective-permute-start.10) | collective-permute-done | bytes 65568 | tf_op jit(solution)/shard_map/ppermute | solution.py:413
  23.9 2.3 %collective-permute-start.16 = (bf16[2,128,128]{2,1,0:T(8,128)(2,1)}, bf16[2,128,128]{2,1,0:T(8,128)(2,1)S(1)}, u32[]{:S(2)}, u32[]{:S(2)}) collective-permute-start(bf16[2,128,128]{2,1,0:T(8,128)(2,1)} %get-tuple-element.81), channel_id=1, source_target_pairs={{0,14},{1,15},{2,12},{3,13},{4,2},{5,3},{6,0},{7,1},{8,6},{9,7},{1... | collective-permute-start | bytes 196616 | tf_op jit(solution)/shard_map/ppermute | solution.py:413
  26.3 3.2 %collective-permute-start.12 = (bf16[2,128,128]{2,1,0:T(8,128)(2,1)}, bf16[2,128,128]{2,1,0:T(8,128)(2,1)S(1)}, u32[]{:S(2)}, u32[]{:S(2)}) collective-permute-start(bf16[2,128,128]{2,1,0:T(8,128)(2,1)} %get-tuple-element.81), channel_id=1, source_target_pairs={{0,10},{1,11},{2,8},{3,9},{4,14},{5,15},{6,12},{7,13},{8,2},{9,3},... | collective-permute-start | bytes 196616 | tf_op jit(solution)/shard_map/ppermute | solution.py:413
  29.4 2.8 %collective-permute-start.8 = (bf16[2,128,128]{2,1,0:T(8,128)(2,1)}, bf16[2,128,128]{2,1,0:T(8,128)(2,1)S(1)}, u32[]{:S(2)}, u32[]{:S(2)}) collective-permute-start(bf16[2,128,128]{2,1,0:T(8,128)(2,1)} %get-tuple-element.81), channel_id=1, source_target_pairs={{0,6},{1,7},{2,4},{3,5},{4,10},{5,11},{6,8},{7,9},{8,14},{9,15},{1... | collective-permute-start | bytes 196616 | tf_op jit(solution)/shard_map/ppermute | solution.py:413
  32.3 0.5 collective-permute-start.4
  32.8 0.0 collective-permute-done.3.rest_1_
  32.8 1.7 %collective-permute-start.17 = (bf16[2,128,128]{2,1,0:T(8,128)(2,1)}, bf16[2,128,128]{2,1,0:T(8,128)(2,1)S(1)}, u32[]{:S(2)}, u32[]{:S(2)}) collective-permute-start(bf16[2,128,128]{2,1,0:T(8,128)(2,1)} %get-tuple-element.82), channel_id=1, source_target_pairs={{0,15},{1,14},{2,13},{3,12},{4,3},{5,2},{6,1},{7,0},{8,7},{9,6},{1... | collective-permute-start | bytes 196616 | tf_op jit(solution)/shard_map/ppermute | solution.py:413
  34.6 0.0 collective-permute-done.16.rest_14_
  34.6 0.5 collective-permute-start.13
  35.1 2.5 %collective-permute-start.9 = (bf16[2,128,128]{2,1,0:T(8,128)(2,1)}, bf16[2,128,128]{2,1,0:T(8,128)(2,1)S(1)}, u32[]{:S(2)}, u32[]{:S(2)}) collective-permute-start(bf16[2,128,128]{2,1,0:T(8,128)(2,1)} %get-tuple-element.82), channel_id=1, source_target_pairs={{0,7},{1,6},{2,5},{3,4},{4,11},{5,10},{6,9},{7,8},{8,15},{9,14},{1... | collective-permute-start | bytes 196616 | tf_op jit(solution)/shard_map/ppermute | solution.py:413
  37.6 1.6 pad_maximum_fusion
  39.2 0.0 collective-permute-done.4.rest_2_
  39.2 0.0 collective-permute-done.17.rest_15_
  39.2 1.0 collective-permute-done.13.rest_11_
  40.3 1.9 %collective-permute-done.9.rest_7_ = bf16[2,128,128]{2,1,0:T(8,128)(2,1)S(1)} collective-permute-done((bf16[2,128,128]{2,1,0:T(8,128)(2,1)}, bf16[2,128,128]{2,1,0:T(8,128)(2,1)S(1)}, u32[]{:S(2)}, u32[]{:S(2)}) %collective-permute-start.9) | collective-permute-done | bytes 65568 | tf_op jit(solution)/shard_map/ppermute | solution.py:413
  42.2 1.6 collective-permute-done.5.rest_3_
  43.8 0.0 all-gather.3.cloned.1.call-update
  43.8 0.0 reduce-scatter.2.cloned.1.call-start
  44.7 39.7 %attend_pair_0.1 = (bf16[512,2048]{1,0:T(8,128)(2,1)}, bf16[512,2048]{1,0:T(8,128)(2,1)}, bf16[512,256]{1,0:T(8,128)(2,1)}, bf16[512,256]{1,0:T(8,128)(2,1)}, bf16[4,2,512,128]{3,2,1,0:T(8,128)(2,1)}) custom-call(s32[1]{0:T(128)S(6)} %copy.21.len_ref, bf16[512,2048]{1,0:T(8,128)(2,1)} %bitcast.11, bf16[512,2048]{1,0:T(8,128)(2,1)} %bitcast.13, ...), custom_call_target="tpu_custom_call" | custom-call | flops 16106127360 | bytes 4194304 | tf_op jit(solution)/shard_map/attend_pair_0/pallas_call | solution.py:296
  84.4 0.0 reduce-scatter.2.cloned.1.call-update
  84.4 0.0 all-gather.3.cloned.1.call-done
  84.4 40.2 %attend_pair_1.1 = (bf16[512,2048]{1,0:T(8,128)(2,1)}, bf16[512,2048]{1,0:T(8,128)(2,1)}, bf16[512,256]{1,0:T(8,128)(2,1)}, bf16[512,256]{1,0:T(8,128)(2,1)}, bf...) custom-call(s32[1]{0:T(128)S(6)} %copy.21.len_ref, ...), custom_call_target="tpu_custom_call", output_to_operand_aliasing={{0}: (6, {}), {1}: (7, {}), {2}: (8, {}), {3}: (9, {})} | custom-call | flops 16106127360 | bytes 4194304 | tf_op jit(solution)/shard_map/attend_pair_1/pallas_call | solution.py:296
  124.7 0.0 reduce-scatter.2.cloned.1.call-done
  124.7 1.6 fusion
  126.3 0.7 collective-permute-start.20
  127.0 0.7 collective-permute-start.19
  127.7 0.5 collective-permute-start.18
  128.1 0.0 collective-permute-start.21
  128.2 1.3 collective-permute-start.22
  129.5 1.1 collective-permute-done.20.refs_3_
  130.6 0.8 collective-permute-start.23
  131.4 0.5 collective-permute-done.19.refs_2_
  132.0 1.2 collective-permute-start.24
  133.2 2.0 %collective-permute-start.26 = (bf16[2,128,128]{2,1,0:T(8,128)(2,1)}, bf16[2,128,128]{2,1,0:T(8,128)(2,1)S(1)}, u32[]{:S(2)}, u32[]{:S(2)}) collective-permute-start(bf16[2,128,128]{2,1,0:T(8,128)(2,1)} %get-tuple-element.132), channel_id=1, source_target_pairs={{0,6},{1,7},{2,4},{3,5},{4,10},{5,11},{6,8},{7,9},{8,14},{9,15},{1... | collective-permute-start | bytes 196616 | tf_op jit(solution)/shard_map/ppermute | solution.py:413
  135.3 2.0 %collective-permute-start.27 = (bf16[2,128,128]{2,1,0:T(8,128)(2,1)}, bf16[2,128,128]{2,1,0:T(8,128)(2,1)S(1)}, u32[]{:S(2)}, u32[]{:S(2)}) collective-permute-start(bf16[2,128,128]{2,1,0:T(8,128)(2,1)} %get-tuple-element.133), channel_id=1, source_target_pairs={{0,7},{1,6},{2,5},{3,4},{4,11},{5,10},{6,9},{7,8},{8,15},{9,14},{1... | collective-permute-start | bytes 196616 | tf_op jit(solution)/shard_map/ppermute | solution.py:413
  137.3 1.5 collective-permute-start.28
  138.8 0.9 collective-permute-start.29
  139.7 1.9 %collective-permute-start.30 = (bf16[2,128,128]{2,1,0:T(8,128)(2,1)}, bf16[2,128,128]{2,1,0:T(8,128)(2,1)S(1)}, u32[]{:S(2)}, u32[]{:S(2)}) collective-permute-start(bf16[2,128,128]{2,1,0:T(8,128)(2,1)} %get-tuple-element.136), channel_id=1, source_target_pairs={{0,10},{1,11},{2,8},{3,9},{4,14},{5,15},{6,12},{7,13},{8,2},{9,3},... | collective-permute-start | bytes 196616 | tf_op jit(solution)/shard_map/ppermute | solution.py:413
  141.7 0.9 collective-permute-done.26.refs_10_
  142.5 0.9 collective-permute-start.31
  143.5 2.4 %collective-permute-start.32 = (bf16[2,128,128]{2,1,0:T(8,128)(2,1)}, bf16[2,128,128]{2,1,0:T(8,128)(2,1)S(1)}, u32[]{:S(2)}, u32[]{:S(2)}) collective-permute-start(bf16[2,128,128]{2,1,0:T(8,128)(2,1)} %get-tuple-element.138), channel_id=1, source_target_pairs={{0,12},{1,13},{2,14},{3,15},{4,0},{5,1},{6,2},{7,3},{8,4},{9,5},{1... | collective-permute-start | bytes 196616 | tf_op jit(solution)/shard_map/ppermute | solution.py:413
  145.9 3.7 %collective-permute-done.28.refs_12_ = bf16[2,128,128]{2,1,0:T(8,128)(2,1)S(1)} collective-permute-done((bf16[2,128,128]{2,1,0:T(8,128)(2,1)}, bf16[2,128,128]{2,1,0:T(8,128)(2,1)S(1)}, u32[]{:S(2)}, u32[]{:S(2)}) %collective-permute-start.28) | collective-permute-done | bytes 65568 | tf_op jit(solution)/shard_map/ppermute | solution.py:413
  149.5 1.4 collective-permute-start.33
  151.0 2.2 %collective-permute-start.34 = (bf16[2,128,128]{2,1,0:T(8,128)(2,1)}, bf16[2,128,128]{2,1,0:T(8,128)(2,1)S(1)}, u32[]{:S(2)}, u32[]{:S(2)}) collective-permute-start(bf16[2,128,128]{2,1,0:T(8,128)(2,1)} %get-tuple-element.140), channel_id=1, source_target_pairs={{0,14},{1,15},{2,12},{3,13},{4,2},{5,3},{6,0},{7,1},{8,6},{9,7},{1... | collective-permute-start | bytes 196616 | tf_op jit(solution)/shard_map/ppermute | solution.py:413
  153.2 0.0 collective-permute-done.30.refs_14_
  153.2 2.2 %collective-permute-start.35 = (bf16[2,128,128]{2,1,0:T(8,128)(2,1)}, bf16[2,128,128]{2,1,0:T(8,128)(2,1)S(1)}, u32[]{:S(2)}, u32[]{:S(2)}) collective-permute-start(bf16[2,128,128]{2,1,0:T(8,128)(2,1)} %get-tuple-element.141), channel_id=1, source_target_pairs={{0,15},{1,14},{2,13},{3,12},{4,3},{5,2},{6,1},{7,0},{8,7},{9,6},{1... | collective-permute-start | bytes 196616 | tf_op jit(solution)/shard_map/ppermute | solution.py:413
  155.4 1.4 collective-permute-done.34.refs_18_
  156.8 1.2 collective-permute-done.35.refs_19_
  158.2 0.5 copy-done.17
  158.6 2.4 %place.1 = (f32[128,1024]{1,0:T(8,128)}, f32[128,1024]{1,0:T(8,128)}) custom-call(bf16[2,128,128]{2,1,0:T(8,128)(2,1)} %get-tuple-element.147.refs_0_, bf16[2,128,128]{2,1,0:T(8,128)(2,1)} %copy-done.2, bf16[2,128,128]{2,1,0:T(8,128)(2,1)} %copy-done.1, bf16[2,128,128]{2,1,0:T(8,128)(2,1)} %copy-done, bf16[2,128,128]{2,1,0:T(8,128)(2,1)} %get-tuple-element.126.refs_4_, ...), custom_call_target="tpu_custom_call" | custom-call | tf_op jit(solution)/shard_map/place/pallas_call | solution.py:388
  (86 shorter events, 0.2 us)
Async XLA Ops:
  7.2 77.3 %all-gather.3.cloned.1.call-start = ((), (), s32[]{:S(2)}) async-start(), calls=%async_computation.2 | async-start | bytes 1310720 | tf_op jit(solution)/shard_map/all_gather | solution.py:441
  9.1 6.9 %collective-permute-start = (bf16[2,128,128]{2,1,0:T(8,128)(2,1)}, bf16[2,128,128]{2,1,0:T(8,128)(2,1)S(1)}, u32[]{:S(2)}, u32[]{:S(2)}) collective-permute-start(bf16[2,128,128]{2,1,0:T(8,128)(2,1)} %get-tuple-element.76), channel_id=1, source_target_pairs={{0,1},{1,0},{2,3},{3,2},{4,5},{5,4},{6,7},{7,6},{8,9},{9,8},{10,11... | collective-permute-start | bytes 196616 | tf_op jit(solution)/shard_map/ppermute | solution.py:400
  9.6 7.5 %collective-permute-start.1 = (bf16[2,128,128]{2,1,0:T(8,128)(2,1)}, bf16[2,128,128]{2,1,0:T(8,128)(2,1)S(1)}, u32[]{:S(2)}, u32[]{:S(2)}) collective-permute-start(bf16[2,128,128]{2,1,0:T(8,128)(2,1)} %get-tuple-element.77), channel_id=1, source_target_pairs={{0,2},{1,3},{2,0},{3,1},{4,6},{5,7},{6,4},{7,5},{8,10},{9,11},{10,... | collective-permute-start | bytes 196616 | tf_op jit(solution)/shard_map/ppermute | solution.py:400
  12.1 7.1 %collective-permute-start.2 = (bf16[2,128,128]{2,1,0:T(8,128)(2,1)}, bf16[2,128,128]{2,1,0:T(8,128)(2,1)S(1)}, u32[]{:S(2)}, u32[]{:S(2)}) collective-permute-start(bf16[2,128,128]{2,1,0:T(8,128)(2,1)} %get-tuple-element.78), channel_id=1, source_target_pairs={{0,3},{1,2},{2,1},{3,0},{4,7},{5,6},{6,5},{7,4},{8,11},{9,10},{10,... | collective-permute-start | bytes 196616 | tf_op jit(solution)/shard_map/ppermute | solution.py:400
  12.2 8.5 %collective-permute-start.14 = (bf16[2,128,128]{2,1,0:T(8,128)(2,1)}, bf16[2,128,128]{2,1,0:T(8,128)(2,1)S(1)}, u32[]{:S(2)}, u32[]{:S(2)}) collective-permute-start(bf16[2,128,128]{2,1,0:T(8,128)(2,1)} %get-tuple-element.84.rest_0_), channel_id=1, source_target_pairs={{0,12},{1,13},{2,14},{3,15},{4,0},{5,1},{6,2},{7,3},{8,4},{9,5},{1... | collective-permute-start | bytes 196616 | tf_op jit(solution)/shard_map/ppermute | solution.py:413
  16.1 7.8 %collective-permute-start.10 = (bf16[2,128,128]{2,1,0:T(8,128)(2,1)}, bf16[2,128,128]{2,1,0:T(8,128)(2,1)S(1)}, u32[]{:S(2)}, u32[]{:S(2)}) collective-permute-start(bf16[2,128,128]{2,1,0:T(8,128)(2,1)} %get-tuple-element.84.rest_0_), channel_id=1, source_target_pairs={{0,8},{1,9},{2,10},{3,11},{4,12},{5,13},{6,14},{7,15},{8,0},{9,1},... | collective-permute-start | bytes 196616 | tf_op jit(solution)/shard_map/ppermute | solution.py:413
  16.1 7.8 %collective-permute-start.6 = (bf16[2,128,128]{2,1,0:T(8,128)(2,1)}, bf16[2,128,128]{2,1,0:T(8,128)(2,1)S(1)}, u32[]{:S(2)}, u32[]{:S(2)}) collective-permute-start(bf16[2,128,128]{2,1,0:T(8,128)(2,1)} %get-tuple-element.84.rest_0_), channel_id=1, source_target_pairs={{0,4},{1,5},{2,6},{3,7},{4,8},{5,9},{6,10},{7,11},{8,12},{9,13},{1... | collective-permute-start | bytes 196616 | tf_op jit(solution)/shard_map/ppermute | solution.py:413
  17.1 9.2 %collective-permute-start.15 = (bf16[2,128,128]{2,1,0:T(8,128)(2,1)}, bf16[2,128,128]{2,1,0:T(8,128)(2,1)S(1)}, u32[]{:S(2)}, u32[]{:S(2)}) collective-permute-start(bf16[2,128,128]{2,1,0:T(8,128)(2,1)} %get-tuple-element.80), channel_id=1, source_target_pairs={{0,13},{1,12},{2,15},{3,14},{4,1},{5,0},{6,3},{7,2},{8,5},{9,4},{1... | collective-permute-start | bytes 196616 | tf_op jit(solution)/shard_map/ppermute | solution.py:413
  19.3 10.2 %collective-permute-start.11 = (bf16[2,128,128]{2,1,0:T(8,128)(2,1)}, bf16[2,128,128]{2,1,0:T(8,128)(2,1)S(1)}, u32[]{:S(2)}, u32[]{:S(2)}) collective-permute-start(bf16[2,128,128]{2,1,0:T(8,128)(2,1)} %get-tuple-element.80), channel_id=1, source_target_pairs={{0,9},{1,8},{2,11},{3,10},{4,13},{5,12},{6,15},{7,14},{8,1},{9,0},... | collective-permute-start | bytes 196616 | tf_op jit(solution)/shard_map/ppermute | solution.py:413
  20.7 23.8 %copy-start.18 = (bf16[2,128,128]{2,1,0:T(8,128)(2,1)}, bf16[2,128,128]{2,1,0:T(8,128)(2,1)S(1)}, u32[]{:S(2)}) copy-start(bf16[2,128,128]{2,1,0:T(8,128)(2,1)S(1)} %collective-permute-done.14.rest_12_) | copy-start | bytes 196612
  20.7 11.5 %collective-permute-start.7 = (bf16[2,128,128]{2,1,0:T(8,128)(2,1)}, bf16[2,128,128]{2,1,0:T(8,128)(2,1)S(1)}, u32[]{:S(2)}, u32[]{:S(2)}) collective-permute-start(bf16[2,128,128]{2,1,0:T(8,128)(2,1)} %get-tuple-element.80), channel_id=1, source_target_pairs={{0,5},{1,4},{2,7},{3,6},{4,9},{5,8},{6,11},{7,10},{8,13},{9,12},{1... | collective-permute-start | bytes 196616 | tf_op jit(solution)/shard_map/ppermute | solution.py:413
  23.9 20.6 %copy-start.19 = (bf16[2,128,128]{2,1,0:T(8,128)(2,1)}, bf16[2,128,128]{2,1,0:T(8,128)(2,1)S(1)}, u32[]{:S(2)}) copy-start(bf16[2,128,128]{2,1,0:T(8,128)(2,1)S(1)} %collective-permute-done.10.rest_8_) | copy-start | bytes 196612
  23.9 8.9 %collective-permute-start.3 = (bf16[2,128,128]{2,1,0:T(8,128)(2,1)}, bf16[2,128,128]{2,1,0:T(8,128)(2,1)S(1)}, u32[]{:S(2)}, u32[]{:S(2)}) collective-permute-start(bf16[2,128,128]{2,1,0:T(8,128)(2,1)} %get-tuple-element.80), channel_id=1, source_target_pairs={{0,1},{1,0},{2,3},{3,2},{4,5},{5,4},{6,7},{7,6},{8,9},{9,8},{10,11... | collective-permute-start | bytes 196616 | tf_op jit(solution)/shard_map/ppermute | solution.py:413
  23.9 20.6 %copy-start.20 = (bf16[2,128,128]{2,1,0:T(8,128)(2,1)}, bf16[2,128,128]{2,1,0:T(8,128)(2,1)S(1)}, u32[]{:S(2)}) copy-start(bf16[2,128,128]{2,1,0:T(8,128)(2,1)S(1)} %collective-permute-done.6.rest_4_) | copy-start | bytes 196612
  23.9 10.7 %collective-permute-start.16 = (bf16[2,128,128]{2,1,0:T(8,128)(2,1)}, bf16[2,128,128]{2,1,0:T(8,128)(2,1)S(1)}, u32[]{:S(2)}, u32[]{:S(2)}) collective-permute-start(bf16[2,128,128]{2,1,0:T(8,128)(2,1)} %get-tuple-element.81), channel_id=1, source_target_pairs={{0,14},{1,15},{2,12},{3,13},{4,2},{5,3},{6,0},{7,1},{8,6},{9,7},{1... | collective-permute-start | bytes 196616 | tf_op jit(solution)/shard_map/ppermute | solution.py:413
  26.3 18.3 %copy-start.21 = (bf16[2,128,128]{2,1,0:T(8,128)(2,1)}, bf16[2,128,128]{2,1,0:T(8,128)(2,1)S(1)}, u32[]{:S(2)}) copy-start(bf16[2,128,128]{2,1,0:T(8,128)(2,1)S(1)} %collective-permute-done.15.rest_13_) | copy-start | bytes 196612
  26.3 8.9 %collective-permute-start.12 = (bf16[2,128,128]{2,1,0:T(8,128)(2,1)}, bf16[2,128,128]{2,1,0:T(8,128)(2,1)S(1)}, u32[]{:S(2)}, u32[]{:S(2)}) collective-permute-start(bf16[2,128,128]{2,1,0:T(8,128)(2,1)} %get-tuple-element.81), channel_id=1, source_target_pairs={{0,10},{1,11},{2,8},{3,9},{4,14},{5,15},{6,12},{7,13},{8,2},{9,3},... | collective-permute-start | bytes 196616 | tf_op jit(solution)/shard_map/ppermute | solution.py:413
  29.4 15.1 %copy-start.22 = (bf16[2,128,128]{2,1,0:T(8,128)(2,1)}, bf16[2,128,128]{2,1,0:T(8,128)(2,1)S(1)}, u32[]{:S(2)}) copy-start(bf16[2,128,128]{2,1,0:T(8,128)(2,1)S(1)} %collective-permute-done.11.rest_9_) | copy-start | bytes 196612
  29.4 8.2 %collective-permute-start.8 = (bf16[2,128,128]{2,1,0:T(8,128)(2,1)}, bf16[2,128,128]{2,1,0:T(8,128)(2,1)S(1)}, u32[]{:S(2)}, u32[]{:S(2)}) collective-permute-start(bf16[2,128,128]{2,1,0:T(8,128)(2,1)} %get-tuple-element.81), channel_id=1, source_target_pairs={{0,6},{1,7},{2,4},{3,5},{4,10},{5,11},{6,8},{7,9},{8,14},{9,15},{1... | collective-permute-start | bytes 196616 | tf_op jit(solution)/shard_map/ppermute | solution.py:413
  32.3 12.3 %copy-start.23 = (bf16[2,128,128]{2,1,0:T(8,128)(2,1)}, bf16[2,128,128]{2,1,0:T(8,128)(2,1)S(1)}, u32[]{:S(2)}) copy-start(bf16[2,128,128]{2,1,0:T(8,128)(2,1)S(1)} %collective-permute-done.7.rest_5_) | copy-start | bytes 196612
  32.3 6.9 %collective-permute-start.4 = (bf16[2,128,128]{2,1,0:T(8,128)(2,1)}, bf16[2,128,128]{2,1,0:T(8,128)(2,1)S(1)}, u32[]{:S(2)}, u32[]{:S(2)}) collective-permute-start(bf16[2,128,128]{2,1,0:T(8,128)(2,1)} %get-tuple-element.81), channel_id=1, source_target_pairs={{0,2},{1,3},{2,0},{3,1},{4,6},{5,7},{6,4},{7,5},{8,10},{9,11},{10,... | collective-permute-start | bytes 196616 | tf_op jit(solution)/shard_map/ppermute | solution.py:413
  32.8 11.7 %copy-start.24 = (bf16[2,128,128]{2,1,0:T(8,128)(2,1)}, bf16[2,128,128]{2,1,0:T(8,128)(2,1)S(1)}, u32[]{:S(2)}) copy-start(bf16[2,128,128]{2,1,0:T(8,128)(2,1)S(1)} %collective-permute-done.3.rest_1_) | copy-start | bytes 196612
  32.8 6.4 %collective-permute-start.17 = (bf16[2,128,128]{2,1,0:T(8,128)(2,1)}, bf16[2,128,128]{2,1,0:T(8,128)(2,1)S(1)}, u32[]{:S(2)}, u32[]{:S(2)}) collective-permute-start(bf16[2,128,128]{2,1,0:T(8,128)(2,1)} %get-tuple-element.82), channel_id=1, source_target_pairs={{0,15},{1,14},{2,13},{3,12},{4,3},{5,2},{6,1},{7,0},{8,7},{9,6},{1... | collective-permute-start | bytes 196616 | tf_op jit(solution)/shard_map/ppermute | solution.py:413
  34.6 10.0 %copy-start.25 = (bf16[2,128,128]{2,1,0:T(8,128)(2,1)}, bf16[2,128,128]{2,1,0:T(8,128)(2,1)S(1)}, u32[]{:S(2)}) copy-start(bf16[2,128,128]{2,1,0:T(8,128)(2,1)S(1)} %collective-permute-done.16.rest_14_) | copy-start | bytes 196612
  34.6 5.7 %collective-permute-start.13 = (bf16[2,128,128]{2,1,0:T(8,128)(2,1)}, bf16[2,128,128]{2,1,0:T(8,128)(2,1)S(1)}, u32[]{:S(2)}, u32[]{:S(2)}) collective-permute-start(bf16[2,128,128]{2,1,0:T(8,128)(2,1)} %get-tuple-element.82), channel_id=1, source_target_pairs={{0,11},{1,10},{2,9},{3,8},{4,15},{5,14},{6,13},{7,12},{8,3},{9,2},... | collective-permute-start | bytes 196616 | tf_op jit(solution)/shard_map/ppermute | solution.py:413
  35.1 9.5 %copy-start.26 = (bf16[2,128,128]{2,1,0:T(8,128)(2,1)}, bf16[2,128,128]{2,1,0:T(8,128)(2,1)S(1)}, u32[]{:S(2)}) copy-start(bf16[2,128,128]{2,1,0:T(8,128)(2,1)S(1)} %collective-permute-done.12.rest_10_) | copy-start | bytes 196612
  35.1 7.1 %collective-permute-start.9 = (bf16[2,128,128]{2,1,0:T(8,128)(2,1)}, bf16[2,128,128]{2,1,0:T(8,128)(2,1)S(1)}, u32[]{:S(2)}, u32[]{:S(2)}) collective-permute-start(bf16[2,128,128]{2,1,0:T(8,128)(2,1)} %get-tuple-element.82), channel_id=1, source_target_pairs={{0,7},{1,6},{2,5},{3,4},{4,11},{5,10},{6,9},{7,8},{8,15},{9,14},{1... | collective-permute-start | bytes 196616 | tf_op jit(solution)/shard_map/ppermute | solution.py:413
  37.6 7.0 %copy-start.27 = (bf16[2,128,128]{2,1,0:T(8,128)(2,1)}, bf16[2,128,128]{2,1,0:T(8,128)(2,1)S(1)}, u32[]{:S(2)}) copy-start(bf16[2,128,128]{2,1,0:T(8,128)(2,1)S(1)} %collective-permute-done.8.rest_6_) | copy-start | bytes 196612
  37.6 6.2 %collective-permute-start.5 = (bf16[2,128,128]{2,1,0:T(8,128)(2,1)}, bf16[2,128,128]{2,1,0:T(8,128)(2,1)S(1)}, u32[]{:S(2)}, u32[]{:S(2)}) collective-permute-start(bf16[2,128,128]{2,1,0:T(8,128)(2,1)} %get-tuple-element.82), channel_id=1, source_target_pairs={{0,3},{1,2},{2,1},{3,0},{4,7},{5,6},{6,5},{7,4},{8,11},{9,10},{10,... | collective-permute-start | bytes 196616 | tf_op jit(solution)/shard_map/ppermute | solution.py:413
  39.2 5.4 %copy-start.28 = (bf16[2,128,128]{2,1,0:T(8,128)(2,1)}, bf16[2,128,128]{2,1,0:T(8,128)(2,1)S(1)}, u32[]{:S(2)}) copy-start(bf16[2,128,128]{2,1,0:T(8,128)(2,1)S(1)} %collective-permute-done.4.rest_2_) | copy-start | bytes 196612
  39.2 5.4 %copy-start.29 = (bf16[2,128,128]{2,1,0:T(8,128)(2,1)}, bf16[2,128,128]{2,1,0:T(8,128)(2,1)S(1)}, u32[]{:S(2)}) copy-start(bf16[2,128,128]{2,1,0:T(8,128)(2,1)S(1)} %collective-permute-done.17.rest_15_) | copy-start | bytes 196612
  40.3 4.4 %copy-start.30 = (bf16[2,128,128]{2,1,0:T(8,128)(2,1)}, bf16[2,128,128]{2,1,0:T(8,128)(2,1)S(1)}, u32[]{:S(2)}) copy-start(bf16[2,128,128]{2,1,0:T(8,128)(2,1)S(1)} %collective-permute-done.13.rest_11_) | copy-start | bytes 196612
  43.8 80.9 %reduce-scatter.2.cloned.1.call-start = ((), (), s32[]{:S(2)}) async-start(), calls=%async_computation.1 | async-start | bytes 1310720 | tf_op jit(solution)/shard_map/reduce_scatter | solution.py:465
  126.3 4.3 %collective-permute-start.20 = (bf16[2,128,128]{2,1,0:T(8,128)(2,1)S(1)}, bf16[2,128,128]{2,1,0:T(8,128)(2,1)S(1)}, u32[]{:S(2)}, u32[]{:S(2)}) collective-permute-start(bf16[2,128,128]{2,1,0:T(8,128)(2,1)S(1)} %get-tuple-element.144), channel_id=1, source_target_pairs={{0,3},{1,2},{2,1},{3,0},{4,7},{5,6},{6,5},{7,4},{8,11},{9,10},{10,... | collective-permute-start | bytes 196616 | tf_op jit(solution)/shard_map/ppermute | solution.py:400
  127.0 5.0 %collective-permute-start.19 = (bf16[2,128,128]{2,1,0:T(8,128)(2,1)S(1)}, bf16[2,128,128]{2,1,0:T(8,128)(2,1)S(1)}, u32[]{:S(2)}, u32[]{:S(2)}) collective-permute-start(bf16[2,128,128]{2,1,0:T(8,128)(2,1)S(1)} %get-tuple-element.145), channel_id=1, source_target_pairs={{0,2},{1,3},{2,0},{3,1},{4,6},{5,7},{6,4},{7,5},{8,10},{9,11},{10,... | collective-permute-start | bytes 196616 | tf_op jit(solution)/shard_map/ppermute | solution.py:400
  127.7 5.5 %collective-permute-start.18 = (bf16[2,128,128]{2,1,0:T(8,128)(2,1)S(1)}, bf16[2,128,128]{2,1,0:T(8,128)(2,1)S(1)}, u32[]{:S(2)}, u32[]{:S(2)}) collective-permute-start(bf16[2,128,128]{2,1,0:T(8,128)(2,1)S(1)} %get-tuple-element.146), channel_id=1, source_target_pairs={{0,1},{1,0},{2,3},{3,2},{4,5},{5,4},{6,7},{7,6},{8,9},{9,8},{10,11... | collective-permute-start | bytes 196616 | tf_op jit(solution)/shard_map/ppermute | solution.py:400
  128.1 5.1 %collective-permute-start.21 = (bf16[2,128,128]{2,1,0:T(8,128)(2,1)}, bf16[2,128,128]{2,1,0:T(8,128)(2,1)S(1)}, u32[]{:S(2)}, u32[]{:S(2)}) collective-permute-start(bf16[2,128,128]{2,1,0:T(8,128)(2,1)} %get-tuple-element.127), channel_id=1, source_target_pairs={{0,1},{1,0},{2,3},{3,2},{4,5},{5,4},{6,7},{7,6},{8,9},{9,8},{10,11... | collective-permute-start | bytes 196616 | tf_op jit(solution)/shard_map/ppermute | solution.py:413
  128.2 7.1 %collective-permute-start.22 = (bf16[2,128,128]{2,1,0:T(8,128)(2,1)}, bf16[2,128,128]{2,1,0:T(8,128)(2,1)S(1)}, u32[]{:S(2)}, u32[]{:S(2)}) collective-permute-start(bf16[2,128,128]{2,1,0:T(8,128)(2,1)} %get-tuple-element.128), channel_id=1, source_target_pairs={{0,2},{1,3},{2,0},{3,1},{4,6},{5,7},{6,4},{7,5},{8,10},{9,11},{10,... | collective-permute-start | bytes 196616 | tf_op jit(solution)/shard_map/ppermute | solution.py:413
  130.6 27.4 %copy-start = (bf16[2,128,128]{2,1,0:T(8,128)(2,1)}, bf16[2,128,128]{2,1,0:T(8,128)(2,1)S(1)}, u32[]{:S(2)}) copy-start(bf16[2,128,128]{2,1,0:T(8,128)(2,1)S(1)} %collective-permute-done.20.refs_3_) | copy-start | bytes 196612
  130.6 6.6 %collective-permute-start.23 = (bf16[2,128,128]{2,1,0:T(8,128)(2,1)}, bf16[2,128,128]{2,1,0:T(8,128)(2,1)S(1)}, u32[]{:S(2)}, u32[]{:S(2)}) collective-permute-start(bf16[2,128,128]{2,1,0:T(8,128)(2,1)} %get-tuple-element.129), channel_id=1, source_target_pairs={{0,3},{1,2},{2,1},{3,0},{4,7},{5,6},{6,5},{7,4},{8,11},{9,10},{10,... | collective-permute-start | bytes 196616 | tf_op jit(solution)/shard_map/ppermute | solution.py:413
  132.0 26.1 %copy-start.1 = (bf16[2,128,128]{2,1,0:T(8,128)(2,1)}, bf16[2,128,128]{2,1,0:T(8,128)(2,1)S(1)}, u32[]{:S(2)}) copy-start(bf16[2,128,128]{2,1,0:T(8,128)(2,1)S(1)} %collective-permute-done.19.refs_2_) | copy-start | bytes 196612
  132.0 6.8 %collective-permute-start.24 = (bf16[2,128,128]{2,1,0:T(8,128)(2,1)}, bf16[2,128,128]{2,1,0:T(8,128)(2,1)S(1)}, u32[]{:S(2)}, u32[]{:S(2)}) collective-permute-start(bf16[2,128,128]{2,1,0:T(8,128)(2,1)} %get-tuple-element.130), channel_id=1, source_target_pairs={{0,4},{1,5},{2,6},{3,7},{4,8},{5,9},{6,10},{7,11},{8,12},{9,13},{1... | collective-permute-start | bytes 196616 | tf_op jit(solution)/shard_map/ppermute | solution.py:413
  133.2 24.8 %copy-start.2 = (bf16[2,128,128]{2,1,0:T(8,128)(2,1)}, bf16[2,128,128]{2,1,0:T(8,128)(2,1)S(1)}, u32[]{:S(2)}) copy-start(bf16[2,128,128]{2,1,0:T(8,128)(2,1)S(1)} %collective-permute-done.18.refs_1_) | copy-start | bytes 196612
  133.2 6.5 %collective-permute-start.25 = (bf16[2,128,128]{2,1,0:T(8,128)(2,1)}, bf16[2,128,128]{2,1,0:T(8,128)(2,1)S(1)}, u32[]{:S(2)}, u32[]{:S(2)}) collective-permute-start(bf16[2,128,128]{2,1,0:T(8,128)(2,1)} %get-tuple-element.131), channel_id=1, source_target_pairs={{0,5},{1,4},{2,7},{3,6},{4,9},{5,8},{6,11},{7,10},{8,13},{9,12},{1... | collective-permute-start | bytes 196616 | tf_op jit(solution)/shard_map/ppermute | solution.py:413
  133.2 24.8 %copy-start.3 = (bf16[2,128,128]{2,1,0:T(8,128)(2,1)}, bf16[2,128,128]{2,1,0:T(8,128)(2,1)S(1)}, u32[]{:S(2)}) copy-start(bf16[2,128,128]{2,1,0:T(8,128)(2,1)S(1)} %collective-permute-done.21.refs_5_) | copy-start | bytes 196612
  133.2 9.3 %collective-permute-start.26 = (bf16[2,128,128]{2,1,0:T(8,128)(2,1)}, bf16[2,128,128]{2,1,0:T(8,128)(2,1)S(1)}, u32[]{:S(2)}, u32[]{:S(2)}) collective-permute-start(bf16[2,128,128]{2,1,0:T(8,128)(2,1)} %get-tuple-element.132), channel_id=1, source_target_pairs={{0,6},{1,7},{2,4},{3,5},{4,10},{5,11},{6,8},{7,9},{8,14},{9,15},{1... | collective-permute-start | bytes 196616 | tf_op jit(solution)/shard_map/ppermute | solution.py:413
  135.3 22.8 %copy-start.4 = (bf16[2,128,128]{2,1,0:T(8,128)(2,1)}, bf16[2,128,128]{2,1,0:T(8,128)(2,1)S(1)}, u32[]{:S(2)}) copy-start(bf16[2,128,128]{2,1,0:T(8,128)(2,1)S(1)} %collective-permute-done.22.refs_6_) | copy-start | bytes 196612
  135.3 8.2 %collective-permute-start.27 = (bf16[2,128,128]{2,1,0:T(8,128)(2,1)}, bf16[2,128,128]{2,1,0:T(8,128)(2,1)S(1)}, u32[]{:S(2)}, u32[]{:S(2)}) collective-permute-start(bf16[2,128,128]{2,1,0:T(8,128)(2,1)} %get-tuple-element.133), channel_id=1, source_target_pairs={{0,7},{1,6},{2,5},{3,4},{4,11},{5,10},{6,9},{7,8},{8,15},{9,14},{1... | collective-permute-start | bytes 196616 | tf_op jit(solution)/shard_map/ppermute | solution.py:413
  137.3 20.8 %copy-start.5 = (bf16[2,128,128]{2,1,0:T(8,128)(2,1)}, bf16[2,128,128]{2,1,0:T(8,128)(2,1)S(1)}, u32[]{:S(2)}) copy-start(bf16[2,128,128]{2,1,0:T(8,128)(2,1)S(1)} %collective-permute-done.23.refs_7_) | copy-start | bytes 196612
  137.3 12.3 %collective-permute-start.28 = (bf16[2,128,128]{2,1,0:T(8,128)(2,1)}, bf16[2,128,128]{2,1,0:T(8,128)(2,1)S(1)}, u32[]{:S(2)}, u32[]{:S(2)}) collective-permute-start(bf16[2,128,128]{2,1,0:T(8,128)(2,1)} %get-tuple-element.134), channel_id=1, source_target_pairs={{0,8},{1,9},{2,10},{3,11},{4,12},{5,13},{6,14},{7,15},{8,0},{9,1},... | collective-permute-start | bytes 196616 | tf_op jit(solution)/shard_map/ppermute | solution.py:413
  138.8 19.3 %copy-start.6 = (bf16[2,128,128]{2,1,0:T(8,128)(2,1)}, bf16[2,128,128]{2,1,0:T(8,128)(2,1)S(1)}, u32[]{:S(2)}) copy-start(bf16[2,128,128]{2,1,0:T(8,128)(2,1)S(1)} %collective-permute-done.24.refs_8_) | copy-start | bytes 196612
  138.8 12.2 %collective-permute-start.29 = (bf16[2,128,128]{2,1,0:T(8,128)(2,1)}, bf16[2,128,128]{2,1,0:T(8,128)(2,1)S(1)}, u32[]{:S(2)}, u32[]{:S(2)}) collective-permute-start(bf16[2,128,128]{2,1,0:T(8,128)(2,1)} %get-tuple-element.135), channel_id=1, source_target_pairs={{0,9},{1,8},{2,11},{3,10},{4,13},{5,12},{6,15},{7,14},{8,1},{9,0},... | collective-permute-start | bytes 196616 | tf_op jit(solution)/shard_map/ppermute | solution.py:413
  139.7 18.3 %copy-start.7 = (bf16[2,128,128]{2,1,0:T(8,128)(2,1)}, bf16[2,128,128]{2,1,0:T(8,128)(2,1)S(1)}, u32[]{:S(2)}) copy-start(bf16[2,128,128]{2,1,0:T(8,128)(2,1)S(1)} %collective-permute-done.25.refs_9_) | copy-start | bytes 196612
  139.7 13.5 %collective-permute-start.30 = (bf16[2,128,128]{2,1,0:T(8,128)(2,1)}, bf16[2,128,128]{2,1,0:T(8,128)(2,1)S(1)}, u32[]{:S(2)}, u32[]{:S(2)}) collective-permute-start(bf16[2,128,128]{2,1,0:T(8,128)(2,1)} %get-tuple-element.136), channel_id=1, source_target_pairs={{0,10},{1,11},{2,8},{3,9},{4,14},{5,15},{6,12},{7,13},{8,2},{9,3},... | collective-permute-start | bytes 196616 | tf_op jit(solution)/shard_map/ppermute | solution.py:413
  142.5 15.5 %copy-start.8 = (bf16[2,128,128]{2,1,0:T(8,128)(2,1)}, bf16[2,128,128]{2,1,0:T(8,128)(2,1)S(1)}, u32[]{:S(2)}) copy-start(bf16[2,128,128]{2,1,0:T(8,128)(2,1)S(1)} %collective-permute-done.26.refs_10_) | copy-start | bytes 196612
  142.5 12.8 %collective-permute-start.31 = (bf16[2,128,128]{2,1,0:T(8,128)(2,1)}, bf16[2,128,128]{2,1,0:T(8,128)(2,1)S(1)}, u32[]{:S(2)}, u32[]{:S(2)}) collective-permute-start(bf16[2,128,128]{2,1,0:T(8,128)(2,1)} %get-tuple-element.137), channel_id=1, source_target_pairs={{0,11},{1,10},{2,9},{3,8},{4,15},{5,14},{6,13},{7,12},{8,3},{9,2},... | collective-permute-start | bytes 196616 | tf_op jit(solution)/shard_map/ppermute | solution.py:413
  143.5 14.6 %copy-start.9 = (bf16[2,128,128]{2,1,0:T(8,128)(2,1)}, bf16[2,128,128]{2,1,0:T(8,128)(2,1)S(1)}, u32[]{:S(2)}) copy-start(bf16[2,128,128]{2,1,0:T(8,128)(2,1)S(1)} %collective-permute-done.27.refs_11_) | copy-start | bytes 196612
  143.5 11.9 %collective-permute-start.32 = (bf16[2,128,128]{2,1,0:T(8,128)(2,1)}, bf16[2,128,128]{2,1,0:T(8,128)(2,1)S(1)}, u32[]{:S(2)}, u32[]{:S(2)}) collective-permute-start(bf16[2,128,128]{2,1,0:T(8,128)(2,1)} %get-tuple-element.138), channel_id=1, source_target_pairs={{0,12},{1,13},{2,14},{3,15},{4,0},{5,1},{6,2},{7,3},{8,4},{9,5},{1... | collective-permute-start | bytes 196616 | tf_op jit(solution)/shard_map/ppermute | solution.py:413
  149.5 8.5 %copy-start.10 = (bf16[2,128,128]{2,1,0:T(8,128)(2,1)}, bf16[2,128,128]{2,1,0:T(8,128)(2,1)S(1)}, u32[]{:S(2)}) copy-start(bf16[2,128,128]{2,1,0:T(8,128)(2,1)S(1)} %collective-permute-done.28.refs_12_) | copy-start | bytes 196612
  149.5 5.8 %collective-permute-start.33 = (bf16[2,128,128]{2,1,0:T(8,128)(2,1)}, bf16[2,128,128]{2,1,0:T(8,128)(2,1)S(1)}, u32[]{:S(2)}, u32[]{:S(2)}) collective-permute-start(bf16[2,128,128]{2,1,0:T(8,128)(2,1)} %get-tuple-element.139), channel_id=1, source_target_pairs={{0,13},{1,12},{2,15},{3,14},{4,1},{5,0},{6,3},{7,2},{8,5},{9,4},{1... | collective-permute-start | bytes 196616 | tf_op jit(solution)/shard_map/ppermute | solution.py:413
  151.0 7.1 %copy-start.11 = (bf16[2,128,128]{2,1,0:T(8,128)(2,1)}, bf16[2,128,128]{2,1,0:T(8,128)(2,1)S(1)}, u32[]{:S(2)}) copy-start(bf16[2,128,128]{2,1,0:T(8,128)(2,1)S(1)} %collective-permute-done.29.refs_13_) | copy-start | bytes 196612
  151.0 5.8 %collective-permute-start.34 = (bf16[2,128,128]{2,1,0:T(8,128)(2,1)}, bf16[2,128,128]{2,1,0:T(8,128)(2,1)S(1)}, u32[]{:S(2)}, u32[]{:S(2)}) collective-permute-start(bf16[2,128,128]{2,1,0:T(8,128)(2,1)} %get-tuple-element.140), channel_id=1, source_target_pairs={{0,14},{1,15},{2,12},{3,13},{4,2},{5,3},{6,0},{7,1},{8,6},{9,7},{1... | collective-permute-start | bytes 196616 | tf_op jit(solution)/shard_map/ppermute | solution.py:413
  153.2 4.9 %copy-start.12 = (bf16[2,128,128]{2,1,0:T(8,128)(2,1)}, bf16[2,128,128]{2,1,0:T(8,128)(2,1)S(1)}, u32[]{:S(2)}) copy-start(bf16[2,128,128]{2,1,0:T(8,128)(2,1)S(1)} %collective-permute-done.30.refs_14_) | copy-start | bytes 196612
  153.2 4.8 %collective-permute-start.35 = (bf16[2,128,128]{2,1,0:T(8,128)(2,1)}, bf16[2,128,128]{2,1,0:T(8,128)(2,1)S(1)}, u32[]{:S(2)}, u32[]{:S(2)}) collective-permute-start(bf16[2,128,128]{2,1,0:T(8,128)(2,1)} %get-tuple-element.141), channel_id=1, source_target_pairs={{0,15},{1,14},{2,13},{3,12},{4,3},{5,2},{6,1},{7,0},{8,7},{9,6},{1... | collective-permute-start | bytes 196616 | tf_op jit(solution)/shard_map/ppermute | solution.py:413
  (7 other events, 13.6 us)
Sparse Core Ops, SparseCore 0:
  43.9 27.5 all-gather.2
  84.5 26.7 reduce-scatter.1

commit v5 on v4

--- a/solution.py
+++ b/solution.py
@@ -10,6 +10,7 @@
 
 HD = 128
 SUB = 128
+LANES = 256
 LOWEST = -1e30
 BF16 = jnp.bfloat16
 F32 = jnp.float32
@@ -47,10 +48,6 @@
         weights_even,
         weights_odd,
         sgrads,
-        score_even,
-        score_odd,
-        dprob_even,
-        dprob_odd,
         fracs,
         deltas,
         dk_sum,
@@ -71,8 +68,6 @@
     step = pl.program_id(0)
     exps = (exps_even, exps_odd)
     weights = (weights_even, weights_odd)
-    scores = (score_even, score_odd)
-    dprobs = (dprob_even, dprob_odd)
 
     @pl.when(step == 0)
     def _():
@@ -97,48 +92,38 @@
 
     def blocks(piece):
         at, size, row = pieces[piece]
-        for u in range(0, size, SUB):
-            for r in range(0, rows - row, SUB):
-                yield u, r, slice(at + u, at + u + SUB), slice(row + r, row + r + SUB)
+        for r in range(row, rows, LANES):
+            for u in range(at, at + size, SUB):
+                yield slice(u, u + SUB), slice(r, r + LANES)
 
     def stat(block_at):
         return slice(block_at.start // SUB * 8, block_at.start // SUB * 8 + 8)
 
-    def score_product(now, piece):
-        at, size, row = pieces[piece]
-        scores[piece % 2][:size, : rows - row] = dot(
-            keys[at : at + size, :], query_t[now, :, row:]
-        )
+    def tiled(block):
+        return block.reshape(SUB // 8, 8, LANES)
 
     def score_chain(now, piece):
-        for u, r, key_at, row_at in blocks(piece):
-            block = scores[piece % 2][u : u + SUB, r : r + SUB]
+        for key_at, row_at in blocks(piece):
+            block = dot(keys[key_at, :], query_t[now, :, row_at])
             if key_at.start >= prompt_rows:
-                j = lax.broadcasted_iota(jnp.int32, (SUB, SUB), 0) + key_at.start - prompt_rows
-                i = lax.broadcasted_iota(jnp.int32, (SUB, SUB), 1) + row_at.start
+                j = lax.broadcasted_iota(jnp.int32, (SUB, LANES), 0) + key_at.start - prompt_rows
+                i = lax.broadcasted_iota(jnp.int32, (SUB, LANES), 1) + row_at.start
                 block = jnp.where((j <= i) & (j < length), block, -jnp.inf)
-            block = block.reshape(SUB // 8, 8, SUB) * factor2
+            block = tiled(block) * factor2
             top = jnp.maximum(jnp.max(block, axis=0), LOWEST)
             exp = jnp.exp2(block - top[None])
-            exps[now][key_at, row_at] = exp.reshape(SUB, SUB)
+            exps[now][key_at, row_at] = exp.reshape(SUB, LANES)
             tops[stat(key_at), row_at] = top
             sums[stat(key_at), row_at] = jnp.sum(exp, axis=0)
 
     def frac(slot, key_at, row_at):
-        block = exps[slot][key_at, row_at].reshape(SUB // 8, 8, SUB)
-        return block * fracs[slot, stat(key_at), row_at][None]
-
-    def dprob_product(before, piece):
-        at, size, row = pieces[piece]
-        dprobs[piece % 2][:size, : rows - row] = dot(
-            values[at : at + size, :], grad_t[before, :, row:]
-        )
+        return tiled(exps[slot][key_at, row_at]) * fracs[slot, stat(key_at), row_at][None]
 
     def grad_chain(before, piece):
-        for u, r, key_at, row_at in blocks(piece):
-            dprob = dprobs[piece % 2][u : u + SUB, r : r + SUB].reshape(SUB // 8, 8, SUB)
+        for key_at, row_at in blocks(piece):
+            dprob = tiled(dot(values[key_at, :], grad_t[before, :, row_at]))
             sgrad = frac(before, key_at, row_at) * (dprob - deltas[before, :, row_at][None])
-            sgrads[key_at, row_at] = sgrad.reshape(SUB, SUB).astype(BF16)
+            sgrads[key_at, row_at] = sgrad.reshape(SUB, LANES).astype(BF16)
 
     def grad_products(before, piece):
         at, size, row = pieces[piece]
@@ -148,19 +133,14 @@
 
     def run(now, with_score, with_grad):
         before = 1 - now
-        for stage in range(-1, count + 1):
-            if stage + 1 < count:
+        for piece in range(count + 1):
+            if piece < count:
                 if with_score:
-                    score_product(now, stage + 1)
+                    score_chain(now, piece)
                 if with_grad:
-                    dprob_product(before, stage + 1)
-            if 0 <= stage < count:
-                if with_score:
-                    score_chain(now, stage)
-                if with_grad:
-                    grad_chain(before, stage)
-            if stage >= 1 and with_grad:
-                grad_products(before, stage - 1)
+                    grad_chain(before, piece)
+            if piece >= 1 and with_grad:
+                grad_products(before, piece - 1)
         if with_grad:
             dquery = dot(keys_t[...], sgrads[...])
             dq_ref[...] = (factor * dquery).T.astype(BF16)
@@ -181,8 +161,8 @@
         total = jnp.sum(scale * sums[...], axis=0, keepdims=True)
         fracs[now] = scale * (1.0 / total)
         for piece in range(count):
-            for _, _, key_at, row_at in blocks(piece):
-                weight = frac(now, key_at, row_at).reshape(SUB, SUB)
+            for key_at, row_at in blocks(piece):
+                weight = frac(now, key_at, row_at).reshape(SUB, LANES)
                 weights[now][key_at, row_at] = weight.astype(BF16)
         mixture = dot(values_t[...], weights[now][...])
         live_lanes = lax.broadcasted_iota(jnp.int32, (HD, rows), 1) < length
@@ -213,17 +193,16 @@
 
 class Gathered:
     def __init__(self, members, ranks, own_rows):
-        self.members, self.ranks, self.own_rows = members, ranks, own_rows
-        self.part_rows = ranks * own_rows
+        self.members, self.part_rows = members, ranks * own_rows
         self.prompt_rows = members * self.part_rows
         self.caches = 1
-        self.dcaches = members * ranks
+        self.dcaches = members
 
     def cache_shapes(self):
         return [(self.members, 2, self.part_rows, HD)]
 
     def dcache_shapes(self):
-        return [(2, self.own_rows, HD)] * self.dcaches
+        return [(2, self.part_rows, HD)] * self.dcaches
 
     def load(self, caches):
         for m in range(self.members):
@@ -234,12 +213,9 @@
         me = lax.axis_index("resp")
         for shift in range(self.members):
             part = lax.rem(me + shift, self.members) * self.part_rows
-            for i in range(self.ranks):
-                at = pl.multiple_of(part + i * self.own_rows, self.own_rows)
-                at = pl.ds(at, self.own_rows)
-                ref = dcaches[shift * self.ranks + i]
-                ref[0] = (factor * dk_sum[at, :]).astype(BF16)
-                ref[1] = dv_sum[at, :].astype(BF16)
+            at = pl.ds(pl.multiple_of(part, self.part_rows), self.part_rows)
+            dcaches[shift][0] = (factor * dk_sum[at, :]).astype(BF16)
+            dcaches[shift][1] = dv_sum[at, :].astype(BF16)
 
 
 class Scattered(Gathered):
@@ -248,14 +224,14 @@
         self.caches, self.dcaches = self.dcaches, self.caches
 
     def cache_shapes(self):
-        return [(2, self.own_rows, HD)] * self.caches
+        return [(2, self.part_rows, HD)] * self.caches
 
     def dcache_shapes(self):
         return [(self.members, 2, self.part_rows, HD)]
 
     def load(self, caches):
         for i, ref in enumerate(caches):
-            yield pl.ds(i * self.own_rows, self.own_rows), ref[0], ref[1]
+            yield pl.ds(i * self.part_rows, self.part_rows), ref[0], ref[1]
 
     def store(self, dcaches, dk_sum, dv_sum, factor):
         me = lax.axis_index("resp")
@@ -319,10 +295,6 @@
             pltpu.VMEM((total_rows, rows), BF16),
             pltpu.VMEM((total_rows, rows), BF16),
             pltpu.VMEM((total_rows, rows), BF16),
-            pltpu.VMEM((rows, rows), F32),
-            pltpu.VMEM((rows, rows), F32),
-            pltpu.VMEM((rows, rows), F32),
-            pltpu.VMEM((rows, rows), F32),
             pltpu.VMEM((2, stats, rows), F32),
             pltpu.VMEM((2, 8, rows), F32),
             pltpu.VMEM((total_rows, HD), F32),
@@ -368,25 +340,22 @@
     return [blocks[p * count // pairs : (p + 1) * count // pairs] for p in range(pairs)]
 
 
-def place_kernel(members, pairs, *refs):
+def place_kernel(pairs, *refs):
     *ins, dk_ref, dv_ref = refs
     me = lax.axis_index("tensor")
-    ranks = dk_ref.shape[1] // HD // pairs
-    for i in range(ranks):
-        at = 0
-        for p, count in enumerate(members):
+    ranks = len(ins) // pairs
+    for p in range(pairs):
+        for i in range(ranks):
             columns = pl.ds(pl.multiple_of(((me ^ i) * pairs + p) * HD, HD), HD)
-            blocks = [ins[at + m * ranks + i] for m in range(count)]
-            at += count * ranks
-            dk_ref[:, columns] = sum(block[0].astype(F32) for block in blocks)
-            dv_ref[:, columns] = sum(block[1].astype(F32) for block in blocks)
-
-
-def place(blocks, members, pairs, columns):
+            dk_ref[:, columns] = ins[p * ranks + i][0].astype(F32)
+            dv_ref[:, columns] = ins[p * ranks + i][1].astype(F32)
+
+
+def place(blocks, pairs, columns):
     _, rows, _ = blocks[0].shape
     shape = (rows, columns)
     return pl.pallas_call(
-        functools.partial(place_kernel, members, pairs),
+        functools.partial(place_kernel, pairs),
         in_specs=[whole_block(blocks[0].shape)] * len(blocks),
         out_specs=[whole_block(shape)] * 2,
         out_shape=[jax.ShapeDtypeStruct(shape, F32)] * 2,
@@ -402,15 +371,8 @@
     ]
 
 
-def send(block, members, ranks, shift, i):
-    if shift == 0 and i == 0:
-        return block
-    pairs = [
-        (m * ranks + j, (m + shift) % members * ranks + (j ^ i))
-        for m in range(members)
-        for j in range(ranks)
-    ]
-    return lax.ppermute(block, ("resp", "tensor"), pairs)
+def send(block, members, shift):
+    return lax.ppermute(block, "resp", [(m, (m + shift) % members) for m in range(members)])
 
 
 def cut_rows(block, count):
@@ -432,16 +394,16 @@
     cuts = cut(prompt_keys, prompt_values, pairs)
     kinds = [Scattered(members, ranks, own_rows)]
     kinds += [Gathered(members, ranks, own_rows) for _ in range(pairs - 1)]
-    caches = [
-        [send(cuts[0][i], members, ranks, shift, i) for shift in range(members) for i in range(ranks)]
-    ]
+    own = jnp.concatenate(swap(cuts[0]), axis=1)
+    if pairs > 1:
+        own, cuts[1:] = lax.optimization_barrier((own, cuts[1:]))
+    caches = [[own] + [send(own, members, shift) for shift in range(1, members)]]
     for p in range(1, pairs):
         own = jnp.concatenate(swap(cuts[p]), axis=1)
         own, caches[0] = lax.optimization_barrier((own, caches[0]))
         caches.append([lax.all_gather(own, "resp", axis=0)])
     earlier = ()
-    total = None
-    blocks, counts = [], []
+    totals = []
     for p in range(pairs):
         results = attend(
             kinds[p],
@@ -456,24 +418,17 @@
             earlier,
         )
         earlier, dcaches = results[:4], results[4:]
-        if total is not None:
-            dcaches, total = lax.optimization_barrier((dcaches, total))
-            blocks += swap(cut_rows(total, ranks))
-            counts.append(1)
-            total = None
+        if totals:
+            dcaches, totals[-1] = lax.optimization_barrier((dcaches, totals[-1]))
         if isinstance(kinds[p], Scattered):
-            total = lax.psum_scatter(dcaches[0], "resp", scatter_dimension=0)
+            totals.append(lax.psum_scatter(dcaches[0], "resp", scatter_dimension=0))
         else:
-            blocks += [
-                send(dcaches[shift * ranks + i], members, ranks, shift, i)
-                for shift in range(members)
-                for i in range(ranks)
+            arrived = [dcaches[0]] + [
+                send(dcaches[shift], members, shift) for shift in range(1, members)
             ]
-            counts.append(members)
-    if total is not None:
-        blocks += swap(cut_rows(total, ranks))
-        counts.append(1)
-    key_grad, value_grad = place(blocks, counts, pairs, columns)
+            totals.append(sum(block.astype(F32) for block in arrived).astype(BF16))
+    blocks = [block for total in totals for block in swap(cut_rows(total, ranks))]
+    key_grad, value_grad = place(blocks, pairs, columns)
     return (*(a[None] for a in earlier), key_grad, value_grad)
 
 

time: 169 us -> 168 us (level)
  the two profiles are of different devices: /device:TPU:0 before, /device:TPU:9 now
where the time goes in v5:
time: 168 us; the launch traced here: 167 us
  Pallas kernels  85.9 us (51%)
  starting transfers between devices  33.6 us (20%)
  waiting for transfers between devices  26.7 us (16%)
  between operations  14.9 us (9%)
  other arithmetic  3.51 us (2%)
  local copies, waits for them, and re-layouts  2.86 us (2%)
    pallas_call x2, Pallas kernels, attend(): pl.pallas_call(functools.partial(attention_kernel, layout, heads_per, len...  81.9 us
    ppermute x12, starting transfers between devices, swap(): lax.ppermute(blocks[i], 'tensor', [(j, j ^ i) for j in range(count)])  25.3 us
    ppermute x6, waiting for transfers between devices, send(): lax.ppermute(block, 'resp', [(m, (m + shift) % members) for m in range(me...  15.6 us
    ppermute x12, waiting for transfers between devices, swap(): lax.ppermute(blocks[i], 'tensor', [(j, j ^ i) for j in range(count)])  11 us
    ppermute x6, starting transfers between devices, send(): lax.ppermute(block, 'resp', [(m, (m + shift) % members) for m in range(me...  8.25 us
  transfers between devices with their start and end apart: 20, of which 11 were waited for; matrix products, arithmetic and copies ran while one was open for 3% of the time, Pallas kernels for 49%

profile of v5, /device:TPU:9, one launch (start us, length us, event | category | flops | bytes accessed | tf_op | source)
XLA Modules:
  0.0 167.4 jit_solution(5049658154465524395)
XLA Ops:
  7.2 0.0 all-gather.3.cloned.1.call-start
  7.2 1.9 %cut.1 = (bf16[2,128,128]{2,1,0:T(8,128)(2,1)}, bf16[2,128,128]{2,1,0:T(8,128)(2,1)}, bf16[2,128,128]{2,1,0:T(8,128)(2,1)}, bf16[2,128,128]{2,1,0:T(8,128)(2,1)}...) custom-call(bf16[128,1024]{1,0:T(8,128)(2,1)} %k_ref.1, ...), custom_call_target="tpu_custom_call" | custom-call | tf_op jit(solution)/shard_map/cut/pallas_call | solution.py:333
  9.2 0.7 collective-permute-start
  9.8 1.2 collective-permute-start.1
  11.0 0.5 collective-permute-start.2
  11.5 0.0 collective-permute-done
  11.5 2.2 %collective-permute-done.1 = bf16[2,128,128]{2,1,0:T(8,128)(2,1)S(1)} collective-permute-done((bf16[2,128,128]{2,1,0:T(8,128)(2,1)}, bf16[2,128,128]{2,1,0:T(8,128)(2,1)S(1)}, u32[]{:S(2)}, u32[]{:S(2)}) %collective-permute-start.1) | collective-permute-done | bytes 65568 | tf_op jit(solution)/shard_map/ppermute | solution.py:369
  13.7 1.6 collective-permute-done.2
  15.3 0.9 pad_maximum_fusion.rest_0_
  16.2 0.0 copy-start
  16.2 0.2 collective-permute-start.8
  16.4 2.3 %collective-permute-start.7 = (bf16[2,512,128]{2,1,0:T(8,128)(2,1)S(1)}, bf16[2,512,128]{2,1,0:T(8,128)(2,1)S(1)}, u32[]{:S(2)}, u32[]{:S(2)}) collective-permute-start(bf16[2,512,128]{2,1,0:T(8,128)(2,1)S(1)} %pad_maximum_fusion.rest_0_), channel_id=1, source_target_pairs={{0,8},{4,12},{8,0},{12,4},{1,9},{5,13},{9,1},{13,5},{2,10},{6,14},... | collective-permute-start | bytes 786440 | tf_op jit(solution)/shard_map/ppermute | solution.py:375
  18.7 2.2 %collective-permute-start.6 = (bf16[2,512,128]{2,1,0:T(8,128)(2,1)S(1)}, bf16[2,512,128]{2,1,0:T(8,128)(2,1)S(1)}, u32[]{:S(2)}, u32[]{:S(2)}) collective-permute-start(bf16[2,512,128]{2,1,0:T(8,128)(2,1)S(1)} %pad_maximum_fusion.rest_0_), channel_id=1, source_target_pairs={{0,4},{4,8},{8,12},{12,0},{1,5},{5,9},{9,13},{13,1},{2,6},{6,10},{... | collective-permute-start | bytes 786440 | tf_op jit(solution)/shard_map/ppermute | solution.py:375
  20.9 1.2 collective-permute-start.3
  22.1 1.0 collective-permute-start.4
  23.2 0.1 collective-permute-done.3
  23.2 1.3 collective-permute-start.5
  24.5 1.5 collective-permute-done.4
  26.1 1.8 %collective-permute-done.5 = bf16[2,128,128]{2,1,0:T(8,128)(2,1)S(1)} collective-permute-done((bf16[2,128,128]{2,1,0:T(8,128)(2,1)}, bf16[2,128,128]{2,1,0:T(8,128)(2,1)S(1)}, u32[]{:S(2)}, u32[]{:S(2)}) %collective-permute-start.5) | collective-permute-done | bytes 65568 | tf_op jit(solution)/shard_map/ppermute | solution.py:369
  27.9 1.6 pad_maximum_fusion.1
  29.4 0.0 collective-permute-done.8.rest_3_
  29.4 0.0 copy-start.7
  29.4 5.8 %collective-permute-done.7.rest_2_ = bf16[2,512,128]{2,1,0:T(8,128)(2,1)S(1)} collective-permute-done((bf16[2,512,128]{2,1,0:T(8,128)(2,1)S(1)}, bf16[2,512,128]{2,1,0:T(8,128)(2,1)S(1)}, u32[]{:S(2)}, u32[]{:S(2)}) %collective-permute-start.7) | collective-permute-done | bytes 262176 | tf_op jit(solution)/shard_map/ppermute | solution.py:375
  35.3 5.6 %collective-permute-done.6.rest_1_ = bf16[2,512,128]{2,1,0:T(8,128)(2,1)S(1)} collective-permute-done((bf16[2,512,128]{2,1,0:T(8,128)(2,1)S(1)}, bf16[2,512,128]{2,1,0:T(8,128)(2,1)S(1)}, u32[]{:S(2)}, u32[]{:S(2)}) %collective-permute-start.6) | collective-permute-done | bytes 262176 | tf_op jit(solution)/shard_map/ppermute | solution.py:375
  40.9 0.0 all-gather.3.cloned.1.call-update
  40.9 0.0 reduce-scatter.2.cloned.1.call-start
  41.6 0.0 copy-done
  41.6 0.0 copy-done.7
  41.7 0.0 copy-done.8
  41.7 0.0 copy-done.9
  41.7 40.6 %attend_pair_0.1 = (bf16[512,2048]{1,0:T(8,128)(2,1)}, bf16[512,2048]{1,0:T(8,128)(2,1)}, bf16[512,256]{1,0:T(8,128)(2,1)}, bf16[512,256]{1,0:T(8,128)(2,1)}, bf16[4,2,512,128]{3,2,1,0:T(8,128)(2,1)}) custom-call(s32[1]{0:T(128)S(6)} %copy.21.len_ref, bf16[512,2048]{1,0:T(8,128)(2,1)} %bitcast.11, bf16[512,2048]{1,0:T(8,128)(2,1)} %bitcast.13, ...), custom_call_target="tpu_custom_call" | custom-call | flops 16106127360 | bytes 4194304 | tf_op jit(solution)/shard_map/attend_pair_0/pallas_call | solution.py:272
  82.3 0.0 reduce-scatter.2.cloned.1.call-update
  82.4 0.0 all-gather.3.cloned.1.call-done
  82.4 41.2 %attend_pair_1.1 = (bf16[512,2048]{1,0:T(8,128)(2,1)}, bf16[512,2048]{1,0:T(8,128)(2,1)}, bf16[512,256]{1,0:T(8,128)(2,1)}, bf16[512,256]{1,0:T(8,128)(2,1)}, bf...) custom-call(s32[1]{0:T(128)S(6)} %copy.21.len_ref, ...), custom_call_target="tpu_custom_call", output_to_operand_aliasing={{0}: (6, {}), {1}: (7, {}), {2}: (8, {}), {3}: (9, {})} | custom-call | flops 16106127360 | bytes 4194304 | tf_op jit(solution)/shard_map/attend_pair_1/pallas_call | solution.py:272
  123.6 0.0 reduce-scatter.2.cloned.1.call-done
  123.6 2.3 %collective-permute-start.12 = (bf16[2,512,128]{2,1,0:T(8,128)(2,1)}, bf16[2,512,128]{2,1,0:T(8,128)(2,1)S(1)}, u32[]{:S(2)}, u32[]{:S(2)}) collective-permute-start(bf16[2,512,128]{2,1,0:T(8,128)(2,1)} %get-tuple-element.77), channel_id=1, source_target_pairs={{0,4},{4,8},{8,12},{12,0},{1,5},{5,9},{9,13},{13,1},{2,6},{6,10},{... | collective-permute-start | bytes 786440 | tf_op jit(solution)/shard_map/ppermute | solution.py:375
  125.9 0.7 collective-permute-start.13
  126.7 0.5 collective-permute-start.14
  127.2 1.6 fusion.1
  128.7 2.9 %collective-permute-start.11 = (bf16[2,128,128]{2,1,0:T(8,128)(2,1)S(1)}, bf16[2,128,128]{2,1,0:T(8,128)(2,1)S(1)}, u32[]{:S(2)}, u32[]{:S(2)}) collective-permute-start(bf16[2,128,128]{2,1,0:T(8,128)(2,1)S(1)} %get-tuple-element.86), channel_id=1, source_target_pairs={{0,3},{1,2},{2,1},{3,0},{4,7},{5,6},{6,5},{7,4},{8,11},{9,10},{10,... | collective-permute-start | bytes 196616 | tf_op jit(solution)/shard_map/ppermute | solution.py:369
  131.6 0.3 collective-permute-start.10
  131.9 0.0 collective-permute-done.12
  131.9 13.8 %collective-permute-start.9 = (bf16[2,128,128]{2,1,0:T(8,128)(2,1)S(1)}, bf16[2,128,128]{2,1,0:T(8,128)(2,1)S(1)}, u32[]{:S(2)}, u32[]{:S(2)}) collective-permute-start(bf16[2,128,128]{2,1,0:T(8,128)(2,1)S(1)} %get-tuple-element.88), channel_id=1, source_target_pairs={{0,1},{1,0},{2,3},{3,2},{4,5},{5,4},{6,7},{7,6},{8,9},{9,8},{10,11... | collective-permute-start | bytes 196616 | tf_op jit(solution)/shard_map/ppermute | solution.py:369
  145.7 1.7 %collective-permute-done.13 = bf16[2,512,128]{2,1,0:T(8,128)(2,1)S(1)} collective-permute-done((bf16[2,512,128]{2,1,0:T(8,128)(2,1)}, bf16[2,512,128]{2,1,0:T(8,128)(2,1)S(1)}, u32[]{:S(2)}, u32[]{:S(2)}) %collective-permute-start.13) | collective-permute-done | bytes 262176 | tf_op jit(solution)/shard_map/ppermute | solution.py:375
  147.4 2.4 %collective-permute-done.14 = bf16[2,512,128]{2,1,0:T(8,128)(2,1)S(1)} collective-permute-done((bf16[2,512,128]{2,1,0:T(8,128)(2,1)}, bf16[2,512,128]{2,1,0:T(8,128)(2,1)S(1)}, u32[]{:S(2)}, u32[]{:S(2)}) %collective-permute-start.14) | collective-permute-done | bytes 262176 | tf_op jit(solution)/shard_map/ppermute | solution.py:375
  149.8 1.1 add_convert_fusion
  150.9 0.6 fusion
  151.6 2.0 %collective-permute-start.17 = (bf16[2,128,128]{2,1,0:T(8,128)(2,1)S(1)}, bf16[2,128,128]{2,1,0:T(8,128)(2,1)S(1)}, u32[]{:S(2)}, u32[]{:S(2)}) collective-permute-start(bf16[2,128,128]{2,1,0:T(8,128)(2,1)S(1)} %get-tuple-element.82), channel_id=1, source_target_pairs={{0,3},{1,2},{2,1},{3,0},{4,7},{5,6},{6,5},{7,4},{8,11},{9,10},{10,... | collective-permute-start | bytes 196616 | tf_op jit(solution)/shard_map/ppermute | solution.py:369
  153.5 0.3 collective-permute-start.16
  153.8 0.0 collective-permute-done.11.refs_3_
  153.8 0.2 collective-permute-start.15
  154.0 0.0 collective-permute-done.10.refs_2_
  154.0 0.0 collective-permute-done.9.refs_1_
  154.0 0.0 copy-start.3
  154.0 2.4 %collective-permute-done.17.refs_7_ = bf16[2,128,128]{2,1,0:T(8,128)(2,1)S(1)} collective-permute-done((bf16[2,128,128]{2,1,0:T(8,128)(2,1)S(1)}, bf16[2,128,128]{2,1,0:T(8,128)(2,1)S(1)}, u32[]{:S(2)}, u32[]{:S(2)}) %collective-permute-start.17) | collective-permute-done | bytes 65568 | tf_op jit(solution)/shard_map/ppermute | solution.py:369
  156.4 1.4 collective-permute-done.16.refs_6_
  157.8 0.0 collective-permute-done.15.refs_5_
  157.8 0.0 copy-done.1
  157.8 0.0 copy-done.2
  157.8 0.0 copy-done.3
  157.8 0.0 copy-done.4
  157.9 0.6 copy-done.5
  158.4 0.0 copy-done.6
  158.5 2.1 %place.1 = (f32[128,1024]{1,0:T(8,128)}, f32[128,1024]{1,0:T(8,128)}) custom-call(bf16[2,128,128]{2,1,0:T(8,128)(2,1)} %get-tuple-element.89.refs_0_, bf16[2,128,128]{2,1,0:T(8,128)(2,1)} %copy-done.3, bf16[2,128,128]{2,1,0:T(8,128)(2,1)} %copy-done.2, bf16[2,128,128]{2,1,0:T(8,128)(2,1)} %copy-done.1, bf16[2,128,128]{2,1,0:T(8,128)(2,1)} %get-tuple-element.85.refs_4_, ...), custom_call_target="tpu_custom_call" | custom-call | tf_op jit(solution)/shard_map/place/pallas_call | solution.py:357
  (7 shorter events, 0.0 us)
Async XLA Ops:
  7.2 75.2 %all-gather.3.cloned.1.call-start = ((), (), s32[]{:S(2)}) async-start(), calls=%async_computation.2 | async-start | bytes 1310720 | tf_op jit(solution)/shard_map/all_gather | solution.py:404
  9.2 2.4 %collective-permute-start = (bf16[2,128,128]{2,1,0:T(8,128)(2,1)}, bf16[2,128,128]{2,1,0:T(8,128)(2,1)S(1)}, u32[]{:S(2)}, u32[]{:S(2)}) collective-permute-start(bf16[2,128,128]{2,1,0:T(8,128)(2,1)} %get-tuple-element.45), channel_id=1, source_target_pairs={{0,1},{1,0},{2,3},{3,2},{4,5},{5,4},{6,7},{7,6},{8,9},{9,8},{10,11... | collective-permute-start | bytes 196616 | tf_op jit(solution)/shard_map/ppermute | solution.py:369
  9.8 3.9 %collective-permute-start.1 = (bf16[2,128,128]{2,1,0:T(8,128)(2,1)}, bf16[2,128,128]{2,1,0:T(8,128)(2,1)S(1)}, u32[]{:S(2)}, u32[]{:S(2)}) collective-permute-start(bf16[2,128,128]{2,1,0:T(8,128)(2,1)} %get-tuple-element.46), channel_id=1, source_target_pairs={{0,2},{1,3},{2,0},{3,1},{4,6},{5,7},{6,4},{7,5},{8,10},{9,11},{10,... | collective-permute-start | bytes 196616 | tf_op jit(solution)/shard_map/ppermute | solution.py:369
  11.0 4.2 %collective-permute-start.2 = (bf16[2,128,128]{2,1,0:T(8,128)(2,1)}, bf16[2,128,128]{2,1,0:T(8,128)(2,1)S(1)}, u32[]{:S(2)}, u32[]{:S(2)}) collective-permute-start(bf16[2,128,128]{2,1,0:T(8,128)(2,1)} %get-tuple-element.47), channel_id=1, source_target_pairs={{0,3},{1,2},{2,1},{3,0},{4,7},{5,6},{6,5},{7,4},{8,11},{9,10},{10,... | collective-permute-start | bytes 196616 | tf_op jit(solution)/shard_map/ppermute | solution.py:369
  16.2 25.5 %copy-start = (bf16[2,512,128]{2,1,0:T(8,128)(2,1)}, bf16[2,512,128]{2,1,0:T(8,128)(2,1)S(1)}, u32[]{:S(2)}) copy-start(bf16[2,512,128]{2,1,0:T(8,128)(2,1)S(1)} %pad_maximum_fusion.rest_0_) | copy-start | bytes 786436
  16.2 13.3 %collective-permute-start.8 = (bf16[2,512,128]{2,1,0:T(8,128)(2,1)S(1)}, bf16[2,512,128]{2,1,0:T(8,128)(2,1)S(1)}, u32[]{:S(2)}, u32[]{:S(2)}) collective-permute-start(bf16[2,512,128]{2,1,0:T(8,128)(2,1)S(1)} %pad_maximum_fusion.rest_0_), channel_id=1, source_target_pairs={{0,12},{4,0},{8,4},{12,8},{1,13},{5,1},{9,5},{13,9},{2,14},{6,2},{... | collective-permute-start | bytes 786440 | tf_op jit(solution)/shard_map/ppermute | solution.py:375
  16.4 18.9 %collective-permute-start.7 = (bf16[2,512,128]{2,1,0:T(8,128)(2,1)S(1)}, bf16[2,512,128]{2,1,0:T(8,128)(2,1)S(1)}, u32[]{:S(2)}, u32[]{:S(2)}) collective-permute-start(bf16[2,512,128]{2,1,0:T(8,128)(2,1)S(1)} %pad_maximum_fusion.rest_0_), channel_id=1, source_target_pairs={{0,8},{4,12},{8,0},{12,4},{1,9},{5,13},{9,1},{13,5},{2,10},{6,14},... | collective-permute-start | bytes 786440 | tf_op jit(solution)/shard_map/ppermute | solution.py:375
  18.7 22.2 %collective-permute-start.6 = (bf16[2,512,128]{2,1,0:T(8,128)(2,1)S(1)}, bf16[2,512,128]{2,1,0:T(8,128)(2,1)S(1)}, u32[]{:S(2)}, u32[]{:S(2)}) collective-permute-start(bf16[2,512,128]{2,1,0:T(8,128)(2,1)S(1)} %pad_maximum_fusion.rest_0_), channel_id=1, source_target_pairs={{0,4},{4,8},{8,12},{12,0},{1,5},{5,9},{9,13},{13,1},{2,6},{6,10},{... | collective-permute-start | bytes 786440 | tf_op jit(solution)/shard_map/ppermute | solution.py:375
  20.9 2.3 %collective-permute-start.3 = (bf16[2,128,128]{2,1,0:T(8,128)(2,1)}, bf16[2,128,128]{2,1,0:T(8,128)(2,1)S(1)}, u32[]{:S(2)}, u32[]{:S(2)}) collective-permute-start(bf16[2,128,128]{2,1,0:T(8,128)(2,1)} %get-tuple-element.53), channel_id=1, source_target_pairs={{0,1},{1,0},{2,3},{3,2},{4,5},{5,4},{6,7},{7,6},{8,9},{9,8},{10,11... | collective-permute-start | bytes 196616 | tf_op jit(solution)/shard_map/ppermute | solution.py:369
  22.1 3.9 %collective-permute-start.4 = (bf16[2,128,128]{2,1,0:T(8,128)(2,1)}, bf16[2,128,128]{2,1,0:T(8,128)(2,1)S(1)}, u32[]{:S(2)}, u32[]{:S(2)}) collective-permute-start(bf16[2,128,128]{2,1,0:T(8,128)(2,1)} %get-tuple-element.54), channel_id=1, source_target_pairs={{0,2},{1,3},{2,0},{3,1},{4,6},{5,7},{6,4},{7,5},{8,10},{9,11},{10,... | collective-permute-start | bytes 196616 | tf_op jit(solution)/shard_map/ppermute | solution.py:369
  23.2 4.6 %collective-permute-start.5 = (bf16[2,128,128]{2,1,0:T(8,128)(2,1)}, bf16[2,128,128]{2,1,0:T(8,128)(2,1)S(1)}, u32[]{:S(2)}, u32[]{:S(2)}) collective-permute-start(bf16[2,128,128]{2,1,0:T(8,128)(2,1)} %get-tuple-element.55), channel_id=1, source_target_pairs={{0,3},{1,2},{2,1},{3,0},{4,7},{5,6},{6,5},{7,4},{8,11},{9,10},{10,... | collective-permute-start | bytes 196616 | tf_op jit(solution)/shard_map/ppermute | solution.py:369
  29.4 12.2 %copy-start.7 = (bf16[2,512,128]{2,1,0:T(8,128)(2,1)}, bf16[2,512,128]{2,1,0:T(8,128)(2,1)S(1)}, u32[]{:S(2)}) copy-start(bf16[2,512,128]{2,1,0:T(8,128)(2,1)S(1)} %collective-permute-done.8.rest_3_) | copy-start | bytes 786436
  35.3 6.4 %copy-start.8 = (bf16[2,512,128]{2,1,0:T(8,128)(2,1)}, bf16[2,512,128]{2,1,0:T(8,128)(2,1)S(1)}, u32[]{:S(2)}) copy-start(bf16[2,512,128]{2,1,0:T(8,128)(2,1)S(1)} %collective-permute-done.7.rest_2_) | copy-start | bytes 786436
  40.9 0.8 copy-start.9
  40.9 82.7 %reduce-scatter.2.cloned.1.call-start = ((), (), s32[]{:S(2)}) async-start(), calls=%async_computation.1 | async-start | bytes 1310720 | tf_op jit(solution)/shard_map/reduce_scatter | solution.py:424
  123.6 8.2 %collective-permute-start.12 = (bf16[2,512,128]{2,1,0:T(8,128)(2,1)}, bf16[2,512,128]{2,1,0:T(8,128)(2,1)S(1)}, u32[]{:S(2)}, u32[]{:S(2)}) collective-permute-start(bf16[2,512,128]{2,1,0:T(8,128)(2,1)} %get-tuple-element.77), channel_id=1, source_target_pairs={{0,4},{4,8},{8,12},{12,0},{1,5},{5,9},{9,13},{13,1},{2,6},{6,10},{... | collective-permute-start | bytes 786440 | tf_op jit(solution)/shard_map/ppermute | solution.py:375
  125.9 21.5 %collective-permute-start.13 = (bf16[2,512,128]{2,1,0:T(8,128)(2,1)}, bf16[2,512,128]{2,1,0:T(8,128)(2,1)S(1)}, u32[]{:S(2)}, u32[]{:S(2)}) collective-permute-start(bf16[2,512,128]{2,1,0:T(8,128)(2,1)} %get-tuple-element.78), channel_id=1, source_target_pairs={{0,8},{4,12},{8,0},{12,4},{1,9},{5,13},{9,1},{13,5},{2,10},{6,14},... | collective-permute-start | bytes 786440 | tf_op jit(solution)/shard_map/ppermute | solution.py:375
  126.7 23.2 %collective-permute-start.14 = (bf16[2,512,128]{2,1,0:T(8,128)(2,1)}, bf16[2,512,128]{2,1,0:T(8,128)(2,1)S(1)}, u32[]{:S(2)}, u32[]{:S(2)}) collective-permute-start(bf16[2,512,128]{2,1,0:T(8,128)(2,1)} %get-tuple-element.79), channel_id=1, source_target_pairs={{0,12},{4,0},{8,4},{12,8},{1,13},{5,1},{9,5},{13,9},{2,14},{6,2},{... | collective-permute-start | bytes 786440 | tf_op jit(solution)/shard_map/ppermute | solution.py:375
  128.7 25.1 %collective-permute-start.11 = (bf16[2,128,128]{2,1,0:T(8,128)(2,1)S(1)}, bf16[2,128,128]{2,1,0:T(8,128)(2,1)S(1)}, u32[]{:S(2)}, u32[]{:S(2)}) collective-permute-start(bf16[2,128,128]{2,1,0:T(8,128)(2,1)S(1)} %get-tuple-element.86), channel_id=1, source_target_pairs={{0,3},{1,2},{2,1},{3,0},{4,7},{5,6},{6,5},{7,4},{8,11},{9,10},{10,... | collective-permute-start | bytes 196616 | tf_op jit(solution)/shard_map/ppermute | solution.py:369
  131.6 22.4 %collective-permute-start.10 = (bf16[2,128,128]{2,1,0:T(8,128)(2,1)S(1)}, bf16[2,128,128]{2,1,0:T(8,128)(2,1)S(1)}, u32[]{:S(2)}, u32[]{:S(2)}) collective-permute-start(bf16[2,128,128]{2,1,0:T(8,128)(2,1)S(1)} %get-tuple-element.87), channel_id=1, source_target_pairs={{0,2},{1,3},{2,0},{3,1},{4,6},{5,7},{6,4},{7,5},{8,10},{9,11},{10,... | collective-permute-start | bytes 196616 | tf_op jit(solution)/shard_map/ppermute | solution.py:369
  131.9 22.1 %collective-permute-start.9 = (bf16[2,128,128]{2,1,0:T(8,128)(2,1)S(1)}, bf16[2,128,128]{2,1,0:T(8,128)(2,1)S(1)}, u32[]{:S(2)}, u32[]{:S(2)}) collective-permute-start(bf16[2,128,128]{2,1,0:T(8,128)(2,1)S(1)} %get-tuple-element.88), channel_id=1, source_target_pairs={{0,1},{1,0},{2,3},{3,2},{4,5},{5,4},{6,7},{7,6},{8,9},{9,8},{10,11... | collective-permute-start | bytes 196616 | tf_op jit(solution)/shard_map/ppermute | solution.py:369
  151.6 4.8 %collective-permute-start.17 = (bf16[2,128,128]{2,1,0:T(8,128)(2,1)S(1)}, bf16[2,128,128]{2,1,0:T(8,128)(2,1)S(1)}, u32[]{:S(2)}, u32[]{:S(2)}) collective-permute-start(bf16[2,128,128]{2,1,0:T(8,128)(2,1)S(1)} %get-tuple-element.82), channel_id=1, source_target_pairs={{0,3},{1,2},{2,1},{3,0},{4,7},{5,6},{6,5},{7,4},{8,11},{9,10},{10,... | collective-permute-start | bytes 196616 | tf_op jit(solution)/shard_map/ppermute | solution.py:369
  153.5 4.3 %collective-permute-start.16 = (bf16[2,128,128]{2,1,0:T(8,128)(2,1)S(1)}, bf16[2,128,128]{2,1,0:T(8,128)(2,1)S(1)}, u32[]{:S(2)}, u32[]{:S(2)}) collective-permute-start(bf16[2,128,128]{2,1,0:T(8,128)(2,1)S(1)} %get-tuple-element.83), channel_id=1, source_target_pairs={{0,2},{1,3},{2,0},{3,1},{4,6},{5,7},{6,4},{7,5},{8,10},{9,11},{10,... | collective-permute-start | bytes 196616 | tf_op jit(solution)/shard_map/ppermute | solution.py:369
  153.8 4.0 %copy-start.1 = (bf16[2,128,128]{2,1,0:T(8,128)(2,1)}, bf16[2,128,128]{2,1,0:T(8,128)(2,1)S(1)}, u32[]{:S(2)}) copy-start(bf16[2,128,128]{2,1,0:T(8,128)(2,1)S(1)} %collective-permute-done.11.refs_3_) | copy-start | bytes 196612
  153.8 4.0 %collective-permute-start.15 = (bf16[2,128,128]{2,1,0:T(8,128)(2,1)S(1)}, bf16[2,128,128]{2,1,0:T(8,128)(2,1)S(1)}, u32[]{:S(2)}, u32[]{:S(2)}) collective-permute-start(bf16[2,128,128]{2,1,0:T(8,128)(2,1)S(1)} %get-tuple-element.84), channel_id=1, source_target_pairs={{0,1},{1,0},{2,3},{3,2},{4,5},{5,4},{6,7},{7,6},{8,9},{9,8},{10,11... | collective-permute-start | bytes 196616 | tf_op jit(solution)/shard_map/ppermute | solution.py:369
  154.0 3.9 %copy-start.2 = (bf16[2,128,128]{2,1,0:T(8,128)(2,1)}, bf16[2,128,128]{2,1,0:T(8,128)(2,1)S(1)}, u32[]{:S(2)}) copy-start(bf16[2,128,128]{2,1,0:T(8,128)(2,1)S(1)} %collective-permute-done.10.refs_2_) | copy-start | bytes 196612
  154.0 3.9 %copy-start.3 = (bf16[2,128,128]{2,1,0:T(8,128)(2,1)}, bf16[2,128,128]{2,1,0:T(8,128)(2,1)S(1)}, u32[]{:S(2)}) copy-start(bf16[2,128,128]{2,1,0:T(8,128)(2,1)S(1)} %collective-permute-done.9.refs_1_) | copy-start | bytes 196612
  156.4 1.4 copy-start.4
  157.8 0.6 copy-start.5
  157.8 0.6 copy-start.6
Sparse Core Ops, SparseCore 0:
  41.0 29.2 all-gather.2
  82.5 26.7 reduce-scatter.1

commit v6 on v5

--- a/solution.py
+++ b/solution.py
@@ -10,7 +10,7 @@
 
 HD = 128
 SUB = 128
-LANES = 256
+PIECE = 1024
 LOWEST = -1e30
 BF16 = jnp.bfloat16
 F32 = jnp.float32
@@ -32,12 +32,11 @@
     *rest,
 ):
     caches, rest = rest[: layout.caches], rest[layout.caches + earlier :]
-    out_ref, dq_ref, dkr_ref, dvr_ref, *rest = rest
+    out_ref, dkr_ref, dvr_ref, sgrads, keys_t, *rest = rest
     dcaches, rest = rest[: layout.dcaches], rest[layout.dcaches :]
     (
         keys,
         values,
-        keys_t,
         values_t,
         query,
         query_t,
@@ -47,7 +46,10 @@
         exps_odd,
         weights_even,
         weights_odd,
-        sgrads,
+        score_even,
+        score_odd,
+        dprob_even,
+        dprob_odd,
         fracs,
         deltas,
         dk_sum,
@@ -59,7 +61,7 @@
     prompt_rows = layout.prompt_rows
     total_rows = prompt_rows + rows
     half = rows // 2
-    pieces = [(at, rows, 0) for at in range(0, prompt_rows, rows)]
+    pieces = [(at, PIECE, 0) for at in range(0, prompt_rows, PIECE)]
     pieces += [(prompt_rows, half, 0), (prompt_rows + half, half, half)]
     count = len(pieces)
     factor = HD ** (-0.5)
@@ -68,6 +70,8 @@
     step = pl.program_id(0)
     exps = (exps_even, exps_odd)
     weights = (weights_even, weights_odd)
+    scores = (score_even, score_odd)
+    dprobs = (dprob_even, dprob_odd)
 
     @pl.when(step == 0)
     def _():
@@ -87,63 +91,77 @@
         dv_sum[...] = jnp.zeros_like(dv_sum)
         tops[...] = jnp.full_like(tops, LOWEST)
         sums[...] = jnp.zeros_like(sums)
-        for ref in (*weights, sgrads):
+        for ref in weights:
             ref[prompt_rows + half :, :half] = jnp.zeros((half, half), BF16)
 
     def blocks(piece):
         at, size, row = pieces[piece]
-        for r in range(row, rows, LANES):
-            for u in range(at, at + size, SUB):
-                yield slice(u, u + SUB), slice(r, r + LANES)
+        for u in range(0, size, SUB):
+            for r in range(0, rows - row, SUB):
+                yield u, r, slice(at + u, at + u + SUB), slice(row + r, row + r + SUB)
 
     def stat(block_at):
         return slice(block_at.start // SUB * 8, block_at.start // SUB * 8 + 8)
 
-    def tiled(block):
-        return block.reshape(SUB // 8, 8, LANES)
+    def score_product(now, piece):
+        at, size, row = pieces[piece]
+        scores[piece % 2][:size, : rows - row] = dot(
+            keys[at : at + size, :], query_t[now, :, row:]
+        )
 
     def score_chain(now, piece):
-        for key_at, row_at in blocks(piece):
-            block = dot(keys[key_at, :], query_t[now, :, row_at])
+        for u, r, key_at, row_at in blocks(piece):
+            block = scores[piece % 2][u : u + SUB, r : r + SUB]
             if key_at.start >= prompt_rows:
-                j = lax.broadcasted_iota(jnp.int32, (SUB, LANES), 0) + key_at.start - prompt_rows
-                i = lax.broadcasted_iota(jnp.int32, (SUB, LANES), 1) + row_at.start
+                j = lax.broadcasted_iota(jnp.int32, (SUB, SUB), 0) + key_at.start - prompt_rows
+                i = lax.broadcasted_iota(jnp.int32, (SUB, SUB), 1) + row_at.start
                 block = jnp.where((j <= i) & (j < length), block, -jnp.inf)
-            block = tiled(block) * factor2
+            block = block.reshape(SUB // 8, 8, SUB) * factor2
             top = jnp.maximum(jnp.max(block, axis=0), LOWEST)
             exp = jnp.exp2(block - top[None])
-            exps[now][key_at, row_at] = exp.reshape(SUB, LANES)
+            exps[now][key_at, row_at] = exp.reshape(SUB, SUB)
             tops[stat(key_at), row_at] = top
             sums[stat(key_at), row_at] = jnp.sum(exp, axis=0)
 
     def frac(slot, key_at, row_at):
-        return tiled(exps[slot][key_at, row_at]) * fracs[slot, stat(key_at), row_at][None]
+        block = exps[slot][key_at, row_at].reshape(SUB // 8, 8, SUB)
+        return block * fracs[slot, stat(key_at), row_at][None]
+
+    def dprob_product(before, piece):
+        at, size, row = pieces[piece]
+        dprobs[piece % 2][:size, : rows - row] = dot(
+            values[at : at + size, :], grad_t[before, :, row:]
+        )
 
     def grad_chain(before, piece):
-        for key_at, row_at in blocks(piece):
-            dprob = tiled(dot(values[key_at, :], grad_t[before, :, row_at]))
+        for u, r, key_at, row_at in blocks(piece):
+            dprob = dprobs[piece % 2][u : u + SUB, r : r + SUB].reshape(SUB // 8, 8, SUB)
             sgrad = frac(before, key_at, row_at) * (dprob - deltas[before, :, row_at][None])
-            sgrads[key_at, row_at] = sgrad.reshape(SUB, LANES).astype(BF16)
+            sgrads[0, key_at, row_at] = sgrad.reshape(SUB, SUB).astype(BF16)
 
     def grad_products(before, piece):
         at, size, row = pieces[piece]
         key_at = slice(at, at + size)
         dv_sum[key_at, :] += dot(weights[before][key_at, row:], grad[before, row:, :])
-        dk_sum[key_at, :] += dot(sgrads[key_at, row:], query[before, row:, :])
+        dk_sum[key_at, :] += dot(sgrads[0, key_at, row:], query[before, row:, :])
 
     def run(now, with_score, with_grad):
         before = 1 - now
-        for piece in range(count + 1):
-            if piece < count:
+        for stage in range(-1, count + 1):
+            if stage + 1 < count:
                 if with_score:
-                    score_chain(now, piece)
+                    score_product(now, stage + 1)
                 if with_grad:
-                    grad_chain(before, piece)
-            if piece >= 1 and with_grad:
-                grad_products(before, piece - 1)
+                    dprob_product(before, stage + 1)
+            if 0 <= stage < count:
+                if with_score:
+                    score_chain(now, stage)
+                if with_grad:
+                    grad_chain(before, stage)
+            if stage >= 1 and with_grad:
+                grad_products(before, stage - 1)
         if with_grad:
-            dquery = dot(keys_t[...], sgrads[...])
-            dq_ref[...] = (factor * dquery).T.astype(BF16)
+            sgrads[0, prompt_rows + half :, :half] = jnp.zeros((half, half), BF16)
         if with_score:
             finish(now)
 
@@ -161,8 +179,8 @@
         total = jnp.sum(scale * sums[...], axis=0, keepdims=True)
         fracs[now] = scale * (1.0 / total)
         for piece in range(count):
-            for key_at, row_at in blocks(piece):
-                weight = frac(now, key_at, row_at).reshape(SUB, LANES)
+            for _, _, key_at, row_at in blocks(piece):
+                weight = frac(now, key_at, row_at).reshape(SUB, SUB)
                 weights[now][key_at, row_at] = weight.astype(BF16)
         mixture = dot(values_t[...], weights[now][...])
         live_lanes = lax.broadcasted_iota(jnp.int32, (HD, rows), 1) < length
@@ -249,7 +267,8 @@
     total_rows = layout.prompt_rows + rows
     first, last = pair * heads_per, (pair + 1) * heads_per - 1
     head_block = pl.BlockSpec((rows, HD), lambda s: (0, jnp.minimum(first + s, last)))
-    late_block = pl.BlockSpec((rows, HD), lambda s: (0, jnp.maximum(first + s - 1, first)))
+    late_block = pl.BlockSpec((1, total_rows, rows), lambda s: (jnp.maximum(s - 1, 0), 0, 0))
+    keys_block = pl.BlockSpec((HD, total_rows), lambda s: (0, 0))
     pair_block = pl.BlockSpec((rows, HD), lambda s: (0, pair))
     cache_blocks = [
         pl.BlockSpec(shape, lambda s, rank=len(shape): (0,) * rank)
@@ -273,18 +292,18 @@
         functools.partial(attention_kernel, layout, heads_per, len(earlier)),
         grid=(heads_per + 1,),
         in_specs=in_specs,
-        out_specs=[head_block, late_block, pair_block, pair_block, *dcache_blocks],
+        out_specs=[head_block, pair_block, pair_block, late_block, keys_block, *dcache_blocks],
         out_shape=[
-            jax.ShapeDtypeStruct(queries.shape, BF16),
             jax.ShapeDtypeStruct(queries.shape, BF16),
             jax.ShapeDtypeStruct(resp_keys.shape, BF16),
             jax.ShapeDtypeStruct(resp_keys.shape, BF16),
+            jax.ShapeDtypeStruct((heads_per, total_rows, rows), BF16),
+            jax.ShapeDtypeStruct((HD, total_rows), BF16),
             *[jax.ShapeDtypeStruct(shape, BF16) for shape in layout.dcache_shapes()],
         ],
         scratch_shapes=[
             pltpu.VMEM((total_rows, HD), BF16),
             pltpu.VMEM((total_rows, HD), BF16),
-            pltpu.VMEM((HD, total_rows), BF16),
             pltpu.VMEM((HD, total_rows), BF16),
             pltpu.VMEM((2, rows, HD), BF16),
             pltpu.VMEM((2, HD, rows), BF16),
@@ -294,7 +313,10 @@
             pltpu.VMEM((total_rows, rows), F32),
             pltpu.VMEM((total_rows, rows), BF16),
             pltpu.VMEM((total_rows, rows), BF16),
-            pltpu.VMEM((total_rows, rows), BF16),
+            pltpu.VMEM((PIECE, rows), F32),
+            pltpu.VMEM((PIECE, rows), F32),
+            pltpu.VMEM((PIECE, rows), F32),
+            pltpu.VMEM((PIECE, rows), F32),
             pltpu.VMEM((2, stats, rows), F32),
             pltpu.VMEM((2, 8, rows), F32),
             pltpu.VMEM((total_rows, HD), F32),
@@ -311,6 +333,45 @@
         compiler_params=pltpu.CompilerParams(vmem_limit_bytes=60 * 1024 * 1024),
         name=f"attend_pair_{pair}",
     )(lengths, queries, out_grad, resp_keys, resp_values, *caches, *earlier)
+
+
+def query_grad_kernel(heads_per, *refs):
+    *ins, dq_ref = refs
+    pairs = len(ins) // 2
+    step = pl.program_id(0)
+    for p in range(pairs):
+        @pl.when((step >= p * heads_per) & (step < (p + 1) * heads_per))
+        def _():
+            dquery = dot(ins[2 * p + 1][...], ins[2 * p][0])
+            dq_ref[...] = (HD ** (-0.5) * dquery).T.astype(BF16)
+
+
+def query_grads(sgrads, keys):
+    heads_per, total_rows, rows = sgrads[0].shape
+    pairs = len(sgrads)
+    in_specs = []
+    for p in range(pairs):
+        in_specs.append(
+            pl.BlockSpec(
+                (1, total_rows, rows),
+                lambda s, p=p: (jnp.clip(s - p * heads_per, 0, heads_per - 1), 0, 0),
+            )
+        )
+        in_specs.append(pl.BlockSpec((HD, total_rows), lambda s: (0, 0)))
+    return pl.pallas_call(
+        functools.partial(query_grad_kernel, heads_per),
+        grid=(pairs * heads_per,),
+        in_specs=in_specs,
+        out_specs=pl.BlockSpec((rows, HD), lambda s: (0, s)),
+        out_shape=jax.ShapeDtypeStruct((rows, pairs * heads_per * HD), BF16),
+        cost_estimate=pl.CostEstimate(
+            flops=2 * pairs * heads_per * rows * total_rows * HD,
+            bytes_accessed=2 * pairs * heads_per * rows * total_rows,
+            transcendentals=0,
+        ),
+        compiler_params=pltpu.CompilerParams(vmem_limit_bytes=60 * 1024 * 1024),
+        name="query_grads",
+    )(*[a for both in zip(sgrads, keys) for a in both])
 
 
 def whole_block(shape):
@@ -403,7 +464,7 @@
         own, caches[0] = lax.optimization_barrier((own, caches[0]))
         caches.append([lax.all_gather(own, "resp", axis=0)])
     earlier = ()
-    totals = []
+    totals, sgrads, keys = [], [], []
     for p in range(pairs):
         results = attend(
             kinds[p],
@@ -417,19 +478,27 @@
             resp_values,
             earlier,
         )
-        earlier, dcaches = results[:4], results[4:]
+        earlier, (sgrad, key), dcaches = results[:3], results[3:5], results[5:]
+        sgrads.append(sgrad)
+        keys.append(key)
         if totals:
             dcaches, totals[-1] = lax.optimization_barrier((dcaches, totals[-1]))
         if isinstance(kinds[p], Scattered):
             totals.append(lax.psum_scatter(dcaches[0], "resp", scatter_dimension=0))
         else:
-            arrived = [dcaches[0]] + [
-                send(dcaches[shift], members, shift) for shift in range(1, members)
-            ]
-            totals.append(sum(block.astype(F32) for block in arrived).astype(BF16))
+            totals.append(
+                [dcaches[0]]
+                + [send(dcaches[shift], members, shift) for shift in range(1, members)]
+            )
+    sgrads = lax.optimization_barrier(sgrads)
+    dquery = query_grads(sgrads, keys)
+    if isinstance(totals[-1], list):
+        dquery, arrived = lax.optimization_barrier((dquery, totals[-1]))
+        totals[-1] = sum(block.astype(F32) for block in arrived).astype(BF16)
     blocks = [block for total in totals for block in swap(cut_rows(total, ranks))]
     key_grad, value_grad = place(blocks, pairs, columns)
-    return (*(a[None] for a in earlier), key_grad, value_grad)
+    attended, resp_key_grad, resp_value_grad = (a[None] for a in earlier)
+    return attended, dquery[None], resp_key_grad, resp_value_grad, key_grad, value_grad
 
 
 def solution(mesh):

time: 168 us -> 167 us (level)
  the two profiles are of different devices: /device:TPU:9 before, /device:TPU:0 now
where the time goes in v6:
time: 167 us
  Pallas kernels  102 us (61%)
  waiting for transfers between devices  26 us (16%)
  starting transfers between devices  19.7 us (12%)
  between operations  14.8 us (9%)
  other arithmetic  2.56 us (2%)
  local copies, waits for them, and re-layouts  1.94 us (1%)
    pallas_call x2, Pallas kernels, attend(): pl.pallas_call(functools.partial(attention_kernel, layout, heads_per, len...  74.8 us
    pallas_call x1, Pallas kernels, query_grads(): pl.pallas_call(functools.partial(query_grad_kernel, heads_per), grid=(pai...  22.7 us
    ppermute x6, waiting for transfers between devices, send(): lax.ppermute(block, 'resp', [(m, (m + shift) % members) for m in range(me...  14.2 us
    ppermute x12, waiting for transfers between devices, swap(): lax.ppermute(blocks[i], 'tensor', [(j, j ^ i) for j in range(count)])  11.8 us
    ppermute x6, starting transfers between devices, send(): lax.ppermute(block, 'resp', [(m, (m + shift) % members) for m in range(me...  10.5 us
    ppermute x12, starting transfers between devices, swap(): lax.ppermute(blocks[i], 'tensor', [(j, j ^ i) for j in range(count)])  9.17 us
  transfers between devices with their start and end apart: 20, of which 9 were waited for; matrix products, arithmetic and copies ran while one was open for 2% of the time, Pallas kernels for 58%

profile of v6, /device:TPU:0, one launch (start us, length us, event | category | flops | bytes accessed | tf_op | source)
XLA Modules:
  0.0 166.7 jit_solution(2720328737119656523)
XLA Ops:
  7.2 0.0 all-gather.3.cloned.1.call-start
  7.2 1.9 %cut.1 = (bf16[2,128,128]{2,1,0:T(8,128)(2,1)}, bf16[2,128,128]{2,1,0:T(8,128)(2,1)}, bf16[2,128,128]{2,1,0:T(8,128)(2,1)}, bf16[2,128,128]{2,1,0:T(8,128)(2,1)}...) custom-call(bf16[128,1024]{1,0:T(8,128)(2,1)} %k_ref.1, ...), custom_call_target="tpu_custom_call" | custom-call | tf_op jit(solution)/shard_map/cut/pallas_call | solution.py:394
  9.1 0.5 collective-permute-start
  9.6 2.5 %collective-permute-start.1 = (bf16[2,128,128]{2,1,0:T(8,128)(2,1)}, bf16[2,128,128]{2,1,0:T(8,128)(2,1)S(1)}, u32[]{:S(2)}, u32[]{:S(2)}) collective-permute-start(bf16[2,128,128]{2,1,0:T(8,128)(2,1)} %get-tuple-element.55), channel_id=1, source_target_pairs={{0,2},{1,3},{2,0},{3,1},{4,6},{5,7},{6,4},{7,5},{8,10},{9,11},{10,... | collective-permute-start | bytes 196616 | tf_op jit(solution)/shard_map/ppermute | solution.py:430
  12.1 0.1 collective-permute-start.2
  12.2 0.0 collective-permute-done
  12.2 2.8 %collective-permute-done.1 = bf16[2,128,128]{2,1,0:T(8,128)(2,1)S(1)} collective-permute-done((bf16[2,128,128]{2,1,0:T(8,128)(2,1)}, bf16[2,128,128]{2,1,0:T(8,128)(2,1)S(1)}, u32[]{:S(2)}, u32[]{:S(2)}) %collective-permute-start.1) | collective-permute-done | bytes 65568 | tf_op jit(solution)/shard_map/ppermute | solution.py:430
  15.1 1.4 collective-permute-done.2
  16.5 0.9 pad_maximum_fusion.rest_0_
  17.3 0.0 copy-start.1
  17.3 3.7 %collective-permute-start.8 = (bf16[2,512,128]{2,1,0:T(8,128)(2,1)S(1)}, bf16[2,512,128]{2,1,0:T(8,128)(2,1)S(1)}, u32[]{:S(2)}, u32[]{:S(2)}) collective-permute-start(bf16[2,512,128]{2,1,0:T(8,128)(2,1)S(1)} %pad_maximum_fusion.rest_0_), channel_id=1, source_target_pairs={{0,12},{4,0},{8,4},{12,8},{1,13},{5,1},{9,5},{13,9},{2,14},{6,2},{... | collective-permute-start | bytes 786440 | tf_op jit(solution)/shard_map/ppermute | solution.py:436
  21.0 0.0 collective-permute-start.7
  21.0 1.0 collective-permute-start.6
  22.0 0.0 collective-permute-start.3
  22.0 1.3 collective-permute-start.4
  23.3 0.2 collective-permute-done.3
  23.5 1.1 collective-permute-start.5
  24.5 2.3 %collective-permute-done.4 = bf16[2,128,128]{2,1,0:T(8,128)(2,1)S(1)} collective-permute-done((bf16[2,128,128]{2,1,0:T(8,128)(2,1)}, bf16[2,128,128]{2,1,0:T(8,128)(2,1)S(1)}, u32[]{:S(2)}, u32[]{:S(2)}) %collective-permute-start.4) | collective-permute-done | bytes 65568 | tf_op jit(solution)/shard_map/ppermute | solution.py:430
  26.8 1.1 collective-permute-done.5
  27.8 1.6 pad_maximum_fusion.1
  29.4 0.0 collective-permute-done.8.rest_3_
  29.4 14.2 %collective-permute-done.7.rest_2_ = bf16[2,512,128]{2,1,0:T(8,128)(2,1)S(1)} collective-permute-done((bf16[2,512,128]{2,1,0:T(8,128)(2,1)S(1)}, bf16[2,512,128]{2,1,0:T(8,128)(2,1)S(1)}, u32[]{:S(2)}, u32[]{:S(2)}) %collective-permute-start.7) | collective-permute-done | bytes 262176 | tf_op jit(solution)/shard_map/ppermute | solution.py:436
  43.6 0.0 collective-permute-done.6.rest_1_
  43.6 0.0 all-gather.3.cloned.1.call-update
  43.6 0.0 reduce-scatter.2.cloned.1.call-start
  44.4 0.0 copy-done.1
  44.4 0.0 copy-done.9
  44.4 0.0 copy-done.10
  44.4 0.0 copy-done.11
  44.4 37.1 %attend_pair_0.1 = (bf16[512,2048]{1,0:T(8,128)(2,1)}, bf16[512,256]{1,0:T(8,128)(2,1)}, bf16[512,256]{1,0:T(8,128)(2,1)}, bf16[8,2560,512]{2,1,0:T(8,128)(2,1)}...) custom-call(s32[1]{0:T(128)S(6)} %copy.19.len_ref, bf16[512,2048]{1,0:T(8,128)(2,1)} %bitcast.12, ...), custom_call_target="tpu_custom_call" | custom-call | flops 16106127360 | bytes 4194304 | tf_op jit(solution)/shard_map/attend_pair_0/pallas_call | solution.py:291
  81.5 0.0 reduce-scatter.2.cloned.1.call-update
  81.6 0.0 all-gather.3.cloned.1.call-done
  81.6 37.7 %attend_pair_1.1 = (bf16[512,2048]{1,0:T(8,128)(2,1)}, bf16[512,256]{1,0:T(8,128)(2,1)}, bf16[512,256]{1,0:T(8,128)(2,1)}, bf16[8,2560,512]{2,1,0:T(8,128)(2,1)}...) custom-call(s32[1]{0:T(128)S(6)} %copy.19.len_ref, ...), custom_call_target="tpu_custom_call", output_to_operand_aliasing={{0}: (6, {}), {1}: (7, {}), {2}: (8, {})} | custom-call | flops 16106127360 | bytes 4194304 | tf_op jit(solution)/shard_map/attend_pair_1/pallas_call | solution.py:291
  119.3 0.0 reduce-scatter.2.cloned.1.call-done
  119.3 1.0 collective-permute-start.9
  120.3 2.0 %collective-permute-start.10 = (bf16[2,512,128]{2,1,0:T(8,128)(2,1)}, bf16[2,512,128]{2,1,0:T(8,128)(2,1)S(1)}, u32[]{:S(2)}, u32[]{:S(2)}) collective-permute-start(bf16[2,512,128]{2,1,0:T(8,128)(2,1)} %get-tuple-element.88), channel_id=1, source_target_pairs={{0,8},{4,12},{8,0},{12,4},{1,9},{5,13},{9,1},{13,5},{2,10},{6,14},... | collective-permute-start | bytes 786440 | tf_op jit(solution)/shard_map/ppermute | solution.py:436
  122.3 2.8 %collective-permute-start.11 = (bf16[2,512,128]{2,1,0:T(8,128)(2,1)}, bf16[2,512,128]{2,1,0:T(8,128)(2,1)S(1)}, u32[]{:S(2)}, u32[]{:S(2)}) collective-permute-start(bf16[2,512,128]{2,1,0:T(8,128)(2,1)} %get-tuple-element.89), channel_id=1, source_target_pairs={{0,12},{4,0},{8,4},{12,8},{1,13},{5,1},{9,5},{13,9},{2,14},{6,2},{... | collective-permute-start | bytes 786440 | tf_op jit(solution)/shard_map/ppermute | solution.py:436
  125.1 22.7 %query_grads.1 = bf16[512,2048]{1,0:T(8,128)(2,1)} custom-call(bf16[8,2560,512]{2,1,0:T(8,128)(2,1)} %get-tuple-element.77.refs_0_, bf16[128,2560]{1,0:T(8,128)(2,1)} %get-tuple-element.78.refs_1_, bf16[8,2560,512]{2,1,0:T(8,128)(2,1)} %get-tuple-element.79.refs_2_, bf16[128,2560]{1,0:T(8,128)(2,1)} %get-tuple-element.80.refs_3_), custom_call_target="tpu_custom_call" | custom-call | flops 5368709120 | bytes 41943040 | tf_op jit(solution)/shard_map/query_grads/pallas_call | solution.py:361
  147.8 0.0 copy-done.2
  147.8 0.6 fusion.1
  148.4 0.0 collective-permute-start.14
  148.4 1.5 collective-permute-start.13
  149.9 0.0 collective-permute-done.9
  149.9 0.4 collective-permute-start.12
  150.3 0.0 collective-permute-done.10
  150.3 0.0 collective-permute-done.11
  150.3 0.0 copy-done
  150.3 0.1 add_convert_fusion
  150.5 0.6 fusion
  151.1 1.1 collective-permute-start.17
  152.2 0.7 collective-permute-start.16
  152.9 0.0 collective-permute-done.14.refs_3_
  152.9 0.1 collective-permute-start.15
  153.0 1.3 collective-permute-done.13.refs_2_
  154.2 0.0 collective-permute-done.12.refs_1_
  154.2 1.2 collective-permute-done.17.refs_7_
  155.4 1.6 collective-permute-done.16.refs_6_
  157.0 0.0 collective-permute-done.15.refs_5_
  157.1 0.0 copy-done.3
  157.1 0.0 copy-done.4
  157.1 0.0 copy-done.5
  157.1 0.6 copy-done.7
  157.7 0.0 copy-done.8
  157.7 2.1 %place.1 = (f32[128,1024]{1,0:T(8,128)}, f32[128,1024]{1,0:T(8,128)}) custom-call(bf16[2,128,128]{2,1,0:T(8,128)(2,1)} %get-tuple-element.107.refs_0_, bf16[2,128,128]{2,1,0:T(8,128)(2,1)} %copy-done.5, bf16[2,128,128]{2,1,0:T(8,128)(2,1)} %copy-done.4, bf16[2,128,128]{2,1,0:T(8,128)(2,1)} %copy-done.3, bf16[2,128,128]{2,1,0:T(8,128)(2,1)} %get-tuple-element.103.refs_4_, ...), custom_call_target="tpu_custom_call" | custom-call | tf_op jit(solution)/shard_map/place/pallas_call | solution.py:418
  (12 shorter events, 0.0 us)
Async XLA Ops:
  7.2 74.4 %all-gather.3.cloned.1.call-start = ((), (), s32[]{:S(2)}) async-start(), calls=%async_computation.2 | async-start | bytes 1310720 | tf_op jit(solution)/shard_map/all_gather | solution.py:465
  9.1 3.1 %collective-permute-start = (bf16[2,128,128]{2,1,0:T(8,128)(2,1)}, bf16[2,128,128]{2,1,0:T(8,128)(2,1)S(1)}, u32[]{:S(2)}, u32[]{:S(2)}) collective-permute-start(bf16[2,128,128]{2,1,0:T(8,128)(2,1)} %get-tuple-element.54), channel_id=1, source_target_pairs={{0,1},{1,0},{2,3},{3,2},{4,5},{5,4},{6,7},{7,6},{8,9},{9,8},{10,11... | collective-permute-start | bytes 196616 | tf_op jit(solution)/shard_map/ppermute | solution.py:430
  9.6 5.5 %collective-permute-start.1 = (bf16[2,128,128]{2,1,0:T(8,128)(2,1)}, bf16[2,128,128]{2,1,0:T(8,128)(2,1)S(1)}, u32[]{:S(2)}, u32[]{:S(2)}) collective-permute-start(bf16[2,128,128]{2,1,0:T(8,128)(2,1)} %get-tuple-element.55), channel_id=1, source_target_pairs={{0,2},{1,3},{2,0},{3,1},{4,6},{5,7},{6,4},{7,5},{8,10},{9,11},{10,... | collective-permute-start | bytes 196616 | tf_op jit(solution)/shard_map/ppermute | solution.py:430
  12.1 4.3 %collective-permute-start.2 = (bf16[2,128,128]{2,1,0:T(8,128)(2,1)}, bf16[2,128,128]{2,1,0:T(8,128)(2,1)S(1)}, u32[]{:S(2)}, u32[]{:S(2)}) collective-permute-start(bf16[2,128,128]{2,1,0:T(8,128)(2,1)} %get-tuple-element.56), channel_id=1, source_target_pairs={{0,3},{1,2},{2,1},{3,0},{4,7},{5,6},{6,5},{7,4},{8,11},{9,10},{10,... | collective-permute-start | bytes 196616 | tf_op jit(solution)/shard_map/ppermute | solution.py:430
  17.3 27.0 %copy-start.1 = (bf16[2,512,128]{2,1,0:T(8,128)(2,1)}, bf16[2,512,128]{2,1,0:T(8,128)(2,1)S(1)}, u32[]{:S(2)}) copy-start(bf16[2,512,128]{2,1,0:T(8,128)(2,1)S(1)} %pad_maximum_fusion.rest_0_) | copy-start | bytes 786436
  17.3 12.1 %collective-permute-start.8 = (bf16[2,512,128]{2,1,0:T(8,128)(2,1)S(1)}, bf16[2,512,128]{2,1,0:T(8,128)(2,1)S(1)}, u32[]{:S(2)}, u32[]{:S(2)}) collective-permute-start(bf16[2,512,128]{2,1,0:T(8,128)(2,1)S(1)} %pad_maximum_fusion.rest_0_), channel_id=1, source_target_pairs={{0,12},{4,0},{8,4},{12,8},{1,13},{5,1},{9,5},{13,9},{2,14},{6,2},{... | collective-permute-start | bytes 786440 | tf_op jit(solution)/shard_map/ppermute | solution.py:436
  21.0 22.6 %collective-permute-start.7 = (bf16[2,512,128]{2,1,0:T(8,128)(2,1)S(1)}, bf16[2,512,128]{2,1,0:T(8,128)(2,1)S(1)}, u32[]{:S(2)}, u32[]{:S(2)}) collective-permute-start(bf16[2,512,128]{2,1,0:T(8,128)(2,1)S(1)} %pad_maximum_fusion.rest_0_), channel_id=1, source_target_pairs={{0,8},{4,12},{8,0},{12,4},{1,9},{5,13},{9,1},{13,5},{2,10},{6,14},... | collective-permute-start | bytes 786440 | tf_op jit(solution)/shard_map/ppermute | solution.py:436
  21.0 22.6 %collective-permute-start.6 = (bf16[2,512,128]{2,1,0:T(8,128)(2,1)S(1)}, bf16[2,512,128]{2,1,0:T(8,128)(2,1)S(1)}, u32[]{:S(2)}, u32[]{:S(2)}) collective-permute-start(bf16[2,512,128]{2,1,0:T(8,128)(2,1)S(1)} %pad_maximum_fusion.rest_0_), channel_id=1, source_target_pairs={{0,4},{4,8},{8,12},{12,0},{1,5},{5,9},{9,13},{13,1},{2,6},{6,10},{... | collective-permute-start | bytes 786440 | tf_op jit(solution)/shard_map/ppermute | solution.py:436
  22.0 1.5 collective-permute-start.3
  22.0 4.8 %collective-permute-start.4 = (bf16[2,128,128]{2,1,0:T(8,128)(2,1)}, bf16[2,128,128]{2,1,0:T(8,128)(2,1)S(1)}, u32[]{:S(2)}, u32[]{:S(2)}) collective-permute-start(bf16[2,128,128]{2,1,0:T(8,128)(2,1)} %get-tuple-element.63), channel_id=1, source_target_pairs={{0,2},{1,3},{2,0},{3,1},{4,6},{5,7},{6,4},{7,5},{8,10},{9,11},{10,... | collective-permute-start | bytes 196616 | tf_op jit(solution)/shard_map/ppermute | solution.py:430
  23.5 4.4 %collective-permute-start.5 = (bf16[2,128,128]{2,1,0:T(8,128)(2,1)}, bf16[2,128,128]{2,1,0:T(8,128)(2,1)S(1)}, u32[]{:S(2)}, u32[]{:S(2)}) collective-permute-start(bf16[2,128,128]{2,1,0:T(8,128)(2,1)} %get-tuple-element.64), channel_id=1, source_target_pairs={{0,3},{1,2},{2,1},{3,0},{4,7},{5,6},{6,5},{7,4},{8,11},{9,10},{10,... | collective-permute-start | bytes 196616 | tf_op jit(solution)/shard_map/ppermute | solution.py:430
  29.4 15.0 %copy-start.9 = (bf16[2,512,128]{2,1,0:T(8,128)(2,1)}, bf16[2,512,128]{2,1,0:T(8,128)(2,1)S(1)}, u32[]{:S(2)}) copy-start(bf16[2,512,128]{2,1,0:T(8,128)(2,1)S(1)} %collective-permute-done.8.rest_3_) | copy-start | bytes 786436
  43.6 0.8 copy-start.10
  43.6 0.8 copy-start.11
  43.6 75.7 %reduce-scatter.2.cloned.1.call-start = ((), (), s32[]{:S(2)}) async-start(), calls=%async_computation.1 | async-start | bytes 1310720 | tf_op jit(solution)/shard_map/reduce_scatter | solution.py:487
  119.3 30.6 %collective-permute-start.9 = (bf16[2,512,128]{2,1,0:T(8,128)(2,1)}, bf16[2,512,128]{2,1,0:T(8,128)(2,1)S(1)}, u32[]{:S(2)}, u32[]{:S(2)}) collective-permute-start(bf16[2,512,128]{2,1,0:T(8,128)(2,1)} %get-tuple-element.87), channel_id=1, source_target_pairs={{0,4},{4,8},{8,12},{12,0},{1,5},{5,9},{9,13},{13,1},{2,6},{6,10},{... | collective-permute-start | bytes 786440 | tf_op jit(solution)/shard_map/ppermute | solution.py:436
  120.3 30.0 %collective-permute-start.10 = (bf16[2,512,128]{2,1,0:T(8,128)(2,1)}, bf16[2,512,128]{2,1,0:T(8,128)(2,1)S(1)}, u32[]{:S(2)}, u32[]{:S(2)}) collective-permute-start(bf16[2,512,128]{2,1,0:T(8,128)(2,1)} %get-tuple-element.88), channel_id=1, source_target_pairs={{0,8},{4,12},{8,0},{12,4},{1,9},{5,13},{9,1},{13,5},{2,10},{6,14},... | collective-permute-start | bytes 786440 | tf_op jit(solution)/shard_map/ppermute | solution.py:436
  122.3 28.0 %collective-permute-start.11 = (bf16[2,512,128]{2,1,0:T(8,128)(2,1)}, bf16[2,512,128]{2,1,0:T(8,128)(2,1)S(1)}, u32[]{:S(2)}, u32[]{:S(2)}) collective-permute-start(bf16[2,512,128]{2,1,0:T(8,128)(2,1)} %get-tuple-element.89), channel_id=1, source_target_pairs={{0,12},{4,0},{8,4},{12,8},{1,13},{5,1},{9,5},{13,9},{2,14},{6,2},{... | collective-permute-start | bytes 786440 | tf_op jit(solution)/shard_map/ppermute | solution.py:436
  125.1 22.7 %copy-start.2 = (bf16[1,2,512,128]{3,2,1,0:T(8,128)(2,1)S(1)}, bf16[1,2,512,128]{3,2,1,0:T(8,128)(2,1)}, u32[]{:S(2)}) copy-start(bf16[1,2,512,128]{3,2,1,0:T(8,128)(2,1)} %reduce-scatter.2.cloned.1.call-done) | copy-start | bytes 786436
  125.1 25.2 %copy-start = (bf16[2,512,128]{2,1,0:T(8,128)(2,1)S(1)}, bf16[2,512,128]{2,1,0:T(8,128)(2,1)}, u32[]{:S(2)}) copy-start(bf16[2,512,128]{2,1,0:T(8,128)(2,1)} %get-tuple-element.94) | copy-start | bytes 786436
  148.4 4.4 %collective-permute-start.14 = (bf16[2,128,128]{2,1,0:T(8,128)(2,1)S(1)}, bf16[2,128,128]{2,1,0:T(8,128)(2,1)S(1)}, u32[]{:S(2)}, u32[]{:S(2)}) collective-permute-start(bf16[2,128,128]{2,1,0:T(8,128)(2,1)S(1)} %get-tuple-element.104), channel_id=1, source_target_pairs={{0,3},{1,2},{2,1},{3,0},{4,7},{5,6},{6,5},{7,4},{8,11},{9,10},{10,... | collective-permute-start | bytes 196616 | tf_op jit(solution)/shard_map/ppermute | solution.py:430
  148.4 5.8 %collective-permute-start.13 = (bf16[2,128,128]{2,1,0:T(8,128)(2,1)S(1)}, bf16[2,128,128]{2,1,0:T(8,128)(2,1)S(1)}, u32[]{:S(2)}, u32[]{:S(2)}) collective-permute-start(bf16[2,128,128]{2,1,0:T(8,128)(2,1)S(1)} %get-tuple-element.105), channel_id=1, source_target_pairs={{0,2},{1,3},{2,0},{3,1},{4,6},{5,7},{6,4},{7,5},{8,10},{9,11},{10,... | collective-permute-start | bytes 196616 | tf_op jit(solution)/shard_map/ppermute | solution.py:430
  149.9 4.3 %collective-permute-start.12 = (bf16[2,128,128]{2,1,0:T(8,128)(2,1)S(1)}, bf16[2,128,128]{2,1,0:T(8,128)(2,1)S(1)}, u32[]{:S(2)}, u32[]{:S(2)}) collective-permute-start(bf16[2,128,128]{2,1,0:T(8,128)(2,1)S(1)} %get-tuple-element.106), channel_id=1, source_target_pairs={{0,1},{1,0},{2,3},{3,2},{4,5},{5,4},{6,7},{7,6},{8,9},{9,8},{10,11... | collective-permute-start | bytes 196616 | tf_op jit(solution)/shard_map/ppermute | solution.py:430
  151.1 4.3 %collective-permute-start.17 = (bf16[2,128,128]{2,1,0:T(8,128)(2,1)S(1)}, bf16[2,128,128]{2,1,0:T(8,128)(2,1)S(1)}, u32[]{:S(2)}, u32[]{:S(2)}) collective-permute-start(bf16[2,128,128]{2,1,0:T(8,128)(2,1)S(1)} %get-tuple-element.100), channel_id=1, source_target_pairs={{0,3},{1,2},{2,1},{3,0},{4,7},{5,6},{6,5},{7,4},{8,11},{9,10},{10,... | collective-permute-start | bytes 196616 | tf_op jit(solution)/shard_map/ppermute | solution.py:430
  152.2 4.9 %collective-permute-start.16 = (bf16[2,128,128]{2,1,0:T(8,128)(2,1)S(1)}, bf16[2,128,128]{2,1,0:T(8,128)(2,1)S(1)}, u32[]{:S(2)}, u32[]{:S(2)}) collective-permute-start(bf16[2,128,128]{2,1,0:T(8,128)(2,1)S(1)} %get-tuple-element.101), channel_id=1, source_target_pairs={{0,2},{1,3},{2,0},{3,1},{4,6},{5,7},{6,4},{7,5},{8,10},{9,11},{10,... | collective-permute-start | bytes 196616 | tf_op jit(solution)/shard_map/ppermute | solution.py:430
  152.9 4.2 %copy-start.3 = (bf16[2,128,128]{2,1,0:T(8,128)(2,1)}, bf16[2,128,128]{2,1,0:T(8,128)(2,1)S(1)}, u32[]{:S(2)}) copy-start(bf16[2,128,128]{2,1,0:T(8,128)(2,1)S(1)} %collective-permute-done.14.refs_3_) | copy-start | bytes 196612
  152.9 4.2 %collective-permute-start.15 = (bf16[2,128,128]{2,1,0:T(8,128)(2,1)S(1)}, bf16[2,128,128]{2,1,0:T(8,128)(2,1)S(1)}, u32[]{:S(2)}, u32[]{:S(2)}) collective-permute-start(bf16[2,128,128]{2,1,0:T(8,128)(2,1)S(1)} %get-tuple-element.102), channel_id=1, source_target_pairs={{0,1},{1,0},{2,3},{3,2},{4,5},{5,4},{6,7},{7,6},{8,9},{9,8},{10,11... | collective-permute-start | bytes 196616 | tf_op jit(solution)/shard_map/ppermute | solution.py:430
  154.2 2.8 %copy-start.4 = (bf16[2,128,128]{2,1,0:T(8,128)(2,1)}, bf16[2,128,128]{2,1,0:T(8,128)(2,1)S(1)}, u32[]{:S(2)}) copy-start(bf16[2,128,128]{2,1,0:T(8,128)(2,1)S(1)} %collective-permute-done.13.refs_2_) | copy-start | bytes 196612
  154.2 2.8 %copy-start.5 = (bf16[2,128,128]{2,1,0:T(8,128)(2,1)}, bf16[2,128,128]{2,1,0:T(8,128)(2,1)S(1)}, u32[]{:S(2)}) copy-start(bf16[2,128,128]{2,1,0:T(8,128)(2,1)S(1)} %collective-permute-done.12.refs_1_) | copy-start | bytes 196612
  155.4 1.7 %copy-start.6 = (bf16[2,128,128]{2,1,0:T(8,128)(2,1)}, bf16[2,128,128]{2,1,0:T(8,128)(2,1)S(1)}, u32[]{:S(2)}) copy-start(bf16[2,128,128]{2,1,0:T(8,128)(2,1)S(1)} %collective-permute-done.17.refs_7_) | copy-start | bytes 196612
  157.0 0.6 copy-start.7
  157.0 0.6 copy-start.8
Sparse Core Ops, SparseCore 0:
  43.7 28.3 all-gather.2
  81.7 27.5 reduce-scatter.1

commit v7 on v5

--- a/solution.py
+++ b/solution.py
@@ -10,7 +10,7 @@
 
 HD = 128
 SUB = 128
-LANES = 256
+WIDE = 256
 LOWEST = -1e30
 BF16 = jnp.bfloat16
 F32 = jnp.float32
@@ -48,12 +48,17 @@
         weights_even,
         weights_odd,
         sgrads,
+        score_even,
+        score_odd,
+        dprob_even,
+        dprob_odd,
         fracs,
         deltas,
         dk_sum,
         dv_sum,
         tops,
         sums,
+        mixture,
     ) = rest
     rows = q_ref.shape[0]
     prompt_rows = layout.prompt_rows
@@ -68,6 +73,8 @@
     step = pl.program_id(0)
     exps = (exps_even, exps_odd)
     weights = (weights_even, weights_odd)
+    scores = (score_even, score_odd)
+    dprobs = (dprob_even, dprob_odd)
 
     @pl.when(step == 0)
     def _():
@@ -92,59 +99,142 @@
 
     def blocks(piece):
         at, size, row = pieces[piece]
-        for r in range(row, rows, LANES):
-            for u in range(at, at + size, SUB):
-                yield slice(u, u + SUB), slice(r, r + LANES)
+        for u in range(0, size, SUB):
+            for r in range(0, rows - row, SUB):
+                yield u, r, slice(at + u, at + u + SUB), slice(row + r, row + r + SUB)
 
     def stat(block_at):
         return slice(block_at.start // SUB * 8, block_at.start // SUB * 8 + 8)
 
     def tiled(block):
-        return block.reshape(SUB // 8, 8, LANES)
-
-    def score_chain(now, piece):
-        for key_at, row_at in blocks(piece):
-            block = dot(keys[key_at, :], query_t[now, :, row_at])
+        return block.reshape(SUB // 8, 8, SUB)
+
+    def score_products(now, piece):
+        at, size, row = pieces[piece]
+
+        def product(r):
+            scores[piece % 2][:size, r - row : r - row + WIDE] = dot(
+                keys[at : at + size, :], query_t[now, :, r : r + WIDE]
+            )
+
+        return [functools.partial(product, r) for r in range(row, rows, WIDE)]
+
+    def dprob_products(before, piece):
+        at, size, row = pieces[piece]
+
+        def product(r):
+            dprobs[piece % 2][:size, r - row : r - row + WIDE] = dot(
+                values[at : at + size, :], grad_t[before, :, r : r + WIDE]
+            )
+
+        return [functools.partial(product, r) for r in range(row, rows, WIDE)]
+
+    def score_chains(now, piece):
+        def chain(u, r, key_at, row_at):
+            block = scores[piece % 2][u : u + SUB, r : r + SUB]
             if key_at.start >= prompt_rows:
-                j = lax.broadcasted_iota(jnp.int32, (SUB, LANES), 0) + key_at.start - prompt_rows
-                i = lax.broadcasted_iota(jnp.int32, (SUB, LANES), 1) + row_at.start
+                j = lax.broadcasted_iota(jnp.int32, (SUB, SUB), 0) + key_at.start - prompt_rows
+                i = lax.broadcasted_iota(jnp.int32, (SUB, SUB), 1) + row_at.start
                 block = jnp.where((j <= i) & (j < length), block, -jnp.inf)
             block = tiled(block) * factor2
             top = jnp.maximum(jnp.max(block, axis=0), LOWEST)
             exp = jnp.exp2(block - top[None])
-            exps[now][key_at, row_at] = exp.reshape(SUB, LANES)
+            exps[now][key_at, row_at] = exp.reshape(SUB, SUB)
             tops[stat(key_at), row_at] = top
             sums[stat(key_at), row_at] = jnp.sum(exp, axis=0)
 
+        return [functools.partial(chain, *block) for block in blocks(piece)]
+
     def frac(slot, key_at, row_at):
         return tiled(exps[slot][key_at, row_at]) * fracs[slot, stat(key_at), row_at][None]
 
-    def grad_chain(before, piece):
-        for key_at, row_at in blocks(piece):
-            dprob = tiled(dot(values[key_at, :], grad_t[before, :, row_at]))
+    def grad_chains(before, piece):
+        def chain(u, r, key_at, row_at):
+            dprob = tiled(dprobs[piece % 2][u : u + SUB, r : r + SUB])
             sgrad = frac(before, key_at, row_at) * (dprob - deltas[before, :, row_at][None])
-            sgrads[key_at, row_at] = sgrad.reshape(SUB, LANES).astype(BF16)
+            sgrads[key_at, row_at] = sgrad.reshape(SUB, SUB).astype(BF16)
+
+        return [functools.partial(chain, *block) for block in blocks(piece)]
+
+    def weight_chains(now, piece):
+        def chain(u, r, key_at, row_at):
+            weight = frac(now, key_at, row_at).reshape(SUB, SUB)
+            weights[now][key_at, row_at] = weight.astype(BF16)
+
+        return [functools.partial(chain, *block) for block in blocks(piece)]
 
     def grad_products(before, piece):
         at, size, row = pieces[piece]
-        key_at = slice(at, at + size)
-        dv_sum[key_at, :] += dot(weights[before][key_at, row:], grad[before, row:, :])
-        dk_sum[key_at, :] += dot(sgrads[key_at, row:], query[before, row:, :])
+
+        def value_product(u):
+            at = slice(u, u + WIDE)
+            dv_sum[at, :] += dot(weights[before][at, row:], grad[before, row:, :])
+
+        def key_product(u):
+            at = slice(u, u + WIDE)
+            dk_sum[at, :] += dot(sgrads[at, row:], query[before, row:, :])
+
+        return [
+            functools.partial(product, u)
+            for u in range(at, at + size, WIDE)
+            for product in (value_product, key_product)
+        ]
+
+    def query_products():
+        def product(r):
+            dquery = dot(keys_t[...], sgrads[:, r : r + WIDE])
+            dq_ref[r : r + WIDE, :] = (factor * dquery).T.astype(BF16)
+
+        return [functools.partial(product, r) for r in range(0, rows, WIDE)]
+
+    def out_products(now, piece):
+        at, size, row = pieces[piece]
+
+        def product(r):
+            term = dot(values_t[:, at : at + size], weights[now][at : at + size, r : r + WIDE])
+            if piece:
+                term += mixture[:, r : r + WIDE]
+            mixture[:, r : r + WIDE] = term
+
+        return [functools.partial(product, r) for r in range(row, rows, WIDE)]
+
+    def weave(products, chains):
+        count = max(len(products), len(chains))
+        for i in range(count):
+            for jobs in (products, chains):
+                for job in jobs[i * len(jobs) // count : (i + 1) * len(jobs) // count]:
+                    job()
 
     def run(now, with_score, with_grad):
         before = 1 - now
-        for piece in range(count + 1):
-            if piece < count:
+        for stage in range(-1, count):
+            products, chains = [], []
+            if stage + 1 < count:
                 if with_score:
-                    score_chain(now, piece)
+                    products += score_products(now, stage + 1)
                 if with_grad:
-                    grad_chain(before, piece)
-            if piece >= 1 and with_grad:
-                grad_products(before, piece - 1)
+                    products += dprob_products(before, stage + 1)
+            if stage >= 1 and with_grad:
+                products += grad_products(before, stage - 1)
+            if stage >= 0:
+                both = [score_chains(now, stage)] if with_score else []
+                both += [grad_chains(before, stage)] if with_grad else []
+                chains = [chain for pair in zip(*both) for chain in pair]
+            weave(products, chains)
+        products = []
         if with_grad:
-            dquery = dot(keys_t[...], sgrads[...])
-            dq_ref[...] = (factor * dquery).T.astype(BF16)
+            products += grad_products(before, count - 1) + query_products()
+        chains = []
         if with_score:
+            set_fracs(now)
+            chains = weight_chains(now, 0)
+        weave(products, chains)
+        if with_score:
+            for piece in range(count):
+                weave(
+                    out_products(now, piece),
+                    weight_chains(now, piece + 1) if piece + 1 < count else [],
+                )
             finish(now)
 
     def prepare(now):
@@ -155,18 +245,15 @@
         query[now] = q_ref[...]
         query_t[now] = q_ref[...].T
 
-    def finish(now):
+    def set_fracs(now):
         top = jnp.max(tops[...], axis=0, keepdims=True)
         scale = jnp.exp2(tops[...] - top)
         total = jnp.sum(scale * sums[...], axis=0, keepdims=True)
         fracs[now] = scale * (1.0 / total)
-        for piece in range(count):
-            for key_at, row_at in blocks(piece):
-                weight = frac(now, key_at, row_at).reshape(SUB, LANES)
-                weights[now][key_at, row_at] = weight.astype(BF16)
-        mixture = dot(values_t[...], weights[now][...])
+
+    def finish(now):
         live_lanes = lax.broadcasted_iota(jnp.int32, (HD, rows), 1) < length
-        attended = jnp.where(live_lanes, mixture, 0.0).astype(BF16).astype(F32)
+        attended = jnp.where(live_lanes, mixture[...], 0.0).astype(BF16).astype(F32)
         out_ref[...] = attended.T.astype(BF16)
         delta = jnp.sum(grad_t[now].astype(F32) * attended, axis=0, keepdims=True)
         deltas[now] = jnp.broadcast_to(delta, (8, rows))
@@ -295,12 +382,17 @@
             pltpu.VMEM((total_rows, rows), BF16),
             pltpu.VMEM((total_rows, rows), BF16),
             pltpu.VMEM((total_rows, rows), BF16),
+            pltpu.VMEM((rows, rows), F32),
+            pltpu.VMEM((rows, rows), F32),
+            pltpu.VMEM((rows, rows), F32),
+            pltpu.VMEM((rows, rows), F32),
             pltpu.VMEM((2, stats, rows), F32),
             pltpu.VMEM((2, 8, rows), F32),
             pltpu.VMEM((total_rows, HD), F32),
             pltpu.VMEM((total_rows, HD), F32),
             pltpu.VMEM((stats, rows), F32),
             pltpu.VMEM((stats, rows), F32),
+            pltpu.VMEM((HD, rows), F32),
         ],
         input_output_aliases=aliases,
         cost_estimate=pl.CostEstimate(

time: 168 us -> 164 us (0.976)
  Pallas kernels: 85.9 us -> 82 us
    pallas_call x2, Pallas kernels: 81.9 us -> 77.9 us  [attend(): pl.pallas_call(functools.partial(attention_kernel, layout, heads_per, len...]
  transfers between devices with their start and end apart: 20 -> 20, of which waited for: 11 -> 11; matrix products, arithmetic and copies ran while one was open for 3% -> 3% of each run, Pallas kernels for 49% -> 48%
where the time goes in v7:
time: 164 us; the launch traced here: 163 us
  Pallas kernels  82 us (50%)
  starting transfers between devices  33.6 us (20%)
  waiting for transfers between devices  26.6 us (16%)
  between operations  14.9 us (9%)
  other arithmetic  3.51 us (2%)
  local copies, waits for them, and re-layouts  2.86 us (2%)
    pallas_call x2, Pallas kernels, attend(): pl.pallas_call(functools.partial(attention_kernel, layout, heads_per, len...  77.9 us
    ppermute x12, starting transfers between devices, swap(): lax.ppermute(blocks[i], 'tensor', [(j, j ^ i) for j in range(count)])  25.3 us
    ppermute x6, waiting for transfers between devices, send(): lax.ppermute(block, 'resp', [(m, (m + shift) % members) for m in range(me...  15.6 us
    ppermute x12, waiting for transfers between devices, swap(): lax.ppermute(blocks[i], 'tensor', [(j, j ^ i) for j in range(count)])  11 us
    ppermute x6, starting transfers between devices, send(): lax.ppermute(block, 'resp', [(m, (m + shift) % members) for m in range(me...  8.26 us
  transfers between devices with their start and end apart: 20, of which 11 were waited for; matrix products, arithmetic and copies ran while one was open for 3% of the time, Pallas kernels for 48%

profile of v7, /device:TPU:9, one launch (start us, length us, event | category | flops | bytes accessed | tf_op | source)
XLA Modules:
  0.0 163.4 jit_solution(13522061077881192231)
XLA Ops:
  7.2 0.0 all-gather.3.cloned.1.call-start
  7.2 1.9 %cut.1 = (bf16[2,128,128]{2,1,0:T(8,128)(2,1)}, bf16[2,128,128]{2,1,0:T(8,128)(2,1)}, bf16[2,128,128]{2,1,0:T(8,128)(2,1)}, bf16[2,128,128]{2,1,0:T(8,128)(2,1)}...) custom-call(bf16[128,1024]{1,0:T(8,128)(2,1)} %k_ref.1, ...), custom_call_target="tpu_custom_call" | custom-call | tf_op jit(solution)/shard_map/cut/pallas_call | solution.py:425
  9.2 0.7 collective-permute-start
  9.8 1.2 collective-permute-start.1
  11.0 0.5 collective-permute-start.2
  11.5 0.0 collective-permute-done
  11.5 2.2 %collective-permute-done.1 = bf16[2,128,128]{2,1,0:T(8,128)(2,1)S(1)} collective-permute-done((bf16[2,128,128]{2,1,0:T(8,128)(2,1)}, bf16[2,128,128]{2,1,0:T(8,128)(2,1)S(1)}, u32[]{:S(2)}, u32[]{:S(2)}) %collective-permute-start.1) | collective-permute-done | bytes 65568 | tf_op jit(solution)/shard_map/ppermute | solution.py:461
  13.7 1.6 collective-permute-done.2
  15.3 0.9 pad_maximum_fusion.rest_0_
  16.2 0.0 copy-start
  16.2 0.2 collective-permute-start.8
  16.4 2.3 %collective-permute-start.7 = (bf16[2,512,128]{2,1,0:T(8,128)(2,1)S(1)}, bf16[2,512,128]{2,1,0:T(8,128)(2,1)S(1)}, u32[]{:S(2)}, u32[]{:S(2)}) collective-permute-start(bf16[2,512,128]{2,1,0:T(8,128)(2,1)S(1)} %pad_maximum_fusion.rest_0_), channel_id=1, source_target_pairs={{0,8},{4,12},{8,0},{12,4},{1,9},{5,13},{9,1},{13,5},{2,10},{6,14},... | collective-permute-start | bytes 786440 | tf_op jit(solution)/shard_map/ppermute | solution.py:467
  18.7 2.2 %collective-permute-start.6 = (bf16[2,512,128]{2,1,0:T(8,128)(2,1)S(1)}, bf16[2,512,128]{2,1,0:T(8,128)(2,1)S(1)}, u32[]{:S(2)}, u32[]{:S(2)}) collective-permute-start(bf16[2,512,128]{2,1,0:T(8,128)(2,1)S(1)} %pad_maximum_fusion.rest_0_), channel_id=1, source_target_pairs={{0,4},{4,8},{8,12},{12,0},{1,5},{5,9},{9,13},{13,1},{2,6},{6,10},{... | collective-permute-start | bytes 786440 | tf_op jit(solution)/shard_map/ppermute | solution.py:467
  20.9 1.2 collective-permute-start.3
  22.1 1.0 collective-permute-start.4
  23.2 0.1 collective-permute-done.3
  23.2 1.3 collective-permute-start.5
  24.5 1.5 collective-permute-done.4
  26.1 1.8 %collective-permute-done.5 = bf16[2,128,128]{2,1,0:T(8,128)(2,1)S(1)} collective-permute-done((bf16[2,128,128]{2,1,0:T(8,128)(2,1)}, bf16[2,128,128]{2,1,0:T(8,128)(2,1)S(1)}, u32[]{:S(2)}, u32[]{:S(2)}) %collective-permute-start.5) | collective-permute-done | bytes 65568 | tf_op jit(solution)/shard_map/ppermute | solution.py:461
  27.9 1.6 pad_maximum_fusion.1
  29.4 0.0 collective-permute-done.8.rest_3_
  29.4 0.0 copy-start.7
  29.4 5.8 %collective-permute-done.7.rest_2_ = bf16[2,512,128]{2,1,0:T(8,128)(2,1)S(1)} collective-permute-done((bf16[2,512,128]{2,1,0:T(8,128)(2,1)S(1)}, bf16[2,512,128]{2,1,0:T(8,128)(2,1)S(1)}, u32[]{:S(2)}, u32[]{:S(2)}) %collective-permute-start.7) | collective-permute-done | bytes 262176 | tf_op jit(solution)/shard_map/ppermute | solution.py:467
  35.3 5.6 %collective-permute-done.6.rest_1_ = bf16[2,512,128]{2,1,0:T(8,128)(2,1)S(1)} collective-permute-done((bf16[2,512,128]{2,1,0:T(8,128)(2,1)S(1)}, bf16[2,512,128]{2,1,0:T(8,128)(2,1)S(1)}, u32[]{:S(2)}, u32[]{:S(2)}) %collective-permute-start.6) | collective-permute-done | bytes 262176 | tf_op jit(solution)/shard_map/ppermute | solution.py:467
  40.9 0.0 all-gather.3.cloned.1.call-update
  40.9 0.0 reduce-scatter.2.cloned.1.call-start
  41.6 0.0 copy-done
  41.6 0.0 copy-done.7
  41.7 0.0 copy-done.8
  41.7 0.0 copy-done.9
  41.7 38.7 %attend_pair_0.1 = (bf16[512,2048]{1,0:T(8,128)(2,1)}, bf16[512,2048]{1,0:T(8,128)(2,1)}, bf16[512,256]{1,0:T(8,128)(2,1)}, bf16[512,256]{1,0:T(8,128)(2,1)}, bf16[4,2,512,128]{3,2,1,0:T(8,128)(2,1)}) custom-call(s32[1]{0:T(128)S(6)} %copy.21.len_ref, bf16[512,2048]{1,0:T(8,128)(2,1)} %bitcast.11, bf16[512,2048]{1,0:T(8,128)(2,1)} %bitcast.13, ...), custom_call_target="tpu_custom_call" | custom-call | flops 16106127360 | bytes 4194304 | tf_op jit(solution)/shard_map/attend_pair_0/pallas_call | solution.py:359
  80.4 0.0 reduce-scatter.2.cloned.1.call-update
  80.4 0.0 all-gather.3.cloned.1.call-done
  80.4 39.2 %attend_pair_1.1 = (bf16[512,2048]{1,0:T(8,128)(2,1)}, bf16[512,2048]{1,0:T(8,128)(2,1)}, bf16[512,256]{1,0:T(8,128)(2,1)}, bf16[512,256]{1,0:T(8,128)(2,1)}, bf...) custom-call(s32[1]{0:T(128)S(6)} %copy.21.len_ref, ...), custom_call_target="tpu_custom_call", output_to_operand_aliasing={{0}: (6, {}), {1}: (7, {}), {2}: (8, {}), {3}: (9, {})} | custom-call | flops 16106127360 | bytes 4194304 | tf_op jit(solution)/shard_map/attend_pair_1/pallas_call | solution.py:359
  119.6 0.0 reduce-scatter.2.cloned.1.call-done
  119.7 2.3 %collective-permute-start.12 = (bf16[2,512,128]{2,1,0:T(8,128)(2,1)}, bf16[2,512,128]{2,1,0:T(8,128)(2,1)S(1)}, u32[]{:S(2)}, u32[]{:S(2)}) collective-permute-start(bf16[2,512,128]{2,1,0:T(8,128)(2,1)} %get-tuple-element.77), channel_id=1, source_target_pairs={{0,4},{4,8},{8,12},{12,0},{1,5},{5,9},{9,13},{13,1},{2,6},{6,10},{... | collective-permute-start | bytes 786440 | tf_op jit(solution)/shard_map/ppermute | solution.py:467
  121.9 0.7 collective-permute-start.13
  122.7 0.5 collective-permute-start.14
  123.2 1.6 fusion.1
  124.8 2.9 %collective-permute-start.11 = (bf16[2,128,128]{2,1,0:T(8,128)(2,1)S(1)}, bf16[2,128,128]{2,1,0:T(8,128)(2,1)S(1)}, u32[]{:S(2)}, u32[]{:S(2)}) collective-permute-start(bf16[2,128,128]{2,1,0:T(8,128)(2,1)S(1)} %get-tuple-element.86), channel_id=1, source_target_pairs={{0,3},{1,2},{2,1},{3,0},{4,7},{5,6},{6,5},{7,4},{8,11},{9,10},{10,... | collective-permute-start | bytes 196616 | tf_op jit(solution)/shard_map/ppermute | solution.py:461
  127.6 0.3 collective-permute-start.10
  127.9 0.0 collective-permute-done.12
  127.9 13.8 %collective-permute-start.9 = (bf16[2,128,128]{2,1,0:T(8,128)(2,1)S(1)}, bf16[2,128,128]{2,1,0:T(8,128)(2,1)S(1)}, u32[]{:S(2)}, u32[]{:S(2)}) collective-permute-start(bf16[2,128,128]{2,1,0:T(8,128)(2,1)S(1)} %get-tuple-element.88), channel_id=1, source_target_pairs={{0,1},{1,0},{2,3},{3,2},{4,5},{5,4},{6,7},{7,6},{8,9},{9,8},{10,11... | collective-permute-start | bytes 196616 | tf_op jit(solution)/shard_map/ppermute | solution.py:461
  141.8 1.7 %collective-permute-done.13 = bf16[2,512,128]{2,1,0:T(8,128)(2,1)S(1)} collective-permute-done((bf16[2,512,128]{2,1,0:T(8,128)(2,1)}, bf16[2,512,128]{2,1,0:T(8,128)(2,1)S(1)}, u32[]{:S(2)}, u32[]{:S(2)}) %collective-permute-start.13) | collective-permute-done | bytes 262176 | tf_op jit(solution)/shard_map/ppermute | solution.py:467
  143.5 2.4 %collective-permute-done.14 = bf16[2,512,128]{2,1,0:T(8,128)(2,1)S(1)} collective-permute-done((bf16[2,512,128]{2,1,0:T(8,128)(2,1)}, bf16[2,512,128]{2,1,0:T(8,128)(2,1)S(1)}, u32[]{:S(2)}, u32[]{:S(2)}) %collective-permute-start.14) | collective-permute-done | bytes 262176 | tf_op jit(solution)/shard_map/ppermute | solution.py:467
  145.9 1.1 add_convert_fusion
  147.0 0.6 fusion
  147.6 2.0 %collective-permute-start.17 = (bf16[2,128,128]{2,1,0:T(8,128)(2,1)S(1)}, bf16[2,128,128]{2,1,0:T(8,128)(2,1)S(1)}, u32[]{:S(2)}, u32[]{:S(2)}) collective-permute-start(bf16[2,128,128]{2,1,0:T(8,128)(2,1)S(1)} %get-tuple-element.82), channel_id=1, source_target_pairs={{0,3},{1,2},{2,1},{3,0},{4,7},{5,6},{6,5},{7,4},{8,11},{9,10},{10,... | collective-permute-start | bytes 196616 | tf_op jit(solution)/shard_map/ppermute | solution.py:461
  149.6 0.3 collective-permute-start.16
  149.8 0.0 collective-permute-done.11.refs_3_
  149.8 0.2 collective-permute-start.15
  150.0 0.0 collective-permute-done.10.refs_2_
  150.0 0.0 collective-permute-done.9.refs_1_
  150.0 0.0 copy-start.3
  150.0 2.4 %collective-permute-done.17.refs_7_ = bf16[2,128,128]{2,1,0:T(8,128)(2,1)S(1)} collective-permute-done((bf16[2,128,128]{2,1,0:T(8,128)(2,1)S(1)}, bf16[2,128,128]{2,1,0:T(8,128)(2,1)S(1)}, u32[]{:S(2)}, u32[]{:S(2)}) %collective-permute-start.17) | collective-permute-done | bytes 65568 | tf_op jit(solution)/shard_map/ppermute | solution.py:461
  152.4 1.4 collective-permute-done.16.refs_6_
  153.8 0.0 collective-permute-done.15.refs_5_
  153.8 0.0 copy-done.1
  153.8 0.0 copy-done.2
  153.8 0.0 copy-done.3
  153.9 0.0 copy-done.4
  153.9 0.6 copy-done.5
  154.4 0.0 copy-done.6
  154.5 2.1 %place.1 = (f32[128,1024]{1,0:T(8,128)}, f32[128,1024]{1,0:T(8,128)}) custom-call(bf16[2,128,128]{2,1,0:T(8,128)(2,1)} %get-tuple-element.89.refs_0_, bf16[2,128,128]{2,1,0:T(8,128)(2,1)} %copy-done.3, bf16[2,128,128]{2,1,0:T(8,128)(2,1)} %copy-done.2, bf16[2,128,128]{2,1,0:T(8,128)(2,1)} %copy-done.1, bf16[2,128,128]{2,1,0:T(8,128)(2,1)} %get-tuple-element.85.refs_4_, ...), custom_call_target="tpu_custom_call" | custom-call | tf_op jit(solution)/shard_map/place/pallas_call | solution.py:449
  (7 shorter events, 0.0 us)
Async XLA Ops:
  7.2 73.2 %all-gather.3.cloned.1.call-start = ((), (), s32[]{:S(2)}) async-start(), calls=%async_computation.2 | async-start | bytes 1310720 | tf_op jit(solution)/shard_map/all_gather | solution.py:496
  9.2 2.4 %collective-permute-start = (bf16[2,128,128]{2,1,0:T(8,128)(2,1)}, bf16[2,128,128]{2,1,0:T(8,128)(2,1)S(1)}, u32[]{:S(2)}, u32[]{:S(2)}) collective-permute-start(bf16[2,128,128]{2,1,0:T(8,128)(2,1)} %get-tuple-element.45), channel_id=1, source_target_pairs={{0,1},{1,0},{2,3},{3,2},{4,5},{5,4},{6,7},{7,6},{8,9},{9,8},{10,11... | collective-permute-start | bytes 196616 | tf_op jit(solution)/shard_map/ppermute | solution.py:461
  9.8 3.9 %collective-permute-start.1 = (bf16[2,128,128]{2,1,0:T(8,128)(2,1)}, bf16[2,128,128]{2,1,0:T(8,128)(2,1)S(1)}, u32[]{:S(2)}, u32[]{:S(2)}) collective-permute-start(bf16[2,128,128]{2,1,0:T(8,128)(2,1)} %get-tuple-element.46), channel_id=1, source_target_pairs={{0,2},{1,3},{2,0},{3,1},{4,6},{5,7},{6,4},{7,5},{8,10},{9,11},{10,... | collective-permute-start | bytes 196616 | tf_op jit(solution)/shard_map/ppermute | solution.py:461
  11.0 4.2 %collective-permute-start.2 = (bf16[2,128,128]{2,1,0:T(8,128)(2,1)}, bf16[2,128,128]{2,1,0:T(8,128)(2,1)S(1)}, u32[]{:S(2)}, u32[]{:S(2)}) collective-permute-start(bf16[2,128,128]{2,1,0:T(8,128)(2,1)} %get-tuple-element.47), channel_id=1, source_target_pairs={{0,3},{1,2},{2,1},{3,0},{4,7},{5,6},{6,5},{7,4},{8,11},{9,10},{10,... | collective-permute-start | bytes 196616 | tf_op jit(solution)/shard_map/ppermute | solution.py:461
  16.2 25.5 %copy-start = (bf16[2,512,128]{2,1,0:T(8,128)(2,1)}, bf16[2,512,128]{2,1,0:T(8,128)(2,1)S(1)}, u32[]{:S(2)}) copy-start(bf16[2,512,128]{2,1,0:T(8,128)(2,1)S(1)} %pad_maximum_fusion.rest_0_) | copy-start | bytes 786436
  16.2 13.3 %collective-permute-start.8 = (bf16[2,512,128]{2,1,0:T(8,128)(2,1)S(1)}, bf16[2,512,128]{2,1,0:T(8,128)(2,1)S(1)}, u32[]{:S(2)}, u32[]{:S(2)}) collective-permute-start(bf16[2,512,128]{2,1,0:T(8,128)(2,1)S(1)} %pad_maximum_fusion.rest_0_), channel_id=1, source_target_pairs={{0,12},{4,0},{8,4},{12,8},{1,13},{5,1},{9,5},{13,9},{2,14},{6,2},{... | collective-permute-start | bytes 786440 | tf_op jit(solution)/shard_map/ppermute | solution.py:467
  16.4 18.9 %collective-permute-start.7 = (bf16[2,512,128]{2,1,0:T(8,128)(2,1)S(1)}, bf16[2,512,128]{2,1,0:T(8,128)(2,1)S(1)}, u32[]{:S(2)}, u32[]{:S(2)}) collective-permute-start(bf16[2,512,128]{2,1,0:T(8,128)(2,1)S(1)} %pad_maximum_fusion.rest_0_), channel_id=1, source_target_pairs={{0,8},{4,12},{8,0},{12,4},{1,9},{5,13},{9,1},{13,5},{2,10},{6,14},... | collective-permute-start | bytes 786440 | tf_op jit(solution)/shard_map/ppermute | solution.py:467
  18.7 22.2 %collective-permute-start.6 = (bf16[2,512,128]{2,1,0:T(8,128)(2,1)S(1)}, bf16[2,512,128]{2,1,0:T(8,128)(2,1)S(1)}, u32[]{:S(2)}, u32[]{:S(2)}) collective-permute-start(bf16[2,512,128]{2,1,0:T(8,128)(2,1)S(1)} %pad_maximum_fusion.rest_0_), channel_id=1, source_target_pairs={{0,4},{4,8},{8,12},{12,0},{1,5},{5,9},{9,13},{13,1},{2,6},{6,10},{... | collective-permute-start | bytes 786440 | tf_op jit(solution)/shard_map/ppermute | solution.py:467
  20.9 2.3 %collective-permute-start.3 = (bf16[2,128,128]{2,1,0:T(8,128)(2,1)}, bf16[2,128,128]{2,1,0:T(8,128)(2,1)S(1)}, u32[]{:S(2)}, u32[]{:S(2)}) collective-permute-start(bf16[2,128,128]{2,1,0:T(8,128)(2,1)} %get-tuple-element.53), channel_id=1, source_target_pairs={{0,1},{1,0},{2,3},{3,2},{4,5},{5,4},{6,7},{7,6},{8,9},{9,8},{10,11... | collective-permute-start | bytes 196616 | tf_op jit(solution)/shard_map/ppermute | solution.py:461
  22.1 3.9 %collective-permute-start.4 = (bf16[2,128,128]{2,1,0:T(8,128)(2,1)}, bf16[2,128,128]{2,1,0:T(8,128)(2,1)S(1)}, u32[]{:S(2)}, u32[]{:S(2)}) collective-permute-start(bf16[2,128,128]{2,1,0:T(8,128)(2,1)} %get-tuple-element.54), channel_id=1, source_target_pairs={{0,2},{1,3},{2,0},{3,1},{4,6},{5,7},{6,4},{7,5},{8,10},{9,11},{10,... | collective-permute-start | bytes 196616 | tf_op jit(solution)/shard_map/ppermute | solution.py:461
  23.2 4.6 %collective-permute-start.5 = (bf16[2,128,128]{2,1,0:T(8,128)(2,1)}, bf16[2,128,128]{2,1,0:T(8,128)(2,1)S(1)}, u32[]{:S(2)}, u32[]{:S(2)}) collective-permute-start(bf16[2,128,128]{2,1,0:T(8,128)(2,1)} %get-tuple-element.55), channel_id=1, source_target_pairs={{0,3},{1,2},{2,1},{3,0},{4,7},{5,6},{6,5},{7,4},{8,11},{9,10},{10,... | collective-permute-start | bytes 196616 | tf_op jit(solution)/shard_map/ppermute | solution.py:461
  29.4 12.2 %copy-start.7 = (bf16[2,512,128]{2,1,0:T(8,128)(2,1)}, bf16[2,512,128]{2,1,0:T(8,128)(2,1)S(1)}, u32[]{:S(2)}) copy-start(bf16[2,512,128]{2,1,0:T(8,128)(2,1)S(1)} %collective-permute-done.8.rest_3_) | copy-start | bytes 786436
  35.3 6.4 %copy-start.8 = (bf16[2,512,128]{2,1,0:T(8,128)(2,1)}, bf16[2,512,128]{2,1,0:T(8,128)(2,1)S(1)}, u32[]{:S(2)}) copy-start(bf16[2,512,128]{2,1,0:T(8,128)(2,1)S(1)} %collective-permute-done.7.rest_2_) | copy-start | bytes 786436
  40.9 0.8 copy-start.9
  40.9 78.8 %reduce-scatter.2.cloned.1.call-start = ((), (), s32[]{:S(2)}) async-start(), calls=%async_computation.1 | async-start | bytes 1310720 | tf_op jit(solution)/shard_map/reduce_scatter | solution.py:516
  119.7 8.3 %collective-permute-start.12 = (bf16[2,512,128]{2,1,0:T(8,128)(2,1)}, bf16[2,512,128]{2,1,0:T(8,128)(2,1)S(1)}, u32[]{:S(2)}, u32[]{:S(2)}) collective-permute-start(bf16[2,512,128]{2,1,0:T(8,128)(2,1)} %get-tuple-element.77), channel_id=1, source_target_pairs={{0,4},{4,8},{8,12},{12,0},{1,5},{5,9},{9,13},{13,1},{2,6},{6,10},{... | collective-permute-start | bytes 786440 | tf_op jit(solution)/shard_map/ppermute | solution.py:467
  121.9 21.5 %collective-permute-start.13 = (bf16[2,512,128]{2,1,0:T(8,128)(2,1)}, bf16[2,512,128]{2,1,0:T(8,128)(2,1)S(1)}, u32[]{:S(2)}, u32[]{:S(2)}) collective-permute-start(bf16[2,512,128]{2,1,0:T(8,128)(2,1)} %get-tuple-element.78), channel_id=1, source_target_pairs={{0,8},{4,12},{8,0},{12,4},{1,9},{5,13},{9,1},{13,5},{2,10},{6,14},... | collective-permute-start | bytes 786440 | tf_op jit(solution)/shard_map/ppermute | solution.py:467
  122.7 23.2 %collective-permute-start.14 = (bf16[2,512,128]{2,1,0:T(8,128)(2,1)}, bf16[2,512,128]{2,1,0:T(8,128)(2,1)S(1)}, u32[]{:S(2)}, u32[]{:S(2)}) collective-permute-start(bf16[2,512,128]{2,1,0:T(8,128)(2,1)} %get-tuple-element.79), channel_id=1, source_target_pairs={{0,12},{4,0},{8,4},{12,8},{1,13},{5,1},{9,5},{13,9},{2,14},{6,2},{... | collective-permute-start | bytes 786440 | tf_op jit(solution)/shard_map/ppermute | solution.py:467
  124.8 25.1 %collective-permute-start.11 = (bf16[2,128,128]{2,1,0:T(8,128)(2,1)S(1)}, bf16[2,128,128]{2,1,0:T(8,128)(2,1)S(1)}, u32[]{:S(2)}, u32[]{:S(2)}) collective-permute-start(bf16[2,128,128]{2,1,0:T(8,128)(2,1)S(1)} %get-tuple-element.86), channel_id=1, source_target_pairs={{0,3},{1,2},{2,1},{3,0},{4,7},{5,6},{6,5},{7,4},{8,11},{9,10},{10,... | collective-permute-start | bytes 196616 | tf_op jit(solution)/shard_map/ppermute | solution.py:461
  127.6 22.4 %collective-permute-start.10 = (bf16[2,128,128]{2,1,0:T(8,128)(2,1)S(1)}, bf16[2,128,128]{2,1,0:T(8,128)(2,1)S(1)}, u32[]{:S(2)}, u32[]{:S(2)}) collective-permute-start(bf16[2,128,128]{2,1,0:T(8,128)(2,1)S(1)} %get-tuple-element.87), channel_id=1, source_target_pairs={{0,2},{1,3},{2,0},{3,1},{4,6},{5,7},{6,4},{7,5},{8,10},{9,11},{10,... | collective-permute-start | bytes 196616 | tf_op jit(solution)/shard_map/ppermute | solution.py:461
  127.9 22.1 %collective-permute-start.9 = (bf16[2,128,128]{2,1,0:T(8,128)(2,1)S(1)}, bf16[2,128,128]{2,1,0:T(8,128)(2,1)S(1)}, u32[]{:S(2)}, u32[]{:S(2)}) collective-permute-start(bf16[2,128,128]{2,1,0:T(8,128)(2,1)S(1)} %get-tuple-element.88), channel_id=1, source_target_pairs={{0,1},{1,0},{2,3},{3,2},{4,5},{5,4},{6,7},{7,6},{8,9},{9,8},{10,11... | collective-permute-start | bytes 196616 | tf_op jit(solution)/shard_map/ppermute | solution.py:461
  147.6 4.8 %collective-permute-start.17 = (bf16[2,128,128]{2,1,0:T(8,128)(2,1)S(1)}, bf16[2,128,128]{2,1,0:T(8,128)(2,1)S(1)}, u32[]{:S(2)}, u32[]{:S(2)}) collective-permute-start(bf16[2,128,128]{2,1,0:T(8,128)(2,1)S(1)} %get-tuple-element.82), channel_id=1, source_target_pairs={{0,3},{1,2},{2,1},{3,0},{4,7},{5,6},{6,5},{7,4},{8,11},{9,10},{10,... | collective-permute-start | bytes 196616 | tf_op jit(solution)/shard_map/ppermute | solution.py:461
  149.6 4.3 %collective-permute-start.16 = (bf16[2,128,128]{2,1,0:T(8,128)(2,1)S(1)}, bf16[2,128,128]{2,1,0:T(8,128)(2,1)S(1)}, u32[]{:S(2)}, u32[]{:S(2)}) collective-permute-start(bf16[2,128,128]{2,1,0:T(8,128)(2,1)S(1)} %get-tuple-element.83), channel_id=1, source_target_pairs={{0,2},{1,3},{2,0},{3,1},{4,6},{5,7},{6,4},{7,5},{8,10},{9,11},{10,... | collective-permute-start | bytes 196616 | tf_op jit(solution)/shard_map/ppermute | solution.py:461
  149.8 4.0 %copy-start.1 = (bf16[2,128,128]{2,1,0:T(8,128)(2,1)}, bf16[2,128,128]{2,1,0:T(8,128)(2,1)S(1)}, u32[]{:S(2)}) copy-start(bf16[2,128,128]{2,1,0:T(8,128)(2,1)S(1)} %collective-permute-done.11.refs_3_) | copy-start | bytes 196612
  149.8 4.0 %collective-permute-start.15 = (bf16[2,128,128]{2,1,0:T(8,128)(2,1)S(1)}, bf16[2,128,128]{2,1,0:T(8,128)(2,1)S(1)}, u32[]{:S(2)}, u32[]{:S(2)}) collective-permute-start(bf16[2,128,128]{2,1,0:T(8,128)(2,1)S(1)} %get-tuple-element.84), channel_id=1, source_target_pairs={{0,1},{1,0},{2,3},{3,2},{4,5},{5,4},{6,7},{7,6},{8,9},{9,8},{10,11... | collective-permute-start | bytes 196616 | tf_op jit(solution)/shard_map/ppermute | solution.py:461
  150.0 3.8 %copy-start.2 = (bf16[2,128,128]{2,1,0:T(8,128)(2,1)}, bf16[2,128,128]{2,1,0:T(8,128)(2,1)S(1)}, u32[]{:S(2)}) copy-start(bf16[2,128,128]{2,1,0:T(8,128)(2,1)S(1)} %collective-permute-done.10.refs_2_) | copy-start | bytes 196612
  150.0 3.8 %copy-start.3 = (bf16[2,128,128]{2,1,0:T(8,128)(2,1)}, bf16[2,128,128]{2,1,0:T(8,128)(2,1)S(1)}, u32[]{:S(2)}) copy-start(bf16[2,128,128]{2,1,0:T(8,128)(2,1)S(1)} %collective-permute-done.9.refs_1_) | copy-start | bytes 196612
  152.4 1.4 copy-start.4
  153.8 0.6 copy-start.5
  153.8 0.6 copy-start.6
Sparse Core Ops, SparseCore 0:
  41.0 29.2 all-gather.2
  80.5 26.7 reduce-scatter.1

commit v8 on v7

--- a/solution.py
+++ b/solution.py
@@ -26,7 +26,9 @@
     earlier,
     len_ref,
     q_ref,
+    qt_ref,
     g_ref,
+    gt_ref,
     kr_ref,
     vr_ref,
     *rest,
@@ -183,7 +185,7 @@
     def query_products():
         def product(r):
             dquery = dot(keys_t[...], sgrads[:, r : r + WIDE])
-            dq_ref[r : r + WIDE, :] = (factor * dquery).T.astype(BF16)
+            dq_ref[:, r : r + WIDE] = (factor * dquery).astype(BF16)
 
         return [functools.partial(product, r) for r in range(0, rows, WIDE)]
 
@@ -239,11 +241,11 @@
 
     def prepare(now):
         live_rows = lax.broadcasted_iota(jnp.int32, (rows, HD), 0) < length
-        live_grad = jnp.where(live_rows, g_ref[...].astype(F32), 0.0)
-        grad[now] = live_grad.astype(BF16)
-        grad_t[now] = live_grad.T.astype(BF16)
+        live_lanes = lax.broadcasted_iota(jnp.int32, (HD, rows), 1) < length
+        grad[now] = jnp.where(live_rows, g_ref[...].astype(F32), 0.0).astype(BF16)
+        grad_t[now] = jnp.where(live_lanes, gt_ref[...].astype(F32), 0.0).astype(BF16)
         query[now] = q_ref[...]
-        query_t[now] = q_ref[...].T
+        query_t[now] = qt_ref[...]
 
     def set_fracs(now):
         top = jnp.max(tops[...], axis=0, keepdims=True)
@@ -253,9 +255,10 @@
 
     def finish(now):
         live_lanes = lax.broadcasted_iota(jnp.int32, (HD, rows), 1) < length
-        attended = jnp.where(live_lanes, mixture[...], 0.0).astype(BF16).astype(F32)
-        out_ref[...] = attended.T.astype(BF16)
-        delta = jnp.sum(grad_t[now].astype(F32) * attended, axis=0, keepdims=True)
+        attended = jnp.where(live_lanes, mixture[...], 0.0).astype(BF16)
+        out_ref[...] = attended
+        delta = grad_t[now].astype(F32) * attended.astype(F32)
+        delta = jnp.sum(delta, axis=0, keepdims=True)
         deltas[now] = jnp.broadcast_to(delta, (8, rows))
 
     @pl.when(step == 0)
@@ -332,11 +335,12 @@
 def attend(
     layout, pair, heads_per, lengths, queries, out_grad, caches, resp_keys, resp_values, earlier
 ):
-    rows, query_width = queries.shape
+    rows, query_width = queries[0].shape
     total_rows = layout.prompt_rows + rows
     first, last = pair * heads_per, (pair + 1) * heads_per - 1
     head_block = pl.BlockSpec((rows, HD), lambda s: (0, jnp.minimum(first + s, last)))
-    late_block = pl.BlockSpec((rows, HD), lambda s: (0, jnp.maximum(first + s - 1, first)))
+    turned_block = pl.BlockSpec((HD, rows), lambda s: (jnp.minimum(first + s, last), 0))
+    late_block = pl.BlockSpec((HD, rows), lambda s: (jnp.maximum(first + s - 1, first), 0))
     pair_block = pl.BlockSpec((rows, HD), lambda s: (0, pair))
     cache_blocks = [
         pl.BlockSpec(shape, lambda s, rank=len(shape): (0,) * rank)
@@ -350,20 +354,22 @@
     in_specs = [
         pl.BlockSpec(memory_space=pltpu.SMEM),
         head_block,
+        turned_block,
         head_block,
+        turned_block,
         pair_block,
         pair_block,
         *cache_blocks,
     ] + [pl.BlockSpec(memory_space=pl.ANY)] * len(earlier)
-    aliases = {5 + layout.caches + i: i for i in range(len(earlier))}
+    aliases = {7 + layout.caches + i: i for i in range(len(earlier))}
     return pl.pallas_call(
         functools.partial(attention_kernel, layout, heads_per, len(earlier)),
         grid=(heads_per + 1,),
         in_specs=in_specs,
-        out_specs=[head_block, late_block, pair_block, pair_block, *dcache_blocks],
+        out_specs=[turned_block, late_block, pair_block, pair_block, *dcache_blocks],
         out_shape=[
-            jax.ShapeDtypeStruct(queries.shape, BF16),
-            jax.ShapeDtypeStruct(queries.shape, BF16),
+            jax.ShapeDtypeStruct((query_width, rows), BF16),
+            jax.ShapeDtypeStruct((query_width, rows), BF16),
             jax.ShapeDtypeStruct(resp_keys.shape, BF16),
             jax.ShapeDtypeStruct(resp_keys.shape, BF16),
             *[jax.ShapeDtypeStruct(shape, BF16) for shape in layout.dcache_shapes()],
@@ -402,7 +408,7 @@
         ),
         compiler_params=pltpu.CompilerParams(vmem_limit_bytes=60 * 1024 * 1024),
         name=f"attend_pair_{pair}",
-    )(lengths, queries, out_grad, resp_keys, resp_values, *caches, *earlier)
+    )(lengths, *queries, *out_grad, resp_keys, resp_values, *caches, *earlier)
 
 
 def whole_block(shape):
@@ -484,6 +490,7 @@
         a[0] for a in (queries, out_grad, resp_keys, resp_values)
     )
     cuts = cut(prompt_keys, prompt_values, pairs)
+    queries, out_grad = (queries, queries.T), (out_grad, out_grad.T)
     kinds = [Scattered(members, ranks, own_rows)]
     kinds += [Gathered(members, ranks, own_rows) for _ in range(pairs - 1)]
     own = jnp.concatenate(swap(cuts[0]), axis=1)
@@ -515,13 +522,20 @@
         if isinstance(kinds[p], Scattered):
             totals.append(lax.psum_scatter(dcaches[0], "resp", scatter_dimension=0))
         else:
-            arrived = [dcaches[0]] + [
-                send(dcaches[shift], members, shift) for shift in range(1, members)
-            ]
-            totals.append(sum(block.astype(F32) for block in arrived).astype(BF16))
+            totals.append(
+                [dcaches[0]]
+                + [send(dcaches[shift], members, shift) for shift in range(1, members)]
+            )
+    attended, query_grad = earlier[0].T, earlier[1].T
+    if isinstance(totals[-1], list):
+        attended, query_grad, arrived = lax.optimization_barrier(
+            (attended, query_grad, totals[-1])
+        )
+        totals[-1] = sum(block.astype(F32) for block in arrived).astype(BF16)
     blocks = [block for total in totals for block in swap(cut_rows(total, ranks))]
     key_grad, value_grad = place(blocks, pairs, columns)
-    return (*(a[None] for a in earlier), key_grad, value_grad)
+    outs = (a[None] for a in (attended, query_grad, *earlier[2:]))
+    return (*outs, key_grad, value_grad)
 
 
 def solution(mesh):

time: 164 us -> 174 us (1.061)
  the two profiles are of different devices: /device:TPU:9 before, /device:TPU:13 now
where the time goes in v8:
time: 174 us; the launch traced here: 173 us
  Pallas kernels  82.6 us (47%)
  starting transfers between devices  33.6 us (19%)
  waiting for transfers between devices  22.8 us (13%)
  local copies, waits for them, and re-layouts  15.7 us (9%)
  between operations  14.9 us (9%)
  other arithmetic  3.51 us (2%)
    pallas_call x2, Pallas kernels, attend(): pl.pallas_call(functools.partial(attention_kernel, layout, heads_per, len...  78.6 us
    ppermute x12, starting transfers between devices, swap(): lax.ppermute(blocks[i], 'tensor', [(j, j ^ i) for j in range(count)])  25.2 us
    ppermute x6, waiting for transfers between devices, send(): lax.ppermute(block, 'resp', [(m, (m + shift) % members) for m in range(me...  15.5 us
    unnamed x28, local copies, waits for them, and re-layouts  13.5 us
    ppermute x6, starting transfers between devices, send(): lax.ppermute(block, 'resp', [(m, (m + shift) % members) for m in range(me...  8.29 us
    ppermute x12, waiting for transfers between devices, swap(): lax.ppermute(blocks[i], 'tensor', [(j, j ^ i) for j in range(count)])  7.26 us
  transfers between devices with their start and end apart: 20, of which 9 were waited for; matrix products, arithmetic and copies ran while one was open for 10% of the time, Pallas kernels for 45%

profile of v8, /device:TPU:13, one launch (start us, length us, event | category | flops | bytes accessed | tf_op | source)
XLA Modules:
  0.0 173.2 jit_solution(12140823561170217186)
XLA Ops:
  7.2 0.0 all-gather.3.cloned.1.call-start
  7.2 1.9 %cut.1 = (bf16[2,128,128]{2,1,0:T(8,128)(2,1)}, bf16[2,128,128]{2,1,0:T(8,128)(2,1)}, bf16[2,128,128]{2,1,0:T(8,128)(2,1)}, bf16[2,128,128]{2,1,0:T(8,128)(2,1)}...) custom-call(bf16[128,1024]{1,0:T(8,128)(2,1)} %k_ref.1, ...), custom_call_target="tpu_custom_call" | custom-call | tf_op jit(solution)/shard_map/cut/pallas_call | solution.py:431
  9.1 0.7 collective-permute-start
  9.8 1.2 collective-permute-start.1
  11.0 0.5 collective-permute-start.2
  11.5 0.0 collective-permute-done
  11.5 2.2 %collective-permute-done.1 = bf16[2,128,128]{2,1,0:T(8,128)(2,1)S(1)} collective-permute-done((bf16[2,128,128]{2,1,0:T(8,128)(2,1)}, bf16[2,128,128]{2,1,0:T(8,128)(2,1)S(1)}, u32[]{:S(2)}, u32[]{:S(2)}) %collective-permute-start.1) | collective-permute-done | bytes 65568 | tf_op jit(solution)/shard_map/ppermute | solution.py:467
  13.7 1.6 collective-permute-done.2
  15.3 0.9 pad_maximum_fusion.rest_0_
  16.2 0.0 copy-start.2
  16.2 0.2 collective-permute-start.8
  16.4 2.3 %collective-permute-start.7 = (bf16[2,512,128]{2,1,0:T(8,128)(2,1)S(1)}, bf16[2,512,128]{2,1,0:T(8,128)(2,1)S(1)}, u32[]{:S(2)}, u32[]{:S(2)}) collective-permute-start(bf16[2,512,128]{2,1,0:T(8,128)(2,1)S(1)} %pad_maximum_fusion.rest_0_), channel_id=1, source_target_pairs={{0,8},{4,12},{8,0},{12,4},{1,9},{5,13},{9,1},{13,5},{2,10},{6,14},... | collective-permute-start | bytes 786440 | tf_op jit(solution)/shard_map/ppermute | solution.py:473
  18.7 2.2 %collective-permute-start.6 = (bf16[2,512,128]{2,1,0:T(8,128)(2,1)S(1)}, bf16[2,512,128]{2,1,0:T(8,128)(2,1)S(1)}, u32[]{:S(2)}, u32[]{:S(2)}) collective-permute-start(bf16[2,512,128]{2,1,0:T(8,128)(2,1)S(1)} %pad_maximum_fusion.rest_0_), channel_id=1, source_target_pairs={{0,4},{4,8},{8,12},{12,0},{1,5},{5,9},{9,13},{13,1},{2,6},{6,10},{... | collective-permute-start | bytes 786440 | tf_op jit(solution)/shard_map/ppermute | solution.py:473
  20.9 1.2 collective-permute-start.3
  22.1 1.0 collective-permute-start.4
  23.2 0.1 collective-permute-done.3
  23.3 1.3 collective-permute-start.5
  24.5 1.6 collective-permute-done.4
  26.1 1.8 %collective-permute-done.5 = bf16[2,128,128]{2,1,0:T(8,128)(2,1)S(1)} collective-permute-done((bf16[2,128,128]{2,1,0:T(8,128)(2,1)}, bf16[2,128,128]{2,1,0:T(8,128)(2,1)S(1)}, u32[]{:S(2)}, u32[]{:S(2)}) %collective-permute-start.5) | collective-permute-done | bytes 65568 | tf_op jit(solution)/shard_map/ppermute | solution.py:467
  27.9 1.6 pad_maximum_fusion.1
  29.4 0.0 collective-permute-done.8.rest_3_
  29.4 5.8 %collective-permute-done.7.rest_2_ = bf16[2,512,128]{2,1,0:T(8,128)(2,1)S(1)} collective-permute-done((bf16[2,512,128]{2,1,0:T(8,128)(2,1)S(1)}, bf16[2,512,128]{2,1,0:T(8,128)(2,1)S(1)}, u32[]{:S(2)}, u32[]{:S(2)}) %collective-permute-start.7) | collective-permute-done | bytes 262176 | tf_op jit(solution)/shard_map/ppermute | solution.py:473
  35.3 5.6 %collective-permute-done.6.rest_1_ = bf16[2,512,128]{2,1,0:T(8,128)(2,1)S(1)} collective-permute-done((bf16[2,512,128]{2,1,0:T(8,128)(2,1)S(1)}, bf16[2,512,128]{2,1,0:T(8,128)(2,1)S(1)}, u32[]{:S(2)}, u32[]{:S(2)}) %collective-permute-start.6) | collective-permute-done | bytes 262176 | tf_op jit(solution)/shard_map/ppermute | solution.py:473
  40.9 0.0 all-gather.3.cloned.1.call-update
  40.9 0.0 reduce-scatter.2.cloned.1.call-start
  41.6 0.0 copy-start
  41.7 4.1 %copy.25 = bf16[1,512,2048]{1,2,0:T(8,128)(2,1)} copy(bf16[1,512,2048]{2,1,0:T(8,128)(2,1)} %param.7) | data formatting | bytes 4194304 | tf_op args[0]
  45.7 0.0 copy-done.2
  45.8 2.5 %copy.26 = bf16[1,512,2048]{1,2,0:T(8,128)(2,1)} copy(bf16[1,512,2048]{2,1,0:T(8,128)(2,1)S(1)} %copy-done) | data formatting | bytes 4194304 | tf_op args[5]
  48.3 39.1 %attend_pair_0.1 = (bf16[2048,512]{1,0:T(8,128)(2,1)}, bf16[2048,512]{1,0:T(8,128)(2,1)}, bf16[512,256]{1,0:T(8,128)(2,1)}, bf16[512,256]{1,0:T(8,128)(2,1)}, bf16[4,2,512,128]{3,2,1,0:T(8,128)(2,1)}) custom-call(s32[1]{0:T(128)S(6)} %copy.39.len_ref, bf16[512,2048]{1,0:T(8,128)(2,1)} %bitcast.18, bf16[2048,512]{1,0:T(8,128)(2,1)} %bitcast.22, ...), custom_call_target="tpu_custom_call" | custom-call | flops 16106127360 | bytes 4194304 | tf_op jit(solution)/shard_map/attend_pair_0/pallas_call | solution.py:365
  87.4 0.0 reduce-scatter.2.cloned.1.call-update
  87.4 0.0 all-gather.3.cloned.1.call-done
  87.4 39.5 %attend_pair_1.1 = (bf16[2048,512]{1,0:T(8,128)(2,1)}, bf16[2048,512]{1,0:T(8,128)(2,1)}, bf16[512,256]{1,0:T(8,128)(2,1)}, bf16[512,256]{1,0:T(8,128)(2,1)}, bf...) custom-call(s32[1]{0:T(128)S(6)} %copy.39.len_ref, ...), custom_call_target="tpu_custom_call", output_to_operand_aliasing={{0}: (8, {}), {1}: (9, {}), {2}: (10, {}), {3}: (11, {})} | custom-call | flops 16106127360 | bytes 4194304 | tf_op jit(solution)/shard_map/attend_pair_1/pallas_call | solution.py:365
  126.9 0.0 reduce-scatter.2.cloned.1.call-done
  126.9 2.3 %collective-permute-start.9 = (bf16[2,512,128]{2,1,0:T(8,128)(2,1)}, bf16[2,512,128]{2,1,0:T(8,128)(2,1)S(1)}, u32[]{:S(2)}, u32[]{:S(2)}) collective-permute-start(bf16[2,512,128]{2,1,0:T(8,128)(2,1)} %get-tuple-element.80), channel_id=1, source_target_pairs={{0,4},{4,8},{8,12},{12,0},{1,5},{5,9},{9,13},{13,1},{2,6},{6,10},{... | collective-permute-start | bytes 786440 | tf_op jit(solution)/shard_map/ppermute | solution.py:473
  129.2 0.7 collective-permute-start.10
  130.0 0.5 collective-permute-start.11
  130.5 1.6 fusion.1
  132.1 2.8 %collective-permute-start.14 = (bf16[2,128,128]{2,1,0:T(8,128)(2,1)S(1)}, bf16[2,128,128]{2,1,0:T(8,128)(2,1)S(1)}, u32[]{:S(2)}, u32[]{:S(2)}) collective-permute-start(bf16[2,128,128]{2,1,0:T(8,128)(2,1)S(1)} %get-tuple-element.110), channel_id=1, source_target_pairs={{0,3},{1,2},{2,1},{3,0},{4,7},{5,6},{6,5},{7,4},{8,11},{9,10},{10,... | collective-permute-start | bytes 196616 | tf_op jit(solution)/shard_map/ppermute | solution.py:467
  134.9 0.3 collective-permute-start.13
  135.2 0.0 collective-permute-done.9
  135.2 13.8 %collective-permute-start.12 = (bf16[2,128,128]{2,1,0:T(8,128)(2,1)S(1)}, bf16[2,128,128]{2,1,0:T(8,128)(2,1)S(1)}, u32[]{:S(2)}, u32[]{:S(2)}) collective-permute-start(bf16[2,128,128]{2,1,0:T(8,128)(2,1)S(1)} %get-tuple-element.112), channel_id=1, source_target_pairs={{0,1},{1,0},{2,3},{3,2},{4,5},{5,4},{6,7},{7,6},{8,9},{9,8},{10,11... | collective-permute-start | bytes 196616 | tf_op jit(solution)/shard_map/ppermute | solution.py:467
  149.1 1.7 collective-permute-done.10
  150.8 2.3 %collective-permute-done.11 = bf16[2,512,128]{2,1,0:T(8,128)(2,1)S(1)} collective-permute-done((bf16[2,512,128]{2,1,0:T(8,128)(2,1)}, bf16[2,512,128]{2,1,0:T(8,128)(2,1)S(1)}, u32[]{:S(2)}, u32[]{:S(2)}) %collective-permute-start.11) | collective-permute-done | bytes 262176 | tf_op jit(solution)/shard_map/ppermute | solution.py:473
  153.1 1.1 add_convert_fusion
  154.2 0.6 fusion
  154.8 1.9 %collective-permute-start.17 = (bf16[2,128,128]{2,1,0:T(8,128)(2,1)S(1)}, bf16[2,128,128]{2,1,0:T(8,128)(2,1)S(1)}, u32[]{:S(2)}, u32[]{:S(2)}) collective-permute-start(bf16[2,128,128]{2,1,0:T(8,128)(2,1)S(1)} %get-tuple-element.106), channel_id=1, source_target_pairs={{0,3},{1,2},{2,1},{3,0},{4,7},{5,6},{6,5},{7,4},{8,11},{9,10},{10,... | collective-permute-start | bytes 196616 | tf_op jit(solution)/shard_map/ppermute | solution.py:467
  156.8 0.3 collective-permute-start.16
  157.1 0.0 collective-permute-done.14.refs_3_
  157.1 0.1 collective-permute-start.15
  157.2 2.4 %copy.31 = bf16[1,512,2048]{2,1,0:T(8,128)(2,1)} copy(bf16[1,512,2048]{1,2,0:T(8,128)(2,1)S(1)} %bitcast.26) | data formatting | bytes 4194304
  159.6 3.9 %copy.32 = bf16[1,512,2048]{2,1,0:T(8,128)(2,1)} copy(bf16[1,512,2048]{1,2,0:T(8,128)(2,1)} %bitcast.27) | data formatting | bytes 4194304
  163.5 0.0 collective-permute-done.13.refs_2_
  163.5 0.0 collective-permute-done.12.refs_1_
  163.5 0.0 collective-permute-done.17.refs_7_
  163.5 0.0 collective-permute-done.16.refs_6_
  163.6 0.0 copy-start.7
  163.6 0.0 collective-permute-done.15.refs_5_
  163.6 0.5 copy-done.4
  164.1 0.0 copy-done.5
  164.1 0.0 copy-done.6
  164.2 0.0 copy-done.7
  164.2 0.0 copy-done.8
  164.2 2.1 %place.1 = (f32[128,1024]{1,0:T(8,128)}, f32[128,1024]{1,0:T(8,128)}) custom-call(bf16[2,128,128]{2,1,0:T(8,128)(2,1)} %get-tuple-element.113.refs_0_, bf16[2,128,128]{2,1,0:T(8,128)(2,1)} %copy-done.5, bf16[2,128,128]{2,1,0:T(8,128)(2,1)} %copy-done.4, bf16[2,128,128]{2,1,0:T(8,128)(2,1)} %copy-done.3, bf16[2,128,128]{2,1,0:T(8,128)(2,1)} %get-tuple-element.109.refs_4_, ...), custom_call_target="tpu_custom_call" | custom-call | tf_op jit(solution)/shard_map/place/pallas_call | solution.py:455
  (15 shorter events, 0.0 us)
Async XLA Ops:
  7.2 80.2 %all-gather.3.cloned.1.call-start = ((), (), s32[]{:S(2)}) async-start(), calls=%async_computation.2 | async-start | bytes 1310720 | tf_op jit(solution)/shard_map/all_gather | solution.py:503
  9.1 2.4 %collective-permute-start = (bf16[2,128,128]{2,1,0:T(8,128)(2,1)}, bf16[2,128,128]{2,1,0:T(8,128)(2,1)S(1)}, u32[]{:S(2)}, u32[]{:S(2)}) collective-permute-start(bf16[2,128,128]{2,1,0:T(8,128)(2,1)} %get-tuple-element.51), channel_id=1, source_target_pairs={{0,1},{1,0},{2,3},{3,2},{4,5},{5,4},{6,7},{7,6},{8,9},{9,8},{10,11... | collective-permute-start | bytes 196616 | tf_op jit(solution)/shard_map/ppermute | solution.py:467
  9.8 3.9 %collective-permute-start.1 = (bf16[2,128,128]{2,1,0:T(8,128)(2,1)}, bf16[2,128,128]{2,1,0:T(8,128)(2,1)S(1)}, u32[]{:S(2)}, u32[]{:S(2)}) collective-permute-start(bf16[2,128,128]{2,1,0:T(8,128)(2,1)} %get-tuple-element.52), channel_id=1, source_target_pairs={{0,2},{1,3},{2,0},{3,1},{4,6},{5,7},{6,4},{7,5},{8,10},{9,11},{10,... | collective-permute-start | bytes 196616 | tf_op jit(solution)/shard_map/ppermute | solution.py:467
  11.0 4.3 %collective-permute-start.2 = (bf16[2,128,128]{2,1,0:T(8,128)(2,1)}, bf16[2,128,128]{2,1,0:T(8,128)(2,1)S(1)}, u32[]{:S(2)}, u32[]{:S(2)}) collective-permute-start(bf16[2,128,128]{2,1,0:T(8,128)(2,1)} %get-tuple-element.53), channel_id=1, source_target_pairs={{0,3},{1,2},{2,1},{3,0},{4,7},{5,6},{6,5},{7,4},{8,11},{9,10},{10,... | collective-permute-start | bytes 196616 | tf_op jit(solution)/shard_map/ppermute | solution.py:467
  16.2 29.6 %copy-start.2 = (bf16[2,512,128]{2,1,0:T(8,128)(2,1)}, bf16[2,512,128]{2,1,0:T(8,128)(2,1)S(1)}, u32[]{:S(2)}) copy-start(bf16[2,512,128]{2,1,0:T(8,128)(2,1)S(1)} %pad_maximum_fusion.rest_0_) | copy-start | bytes 786436
  16.2 13.3 %collective-permute-start.8 = (bf16[2,512,128]{2,1,0:T(8,128)(2,1)S(1)}, bf16[2,512,128]{2,1,0:T(8,128)(2,1)S(1)}, u32[]{:S(2)}, u32[]{:S(2)}) collective-permute-start(bf16[2,512,128]{2,1,0:T(8,128)(2,1)S(1)} %pad_maximum_fusion.rest_0_), channel_id=1, source_target_pairs={{0,12},{4,0},{8,4},{12,8},{1,13},{5,1},{9,5},{13,9},{2,14},{6,2},{... | collective-permute-start | bytes 786440 | tf_op jit(solution)/shard_map/ppermute | solution.py:473
  16.4 18.9 %collective-permute-start.7 = (bf16[2,512,128]{2,1,0:T(8,128)(2,1)S(1)}, bf16[2,512,128]{2,1,0:T(8,128)(2,1)S(1)}, u32[]{:S(2)}, u32[]{:S(2)}) collective-permute-start(bf16[2,512,128]{2,1,0:T(8,128)(2,1)S(1)} %pad_maximum_fusion.rest_0_), channel_id=1, source_target_pairs={{0,8},{4,12},{8,0},{12,4},{1,9},{5,13},{9,1},{13,5},{2,10},{6,14},... | collective-permute-start | bytes 786440 | tf_op jit(solution)/shard_map/ppermute | solution.py:473
  18.7 22.2 %collective-permute-start.6 = (bf16[2,512,128]{2,1,0:T(8,128)(2,1)S(1)}, bf16[2,512,128]{2,1,0:T(8,128)(2,1)S(1)}, u32[]{:S(2)}, u32[]{:S(2)}) collective-permute-start(bf16[2,512,128]{2,1,0:T(8,128)(2,1)S(1)} %pad_maximum_fusion.rest_0_), channel_id=1, source_target_pairs={{0,4},{4,8},{8,12},{12,0},{1,5},{5,9},{9,13},{13,1},{2,6},{6,10},{... | collective-permute-start | bytes 786440 | tf_op jit(solution)/shard_map/ppermute | solution.py:473
  20.9 2.3 %collective-permute-start.3 = (bf16[2,128,128]{2,1,0:T(8,128)(2,1)}, bf16[2,128,128]{2,1,0:T(8,128)(2,1)S(1)}, u32[]{:S(2)}, u32[]{:S(2)}) collective-permute-start(bf16[2,128,128]{2,1,0:T(8,128)(2,1)} %get-tuple-element.59), channel_id=1, source_target_pairs={{0,1},{1,0},{2,3},{3,2},{4,5},{5,4},{6,7},{7,6},{8,9},{9,8},{10,11... | collective-permute-start | bytes 196616 | tf_op jit(solution)/shard_map/ppermute | solution.py:467
  22.1 3.9 %collective-permute-start.4 = (bf16[2,128,128]{2,1,0:T(8,128)(2,1)}, bf16[2,128,128]{2,1,0:T(8,128)(2,1)S(1)}, u32[]{:S(2)}, u32[]{:S(2)}) collective-permute-start(bf16[2,128,128]{2,1,0:T(8,128)(2,1)} %get-tuple-element.60), channel_id=1, source_target_pairs={{0,2},{1,3},{2,0},{3,1},{4,6},{5,7},{6,4},{7,5},{8,10},{9,11},{10,... | collective-permute-start | bytes 196616 | tf_op jit(solution)/shard_map/ppermute | solution.py:467
  23.3 4.6 %collective-permute-start.5 = (bf16[2,128,128]{2,1,0:T(8,128)(2,1)}, bf16[2,128,128]{2,1,0:T(8,128)(2,1)S(1)}, u32[]{:S(2)}, u32[]{:S(2)}) collective-permute-start(bf16[2,128,128]{2,1,0:T(8,128)(2,1)} %get-tuple-element.61), channel_id=1, source_target_pairs={{0,3},{1,2},{2,1},{3,0},{4,7},{5,6},{6,5},{7,4},{8,11},{9,10},{10,... | collective-permute-start | bytes 196616 | tf_op jit(solution)/shard_map/ppermute | solution.py:467
  29.4 16.3 %copy-start.9 = (bf16[2,512,128]{2,1,0:T(8,128)(2,1)}, bf16[2,512,128]{2,1,0:T(8,128)(2,1)S(1)}, u32[]{:S(2)}) copy-start(bf16[2,512,128]{2,1,0:T(8,128)(2,1)S(1)} %collective-permute-done.8.rest_3_) | copy-start | bytes 786436
  35.3 10.5 %copy-start.10 = (bf16[2,512,128]{2,1,0:T(8,128)(2,1)}, bf16[2,512,128]{2,1,0:T(8,128)(2,1)S(1)}, u32[]{:S(2)}) copy-start(bf16[2,512,128]{2,1,0:T(8,128)(2,1)S(1)} %collective-permute-done.7.rest_2_) | copy-start | bytes 786436
  40.9 4.9 %copy-start.11 = (bf16[2,512,128]{2,1,0:T(8,128)(2,1)}, bf16[2,512,128]{2,1,0:T(8,128)(2,1)S(1)}, u32[]{:S(2)}) copy-start(bf16[2,512,128]{2,1,0:T(8,128)(2,1)S(1)} %collective-permute-done.6.rest_1_) | copy-start | bytes 786436
  40.9 86.0 %reduce-scatter.2.cloned.1.call-start = ((), (), s32[]{:S(2)}) async-start(), calls=%async_computation.1 | async-start | bytes 1310720 | tf_op jit(solution)/shard_map/reduce_scatter | solution.py:523
  41.6 4.1 %copy-start = (bf16[1,512,2048]{2,1,0:T(8,128)(2,1)S(1)}, bf16[1,512,2048]{2,1,0:T(8,128)(2,1)}, u32[]{:S(2)}) copy-start(bf16[1,512,2048]{2,1,0:T(8,128)(2,1)} %param.12) | copy-start | bytes 6291460
  126.9 30.3 %copy-start.1 = (bf16[2048,512]{1,0:T(8,128)(2,1)S(1)}, bf16[2048,512]{1,0:T(8,128)(2,1)}, u32[]{:S(2)}) copy-start(bf16[2048,512]{1,0:T(8,128)(2,1)} %get-tuple-element.72) | copy-start | bytes 6291460
  126.9 8.3 %collective-permute-start.9 = (bf16[2,512,128]{2,1,0:T(8,128)(2,1)}, bf16[2,512,128]{2,1,0:T(8,128)(2,1)S(1)}, u32[]{:S(2)}, u32[]{:S(2)}) collective-permute-start(bf16[2,512,128]{2,1,0:T(8,128)(2,1)} %get-tuple-element.80), channel_id=1, source_target_pairs={{0,4},{4,8},{8,12},{12,0},{1,5},{5,9},{9,13},{13,1},{2,6},{6,10},{... | collective-permute-start | bytes 786440 | tf_op jit(solution)/shard_map/ppermute | solution.py:473
  129.2 21.5 %collective-permute-start.10 = (bf16[2,512,128]{2,1,0:T(8,128)(2,1)}, bf16[2,512,128]{2,1,0:T(8,128)(2,1)S(1)}, u32[]{:S(2)}, u32[]{:S(2)}) collective-permute-start(bf16[2,512,128]{2,1,0:T(8,128)(2,1)} %get-tuple-element.81), channel_id=1, source_target_pairs={{0,8},{4,12},{8,0},{12,4},{1,9},{5,13},{9,1},{13,5},{2,10},{6,14},... | collective-permute-start | bytes 786440 | tf_op jit(solution)/shard_map/ppermute | solution.py:473
  130.0 23.2 %collective-permute-start.11 = (bf16[2,512,128]{2,1,0:T(8,128)(2,1)}, bf16[2,512,128]{2,1,0:T(8,128)(2,1)S(1)}, u32[]{:S(2)}, u32[]{:S(2)}) collective-permute-start(bf16[2,512,128]{2,1,0:T(8,128)(2,1)} %get-tuple-element.82), channel_id=1, source_target_pairs={{0,12},{4,0},{8,4},{12,8},{1,13},{5,1},{9,5},{13,9},{2,14},{6,2},{... | collective-permute-start | bytes 786440 | tf_op jit(solution)/shard_map/ppermute | solution.py:473
  132.1 25.0 %collective-permute-start.14 = (bf16[2,128,128]{2,1,0:T(8,128)(2,1)S(1)}, bf16[2,128,128]{2,1,0:T(8,128)(2,1)S(1)}, u32[]{:S(2)}, u32[]{:S(2)}) collective-permute-start(bf16[2,128,128]{2,1,0:T(8,128)(2,1)S(1)} %get-tuple-element.110), channel_id=1, source_target_pairs={{0,3},{1,2},{2,1},{3,0},{4,7},{5,6},{6,5},{7,4},{8,11},{9,10},{10,... | collective-permute-start | bytes 196616 | tf_op jit(solution)/shard_map/ppermute | solution.py:467
  134.9 28.6 %collective-permute-start.13 = (bf16[2,128,128]{2,1,0:T(8,128)(2,1)S(1)}, bf16[2,128,128]{2,1,0:T(8,128)(2,1)S(1)}, u32[]{:S(2)}, u32[]{:S(2)}) collective-permute-start(bf16[2,128,128]{2,1,0:T(8,128)(2,1)S(1)} %get-tuple-element.111), channel_id=1, source_target_pairs={{0,2},{1,3},{2,0},{3,1},{4,6},{5,7},{6,4},{7,5},{8,10},{9,11},{10,... | collective-permute-start | bytes 196616 | tf_op jit(solution)/shard_map/ppermute | solution.py:467
  135.2 28.3 %collective-permute-start.12 = (bf16[2,128,128]{2,1,0:T(8,128)(2,1)S(1)}, bf16[2,128,128]{2,1,0:T(8,128)(2,1)S(1)}, u32[]{:S(2)}, u32[]{:S(2)}) collective-permute-start(bf16[2,128,128]{2,1,0:T(8,128)(2,1)S(1)} %get-tuple-element.112), channel_id=1, source_target_pairs={{0,1},{1,0},{2,3},{3,2},{4,5},{5,4},{6,7},{7,6},{8,9},{9,8},{10,11... | collective-permute-start | bytes 196616 | tf_op jit(solution)/shard_map/ppermute | solution.py:467
  154.8 8.7 %collective-permute-start.17 = (bf16[2,128,128]{2,1,0:T(8,128)(2,1)S(1)}, bf16[2,128,128]{2,1,0:T(8,128)(2,1)S(1)}, u32[]{:S(2)}, u32[]{:S(2)}) collective-permute-start(bf16[2,128,128]{2,1,0:T(8,128)(2,1)S(1)} %get-tuple-element.106), channel_id=1, source_target_pairs={{0,3},{1,2},{2,1},{3,0},{4,7},{5,6},{6,5},{7,4},{8,11},{9,10},{10,... | collective-permute-start | bytes 196616 | tf_op jit(solution)/shard_map/ppermute | solution.py:467
  156.8 6.8 %collective-permute-start.16 = (bf16[2,128,128]{2,1,0:T(8,128)(2,1)S(1)}, bf16[2,128,128]{2,1,0:T(8,128)(2,1)S(1)}, u32[]{:S(2)}, u32[]{:S(2)}) collective-permute-start(bf16[2,128,128]{2,1,0:T(8,128)(2,1)S(1)} %get-tuple-element.107), channel_id=1, source_target_pairs={{0,2},{1,3},{2,0},{3,1},{4,6},{5,7},{6,4},{7,5},{8,10},{9,11},{10,... | collective-permute-start | bytes 196616 | tf_op jit(solution)/shard_map/ppermute | solution.py:467
  157.1 2.5 %copy-start.3 = (bf16[2,128,128]{2,1,0:T(8,128)(2,1)}, bf16[2,128,128]{2,1,0:T(8,128)(2,1)S(1)}, u32[]{:S(2)}) copy-start(bf16[2,128,128]{2,1,0:T(8,128)(2,1)S(1)} %collective-permute-done.14.refs_3_) | copy-start | bytes 196612
  157.1 6.5 %collective-permute-start.15 = (bf16[2,128,128]{2,1,0:T(8,128)(2,1)S(1)}, bf16[2,128,128]{2,1,0:T(8,128)(2,1)S(1)}, u32[]{:S(2)}, u32[]{:S(2)}) collective-permute-start(bf16[2,128,128]{2,1,0:T(8,128)(2,1)S(1)} %get-tuple-element.108), channel_id=1, source_target_pairs={{0,1},{1,0},{2,3},{3,2},{4,5},{5,4},{6,7},{7,6},{8,9},{9,8},{10,11... | collective-permute-start | bytes 196616 | tf_op jit(solution)/shard_map/ppermute | solution.py:467
  163.5 0.6 copy-start.4
  163.5 0.6 copy-start.5
  163.5 0.6 copy-start.6
  163.6 0.7 copy-start.7
  163.6 0.7 copy-start.8
Sparse Core Ops, SparseCore 0:
  41.0 29.1 all-gather.2
  87.5 26.6 reduce-scatter.1

commit v9 on v7

--- a/solution.py
+++ b/solution.py
@@ -78,9 +78,7 @@
 
     @pl.when(step == 0)
     def _():
-        for at, key_block, value_block in layout.load(caches):
-            keys[at, :] = key_block
-            values[at, :] = value_block
+        layout.load(caches, keys, values)
         for at in range(0, prompt_rows, rows):
             at = pl.ds(at, rows)
             keys_t[:, at] = keys[at, :].T
@@ -278,12 +276,17 @@
         dvr_ref[...] = dv_sum[at, :].astype(BF16)
 
 
+def fill(keys, values, at, ref):
+    keys[at, :] = ref[0]
+    values[at, :] = ref[1]
+
+
 class Gathered:
-    def __init__(self, members, ranks, own_rows):
-        self.members, self.part_rows = members, ranks * own_rows
+    def __init__(self, members, part_rows):
+        self.members, self.part_rows = members, part_rows
         self.prompt_rows = members * self.part_rows
         self.caches = 1
-        self.dcaches = members
+        self.dcaches = members + (members == 4)
 
     def cache_shapes(self):
         return [(self.members, 2, self.part_rows, HD)]
@@ -291,23 +294,24 @@
     def dcache_shapes(self):
         return [(2, self.part_rows, HD)] * self.dcaches
 
-    def load(self, caches):
+    def load(self, caches, keys, values):
         for m in range(self.members):
-            at = pl.ds(m * self.part_rows, self.part_rows)
-            yield at, caches[0][m, 0], caches[0][m, 1]
+            fill(keys, values, pl.ds(m * self.part_rows, self.part_rows), caches[0].at[m])
 
     def store(self, dcaches, dk_sum, dv_sum, factor):
         me = lax.axis_index("resp")
-        for shift in range(self.members):
-            part = lax.rem(me + shift, self.members) * self.part_rows
-            at = pl.ds(pl.multiple_of(part, self.part_rows), self.part_rows)
-            dcaches[shift][0] = (factor * dk_sum[at, :]).astype(BF16)
-            dcaches[shift][1] = dv_sum[at, :].astype(BF16)
+        parts = [lax.rem(me + shift, self.members) for shift in range(self.members)]
+        if self.members == 4:
+            parts = [parts[0], parts[1], parts[3], parts[2], 3 - me]
+        for part, ref in zip(parts, dcaches):
+            at = pl.ds(pl.multiple_of(part * self.part_rows, self.part_rows), self.part_rows)
+            ref[0] = (factor * dk_sum[at, :]).astype(BF16)
+            ref[1] = dv_sum[at, :].astype(BF16)
 
 
 class Scattered(Gathered):
-    def __init__(self, members, ranks, own_rows):
-        super().__init__(members, ranks, own_rows)
+    def __init__(self, members, part_rows):
+        super().__init__(members, part_rows)
         self.caches, self.dcaches = self.dcaches, self.caches
 
     def cache_shapes(self):
@@ -316,9 +320,22 @@
     def dcache_shapes(self):
         return [(self.members, 2, self.part_rows, HD)]
 
-    def load(self, caches):
-        for i, ref in enumerate(caches):
-            yield pl.ds(i * self.part_rows, self.part_rows), ref[0], ref[1]
+    def load(self, caches, keys, values):
+        ats = [pl.ds(m * self.part_rows, self.part_rows) for m in range(self.members)]
+        if self.members != 4:
+            for at, ref in zip(ats, caches):
+                fill(keys, values, at, ref)
+            return
+        own, left, right, two, far = caches
+        me = lax.axis_index("resp")
+        fill(keys, values, ats[0], own)
+        fill(keys, values, ats[1], left)
+        fill(keys, values, ats[2], two)
+        fill(keys, values, ats[3], right)
+        for end, at in ((0, ats[1]), (3, ats[3])):
+            @pl.when(me == end)
+            def _():
+                fill(keys, values, at, far)
 
     def store(self, dcaches, dk_sum, dv_sum, factor):
         me = lax.axis_index("resp")
@@ -463,8 +480,30 @@
     ]
 
 
-def send(block, members, shift):
+def shift_all(block, members, shift):
     return lax.ppermute(block, "resp", [(m, (m + shift) % members) for m in range(members)])
+
+
+RIGHT, LEFT = [(0, 1), (1, 2), (2, 3)], [(1, 0), (2, 1), (3, 2)]
+
+
+def spread(own, members):
+    if members != 4:
+        return [own] + [shift_all(own, members, shift) for shift in range(1, members)]
+    two = shift_all(own, members, 2)
+    right, left = lax.ppermute(own, "resp", RIGHT), lax.ppermute(own, "resp", LEFT)
+    far = lax.ppermute(two, "resp", [(2, 3), (1, 0)])
+    return [own, right, left, two, far]
+
+
+def collect(parts, members):
+    if members != 4:
+        return [parts[0]] + [shift_all(parts[s], members, s) for s in range(1, members)]
+    own, right, left, two, far = parts
+    far = lax.ppermute(far, "resp", [(3, 2), (0, 1)])
+    right, left = lax.ppermute(right, "resp", RIGHT), lax.ppermute(left, "resp", LEFT)
+    two = (two.astype(F32) + far.astype(F32)).astype(BF16)
+    return [own, right, left, shift_all(two, members, 2)]
 
 
 def cut_rows(block, count):
@@ -484,12 +523,12 @@
         a[0] for a in (queries, out_grad, resp_keys, resp_values)
     )
     cuts = cut(prompt_keys, prompt_values, pairs)
-    kinds = [Scattered(members, ranks, own_rows)]
-    kinds += [Gathered(members, ranks, own_rows) for _ in range(pairs - 1)]
+    kinds = [Scattered(members, ranks * own_rows)]
+    kinds += [Gathered(members, ranks * own_rows) for _ in range(pairs - 1)]
     own = jnp.concatenate(swap(cuts[0]), axis=1)
     if pairs > 1:
         own, cuts[1:] = lax.optimization_barrier((own, cuts[1:]))
-    caches = [[own] + [send(own, members, shift) for shift in range(1, members)]]
+    caches = [spread(own, members)]
     for p in range(1, pairs):
         own = jnp.concatenate(swap(cuts[p]), axis=1)
         own, caches[0] = lax.optimization_barrier((own, caches[0]))
@@ -515,9 +554,7 @@
         if isinstance(kinds[p], Scattered):
             totals.append(lax.psum_scatter(dcaches[0], "resp", scatter_dimension=0))
         else:
-            arrived = [dcaches[0]] + [
-                send(dcaches[shift], members, shift) for shift in range(1, members)
-            ]
+            arrived = collect(dcaches, members)
             totals.append(sum(block.astype(F32) for block in arrived).astype(BF16))
     blocks = [block for total in totals for block in swap(cut_rows(total, ranks))]
     key_grad, value_grad = place(blocks, pairs, columns)

time: 164 us -> 168 us (1.024)
  the two profiles are of different devices: /device:TPU:9 before, /device:TPU:0 now
where the time goes in v9:
time: 168 us; the launch traced here: 167 us
  Pallas kernels  82.3 us (49%)
  waiting for transfers between devices  33.3 us (20%)
  starting transfers between devices  29.4 us (18%)
  between operations  14.9 us (9%)
  other arithmetic  4.53 us (3%)
  local copies, waits for them, and re-layouts  2.95 us (2%)
    pallas_call x2, Pallas kernels, attend(): pl.pallas_call(functools.partial(attention_kernel, layout, heads_per, len...  78.2 us
    ppermute x2, waiting for transfers between devices, shift_all(): lax.ppermute(block, 'resp', [(m, (m + shift) % members) for m in range(me...  17.3 us
    ppermute x12, waiting for transfers between devices, swap(): lax.ppermute(blocks[i], 'tensor', [(j, j ^ i) for j in range(count)])  11.6 us
    ppermute x12, starting transfers between devices, swap(): lax.ppermute(blocks[i], 'tensor', [(j, j ^ i) for j in range(count)])  9.3 us
    ppermute x2, starting transfers between devices, shift_all(): lax.ppermute(block, 'resp', [(m, (m + shift) % members) for m in range(me...  5.8 us
    ppermute x1, starting transfers between devices, spread(): lax.ppermute(own, 'resp', RIGHT)  4.56 us
    ppermute x1, starting transfers between devices, collect(): far = lax.ppermute(far, 'resp', [(3, 2), (0, 1)])  4.53 us
    ppermute x1, waiting for transfers between devices, collect(): far = lax.ppermute(far, 'resp', [(3, 2), (0, 1)])  4.34 us
  transfers between devices with their start and end apart: 22, of which 10 were waited for; matrix products, arithmetic and copies ran while one was open for 4% of the time, Pallas kernels for 47%

profile of v9, /device:TPU:0, one launch (start us, length us, event | category | flops | bytes accessed | tf_op | source)
XLA Modules:
  0.0 167.4 jit_solution(13068857677307282030)
XLA Ops:
  7.2 0.0 all-gather.3.cloned.1.call-start
  7.2 1.9 %cut.1 = (bf16[2,128,128]{2,1,0:T(8,128)(2,1)}, bf16[2,128,128]{2,1,0:T(8,128)(2,1)}, bf16[2,128,128]{2,1,0:T(8,128)(2,1)}, bf16[2,128,128]{2,1,0:T(8,128)(2,1)}...) custom-call(bf16[128,1024]{1,0:T(8,128)(2,1)} %k_ref.1, ...), custom_call_target="tpu_custom_call" | custom-call | tf_op jit(solution)/shard_map/cut/pallas_call | solution.py:442
  9.2 0.5 collective-permute-start
  9.6 2.5 %collective-permute-start.1 = (bf16[2,128,128]{2,1,0:T(8,128)(2,1)}, bf16[2,128,128]{2,1,0:T(8,128)(2,1)S(1)}, u32[]{:S(2)}, u32[]{:S(2)}) collective-permute-start(bf16[2,128,128]{2,1,0:T(8,128)(2,1)} %get-tuple-element.49), channel_id=1, source_target_pairs={{0,2},{1,3},{2,0},{3,1},{4,6},{5,7},{6,4},{7,5},{8,10},{9,11},{10,... | collective-permute-start | bytes 196616 | tf_op jit(solution)/shard_map/ppermute | solution.py:478
  12.1 0.1 collective-permute-start.2
  12.2 0.0 collective-permute-done
  12.2 2.8 %collective-permute-done.1 = bf16[2,128,128]{2,1,0:T(8,128)(2,1)S(1)} collective-permute-done((bf16[2,128,128]{2,1,0:T(8,128)(2,1)}, bf16[2,128,128]{2,1,0:T(8,128)(2,1)S(1)}, u32[]{:S(2)}, u32[]{:S(2)}) %collective-permute-start.1) | collective-permute-done | bytes 65568 | tf_op jit(solution)/shard_map/ppermute | solution.py:478
  15.1 1.4 collective-permute-done.2
  16.5 0.9 pad_maximum_fusion.rest_0_
  17.3 0.0 copy-start
  17.3 2.7 %collective-permute-start.8 = (bf16[2,512,128]{2,1,0:T(8,128)(2,1)S(1)}, bf16[2,512,128]{2,1,0:T(8,128)(2,1)S(1)}, u32[]{:S(2)}, u32[]{:S(2)}) collective-permute-start(bf16[2,512,128]{2,1,0:T(8,128)(2,1)S(1)} %pad_maximum_fusion.rest_0_), channel_id=1, source_target_pairs={{0,8},{4,12},{8,0},{12,4},{1,9},{5,13},{9,1},{13,5},{2,10},{6,14},... | collective-permute-start | bytes 786440 | tf_op jit(solution)/shard_map/ppermute | solution.py:484
  20.0 1.3 collective-permute-start.7
  21.3 4.6 %collective-permute-start.6 = (bf16[2,512,128]{2,1,0:T(8,128)(2,1)S(1)}, bf16[2,512,128]{2,1,0:T(8,128)(2,1)S(1)}, u32[]{:S(2)}, u32[]{:S(2)}) collective-permute-start(bf16[2,512,128]{2,1,0:T(8,128)(2,1)S(1)} %pad_maximum_fusion.rest_0_), channel_id=1, source_target_pairs={{0,4},{4,8},{8,12},{1,5},{5,9},{9,13},{2,6},{6,10},{10,14},{3,7},{... | collective-permute-start | bytes 786440 | tf_op jit(solution)/shard_map/ppermute | solution.py:494
  25.9 7.3 %collective-permute-done.8.rest_3_ = bf16[2,512,128]{2,1,0:T(8,128)(2,1)S(1)} collective-permute-done((bf16[2,512,128]{2,1,0:T(8,128)(2,1)S(1)}, bf16[2,512,128]{2,1,0:T(8,128)(2,1)S(1)}, u32[]{:S(2)}, u32[]{:S(2)}) %collective-permute-start.8) | collective-permute-done | bytes 262176 | tf_op jit(solution)/shard_map/ppermute | solution.py:484
  33.1 1.3 collective-permute-start.9
  34.4 0.1 collective-permute-start.3
  34.5 1.4 collective-permute-start.4
  35.9 0.1 collective-permute-done.3
  35.9 1.1 collective-permute-start.5
  37.0 2.3 %collective-permute-done.4 = bf16[2,128,128]{2,1,0:T(8,128)(2,1)S(1)} collective-permute-done((bf16[2,128,128]{2,1,0:T(8,128)(2,1)}, bf16[2,128,128]{2,1,0:T(8,128)(2,1)S(1)}, u32[]{:S(2)}, u32[]{:S(2)}) %collective-permute-start.4) | collective-permute-done | bytes 65568 | tf_op jit(solution)/shard_map/ppermute | solution.py:478
  39.3 1.0 collective-permute-done.5
  40.3 1.6 pad_maximum_fusion.1
  41.9 0.0 collective-permute-done.7.rest_2_
  41.9 0.0 collective-permute-done.6.rest_1_
  41.9 0.0 copy-start.9
  41.9 0.0 collective-permute-done.9.rest_4_
  41.9 0.0 all-gather.3.cloned.1.call-update
  42.0 0.0 reduce-scatter.2.cloned.1.call-start
  42.7 0.0 copy-done.9
  42.7 0.1 copy-done.10
  42.8 38.7 %attend_pair_0.1 = (bf16[512,2048]{1,0:T(8,128)(2,1)}, bf16[512,2048]{1,0:T(8,128)(2,1)}, bf16[512,256]{1,0:T(8,128)(2,1)}, bf16[512,256]{1,0:T(8,128)(2,1)}, bf16[4,2,512,128]{3,2,1,0:T(8,128)(2,1)}) custom-call(s32[1]{0:T(128)S(6)} %copy.21.len_ref, bf16[512,2048]{1,0:T(8,128)(2,1)} %bitcast.11, bf16[512,2048]{1,0:T(8,128)(2,1)} %bitcast.13, ...), custom_call_target="tpu_custom_call" | custom-call | flops 16106127360 | bytes 4194304 | tf_op jit(solution)/shard_map/attend_pair_0/pallas_call | solution.py:376
  81.5 0.0 reduce-scatter.2.cloned.1.call-update
  81.6 0.0 all-gather.3.cloned.1.call-done
  81.6 39.5 %attend_pair_1.1 = (bf16[512,2048]{1,0:T(8,128)(2,1)}, bf16[512,2048]{1,0:T(8,128)(2,1)}, bf16[512,256]{1,0:T(8,128)(2,1)}, bf16[512,256]{1,0:T(8,128)(2,1)}, bf...) custom-call(s32[1]{0:T(128)S(6)} %copy.21.len_ref, ...), custom_call_target="tpu_custom_call", output_to_operand_aliasing={{0}: (6, {}), {1}: (7, {}), {2}: (8, {}), {3}: (9, {})} | custom-call | flops 16106127360 | bytes 4194304 | tf_op jit(solution)/shard_map/attend_pair_1/pallas_call | solution.py:376
  121.1 0.0 reduce-scatter.2.cloned.1.call-done
  121.1 4.5 %collective-permute-start.15 = (bf16[2,512,128]{2,1,0:T(8,128)(2,1)}, bf16[2,512,128]{2,1,0:T(8,128)(2,1)S(1)}, u32[]{:S(2)}, u32[]{:S(2)}) collective-permute-start(bf16[2,512,128]{2,1,0:T(8,128)(2,1)} %get-tuple-element.85), channel_id=1, source_target_pairs={{12,8},{0,4},{13,9},{1,5},{14,10},{2,6},{15,11},{3,7},{28,24},{16,... | collective-permute-start | bytes 786440 | tf_op jit(solution)/shard_map/ppermute | solution.py:503
  125.7 1.3 collective-permute-start.13
  127.0 1.3 collective-permute-start.14
  128.3 4.3 %collective-permute-done.15 = bf16[2,512,128]{2,1,0:T(8,128)(2,1)S(1)} collective-permute-done((bf16[2,512,128]{2,1,0:T(8,128)(2,1)}, bf16[2,512,128]{2,1,0:T(8,128)(2,1)S(1)}, u32[]{:S(2)}, u32[]{:S(2)}) %collective-permute-start.15) | collective-permute-done | bytes 262176 | tf_op jit(solution)/shard_map/ppermute | solution.py:503
  132.6 1.0 add_convert_fusion.1
  133.7 3.1 %collective-permute-start.16 = (bf16[2,512,128]{2,1,0:T(8,128)(2,1)S(1)}, bf16[2,512,128]{2,1,0:T(8,128)(2,1)S(1)}, u32[]{:S(2)}, u32[]{:S(2)}) collective-permute-start(bf16[2,512,128]{2,1,0:T(8,128)(2,1)S(1)} %add_convert_fusion.1), channel_id=1, source_target_pairs={{0,8},{4,12},{8,0},{12,4},{1,9},{5,13},{9,1},{13,5},{2,10},{6,14},... | collective-permute-start | bytes 786440 | tf_op jit(solution)/shard_map/ppermute | solution.py:484
  136.8 1.6 fusion.1
  138.4 0.0 collective-permute-start.12
  138.4 1.5 collective-permute-start.11
  139.9 0.0 collective-permute-done.13
  139.9 0.4 collective-permute-start.10
  140.2 0.0 collective-permute-done.14
  140.2 10.0 %collective-permute-done.16 = bf16[2,512,128]{2,1,0:T(8,128)(2,1)S(1)} collective-permute-done((bf16[2,512,128]{2,1,0:T(8,128)(2,1)S(1)}, bf16[2,512,128]{2,1,0:T(8,128)(2,1)S(1)}, u32[]{:S(2)}, u32[]{:S(2)}) %collective-permute-start.16) | collective-permute-done | bytes 262176 | tf_op jit(solution)/shard_map/ppermute | solution.py:484
  150.3 1.1 add_convert_fusion
  151.4 0.7 fusion
  152.0 0.0 collective-permute-start.19
  152.0 1.5 collective-permute-start.18
  153.5 0.0 collective-permute-done.12.refs_3_
  153.5 0.4 collective-permute-start.17
  153.9 0.0 collective-permute-done.11.refs_2_
  153.9 0.0 collective-permute-done.10.refs_1_
  153.9 0.0 copy-start.3
  153.9 2.5 %collective-permute-done.19.refs_7_ = bf16[2,128,128]{2,1,0:T(8,128)(2,1)S(1)} collective-permute-done((bf16[2,128,128]{2,1,0:T(8,128)(2,1)S(1)}, bf16[2,128,128]{2,1,0:T(8,128)(2,1)S(1)}, u32[]{:S(2)}, u32[]{:S(2)}) %collective-permute-start.19) | collective-permute-done | bytes 65568 | tf_op jit(solution)/shard_map/ppermute | solution.py:478
  156.4 1.4 collective-permute-done.18.refs_6_
  157.8 0.0 collective-permute-done.17.refs_5_
  157.8 0.0 copy-done.2
  157.9 0.6 copy-done.5
  158.4 0.0 copy-done.6
  158.5 2.1 %place.1 = (f32[128,1024]{1,0:T(8,128)}, f32[128,1024]{1,0:T(8,128)}) custom-call(bf16[2,128,128]{2,1,0:T(8,128)(2,1)} %get-tuple-element.95.refs_0_, bf16[2,128,128]{2,1,0:T(8,128)(2,1)} %copy-done.3, bf16[2,128,128]{2,1,0:T(8,128)(2,1)} %copy-done.2, bf16[2,128,128]{2,1,0:T(8,128)(2,1)} %copy-done.1, bf16[2,128,128]{2,1,0:T(8,128)(2,1)} %get-tuple-element.91.refs_4_, ...), custom_call_target="tpu_custom_call" | custom-call | tf_op jit(solution)/shard_map/place/pallas_call | solution.py:466
  (14 shorter events, 0.0 us)
Async XLA Ops:
  7.2 74.4 %all-gather.3.cloned.1.call-start = ((), (), s32[]{:S(2)}) async-start(), calls=%async_computation.2 | async-start | bytes 1310720 | tf_op jit(solution)/shard_map/all_gather | solution.py:535
  9.2 3.1 %collective-permute-start = (bf16[2,128,128]{2,1,0:T(8,128)(2,1)}, bf16[2,128,128]{2,1,0:T(8,128)(2,1)S(1)}, u32[]{:S(2)}, u32[]{:S(2)}) collective-permute-start(bf16[2,128,128]{2,1,0:T(8,128)(2,1)} %get-tuple-element.48), channel_id=1, source_target_pairs={{0,1},{1,0},{2,3},{3,2},{4,5},{5,4},{6,7},{7,6},{8,9},{9,8},{10,11... | collective-permute-start | bytes 196616 | tf_op jit(solution)/shard_map/ppermute | solution.py:478
  9.6 5.5 %collective-permute-start.1 = (bf16[2,128,128]{2,1,0:T(8,128)(2,1)}, bf16[2,128,128]{2,1,0:T(8,128)(2,1)S(1)}, u32[]{:S(2)}, u32[]{:S(2)}) collective-permute-start(bf16[2,128,128]{2,1,0:T(8,128)(2,1)} %get-tuple-element.49), channel_id=1, source_target_pairs={{0,2},{1,3},{2,0},{3,1},{4,6},{5,7},{6,4},{7,5},{8,10},{9,11},{10,... | collective-permute-start | bytes 196616 | tf_op jit(solution)/shard_map/ppermute | solution.py:478
  12.1 4.3 %collective-permute-start.2 = (bf16[2,128,128]{2,1,0:T(8,128)(2,1)}, bf16[2,128,128]{2,1,0:T(8,128)(2,1)S(1)}, u32[]{:S(2)}, u32[]{:S(2)}) collective-permute-start(bf16[2,128,128]{2,1,0:T(8,128)(2,1)} %get-tuple-element.50), channel_id=1, source_target_pairs={{0,3},{1,2},{2,1},{3,0},{4,7},{5,6},{6,5},{7,4},{8,11},{9,10},{10,... | collective-permute-start | bytes 196616 | tf_op jit(solution)/shard_map/ppermute | solution.py:478
  17.3 25.4 %copy-start = (bf16[2,512,128]{2,1,0:T(8,128)(2,1)}, bf16[2,512,128]{2,1,0:T(8,128)(2,1)S(1)}, u32[]{:S(2)}) copy-start(bf16[2,512,128]{2,1,0:T(8,128)(2,1)S(1)} %pad_maximum_fusion.rest_0_) | copy-start | bytes 786436
  17.3 15.8 %collective-permute-start.8 = (bf16[2,512,128]{2,1,0:T(8,128)(2,1)S(1)}, bf16[2,512,128]{2,1,0:T(8,128)(2,1)S(1)}, u32[]{:S(2)}, u32[]{:S(2)}) collective-permute-start(bf16[2,512,128]{2,1,0:T(8,128)(2,1)S(1)} %pad_maximum_fusion.rest_0_), channel_id=1, source_target_pairs={{0,8},{4,12},{8,0},{12,4},{1,9},{5,13},{9,1},{13,5},{2,10},{6,14},... | collective-permute-start | bytes 786440 | tf_op jit(solution)/shard_map/ppermute | solution.py:484
  20.0 21.9 %collective-permute-start.7 = (bf16[2,512,128]{2,1,0:T(8,128)(2,1)S(1)}, bf16[2,512,128]{2,1,0:T(8,128)(2,1)S(1)}, u32[]{:S(2)}, u32[]{:S(2)}) collective-permute-start(bf16[2,512,128]{2,1,0:T(8,128)(2,1)S(1)} %pad_maximum_fusion.rest_0_), channel_id=1, source_target_pairs={{4,0},{8,4},{12,8},{5,1},{9,5},{13,9},{6,2},{10,6},{14,10},{7,3},{... | collective-permute-start | bytes 786440 | tf_op jit(solution)/shard_map/ppermute | solution.py:494
  21.3 20.6 %collective-permute-start.6 = (bf16[2,512,128]{2,1,0:T(8,128)(2,1)S(1)}, bf16[2,512,128]{2,1,0:T(8,128)(2,1)S(1)}, u32[]{:S(2)}, u32[]{:S(2)}) collective-permute-start(bf16[2,512,128]{2,1,0:T(8,128)(2,1)S(1)} %pad_maximum_fusion.rest_0_), channel_id=1, source_target_pairs={{0,4},{4,8},{8,12},{1,5},{5,9},{9,13},{2,6},{6,10},{10,14},{3,7},{... | collective-permute-start | bytes 786440 | tf_op jit(solution)/shard_map/ppermute | solution.py:494
  33.1 9.6 %copy-start.7 = (bf16[2,512,128]{2,1,0:T(8,128)(2,1)}, bf16[2,512,128]{2,1,0:T(8,128)(2,1)S(1)}, u32[]{:S(2)}) copy-start(bf16[2,512,128]{2,1,0:T(8,128)(2,1)S(1)} %collective-permute-done.8.rest_3_) | copy-start | bytes 786436
  33.1 8.8 %collective-permute-start.9 = (bf16[2,512,128]{2,1,0:T(8,128)(2,1)S(1)}, bf16[2,512,128]{2,1,0:T(8,128)(2,1)S(1)}, u32[]{:S(2)}, u32[]{:S(2)}) collective-permute-start(bf16[2,512,128]{2,1,0:T(8,128)(2,1)S(1)} %collective-permute-done.8.rest_3_), channel_id=1, source_target_pairs={{8,12},{4,0},{9,13},{5,1},{10,14},{6,2},{11,15},{7,3},{24,28},{20,... | collective-permute-start | bytes 786440 | tf_op jit(solution)/shard_map/ppermute | solution.py:495
  34.4 1.5 collective-permute-start.3
  34.5 4.8 %collective-permute-start.4 = (bf16[2,128,128]{2,1,0:T(8,128)(2,1)}, bf16[2,128,128]{2,1,0:T(8,128)(2,1)S(1)}, u32[]{:S(2)}, u32[]{:S(2)}) collective-permute-start(bf16[2,128,128]{2,1,0:T(8,128)(2,1)} %get-tuple-element.57), channel_id=1, source_target_pairs={{0,2},{1,3},{2,0},{3,1},{4,6},{5,7},{6,4},{7,5},{8,10},{9,11},{10,... | collective-permute-start | bytes 196616 | tf_op jit(solution)/shard_map/ppermute | solution.py:478
  35.9 4.4 %collective-permute-start.5 = (bf16[2,128,128]{2,1,0:T(8,128)(2,1)}, bf16[2,128,128]{2,1,0:T(8,128)(2,1)S(1)}, u32[]{:S(2)}, u32[]{:S(2)}) collective-permute-start(bf16[2,128,128]{2,1,0:T(8,128)(2,1)} %get-tuple-element.58), channel_id=1, source_target_pairs={{0,3},{1,2},{2,1},{3,0},{4,7},{5,6},{6,5},{7,4},{8,11},{9,10},{10,... | collective-permute-start | bytes 196616 | tf_op jit(solution)/shard_map/ppermute | solution.py:478
  41.9 0.8 copy-start.8
  41.9 0.8 copy-start.9
  41.9 0.9 copy-start.10
  42.0 79.2 %reduce-scatter.2.cloned.1.call-start = ((), (), s32[]{:S(2)}) async-start(), calls=%async_computation.1 | async-start | bytes 1310720 | tf_op jit(solution)/shard_map/reduce_scatter | solution.py:555
  121.1 11.5 %collective-permute-start.15 = (bf16[2,512,128]{2,1,0:T(8,128)(2,1)}, bf16[2,512,128]{2,1,0:T(8,128)(2,1)S(1)}, u32[]{:S(2)}, u32[]{:S(2)}) collective-permute-start(bf16[2,512,128]{2,1,0:T(8,128)(2,1)} %get-tuple-element.85), channel_id=1, source_target_pairs={{12,8},{0,4},{13,9},{1,5},{14,10},{2,6},{15,11},{3,7},{28,24},{16,... | collective-permute-start | bytes 786440 | tf_op jit(solution)/shard_map/ppermute | solution.py:503
  125.7 14.2 %collective-permute-start.13 = (bf16[2,512,128]{2,1,0:T(8,128)(2,1)}, bf16[2,512,128]{2,1,0:T(8,128)(2,1)S(1)}, u32[]{:S(2)}, u32[]{:S(2)}) collective-permute-start(bf16[2,512,128]{2,1,0:T(8,128)(2,1)} %get-tuple-element.82), channel_id=1, source_target_pairs={{0,4},{4,8},{8,12},{1,5},{5,9},{9,13},{2,6},{6,10},{10,14},{3,7},{... | collective-permute-start | bytes 786440 | tf_op jit(solution)/shard_map/ppermute | solution.py:504
  127.0 13.3 %collective-permute-start.14 = (bf16[2,512,128]{2,1,0:T(8,128)(2,1)}, bf16[2,512,128]{2,1,0:T(8,128)(2,1)S(1)}, u32[]{:S(2)}, u32[]{:S(2)}) collective-permute-start(bf16[2,512,128]{2,1,0:T(8,128)(2,1)} %get-tuple-element.83), channel_id=1, source_target_pairs={{4,0},{8,4},{12,8},{5,1},{9,5},{13,9},{6,2},{10,6},{14,10},{7,3},{... | collective-permute-start | bytes 786440 | tf_op jit(solution)/shard_map/ppermute | solution.py:504
  133.7 16.6 %collective-permute-start.16 = (bf16[2,512,128]{2,1,0:T(8,128)(2,1)S(1)}, bf16[2,512,128]{2,1,0:T(8,128)(2,1)S(1)}, u32[]{:S(2)}, u32[]{:S(2)}) collective-permute-start(bf16[2,512,128]{2,1,0:T(8,128)(2,1)S(1)} %add_convert_fusion.1), channel_id=1, source_target_pairs={{0,8},{4,12},{8,0},{12,4},{1,9},{5,13},{9,1},{13,5},{2,10},{6,14},... | collective-permute-start | bytes 786440 | tf_op jit(solution)/shard_map/ppermute | solution.py:484
  138.4 15.2 %collective-permute-start.12 = (bf16[2,128,128]{2,1,0:T(8,128)(2,1)S(1)}, bf16[2,128,128]{2,1,0:T(8,128)(2,1)S(1)}, u32[]{:S(2)}, u32[]{:S(2)}) collective-permute-start(bf16[2,128,128]{2,1,0:T(8,128)(2,1)S(1)} %get-tuple-element.92), channel_id=1, source_target_pairs={{0,3},{1,2},{2,1},{3,0},{4,7},{5,6},{6,5},{7,4},{8,11},{9,10},{10,... | collective-permute-start | bytes 196616 | tf_op jit(solution)/shard_map/ppermute | solution.py:478
  138.4 15.5 %collective-permute-start.11 = (bf16[2,128,128]{2,1,0:T(8,128)(2,1)S(1)}, bf16[2,128,128]{2,1,0:T(8,128)(2,1)S(1)}, u32[]{:S(2)}, u32[]{:S(2)}) collective-permute-start(bf16[2,128,128]{2,1,0:T(8,128)(2,1)S(1)} %get-tuple-element.93), channel_id=1, source_target_pairs={{0,2},{1,3},{2,0},{3,1},{4,6},{5,7},{6,4},{7,5},{8,10},{9,11},{10,... | collective-permute-start | bytes 196616 | tf_op jit(solution)/shard_map/ppermute | solution.py:478
  139.9 14.0 %collective-permute-start.10 = (bf16[2,128,128]{2,1,0:T(8,128)(2,1)S(1)}, bf16[2,128,128]{2,1,0:T(8,128)(2,1)S(1)}, u32[]{:S(2)}, u32[]{:S(2)}) collective-permute-start(bf16[2,128,128]{2,1,0:T(8,128)(2,1)S(1)} %get-tuple-element.94), channel_id=1, source_target_pairs={{0,1},{1,0},{2,3},{3,2},{4,5},{5,4},{6,7},{7,6},{8,9},{9,8},{10,11... | collective-permute-start | bytes 196616 | tf_op jit(solution)/shard_map/ppermute | solution.py:478
  152.0 4.4 %collective-permute-start.19 = (bf16[2,128,128]{2,1,0:T(8,128)(2,1)S(1)}, bf16[2,128,128]{2,1,0:T(8,128)(2,1)S(1)}, u32[]{:S(2)}, u32[]{:S(2)}) collective-permute-start(bf16[2,128,128]{2,1,0:T(8,128)(2,1)S(1)} %get-tuple-element.88), channel_id=1, source_target_pairs={{0,3},{1,2},{2,1},{3,0},{4,7},{5,6},{6,5},{7,4},{8,11},{9,10},{10,... | collective-permute-start | bytes 196616 | tf_op jit(solution)/shard_map/ppermute | solution.py:478
  152.0 5.8 %collective-permute-start.18 = (bf16[2,128,128]{2,1,0:T(8,128)(2,1)S(1)}, bf16[2,128,128]{2,1,0:T(8,128)(2,1)S(1)}, u32[]{:S(2)}, u32[]{:S(2)}) collective-permute-start(bf16[2,128,128]{2,1,0:T(8,128)(2,1)S(1)} %get-tuple-element.89), channel_id=1, source_target_pairs={{0,2},{1,3},{2,0},{3,1},{4,6},{5,7},{6,4},{7,5},{8,10},{9,11},{10,... | collective-permute-start | bytes 196616 | tf_op jit(solution)/shard_map/ppermute | solution.py:478
  153.5 4.3 %copy-start.1 = (bf16[2,128,128]{2,1,0:T(8,128)(2,1)}, bf16[2,128,128]{2,1,0:T(8,128)(2,1)S(1)}, u32[]{:S(2)}) copy-start(bf16[2,128,128]{2,1,0:T(8,128)(2,1)S(1)} %collective-permute-done.12.refs_3_) | copy-start | bytes 196612
  153.5 4.3 %collective-permute-start.17 = (bf16[2,128,128]{2,1,0:T(8,128)(2,1)S(1)}, bf16[2,128,128]{2,1,0:T(8,128)(2,1)S(1)}, u32[]{:S(2)}, u32[]{:S(2)}) collective-permute-start(bf16[2,128,128]{2,1,0:T(8,128)(2,1)S(1)} %get-tuple-element.90), channel_id=1, source_target_pairs={{0,1},{1,0},{2,3},{3,2},{4,5},{5,4},{6,7},{7,6},{8,9},{9,8},{10,11... | collective-permute-start | bytes 196616 | tf_op jit(solution)/shard_map/ppermute | solution.py:478
  153.9 3.9 %copy-start.2 = (bf16[2,128,128]{2,1,0:T(8,128)(2,1)}, bf16[2,128,128]{2,1,0:T(8,128)(2,1)S(1)}, u32[]{:S(2)}) copy-start(bf16[2,128,128]{2,1,0:T(8,128)(2,1)S(1)} %collective-permute-done.11.refs_2_) | copy-start | bytes 196612
  153.9 3.9 %copy-start.3 = (bf16[2,128,128]{2,1,0:T(8,128)(2,1)}, bf16[2,128,128]{2,1,0:T(8,128)(2,1)S(1)}, u32[]{:S(2)}) copy-start(bf16[2,128,128]{2,1,0:T(8,128)(2,1)S(1)} %collective-permute-done.10.refs_1_) | copy-start | bytes 196612
  156.4 1.5 copy-start.4
  157.8 0.6 copy-start.5
  157.8 0.6 copy-start.6
Sparse Core Ops, SparseCore 0:
  42.1 29.5 all-gather.2
  81.7 28.6 reduce-scatter.1

commit v10 on v7

--- a/solution.py
+++ b/solution.py
@@ -14,6 +14,10 @@
 LOWEST = -1e30
 BF16 = jnp.bfloat16
 F32 = jnp.float32
+
+
+def dot_last(a, b):
+    return lax.dot_general(a, b, (((1,), (1,)), ((), ())), preferred_element_type=F32)
 
 
 def dot(a, b):
@@ -166,19 +170,15 @@
     def grad_products(before, piece):
         at, size, row = pieces[piece]
 
-        def value_product(u):
-            at = slice(u, u + WIDE)
-            dv_sum[at, :] += dot(weights[before][at, row:], grad[before, row:, :])
-
-        def key_product(u):
-            at = slice(u, u + WIDE)
-            dk_sum[at, :] += dot(sgrads[at, row:], query[before, row:, :])
-
-        return [
-            functools.partial(product, u)
-            for u in range(at, at + size, WIDE)
-            for product in (value_product, key_product)
-        ]
+        key_at = slice(at, at + size)
+
+        def value_product():
+            dv_sum[:, key_at] += dot_last(grad_t[before, :, row:], weights[before][key_at, row:])
+
+        def key_product():
+            dk_sum[:, key_at] += dot_last(query_t[before, :, row:], sgrads[key_at, row:])
+
+        return [value_product, key_product]
 
     def query_products():
         def product(r):
@@ -274,22 +274,22 @@
         run(heads_per % 2, False, True)
         layout.store(dcaches, dk_sum, dv_sum, factor)
         at = pl.ds(prompt_rows, rows)
-        dkr_ref[...] = (factor * dk_sum[at, :]).astype(BF16)
-        dvr_ref[...] = dv_sum[at, :].astype(BF16)
+        dkr_ref[...] = (factor * dk_sum[:, at]).T.astype(BF16)
+        dvr_ref[...] = dv_sum[:, at].T.astype(BF16)
 
 
 class Gathered:
-    def __init__(self, members, ranks, own_rows):
-        self.members, self.part_rows = members, ranks * own_rows
-        self.prompt_rows = members * self.part_rows
-        self.caches = 1
-        self.dcaches = members
+    def __init__(self, members, part_rows):
+        self.members, self.part_rows = members, part_rows
+        self.prompt_rows = members * part_rows
+        self.caches, self.dcaches = 1, members + 1
 
     def cache_shapes(self):
         return [(self.members, 2, self.part_rows, HD)]
 
     def dcache_shapes(self):
-        return [(2, self.part_rows, HD)] * self.dcaches
+        part = (self.part_rows, HD)
+        return [part] * self.members + [(self.members, *part)]
 
     def load(self, caches):
         for m in range(self.members):
@@ -301,32 +301,35 @@
         for shift in range(self.members):
             part = lax.rem(me + shift, self.members) * self.part_rows
             at = pl.ds(pl.multiple_of(part, self.part_rows), self.part_rows)
-            dcaches[shift][0] = (factor * dk_sum[at, :]).astype(BF16)
-            dcaches[shift][1] = dv_sum[at, :].astype(BF16)
+            dcaches[shift][...] = (factor * dk_sum[:, at]).T.astype(BF16)
+            at = pl.ds(shift * self.part_rows, self.part_rows)
+            dcaches[self.members][shift] = dv_sum[:, at].T.astype(BF16)
 
 
 class Scattered(Gathered):
-    def __init__(self, members, ranks, own_rows):
-        super().__init__(members, ranks, own_rows)
+    def __init__(self, members, part_rows):
+        super().__init__(members, part_rows)
         self.caches, self.dcaches = self.dcaches, self.caches
 
     def cache_shapes(self):
-        return [(2, self.part_rows, HD)] * self.caches
+        return super().dcache_shapes()
 
     def dcache_shapes(self):
-        return [(self.members, 2, self.part_rows, HD)]
+        return super().cache_shapes()
+
+    def part(self, shift):
+        return lax.rem(lax.axis_index("resp") - shift + self.members, self.members)
 
     def load(self, caches):
-        for i, ref in enumerate(caches):
-            yield pl.ds(i * self.part_rows, self.part_rows), ref[0], ref[1]
+        for shift in range(self.members):
+            at = pl.ds(shift * self.part_rows, self.part_rows)
+            yield at, caches[shift][...], caches[self.members][self.part(shift)]
 
     def store(self, dcaches, dk_sum, dv_sum, factor):
-        me = lax.axis_index("resp")
         for shift in range(self.members):
-            part = lax.rem(me - shift + self.members, self.members)
             at = pl.ds(shift * self.part_rows, self.part_rows)
-            dcaches[0][part, 0] = (factor * dk_sum[at, :]).astype(BF16)
-            dcaches[0][part, 1] = dv_sum[at, :].astype(BF16)
+            dcaches[0][self.part(shift), 0] = (factor * dk_sum[:, at]).T.astype(BF16)
+            dcaches[0][self.part(shift), 1] = dv_sum[:, at].T.astype(BF16)
 
 
 def attend(
@@ -388,8 +391,8 @@
             pltpu.VMEM((rows, rows), F32),
             pltpu.VMEM((2, stats, rows), F32),
             pltpu.VMEM((2, 8, rows), F32),
-            pltpu.VMEM((total_rows, HD), F32),
-            pltpu.VMEM((total_rows, HD), F32),
+            pltpu.VMEM((HD, total_rows), F32),
+            pltpu.VMEM((HD, total_rows), F32),
             pltpu.VMEM((stats, rows), F32),
             pltpu.VMEM((stats, rows), F32),
             pltpu.VMEM((HD, rows), F32),
@@ -484,12 +487,14 @@
         a[0] for a in (queries, out_grad, resp_keys, resp_values)
     )
     cuts = cut(prompt_keys, prompt_values, pairs)
-    kinds = [Scattered(members, ranks, own_rows)]
-    kinds += [Gathered(members, ranks, own_rows) for _ in range(pairs - 1)]
-    own = jnp.concatenate(swap(cuts[0]), axis=1)
+    kinds = [Scattered(members, ranks * own_rows)]
+    kinds += [Gathered(members, ranks * own_rows) for _ in range(pairs - 1)]
+    swapped = swap(cuts[0])
+    key, value = (jnp.concatenate([block[i] for block in swapped], axis=0) for i in range(2))
     if pairs > 1:
-        own, cuts[1:] = lax.optimization_barrier((own, cuts[1:]))
-    caches = [[own] + [send(own, members, shift) for shift in range(1, members)]]
+        key, value, cuts[1:] = lax.optimization_barrier((key, value, cuts[1:]))
+    caches = [[key] + [send(key, members, shift) for shift in range(1, members)]]
+    caches[0].append(lax.all_gather(value, "resp", axis=0))
     for p in range(1, pairs):
         own = jnp.concatenate(swap(cuts[p]), axis=1)
         own, caches[0] = lax.optimization_barrier((own, caches[0]))
@@ -518,7 +523,9 @@
             arrived = [dcaches[0]] + [
                 send(dcaches[shift], members, shift) for shift in range(1, members)
             ]
-            totals.append(sum(block.astype(F32) for block in arrived).astype(BF16))
+            dkey = sum(block.astype(F32) for block in arrived).astype(BF16)
+            dvalue = lax.psum_scatter(dcaches[members], "resp", scatter_dimension=0)
+            totals.append(jnp.stack([dkey, dvalue]))
     blocks = [block for total in totals for block in swap(cut_rows(total, ranks))]
     key_grad, value_grad = place(blocks, pairs, columns)
     return (*(a[None] for a in earlier), key_grad, value_grad)

time: 164 us -> 165 us (level)
  the two profiles are of different devices: /device:TPU:9 before, /device:TPU:0 now
where the time goes in v10:
time: 165 us
  Pallas kernels  83.2 us (50%)
  blocking collectives  22.5 us (14%)
  waiting for transfers between devices  20.7 us (13%)
  starting transfers between devices  16.8 us (10%)
  between operations  14.6 us (9%)
  other arithmetic  4.01 us (2%)
  local copies, waits for them, and re-layouts  3.02 us (2%)
    pallas_call x2, Pallas kernels, attend(): pl.pallas_call(functools.partial(attention_kernel, layout, heads_per, len...  79.1 us
    all_gather x1, blocking collectives, per_device(): caches[0].append(lax.all_gather(value, 'resp', axis=0))  22.5 us
    ppermute x6, starting transfers between devices, send(): lax.ppermute(block, 'resp', [(m, (m + shift) % members) for m in range(me...  8.52 us
    ppermute x12, starting transfers between devices, swap(): lax.ppermute(blocks[i], 'tensor', [(j, j ^ i) for j in range(count)])  8.12 us
    ppermute x6, waiting for transfers between devices, send(): lax.ppermute(block, 'resp', [(m, (m + shift) % members) for m in range(me...  7.24 us
    ppermute x12, waiting for transfers between devices, swap(): lax.ppermute(blocks[i], 'tensor', [(j, j ^ i) for j in range(count)])  6.94 us
    reduce_scatter x1, waiting for transfers between devices, per_device(): dvalue = lax.psum_scatter(dcaches[members], 'resp', scatter_dimension=0)  6.46 us
  transfers between devices with their start and end apart: 21, of which 7 were waited for; matrix products, arithmetic and copies ran while one was open for 4% of the time, Pallas kernels for 48%

profile of v10, /device:TPU:0, one launch (start us, length us, event | category | flops | bytes accessed | tf_op | source)
XLA Modules:
  0.0 164.7 jit_solution(4213248630382486044)
XLA Ops:
  7.2 0.0 all-gather.4.cloned.1.call-start
  7.2 1.9 %cut.1 = (bf16[2,128,128]{2,1,0:T(8,128)(2,1)}, bf16[2,128,128]{2,1,0:T(8,128)(2,1)}, bf16[2,128,128]{2,1,0:T(8,128)(2,1)}, bf16[2,128,128]{2,1,0:T(8,128)(2,1)}...) custom-call(bf16[128,1024]{1,0:T(8,128)(2,1)} %k_ref.1, ...), custom_call_target="tpu_custom_call" | custom-call | tf_op jit(solution)/shard_map/cut/pallas_call | solution.py:428
  9.1 0.5 collective-permute-start
  9.6 2.5 %collective-permute-start.1 = (bf16[2,128,128]{2,1,0:T(8,128)(2,1)}, bf16[2,128,128]{2,1,0:T(8,128)(2,1)S(1)}, u32[]{:S(2)}, u32[]{:S(2)}) collective-permute-start(bf16[2,128,128]{2,1,0:T(8,128)(2,1)} %get-tuple-element.50), channel_id=1, source_target_pairs={{0,2},{1,3},{2,0},{3,1},{4,6},{5,7},{6,4},{7,5},{8,10},{9,11},{10,... | collective-permute-start | bytes 196616 | tf_op jit(solution)/shard_map/ppermute | solution.py:464
  12.1 0.1 collective-permute-start.2
  12.2 0.8 slice_bitcast_fusion.6
  13.0 0.0 collective-permute-done
  13.0 2.0 %collective-permute-done.1 = bf16[2,128,128]{2,1,0:T(8,128)(2,1)S(1)} collective-permute-done((bf16[2,128,128]{2,1,0:T(8,128)(2,1)}, bf16[2,128,128]{2,1,0:T(8,128)(2,1)S(1)}, u32[]{:S(2)}, u32[]{:S(2)}) %collective-permute-start.1) | collective-permute-done | bytes 65568 | tf_op jit(solution)/shard_map/ppermute | solution.py:464
  15.1 1.4 collective-permute-done.2
  16.5 0.0 copy-start
  16.5 0.2 collective-permute-start.3
  16.7 3.6 %collective-permute-start.8 = (bf16[512,128]{1,0:T(8,128)(2,1)S(1)}, bf16[512,128]{1,0:T(8,128)(2,1)S(1)}, u32[]{:S(2)}, u32[]{:S(2)}) collective-permute-start(bf16[512,128]{1,0:T(8,128)(2,1)S(1)} %get-tuple-element.63.rest_0_), channel_id=1, source_target_pairs={{0,12},{4,0},{8,4},{12,8},{1,13},{5,1},{9,5},{13,9},{2,14},{6,2},{... | collective-permute-start | bytes 393224 | tf_op jit(solution)/shard_map/ppermute | solution.py:470
  20.3 0.0 collective-permute-start.7
  20.3 1.0 collective-permute-start.6
  21.3 1.4 collective-permute-start.4
  22.8 0.0 collective-permute-done.3
  22.8 0.0 collective-permute-start.5
  22.8 22.5 %all-gather = bf16[2048,128]{1,0:T(8,128)(2,1)} all-gather(bf16[512,128]{1,0:T(8,128)(2,1)S(1)} %get-tuple-element.61), channel_id=2, replica_groups=mesh['group'=2,'resp'=4,'tensor'=4] {'resp'}, dimensions={0}, use_global_device_ids=true | all-gather | bytes 655360 | tf_op jit(solution)/shard_map/all_gather | solution.py:497
  45.2 0.0 collective-permute-done.4
  45.2 0.0 collective-permute-done.5
  45.2 1.6 pad_maximum_fusion
  46.8 0.0 collective-permute-done.8.rest_3_
  46.8 0.0 collective-permute-done.7.rest_2_
  46.8 0.0 copy-start.8
  46.8 0.0 collective-permute-done.6.rest_1_
  46.8 0.0 copy-start.9
  46.8 0.0 all-gather.4.cloned.1.call-update
  46.9 0.0 reduce-scatter.3.cloned.1.call-start
  47.6 0.0 copy-done
  47.6 0.0 copy-done.7
  47.6 39.4 %attend_pair_0.1 = (bf16[512,2048]{1,0:T(8,128)(2,1)}, bf16[512,2048]{1,0:T(8,128)(2,1)}, bf16[512,256]{1,0:T(8,128)(2,1)}, bf16[512,256]{1,0:T(8,128)(2,1)}, bf16[4,2,512,128]{3,2,1,0:T(8,128)(2,1)}) custom-call(s32[1]{0:T(128)S(6)} %copy.21.len_ref, bf16[512,2048]{1,0:T(8,128)(2,1)} %bitcast.31, bf16[512,2048]{1,0:T(8,128)(2,1)} %bitcast.33, ...), custom_call_target="tpu_custom_call" | custom-call | flops 16106127360 | bytes 4194304 | tf_op jit(solution)/shard_map/attend_pair_0/pallas_call | solution.py:362
  87.0 0.0 reduce-scatter.3.cloned.1.call-update
  87.0 0.0 reduce-scatter.5.cloned.1.call-start
  87.1 0.0 all-gather.4.cloned.1.call-done
  87.1 39.8 %attend_pair_1.1 = (bf16[512,2048]{1,0:T(8,128)(2,1)}, bf16[512,2048]{1,0:T(8,128)(2,1)}, bf16[512,256]{1,0:T(8,128)(2,1)}, bf16[512,256]{1,0:T(8,128)(2,1)}, bf...) custom-call(s32[1]{0:T(128)S(6)} %copy.21.len_ref, ...), custom_call_target="tpu_custom_call", output_to_operand_aliasing={{0}: (6, {}), {1}: (7, {}), {2}: (8, {}), {3}: (9, {})} | custom-call | flops 16106127360 | bytes 4194304 | tf_op jit(solution)/shard_map/attend_pair_1/pallas_call | solution.py:362
  126.8 0.0 reduce-scatter.3.cloned.1.call-done
  126.9 0.0 reduce-scatter.5.cloned.1.call-update
  126.9 0.1 collective-permute-start.12
  127.0 0.8 collective-permute-start.13
  127.8 3.0 %collective-permute-start.14 = (bf16[512,128]{1,0:T(8,128)(2,1)}, bf16[512,128]{1,0:T(8,128)(2,1)S(1)}, u32[]{:S(2)}, u32[]{:S(2)}) collective-permute-start(bf16[512,128]{1,0:T(8,128)(2,1)} %get-tuple-element.86), channel_id=1, source_target_pairs={{0,12},{4,0},{8,4},{12,8},{1,13},{5,1},{9,5},{13,9},{2,14},{6,2},{... | collective-permute-start | bytes 393224 | tf_op jit(solution)/shard_map/ppermute | solution.py:470
  130.8 1.6 fusion.4
  132.4 0.0 collective-permute-start.11
  132.4 1.3 collective-permute-start.10
  133.7 0.8 collective-permute-done.12
  134.5 0.0 collective-permute-start.9
  134.5 6.4 %collective-permute-done.13 = bf16[512,128]{1,0:T(8,128)(2,1)S(1)} collective-permute-done((bf16[512,128]{1,0:T(8,128)(2,1)}, bf16[512,128]{1,0:T(8,128)(2,1)S(1)}, u32[]{:S(2)}, u32[]{:S(2)}) %collective-permute-start.13) | collective-permute-done | bytes 131104 | tf_op jit(solution)/shard_map/ppermute | solution.py:470
  140.9 0.0 collective-permute-done.14
  140.9 1.0 fusion
  141.9 6.5 %reduce-scatter.5.cloned.1.call-done = bf16[1,512,128]{2,1,0:T(8,128)(2,1)} async-done(((bf16[4,512,128]{2,1,0:T(8,128)(2,1)}), bf16[1,512,128]{2,1,0:T(8,128)(2,1)}) %reduce-scatter.5.cloned.1.call-update) | async-done | bytes 131088 | tf_op jit(solution)/shard_map/reduce_scatter | solution.py:527
  148.4 1.4 pad_maximum_fusion.3
  149.8 0.2 collective-permute-start.17
  150.0 1.2 collective-permute-start.15
  151.2 0.0 collective-permute-done.11.refs_3_
  151.2 0.7 collective-permute-start.16
  151.9 0.0 collective-permute-done.10.refs_2_
  152.0 0.0 collective-permute-done.9.refs_1_
  152.0 2.1 %collective-permute-done.17.refs_7_ = bf16[2,128,128]{2,1,0:T(8,128)(2,1)S(1)} collective-permute-done((bf16[2,128,128]{2,1,0:T(8,128)(2,1)S(1)}, bf16[2,128,128]{2,1,0:T(8,128)(2,1)S(1)}, u32[]{:S(2)}, u32[]{:S(2)}) %collective-permute-start.17) | collective-permute-done | bytes 65568 | tf_op jit(solution)/shard_map/ppermute | solution.py:464
  154.0 0.0 collective-permute-done.15.refs_5_
  154.0 1.4 collective-permute-done.16.refs_6_
  155.5 0.0 copy-done.2
  155.5 0.0 copy-done.4
  155.5 0.0 copy-done.5
  155.5 0.6 copy-done.6
  156.1 2.1 %place.1 = (f32[128,1024]{1,0:T(8,128)}, f32[128,1024]{1,0:T(8,128)}) custom-call(bf16[2,128,128]{2,1,0:T(8,128)(2,1)} %get-tuple-element.97.refs_0_, bf16[2,128,128]{2,1,0:T(8,128)(2,1)} %copy-done.3, bf16[2,128,128]{2,1,0:T(8,128)(2,1)} %copy-done.2, bf16[2,128,128]{2,1,0:T(8,128)(2,1)} %copy-done.1, bf16[2,128,128]{2,1,0:T(8,128)(2,1)} %get-tuple-element.91.refs_4_, ...), custom_call_target="tpu_custom_call" | custom-call | tf_op jit(solution)/shard_map/place/pallas_call | solution.py:452
  (15 shorter events, 0.1 us)
Async XLA Ops:
  7.2 79.9 %all-gather.4.cloned.1.call-start = ((), (), s32[]{:S(2)}) async-start(), calls=%async_computation.4 | async-start | bytes 1310720 | tf_op jit(solution)/shard_map/all_gather | solution.py:501
  9.1 3.9 %collective-permute-start = (bf16[2,128,128]{2,1,0:T(8,128)(2,1)}, bf16[2,128,128]{2,1,0:T(8,128)(2,1)S(1)}, u32[]{:S(2)}, u32[]{:S(2)}) collective-permute-start(bf16[2,128,128]{2,1,0:T(8,128)(2,1)} %get-tuple-element.49), channel_id=1, source_target_pairs={{0,1},{1,0},{2,3},{3,2},{4,5},{5,4},{6,7},{7,6},{8,9},{9,8},{10,11... | collective-permute-start | bytes 196616 | tf_op jit(solution)/shard_map/ppermute | solution.py:464
  9.6 5.5 %collective-permute-start.1 = (bf16[2,128,128]{2,1,0:T(8,128)(2,1)}, bf16[2,128,128]{2,1,0:T(8,128)(2,1)S(1)}, u32[]{:S(2)}, u32[]{:S(2)}) collective-permute-start(bf16[2,128,128]{2,1,0:T(8,128)(2,1)} %get-tuple-element.50), channel_id=1, source_target_pairs={{0,2},{1,3},{2,0},{3,1},{4,6},{5,7},{6,4},{7,5},{8,10},{9,11},{10,... | collective-permute-start | bytes 196616 | tf_op jit(solution)/shard_map/ppermute | solution.py:464
  12.1 4.3 %collective-permute-start.2 = (bf16[2,128,128]{2,1,0:T(8,128)(2,1)}, bf16[2,128,128]{2,1,0:T(8,128)(2,1)S(1)}, u32[]{:S(2)}, u32[]{:S(2)}) collective-permute-start(bf16[2,128,128]{2,1,0:T(8,128)(2,1)} %get-tuple-element.51), channel_id=1, source_target_pairs={{0,3},{1,2},{2,1},{3,0},{4,7},{5,6},{6,5},{7,4},{8,11},{9,10},{10,... | collective-permute-start | bytes 196616 | tf_op jit(solution)/shard_map/ppermute | solution.py:464
  16.5 31.1 %copy-start = (bf16[512,128]{1,0:T(8,128)(2,1)}, bf16[512,128]{1,0:T(8,128)(2,1)S(1)}, u32[]{:S(2)}) copy-start(bf16[512,128]{1,0:T(8,128)(2,1)S(1)} %get-tuple-element.63.rest_0_) | copy-start | bytes 393220
  16.5 6.2 %collective-permute-start.3 = (bf16[2,128,128]{2,1,0:T(8,128)(2,1)}, bf16[2,128,128]{2,1,0:T(8,128)(2,1)S(1)}, u32[]{:S(2)}, u32[]{:S(2)}) collective-permute-start(bf16[2,128,128]{2,1,0:T(8,128)(2,1)} %get-tuple-element.57), channel_id=1, source_target_pairs={{0,1},{1,0},{2,3},{3,2},{4,5},{5,4},{6,7},{7,6},{8,9},{9,8},{10,11... | collective-permute-start | bytes 196616 | tf_op jit(solution)/shard_map/ppermute | solution.py:464
  16.7 30.1 %collective-permute-start.8 = (bf16[512,128]{1,0:T(8,128)(2,1)S(1)}, bf16[512,128]{1,0:T(8,128)(2,1)S(1)}, u32[]{:S(2)}, u32[]{:S(2)}) collective-permute-start(bf16[512,128]{1,0:T(8,128)(2,1)S(1)} %get-tuple-element.63.rest_0_), channel_id=1, source_target_pairs={{0,12},{4,0},{8,4},{12,8},{1,13},{5,1},{9,5},{13,9},{2,14},{6,2},{... | collective-permute-start | bytes 393224 | tf_op jit(solution)/shard_map/ppermute | solution.py:470
  20.3 26.5 %collective-permute-start.7 = (bf16[512,128]{1,0:T(8,128)(2,1)S(1)}, bf16[512,128]{1,0:T(8,128)(2,1)S(1)}, u32[]{:S(2)}, u32[]{:S(2)}) collective-permute-start(bf16[512,128]{1,0:T(8,128)(2,1)S(1)} %get-tuple-element.63.rest_0_), channel_id=1, source_target_pairs={{0,8},{4,12},{8,0},{12,4},{1,9},{5,13},{9,1},{13,5},{2,10},{6,14},... | collective-permute-start | bytes 393224 | tf_op jit(solution)/shard_map/ppermute | solution.py:470
  20.3 26.5 %collective-permute-start.6 = (bf16[512,128]{1,0:T(8,128)(2,1)S(1)}, bf16[512,128]{1,0:T(8,128)(2,1)S(1)}, u32[]{:S(2)}, u32[]{:S(2)}) collective-permute-start(bf16[512,128]{1,0:T(8,128)(2,1)S(1)} %get-tuple-element.63.rest_0_), channel_id=1, source_target_pairs={{0,4},{4,8},{8,12},{12,0},{1,5},{5,9},{9,13},{13,1},{2,6},{6,10},{... | collective-permute-start | bytes 393224 | tf_op jit(solution)/shard_map/ppermute | solution.py:470
  21.3 23.9 %collective-permute-start.4 = (bf16[2,128,128]{2,1,0:T(8,128)(2,1)}, bf16[2,128,128]{2,1,0:T(8,128)(2,1)S(1)}, u32[]{:S(2)}, u32[]{:S(2)}) collective-permute-start(bf16[2,128,128]{2,1,0:T(8,128)(2,1)} %get-tuple-element.58), channel_id=1, source_target_pairs={{0,2},{1,3},{2,0},{3,1},{4,6},{5,7},{6,4},{7,5},{8,10},{9,11},{10,... | collective-permute-start | bytes 196616 | tf_op jit(solution)/shard_map/ppermute | solution.py:464
  22.8 22.5 %collective-permute-start.5 = (bf16[2,128,128]{2,1,0:T(8,128)(2,1)}, bf16[2,128,128]{2,1,0:T(8,128)(2,1)S(1)}, u32[]{:S(2)}, u32[]{:S(2)}) collective-permute-start(bf16[2,128,128]{2,1,0:T(8,128)(2,1)} %get-tuple-element.59), channel_id=1, source_target_pairs={{0,3},{1,2},{2,1},{3,0},{4,7},{5,6},{6,5},{7,4},{8,11},{9,10},{10,... | collective-permute-start | bytes 196616 | tf_op jit(solution)/shard_map/ppermute | solution.py:464
  46.8 0.8 copy-start.7
  46.8 0.8 copy-start.8
  46.8 0.8 copy-start.9
  46.9 80.0 %reduce-scatter.3.cloned.1.call-start = ((), (), s32[]{:S(2)}) async-start(), calls=%async_computation.2 | async-start | bytes 1310720 | tf_op jit(solution)/shard_map/reduce_scatter | solution.py:521
  87.0 61.3 %reduce-scatter.5.cloned.1.call-start = ((), (), s32[]{:S(2)}) async-start(), calls=%async_computation.3 | async-start | bytes 655360 | tf_op jit(solution)/shard_map/reduce_scatter | solution.py:527
  126.9 7.6 %collective-permute-start.12 = (bf16[512,128]{1,0:T(8,128)(2,1)}, bf16[512,128]{1,0:T(8,128)(2,1)S(1)}, u32[]{:S(2)}, u32[]{:S(2)}) collective-permute-start(bf16[512,128]{1,0:T(8,128)(2,1)} %get-tuple-element.84), channel_id=1, source_target_pairs={{0,4},{4,8},{8,12},{12,0},{1,5},{5,9},{9,13},{13,1},{2,6},{6,10},{... | collective-permute-start | bytes 393224 | tf_op jit(solution)/shard_map/ppermute | solution.py:470
  127.0 13.9 %collective-permute-start.13 = (bf16[512,128]{1,0:T(8,128)(2,1)}, bf16[512,128]{1,0:T(8,128)(2,1)S(1)}, u32[]{:S(2)}, u32[]{:S(2)}) collective-permute-start(bf16[512,128]{1,0:T(8,128)(2,1)} %get-tuple-element.85), channel_id=1, source_target_pairs={{0,8},{4,12},{8,0},{12,4},{1,9},{5,13},{9,1},{13,5},{2,10},{6,14},... | collective-permute-start | bytes 393224 | tf_op jit(solution)/shard_map/ppermute | solution.py:470
  127.8 13.1 %collective-permute-start.14 = (bf16[512,128]{1,0:T(8,128)(2,1)}, bf16[512,128]{1,0:T(8,128)(2,1)S(1)}, u32[]{:S(2)}, u32[]{:S(2)}) collective-permute-start(bf16[512,128]{1,0:T(8,128)(2,1)} %get-tuple-element.86), channel_id=1, source_target_pairs={{0,12},{4,0},{8,4},{12,8},{1,13},{5,1},{9,5},{13,9},{2,14},{6,2},{... | collective-permute-start | bytes 393224 | tf_op jit(solution)/shard_map/ppermute | solution.py:470
  132.4 18.8 %collective-permute-start.11 = (bf16[2,128,128]{2,1,0:T(8,128)(2,1)S(1)}, bf16[2,128,128]{2,1,0:T(8,128)(2,1)S(1)}, u32[]{:S(2)}, u32[]{:S(2)}) collective-permute-start(bf16[2,128,128]{2,1,0:T(8,128)(2,1)S(1)} %get-tuple-element.94), channel_id=1, source_target_pairs={{0,3},{1,2},{2,1},{3,0},{4,7},{5,6},{6,5},{7,4},{8,11},{9,10},{10,... | collective-permute-start | bytes 196616 | tf_op jit(solution)/shard_map/ppermute | solution.py:464
  132.4 19.6 %collective-permute-start.10 = (bf16[2,128,128]{2,1,0:T(8,128)(2,1)S(1)}, bf16[2,128,128]{2,1,0:T(8,128)(2,1)S(1)}, u32[]{:S(2)}, u32[]{:S(2)}) collective-permute-start(bf16[2,128,128]{2,1,0:T(8,128)(2,1)S(1)} %get-tuple-element.95), channel_id=1, source_target_pairs={{0,2},{1,3},{2,0},{3,1},{4,6},{5,7},{6,4},{7,5},{8,10},{9,11},{10,... | collective-permute-start | bytes 196616 | tf_op jit(solution)/shard_map/ppermute | solution.py:464
  134.5 17.5 %collective-permute-start.9 = (bf16[2,128,128]{2,1,0:T(8,128)(2,1)S(1)}, bf16[2,128,128]{2,1,0:T(8,128)(2,1)S(1)}, u32[]{:S(2)}, u32[]{:S(2)}) collective-permute-start(bf16[2,128,128]{2,1,0:T(8,128)(2,1)S(1)} %get-tuple-element.96), channel_id=1, source_target_pairs={{0,1},{1,0},{2,3},{3,2},{4,5},{5,4},{6,7},{7,6},{8,9},{9,8},{10,11... | collective-permute-start | bytes 196616 | tf_op jit(solution)/shard_map/ppermute | solution.py:464
  149.8 4.2 %collective-permute-start.17 = (bf16[2,128,128]{2,1,0:T(8,128)(2,1)S(1)}, bf16[2,128,128]{2,1,0:T(8,128)(2,1)S(1)}, u32[]{:S(2)}, u32[]{:S(2)}) collective-permute-start(bf16[2,128,128]{2,1,0:T(8,128)(2,1)S(1)} %get-tuple-element.90), channel_id=1, source_target_pairs={{0,3},{1,2},{2,1},{3,0},{4,7},{5,6},{6,5},{7,4},{8,11},{9,10},{10,... | collective-permute-start | bytes 196616 | tf_op jit(solution)/shard_map/ppermute | solution.py:464
  150.0 4.0 %collective-permute-start.15 = (bf16[2,128,128]{2,1,0:T(8,128)(2,1)S(1)}, bf16[2,128,128]{2,1,0:T(8,128)(2,1)S(1)}, u32[]{:S(2)}, u32[]{:S(2)}) collective-permute-start(bf16[2,128,128]{2,1,0:T(8,128)(2,1)S(1)} %get-tuple-element.92), channel_id=1, source_target_pairs={{0,1},{1,0},{2,3},{3,2},{4,5},{5,4},{6,7},{7,6},{8,9},{9,8},{10,11... | collective-permute-start | bytes 196616 | tf_op jit(solution)/shard_map/ppermute | solution.py:464
  151.2 4.3 %copy-start.1 = (bf16[2,128,128]{2,1,0:T(8,128)(2,1)}, bf16[2,128,128]{2,1,0:T(8,128)(2,1)S(1)}, u32[]{:S(2)}) copy-start(bf16[2,128,128]{2,1,0:T(8,128)(2,1)S(1)} %collective-permute-done.11.refs_3_) | copy-start | bytes 196612
  151.2 4.3 %collective-permute-start.16 = (bf16[2,128,128]{2,1,0:T(8,128)(2,1)S(1)}, bf16[2,128,128]{2,1,0:T(8,128)(2,1)S(1)}, u32[]{:S(2)}, u32[]{:S(2)}) collective-permute-start(bf16[2,128,128]{2,1,0:T(8,128)(2,1)S(1)} %get-tuple-element.93), channel_id=1, source_target_pairs={{0,2},{1,3},{2,0},{3,1},{4,6},{5,7},{6,4},{7,5},{8,10},{9,11},{10,... | collective-permute-start | bytes 196616 | tf_op jit(solution)/shard_map/ppermute | solution.py:464
  151.9 3.5 %copy-start.2 = (bf16[2,128,128]{2,1,0:T(8,128)(2,1)}, bf16[2,128,128]{2,1,0:T(8,128)(2,1)S(1)}, u32[]{:S(2)}) copy-start(bf16[2,128,128]{2,1,0:T(8,128)(2,1)S(1)} %collective-permute-done.10.refs_2_) | copy-start | bytes 196612
  152.0 3.5 %copy-start.3 = (bf16[2,128,128]{2,1,0:T(8,128)(2,1)}, bf16[2,128,128]{2,1,0:T(8,128)(2,1)S(1)}, u32[]{:S(2)}) copy-start(bf16[2,128,128]{2,1,0:T(8,128)(2,1)S(1)} %collective-permute-done.9.refs_1_) | copy-start | bytes 196612
  154.0 1.5 copy-start.4
  154.0 1.5 copy-start.5
  155.5 0.6 copy-start.6
Sparse Core Ops, SparseCore 0:
  47.0 26.0 all-gather.3
  87.1 25.2 reduce-scatter.2
  127.0 21.2 reduce-scatter.4

commit v11 on v7

--- a/solution.py
+++ b/solution.py
@@ -59,6 +59,7 @@
         tops,
         sums,
         mixture,
+        held,
     ) = rest
     rows = q_ref.shape[0]
     prompt_rows = layout.prompt_rows
@@ -76,8 +77,7 @@
     scores = (score_even, score_odd)
     dprobs = (dprob_even, dprob_odd)
 
-    @pl.when(step == 0)
-    def _():
+    def init():
         for at, key_block, value_block in layout.load(caches):
             keys[at, :] = key_block
             values[at, :] = value_block
@@ -180,10 +180,14 @@
             for product in (value_product, key_product)
         ]
 
-    def query_products():
+    def query_products(before):
         def product(r):
-            dquery = dot(keys_t[...], sgrads[:, r : r + WIDE])
-            dq_ref[r : r + WIDE, :] = (factor * dquery).T.astype(BF16)
+            dquery = (factor * dot(keys_t[...], sgrads[:, r : r + WIDE])).T.astype(BF16)
+            if before:
+                dq_ref[r : r + WIDE, HD:] = dquery
+                dq_ref[r : r + WIDE, :HD] = held[r : r + WIDE, :]
+            else:
+                held[r : r + WIDE, :] = dquery
 
         return [functools.partial(product, r) for r in range(0, rows, WIDE)]
 
@@ -223,7 +227,7 @@
             weave(products, chains)
         products = []
         if with_grad:
-            products += grad_products(before, count - 1) + query_products()
+            products += grad_products(before, count - 1) + query_products(before)
         chains = []
         if with_score:
             set_fracs(now)
@@ -238,12 +242,13 @@
             finish(now)
 
     def prepare(now):
+        columns = slice(now * HD, (now + 1) * HD)
         live_rows = lax.broadcasted_iota(jnp.int32, (rows, HD), 0) < length
-        live_grad = jnp.where(live_rows, g_ref[...].astype(F32), 0.0)
+        live_grad = jnp.where(live_rows, g_ref[:, columns].astype(F32), 0.0)
         grad[now] = live_grad.astype(BF16)
         grad_t[now] = live_grad.T.astype(BF16)
-        query[now] = q_ref[...]
-        query_t[now] = q_ref[...].T
+        query[now] = q_ref[:, columns]
+        query_t[now] = q_ref[:, columns].T
 
     def set_fracs(now):
         top = jnp.max(tops[...], axis=0, keepdims=True)
@@ -254,24 +259,31 @@
     def finish(now):
         live_lanes = lax.broadcasted_iota(jnp.int32, (HD, rows), 1) < length
         attended = jnp.where(live_lanes, mixture[...], 0.0).astype(BF16).astype(F32)
-        out_ref[...] = attended.T.astype(BF16)
+        out_ref[:, now * HD : (now + 1) * HD] = attended.T.astype(BF16)
         delta = jnp.sum(grad_t[now].astype(F32) * attended, axis=0, keepdims=True)
         deltas[now] = jnp.broadcast_to(delta, (8, rows))
 
+    steps = heads_per // 2
+
     @pl.when(step == 0)
     def _():
+        init()
         prepare(0)
         run(0, True, False)
 
-    for now in range(2):
-        @pl.when((step > 0) & (step < heads_per) & (lax.rem(step, 2) == now))
-        def _():
-            prepare(now)
-            run(now, True, True)
-
-    @pl.when(step == heads_per)
+    @pl.when((step > 0) & (step < steps))
     def _():
-        run(heads_per % 2, False, True)
+        prepare(0)
+        run(0, True, True)
+
+    @pl.when(step < steps)
+    def _():
+        prepare(1)
+        run(1, True, True)
+
+    @pl.when(step == steps)
+    def _():
+        run(0, False, True)
         layout.store(dcaches, dk_sum, dv_sum, factor)
         at = pl.ds(prompt_rows, rows)
         dkr_ref[...] = (factor * dk_sum[at, :]).astype(BF16)
@@ -279,17 +291,17 @@
 
 
 class Gathered:
-    def __init__(self, members, ranks, own_rows):
-        self.members, self.part_rows = members, ranks * own_rows
-        self.prompt_rows = members * self.part_rows
-        self.caches = 1
-        self.dcaches = members
+    def __init__(self, members, part_rows):
+        self.members, self.part_rows = members, part_rows
+        self.prompt_rows = members * part_rows
+        self.caches, self.dcaches = 1, members + 1
 
     def cache_shapes(self):
         return [(self.members, 2, self.part_rows, HD)]
 
     def dcache_shapes(self):
-        return [(2, self.part_rows, HD)] * self.dcaches
+        part = (self.part_rows, HD)
+        return [part] * self.members + [(self.members, *part)]
 
     def load(self, caches):
         for m in range(self.members):
@@ -301,24 +313,25 @@
         for shift in range(self.members):
             part = lax.rem(me + shift, self.members) * self.part_rows
             at = pl.ds(pl.multiple_of(part, self.part_rows), self.part_rows)
-            dcaches[shift][0] = (factor * dk_sum[at, :]).astype(BF16)
-            dcaches[shift][1] = dv_sum[at, :].astype(BF16)
+            dcaches[shift][...] = (factor * dk_sum[at, :]).astype(BF16)
+            at = pl.ds(shift * self.part_rows, self.part_rows)
+            dcaches[self.members][shift] = dv_sum[at, :].astype(BF16)
 
 
 class Scattered(Gathered):
-    def __init__(self, members, ranks, own_rows):
-        super().__init__(members, ranks, own_rows)
-        self.caches, self.dcaches = self.dcaches, self.caches
+    def __init__(self, members, part_rows):
+        super().__init__(members, part_rows)
+        self.caches, self.dcaches = members, 1
 
     def cache_shapes(self):
-        return [(2, self.part_rows, HD)] * self.caches
+        return [(2, self.part_rows, HD)] * self.members
 
     def dcache_shapes(self):
-        return [(self.members, 2, self.part_rows, HD)]
+        return super().cache_shapes()
 
     def load(self, caches):
-        for i, ref in enumerate(caches):
-            yield pl.ds(i * self.part_rows, self.part_rows), ref[0], ref[1]
+        for shift, ref in enumerate(caches):
+            yield pl.ds(shift * self.part_rows, self.part_rows), ref[0], ref[1]
 
     def store(self, dcaches, dk_sum, dv_sum, factor):
         me = lax.axis_index("resp")
@@ -334,9 +347,10 @@
 ):
     rows, query_width = queries.shape
     total_rows = layout.prompt_rows + rows
-    first, last = pair * heads_per, (pair + 1) * heads_per - 1
-    head_block = pl.BlockSpec((rows, HD), lambda s: (0, jnp.minimum(first + s, last)))
-    late_block = pl.BlockSpec((rows, HD), lambda s: (0, jnp.maximum(first + s - 1, first)))
+    steps = heads_per // 2
+    first, last = pair * steps, (pair + 1) * steps - 1
+    head_block = pl.BlockSpec((rows, 2 * HD), lambda s: (0, jnp.minimum(first + s, last)))
+    late_block = pl.BlockSpec((rows, 2 * HD), lambda s: (0, jnp.maximum(first + s - 1, first)))
     pair_block = pl.BlockSpec((rows, HD), lambda s: (0, pair))
     cache_blocks = [
         pl.BlockSpec(shape, lambda s, rank=len(shape): (0,) * rank)
@@ -358,7 +372,7 @@
     aliases = {5 + layout.caches + i: i for i in range(len(earlier))}
     return pl.pallas_call(
         functools.partial(attention_kernel, layout, heads_per, len(earlier)),
-        grid=(heads_per + 1,),
+        grid=(steps + 1,),
         in_specs=in_specs,
         out_specs=[head_block, late_block, pair_block, pair_block, *dcache_blocks],
         out_shape=[
@@ -393,6 +407,7 @@
             pltpu.VMEM((stats, rows), F32),
             pltpu.VMEM((stats, rows), F32),
             pltpu.VMEM((HD, rows), F32),
+            pltpu.VMEM((rows, HD), BF16),
         ],
         input_output_aliases=aliases,
         cost_estimate=pl.CostEstimate(
@@ -484,8 +499,8 @@
         a[0] for a in (queries, out_grad, resp_keys, resp_values)
     )
     cuts = cut(prompt_keys, prompt_values, pairs)
-    kinds = [Scattered(members, ranks, own_rows)]
-    kinds += [Gathered(members, ranks, own_rows) for _ in range(pairs - 1)]
+    kinds = [Scattered(members, ranks * own_rows)]
+    kinds += [Gathered(members, ranks * own_rows) for _ in range(pairs - 1)]
     own = jnp.concatenate(swap(cuts[0]), axis=1)
     if pairs > 1:
         own, cuts[1:] = lax.optimization_barrier((own, cuts[1:]))
@@ -518,7 +533,9 @@
             arrived = [dcaches[0]] + [
                 send(dcaches[shift], members, shift) for shift in range(1, members)
             ]
-            totals.append(sum(block.astype(F32) for block in arrived).astype(BF16))
+            dkey = sum(block.astype(F32) for block in arrived).astype(BF16)
+            dvalue = lax.psum_scatter(dcaches[members], "resp", scatter_dimension=0)
+            totals.append(jnp.stack([dkey, dvalue]))
     blocks = [block for total in totals for block in swap(cut_rows(total, ranks))]
     key_grad, value_grad = place(blocks, pairs, columns)
     return (*(a[None] for a in earlier), key_grad, value_grad)

time: 164 us -> 164 us (level)
  the two profiles are of different devices: /device:TPU:9 before, /device:TPU:0 now
where the time goes in v11:
time: 164 us; the launch traced here: 163 us
  Pallas kernels  81.5 us (50%)
  waiting for transfers between devices  40 us (24%)
  starting transfers between devices  20.1 us (12%)
  between operations  14.5 us (9%)
  other arithmetic  4.84 us (3%)
  local copies, waits for them, and re-layouts  2.23 us (1%)
    pallas_call x2, Pallas kernels, attend(): pl.pallas_call(functools.partial(attention_kernel, layout, heads_per, len...  77.5 us
    ppermute x6, waiting for transfers between devices, send(): lax.ppermute(block, 'resp', [(m, (m + shift) % members) for m in range(me...  21.1 us
    ppermute x12, waiting for transfers between devices, swap(): lax.ppermute(blocks[i], 'tensor', [(j, j ^ i) for j in range(count)])  11.3 us
    ppermute x6, starting transfers between devices, send(): lax.ppermute(block, 'resp', [(m, (m + shift) % members) for m in range(me...  10.5 us
    ppermute x12, starting transfers between devices, swap(): lax.ppermute(blocks[i], 'tensor', [(j, j ^ i) for j in range(count)])  9.5 us
    reduce_scatter x1, waiting for transfers between devices, per_device(): dvalue = lax.psum_scatter(dcaches[members], 'resp', scatter_dimension=0)  7.58 us
  transfers between devices with their start and end apart: 21, of which 10 were waited for; matrix products, arithmetic and copies ran while one was open for 3% of the time, Pallas kernels for 47%

profile of v11, /device:TPU:0, one launch (start us, length us, event | category | flops | bytes accessed | tf_op | source)
XLA Modules:
  0.0 163.3 jit_solution(13705286097537899543)
XLA Ops:
  7.2 0.0 all-gather.3.cloned.1.call-start
  7.2 1.9 %cut.1 = (bf16[2,128,128]{2,1,0:T(8,128)(2,1)}, bf16[2,128,128]{2,1,0:T(8,128)(2,1)}, bf16[2,128,128]{2,1,0:T(8,128)(2,1)}, bf16[2,128,128]{2,1,0:T(8,128)(2,1)}...) custom-call(bf16[128,1024]{1,0:T(8,128)(2,1)} %k_ref.1, ...), custom_call_target="tpu_custom_call" | custom-call | tf_op jit(solution)/shard_map/cut/pallas_call | solution.py:440
  9.2 0.5 collective-permute-start
  9.6 2.5 %collective-permute-start.1 = (bf16[2,128,128]{2,1,0:T(8,128)(2,1)}, bf16[2,128,128]{2,1,0:T(8,128)(2,1)S(1)}, u32[]{:S(2)}, u32[]{:S(2)}) collective-permute-start(bf16[2,128,128]{2,1,0:T(8,128)(2,1)} %get-tuple-element.48), channel_id=1, source_target_pairs={{0,2},{1,3},{2,0},{3,1},{4,6},{5,7},{6,4},{7,5},{8,10},{9,11},{10,... | collective-permute-start | bytes 196616 | tf_op jit(solution)/shard_map/ppermute | solution.py:476
  12.1 0.1 collective-permute-start.2
  12.2 0.0 collective-permute-done
  12.2 2.8 %collective-permute-done.1 = bf16[2,128,128]{2,1,0:T(8,128)(2,1)S(1)} collective-permute-done((bf16[2,128,128]{2,1,0:T(8,128)(2,1)}, bf16[2,128,128]{2,1,0:T(8,128)(2,1)S(1)}, u32[]{:S(2)}, u32[]{:S(2)}) %collective-permute-start.1) | collective-permute-done | bytes 65568 | tf_op jit(solution)/shard_map/ppermute | solution.py:476
  15.1 1.4 collective-permute-done.2
  16.5 0.9 pad_maximum_fusion.rest_0_
  17.3 0.0 copy-start
  17.3 3.7 %collective-permute-start.8 = (bf16[2,512,128]{2,1,0:T(8,128)(2,1)S(1)}, bf16[2,512,128]{2,1,0:T(8,128)(2,1)S(1)}, u32[]{:S(2)}, u32[]{:S(2)}) collective-permute-start(bf16[2,512,128]{2,1,0:T(8,128)(2,1)S(1)} %pad_maximum_fusion.rest_0_), channel_id=1, source_target_pairs={{0,12},{4,0},{8,4},{12,8},{1,13},{5,1},{9,5},{13,9},{2,14},{6,2},{... | collective-permute-start | bytes 786440 | tf_op jit(solution)/shard_map/ppermute | solution.py:482
  21.0 0.0 collective-permute-start.7
  21.0 1.0 collective-permute-start.6
  22.0 0.0 collective-permute-start.3
  22.0 1.3 collective-permute-start.4
  23.3 0.1 collective-permute-done.3
  23.5 1.1 collective-permute-start.5
  24.6 2.2 %collective-permute-done.4 = bf16[2,128,128]{2,1,0:T(8,128)(2,1)S(1)} collective-permute-done((bf16[2,128,128]{2,1,0:T(8,128)(2,1)}, bf16[2,128,128]{2,1,0:T(8,128)(2,1)S(1)}, u32[]{:S(2)}, u32[]{:S(2)}) %collective-permute-start.4) | collective-permute-done | bytes 65568 | tf_op jit(solution)/shard_map/ppermute | solution.py:476
  26.8 1.1 collective-permute-done.5
  27.8 1.6 pad_maximum_fusion.1
  29.4 0.0 collective-permute-done.8.rest_3_
  29.4 14.2 %collective-permute-done.7.rest_2_ = bf16[2,512,128]{2,1,0:T(8,128)(2,1)S(1)} collective-permute-done((bf16[2,512,128]{2,1,0:T(8,128)(2,1)S(1)}, bf16[2,512,128]{2,1,0:T(8,128)(2,1)S(1)}, u32[]{:S(2)}, u32[]{:S(2)}) %collective-permute-start.7) | collective-permute-done | bytes 262176 | tf_op jit(solution)/shard_map/ppermute | solution.py:482
  43.6 0.0 collective-permute-done.6.rest_1_
  43.6 0.0 all-gather.3.cloned.1.call-update
  43.6 0.0 reduce-scatter.3.cloned.1.call-start
  44.3 0.0 copy-done
  44.4 0.0 copy-done.7
  44.4 0.0 copy-done.8
  44.4 0.0 copy-done.9
  44.4 38.5 %attend_pair_0.1 = (bf16[512,2048]{1,0:T(8,128)(2,1)}, bf16[512,2048]{1,0:T(8,128)(2,1)}, bf16[512,256]{1,0:T(8,128)(2,1)}, bf16[512,256]{1,0:T(8,128)(2,1)}, bf16[4,2,512,128]{3,2,1,0:T(8,128)(2,1)}) custom-call(s32[1]{0:T(128)S(6)} %copy.21.len_ref, bf16[512,2048]{1,0:T(8,128)(2,1)} %bitcast.13, bf16[512,2048]{1,0:T(8,128)(2,1)} %bitcast.15, ...), custom_call_target="tpu_custom_call" | custom-call | flops 16106127360 | bytes 4194304 | tf_op jit(solution)/shard_map/attend_pair_0/pallas_call | solution.py:373
  82.9 0.0 reduce-scatter.3.cloned.1.call-update
  83.0 0.0 reduce-scatter.5.cloned.1.call-start
  83.0 0.0 all-gather.3.cloned.1.call-done
  83.0 38.9 %attend_pair_1.1 = (bf16[512,2048]{1,0:T(8,128)(2,1)}, bf16[512,2048]{1,0:T(8,128)(2,1)}, bf16[512,256]{1,0:T(8,128)(2,1)}, bf16[512,256]{1,0:T(8,128)(2,1)}, bf...) custom-call(s32[1]{0:T(128)S(6)} %copy.21.len_ref, ...), custom_call_target="tpu_custom_call", output_to_operand_aliasing={{0}: (6, {}), {1}: (7, {}), {2}: (8, {}), {3}: (9, {})} | custom-call | flops 16106127360 | bytes 4194304 | tf_op jit(solution)/shard_map/attend_pair_1/pallas_call | solution.py:373
  122.0 0.0 reduce-scatter.3.cloned.1.call-done
  122.0 0.0 reduce-scatter.5.cloned.1.call-update
  122.0 0.9 collective-permute-start.12
  123.0 2.0 %collective-permute-start.13 = (bf16[512,128]{1,0:T(8,128)(2,1)}, bf16[512,128]{1,0:T(8,128)(2,1)S(1)}, u32[]{:S(2)}, u32[]{:S(2)}) collective-permute-start(bf16[512,128]{1,0:T(8,128)(2,1)} %get-tuple-element.81), channel_id=1, source_target_pairs={{0,8},{4,12},{8,0},{12,4},{1,9},{5,13},{9,1},{13,5},{2,10},{6,14},... | collective-permute-start | bytes 393224 | tf_op jit(solution)/shard_map/ppermute | solution.py:482
  125.0 2.8 %collective-permute-start.14 = (bf16[512,128]{1,0:T(8,128)(2,1)}, bf16[512,128]{1,0:T(8,128)(2,1)S(1)}, u32[]{:S(2)}, u32[]{:S(2)}) collective-permute-start(bf16[512,128]{1,0:T(8,128)(2,1)} %get-tuple-element.82), channel_id=1, source_target_pairs={{0,12},{4,0},{8,4},{12,8},{1,13},{5,1},{9,5},{13,9},{2,14},{6,2},{... | collective-permute-start | bytes 393224 | tf_op jit(solution)/shard_map/ppermute | solution.py:482
  127.8 1.6 fusion.4
  129.4 0.0 collective-permute-start.11
  129.4 1.5 collective-permute-start.10
  130.9 0.0 collective-permute-done.12
  130.9 0.4 collective-permute-start.9
  131.3 6.9 %collective-permute-done.13 = bf16[512,128]{1,0:T(8,128)(2,1)S(1)} collective-permute-done((bf16[512,128]{1,0:T(8,128)(2,1)}, bf16[512,128]{1,0:T(8,128)(2,1)S(1)}, u32[]{:S(2)}, u32[]{:S(2)}) %collective-permute-start.13) | collective-permute-done | bytes 131104 | tf_op jit(solution)/shard_map/ppermute | solution.py:482
  138.2 0.0 collective-permute-done.14
  138.2 1.0 fusion
  139.2 7.6 %reduce-scatter.5.cloned.1.call-done = bf16[1,512,128]{2,1,0:T(8,128)(2,1)} async-done(((bf16[4,512,128]{2,1,0:T(8,128)(2,1)}), bf16[1,512,128]{2,1,0:T(8,128)(2,1)}) %reduce-scatter.5.cloned.1.call-update) | async-done | bytes 131088 | tf_op jit(solution)/shard_map/reduce_scatter | solution.py:537
  146.8 1.4 pad_maximum_fusion.2
  148.2 0.0 collective-permute-start.17
  148.2 1.5 collective-permute-start.15
  149.7 0.0 collective-permute-done.11.refs_3_
  149.7 0.6 collective-permute-start.16
  150.3 0.0 collective-permute-done.10.refs_2_
  150.4 0.0 collective-permute-done.9.refs_1_
  150.4 0.0 copy-start.3
  150.4 2.2 %collective-permute-done.17.refs_7_ = bf16[2,128,128]{2,1,0:T(8,128)(2,1)S(1)} collective-permute-done((bf16[2,128,128]{2,1,0:T(8,128)(2,1)S(1)}, bf16[2,128,128]{2,1,0:T(8,128)(2,1)S(1)}, u32[]{:S(2)}, u32[]{:S(2)}) %collective-permute-start.17) | collective-permute-done | bytes 65568 | tf_op jit(solution)/shard_map/ppermute | solution.py:476
  152.6 0.0 collective-permute-done.15.refs_5_
  152.6 1.4 collective-permute-done.16.refs_6_
  154.0 0.0 copy-done.2
  154.0 0.0 copy-done.4
  154.0 0.0 copy-done.5
  154.0 0.6 copy-done.6
  154.6 2.1 %place.1 = (f32[128,1024]{1,0:T(8,128)}, f32[128,1024]{1,0:T(8,128)}) custom-call(bf16[2,128,128]{2,1,0:T(8,128)(2,1)} %get-tuple-element.93.refs_0_, bf16[2,128,128]{2,1,0:T(8,128)(2,1)} %copy-done.3, bf16[2,128,128]{2,1,0:T(8,128)(2,1)} %copy-done.2, bf16[2,128,128]{2,1,0:T(8,128)(2,1)} %copy-done.1, bf16[2,128,128]{2,1,0:T(8,128)(2,1)} %get-tuple-element.87.refs_4_, ...), custom_call_target="tpu_custom_call" | custom-call | tf_op jit(solution)/shard_map/place/pallas_call | solution.py:464
  (10 shorter events, 0.0 us)
Async XLA Ops:
  7.2 75.9 %all-gather.3.cloned.1.call-start = ((), (), s32[]{:S(2)}) async-start(), calls=%async_computation.4 | async-start | bytes 1310720 | tf_op jit(solution)/shard_map/all_gather | solution.py:511
  9.2 3.1 %collective-permute-start = (bf16[2,128,128]{2,1,0:T(8,128)(2,1)}, bf16[2,128,128]{2,1,0:T(8,128)(2,1)S(1)}, u32[]{:S(2)}, u32[]{:S(2)}) collective-permute-start(bf16[2,128,128]{2,1,0:T(8,128)(2,1)} %get-tuple-element.47), channel_id=1, source_target_pairs={{0,1},{1,0},{2,3},{3,2},{4,5},{5,4},{6,7},{7,6},{8,9},{9,8},{10,11... | collective-permute-start | bytes 196616 | tf_op jit(solution)/shard_map/ppermute | solution.py:476
  9.6 5.5 %collective-permute-start.1 = (bf16[2,128,128]{2,1,0:T(8,128)(2,1)}, bf16[2,128,128]{2,1,0:T(8,128)(2,1)S(1)}, u32[]{:S(2)}, u32[]{:S(2)}) collective-permute-start(bf16[2,128,128]{2,1,0:T(8,128)(2,1)} %get-tuple-element.48), channel_id=1, source_target_pairs={{0,2},{1,3},{2,0},{3,1},{4,6},{5,7},{6,4},{7,5},{8,10},{9,11},{10,... | collective-permute-start | bytes 196616 | tf_op jit(solution)/shard_map/ppermute | solution.py:476
  12.1 4.3 %collective-permute-start.2 = (bf16[2,128,128]{2,1,0:T(8,128)(2,1)}, bf16[2,128,128]{2,1,0:T(8,128)(2,1)S(1)}, u32[]{:S(2)}, u32[]{:S(2)}) collective-permute-start(bf16[2,128,128]{2,1,0:T(8,128)(2,1)} %get-tuple-element.49), channel_id=1, source_target_pairs={{0,3},{1,2},{2,1},{3,0},{4,7},{5,6},{6,5},{7,4},{8,11},{9,10},{10,... | collective-permute-start | bytes 196616 | tf_op jit(solution)/shard_map/ppermute | solution.py:476
  17.3 27.0 %copy-start = (bf16[2,512,128]{2,1,0:T(8,128)(2,1)}, bf16[2,512,128]{2,1,0:T(8,128)(2,1)S(1)}, u32[]{:S(2)}) copy-start(bf16[2,512,128]{2,1,0:T(8,128)(2,1)S(1)} %pad_maximum_fusion.rest_0_) | copy-start | bytes 786436
  17.3 12.1 %collective-permute-start.8 = (bf16[2,512,128]{2,1,0:T(8,128)(2,1)S(1)}, bf16[2,512,128]{2,1,0:T(8,128)(2,1)S(1)}, u32[]{:S(2)}, u32[]{:S(2)}) collective-permute-start(bf16[2,512,128]{2,1,0:T(8,128)(2,1)S(1)} %pad_maximum_fusion.rest_0_), channel_id=1, source_target_pairs={{0,12},{4,0},{8,4},{12,8},{1,13},{5,1},{9,5},{13,9},{2,14},{6,2},{... | collective-permute-start | bytes 786440 | tf_op jit(solution)/shard_map/ppermute | solution.py:482
  21.0 22.6 %collective-permute-start.7 = (bf16[2,512,128]{2,1,0:T(8,128)(2,1)S(1)}, bf16[2,512,128]{2,1,0:T(8,128)(2,1)S(1)}, u32[]{:S(2)}, u32[]{:S(2)}) collective-permute-start(bf16[2,512,128]{2,1,0:T(8,128)(2,1)S(1)} %pad_maximum_fusion.rest_0_), channel_id=1, source_target_pairs={{0,8},{4,12},{8,0},{12,4},{1,9},{5,13},{9,1},{13,5},{2,10},{6,14},... | collective-permute-start | bytes 786440 | tf_op jit(solution)/shard_map/ppermute | solution.py:482
  21.0 22.6 %collective-permute-start.6 = (bf16[2,512,128]{2,1,0:T(8,128)(2,1)S(1)}, bf16[2,512,128]{2,1,0:T(8,128)(2,1)S(1)}, u32[]{:S(2)}, u32[]{:S(2)}) collective-permute-start(bf16[2,512,128]{2,1,0:T(8,128)(2,1)S(1)} %pad_maximum_fusion.rest_0_), channel_id=1, source_target_pairs={{0,4},{4,8},{8,12},{12,0},{1,5},{5,9},{9,13},{13,1},{2,6},{6,10},{... | collective-permute-start | bytes 786440 | tf_op jit(solution)/shard_map/ppermute | solution.py:482
  22.0 1.5 collective-permute-start.3
  22.0 4.8 %collective-permute-start.4 = (bf16[2,128,128]{2,1,0:T(8,128)(2,1)}, bf16[2,128,128]{2,1,0:T(8,128)(2,1)S(1)}, u32[]{:S(2)}, u32[]{:S(2)}) collective-permute-start(bf16[2,128,128]{2,1,0:T(8,128)(2,1)} %get-tuple-element.56), channel_id=1, source_target_pairs={{0,2},{1,3},{2,0},{3,1},{4,6},{5,7},{6,4},{7,5},{8,10},{9,11},{10,... | collective-permute-start | bytes 196616 | tf_op jit(solution)/shard_map/ppermute | solution.py:476
  23.5 4.4 %collective-permute-start.5 = (bf16[2,128,128]{2,1,0:T(8,128)(2,1)}, bf16[2,128,128]{2,1,0:T(8,128)(2,1)S(1)}, u32[]{:S(2)}, u32[]{:S(2)}) collective-permute-start(bf16[2,128,128]{2,1,0:T(8,128)(2,1)} %get-tuple-element.57), channel_id=1, source_target_pairs={{0,3},{1,2},{2,1},{3,0},{4,7},{5,6},{6,5},{7,4},{8,11},{9,10},{10,... | collective-permute-start | bytes 196616 | tf_op jit(solution)/shard_map/ppermute | solution.py:476
  29.4 15.0 %copy-start.7 = (bf16[2,512,128]{2,1,0:T(8,128)(2,1)}, bf16[2,512,128]{2,1,0:T(8,128)(2,1)S(1)}, u32[]{:S(2)}) copy-start(bf16[2,512,128]{2,1,0:T(8,128)(2,1)S(1)} %collective-permute-done.8.rest_3_) | copy-start | bytes 786436
  43.6 0.8 copy-start.8
  43.6 0.8 copy-start.9
  43.6 78.4 %reduce-scatter.3.cloned.1.call-start = ((), (), s32[]{:S(2)}) async-start(), calls=%async_computation.2 | async-start | bytes 1310720 | tf_op jit(solution)/shard_map/reduce_scatter | solution.py:531
  83.0 63.8 %reduce-scatter.5.cloned.1.call-start = ((), (), s32[]{:S(2)}) async-start(), calls=%async_computation.3 | async-start | bytes 655360 | tf_op jit(solution)/shard_map/reduce_scatter | solution.py:537
  122.0 8.9 %collective-permute-start.12 = (bf16[512,128]{1,0:T(8,128)(2,1)}, bf16[512,128]{1,0:T(8,128)(2,1)S(1)}, u32[]{:S(2)}, u32[]{:S(2)}) collective-permute-start(bf16[512,128]{1,0:T(8,128)(2,1)} %get-tuple-element.80), channel_id=1, source_target_pairs={{0,4},{4,8},{8,12},{12,0},{1,5},{5,9},{9,13},{13,1},{2,6},{6,10},{... | collective-permute-start | bytes 393224 | tf_op jit(solution)/shard_map/ppermute | solution.py:482
  123.0 15.2 %collective-permute-start.13 = (bf16[512,128]{1,0:T(8,128)(2,1)}, bf16[512,128]{1,0:T(8,128)(2,1)S(1)}, u32[]{:S(2)}, u32[]{:S(2)}) collective-permute-start(bf16[512,128]{1,0:T(8,128)(2,1)} %get-tuple-element.81), channel_id=1, source_target_pairs={{0,8},{4,12},{8,0},{12,4},{1,9},{5,13},{9,1},{13,5},{2,10},{6,14},... | collective-permute-start | bytes 393224 | tf_op jit(solution)/shard_map/ppermute | solution.py:482
  125.0 13.2 %collective-permute-start.14 = (bf16[512,128]{1,0:T(8,128)(2,1)}, bf16[512,128]{1,0:T(8,128)(2,1)S(1)}, u32[]{:S(2)}, u32[]{:S(2)}) collective-permute-start(bf16[512,128]{1,0:T(8,128)(2,1)} %get-tuple-element.82), channel_id=1, source_target_pairs={{0,12},{4,0},{8,4},{12,8},{1,13},{5,1},{9,5},{13,9},{2,14},{6,2},{... | collective-permute-start | bytes 393224 | tf_op jit(solution)/shard_map/ppermute | solution.py:482
  129.4 20.3 %collective-permute-start.11 = (bf16[2,128,128]{2,1,0:T(8,128)(2,1)S(1)}, bf16[2,128,128]{2,1,0:T(8,128)(2,1)S(1)}, u32[]{:S(2)}, u32[]{:S(2)}) collective-permute-start(bf16[2,128,128]{2,1,0:T(8,128)(2,1)S(1)} %get-tuple-element.90), channel_id=1, source_target_pairs={{0,3},{1,2},{2,1},{3,0},{4,7},{5,6},{6,5},{7,4},{8,11},{9,10},{10,... | collective-permute-start | bytes 196616 | tf_op jit(solution)/shard_map/ppermute | solution.py:476
  129.4 20.9 %collective-permute-start.10 = (bf16[2,128,128]{2,1,0:T(8,128)(2,1)S(1)}, bf16[2,128,128]{2,1,0:T(8,128)(2,1)S(1)}, u32[]{:S(2)}, u32[]{:S(2)}) collective-permute-start(bf16[2,128,128]{2,1,0:T(8,128)(2,1)S(1)} %get-tuple-element.91), channel_id=1, source_target_pairs={{0,2},{1,3},{2,0},{3,1},{4,6},{5,7},{6,4},{7,5},{8,10},{9,11},{10,... | collective-permute-start | bytes 196616 | tf_op jit(solution)/shard_map/ppermute | solution.py:476
  130.9 19.5 %collective-permute-start.9 = (bf16[2,128,128]{2,1,0:T(8,128)(2,1)S(1)}, bf16[2,128,128]{2,1,0:T(8,128)(2,1)S(1)}, u32[]{:S(2)}, u32[]{:S(2)}) collective-permute-start(bf16[2,128,128]{2,1,0:T(8,128)(2,1)S(1)} %get-tuple-element.92), channel_id=1, source_target_pairs={{0,1},{1,0},{2,3},{3,2},{4,5},{5,4},{6,7},{7,6},{8,9},{9,8},{10,11... | collective-permute-start | bytes 196616 | tf_op jit(solution)/shard_map/ppermute | solution.py:476
  148.2 4.4 %collective-permute-start.17 = (bf16[2,128,128]{2,1,0:T(8,128)(2,1)S(1)}, bf16[2,128,128]{2,1,0:T(8,128)(2,1)S(1)}, u32[]{:S(2)}, u32[]{:S(2)}) collective-permute-start(bf16[2,128,128]{2,1,0:T(8,128)(2,1)S(1)} %get-tuple-element.86), channel_id=1, source_target_pairs={{0,3},{1,2},{2,1},{3,0},{4,7},{5,6},{6,5},{7,4},{8,11},{9,10},{10,... | collective-permute-start | bytes 196616 | tf_op jit(solution)/shard_map/ppermute | solution.py:476
  148.2 4.4 %collective-permute-start.15 = (bf16[2,128,128]{2,1,0:T(8,128)(2,1)S(1)}, bf16[2,128,128]{2,1,0:T(8,128)(2,1)S(1)}, u32[]{:S(2)}, u32[]{:S(2)}) collective-permute-start(bf16[2,128,128]{2,1,0:T(8,128)(2,1)S(1)} %get-tuple-element.88), channel_id=1, source_target_pairs={{0,1},{1,0},{2,3},{3,2},{4,5},{5,4},{6,7},{7,6},{8,9},{9,8},{10,11... | collective-permute-start | bytes 196616 | tf_op jit(solution)/shard_map/ppermute | solution.py:476
  149.7 4.3 %copy-start.1 = (bf16[2,128,128]{2,1,0:T(8,128)(2,1)}, bf16[2,128,128]{2,1,0:T(8,128)(2,1)S(1)}, u32[]{:S(2)}) copy-start(bf16[2,128,128]{2,1,0:T(8,128)(2,1)S(1)} %collective-permute-done.11.refs_3_) | copy-start | bytes 196612
  149.7 4.3 %collective-permute-start.16 = (bf16[2,128,128]{2,1,0:T(8,128)(2,1)S(1)}, bf16[2,128,128]{2,1,0:T(8,128)(2,1)S(1)}, u32[]{:S(2)}, u32[]{:S(2)}) collective-permute-start(bf16[2,128,128]{2,1,0:T(8,128)(2,1)S(1)} %get-tuple-element.89), channel_id=1, source_target_pairs={{0,2},{1,3},{2,0},{3,1},{4,6},{5,7},{6,4},{7,5},{8,10},{9,11},{10,... | collective-permute-start | bytes 196616 | tf_op jit(solution)/shard_map/ppermute | solution.py:476
  150.3 3.7 %copy-start.2 = (bf16[2,128,128]{2,1,0:T(8,128)(2,1)}, bf16[2,128,128]{2,1,0:T(8,128)(2,1)S(1)}, u32[]{:S(2)}) copy-start(bf16[2,128,128]{2,1,0:T(8,128)(2,1)S(1)} %collective-permute-done.10.refs_2_) | copy-start | bytes 196612
  150.4 3.6 %copy-start.3 = (bf16[2,128,128]{2,1,0:T(8,128)(2,1)}, bf16[2,128,128]{2,1,0:T(8,128)(2,1)S(1)}, u32[]{:S(2)}) copy-start(bf16[2,128,128]{2,1,0:T(8,128)(2,1)S(1)} %collective-permute-done.9.refs_1_) | copy-start | bytes 196612
  152.6 1.5 copy-start.4
  152.6 1.5 copy-start.5
  154.0 0.6 copy-start.6
Sparse Core Ops, SparseCore 0:
  43.7 28.3 all-gather.2
  83.1 27.5 reduce-scatter.2
  122.1 24.5 reduce-scatter.4

commit v12 on v11

--- a/solution.py
+++ b/solution.py
@@ -48,10 +48,6 @@
         weights_even,
         weights_odd,
         sgrads,
-        score_even,
-        score_odd,
-        dprob_even,
-        dprob_odd,
         fracs,
         deltas,
         dk_sum,
@@ -74,8 +70,6 @@
     step = pl.program_id(0)
     exps = (exps_even, exps_odd)
     weights = (weights_even, weights_odd)
-    scores = (score_even, score_odd)
-    dprobs = (dprob_even, dprob_odd)
 
     def init():
         for at, key_block, value_block in layout.load(caches):
@@ -109,52 +103,46 @@
     def tiled(block):
         return block.reshape(SUB // 8, 8, SUB)
 
-    def score_products(now, piece):
+    def units(piece):
         at, size, row = pieces[piece]
-
-        def product(r):
-            scores[piece % 2][:size, r - row : r - row + WIDE] = dot(
-                keys[at : at + size, :], query_t[now, :, r : r + WIDE]
-            )
-
-        return [functools.partial(product, r) for r in range(row, rows, WIDE)]
-
-    def dprob_products(before, piece):
-        at, size, row = pieces[piece]
-
-        def product(r):
-            dprobs[piece % 2][:size, r - row : r - row + WIDE] = dot(
-                values[at : at + size, :], grad_t[before, :, r : r + WIDE]
-            )
-
-        return [functools.partial(product, r) for r in range(row, rows, WIDE)]
+        return [(u, r) for r in range(row, rows, WIDE) for u in range(at, at + size, WIDE)]
+
+    def inner(u, r):
+        for du in range(0, WIDE, SUB):
+            for dr in range(0, WIDE, SUB):
+                block = (slice(du, du + SUB), slice(dr, dr + SUB))
+                yield block, slice(u + du, u + du + SUB), slice(r + dr, r + dr + SUB)
 
     def score_chains(now, piece):
-        def chain(u, r, key_at, row_at):
-            block = scores[piece % 2][u : u + SUB, r : r + SUB]
-            if key_at.start >= prompt_rows:
-                j = lax.broadcasted_iota(jnp.int32, (SUB, SUB), 0) + key_at.start - prompt_rows
-                i = lax.broadcasted_iota(jnp.int32, (SUB, SUB), 1) + row_at.start
-                block = jnp.where((j <= i) & (j < length), block, -jnp.inf)
-            block = tiled(block) * factor2
-            top = jnp.maximum(jnp.max(block, axis=0), LOWEST)
-            exp = jnp.exp2(block - top[None])
-            exps[now][key_at, row_at] = exp.reshape(SUB, SUB)
-            tops[stat(key_at), row_at] = top
-            sums[stat(key_at), row_at] = jnp.sum(exp, axis=0)
-
-        return [functools.partial(chain, *block) for block in blocks(piece)]
+        def chain(u, r):
+            score = dot(keys[u : u + WIDE, :], query_t[now, :, r : r + WIDE])
+            for at, key_at, row_at in inner(u, r):
+                block = score[at]
+                if key_at.start >= prompt_rows:
+                    j = lax.broadcasted_iota(jnp.int32, (SUB, SUB), 0) + key_at.start - prompt_rows
+                    i = lax.broadcasted_iota(jnp.int32, (SUB, SUB), 1) + row_at.start
+                    block = jnp.where((j <= i) & (j < length), block, -jnp.inf)
+                block = tiled(block) * factor2
+                top = jnp.maximum(jnp.max(block, axis=0), LOWEST)
+                exp = jnp.exp2(block - top[None])
+                exps[now][key_at, row_at] = exp.reshape(SUB, SUB)
+                tops[stat(key_at), row_at] = top
+                sums[stat(key_at), row_at] = jnp.sum(exp, axis=0)
+
+        return [functools.partial(chain, *unit) for unit in units(piece)]
 
     def frac(slot, key_at, row_at):
         return tiled(exps[slot][key_at, row_at]) * fracs[slot, stat(key_at), row_at][None]
 
     def grad_chains(before, piece):
-        def chain(u, r, key_at, row_at):
-            dprob = tiled(dprobs[piece % 2][u : u + SUB, r : r + SUB])
-            sgrad = frac(before, key_at, row_at) * (dprob - deltas[before, :, row_at][None])
-            sgrads[key_at, row_at] = sgrad.reshape(SUB, SUB).astype(BF16)
-
-        return [functools.partial(chain, *block) for block in blocks(piece)]
+        def chain(u, r):
+            dprob = dot(values[u : u + WIDE, :], grad_t[before, :, r : r + WIDE])
+            for at, key_at, row_at in inner(u, r):
+                sgrad = tiled(dprob[at]) - deltas[before, :, row_at][None]
+                sgrad = frac(before, key_at, row_at) * sgrad
+                sgrads[key_at, row_at] = sgrad.reshape(SUB, SUB).astype(BF16)
+
+        return [functools.partial(chain, *unit) for unit in units(piece)]
 
     def weight_chains(now, piece):
         def chain(u, r, key_at, row_at):
@@ -211,19 +199,13 @@
 
     def run(now, with_score, with_grad):
         before = 1 - now
-        for stage in range(-1, count):
+        for stage in range(count):
             products, chains = [], []
-            if stage + 1 < count:
-                if with_score:
-                    products += score_products(now, stage + 1)
-                if with_grad:
-                    products += dprob_products(before, stage + 1)
             if stage >= 1 and with_grad:
                 products += grad_products(before, stage - 1)
-            if stage >= 0:
-                both = [score_chains(now, stage)] if with_score else []
-                both += [grad_chains(before, stage)] if with_grad else []
-                chains = [chain for pair in zip(*both) for chain in pair]
+            both = [score_chains(now, stage)] if with_score else []
+            both += [grad_chains(before, stage)] if with_grad else []
+            chains = [chain for pair in zip(*both) for chain in pair]
             weave(products, chains)
         products = []
         if with_grad:
@@ -294,14 +276,15 @@
     def __init__(self, members, part_rows):
         self.members, self.part_rows = members, part_rows
         self.prompt_rows = members * part_rows
+        self.share = part_rows // 2
         self.caches, self.dcaches = 1, members + 1
 
     def cache_shapes(self):
         return [(self.members, 2, self.part_rows, HD)]
 
     def dcache_shapes(self):
-        part = (self.part_rows, HD)
-        return [part] * self.members + [(self.members, *part)]
+        shape = (self.part_rows + self.share, HD)
+        return [shape] * self.members + [(self.members, self.part_rows - self.share, HD)]
 
     def load(self, caches):
         for m in range(self.members):
@@ -311,10 +294,11 @@
     def store(self, dcaches, dk_sum, dv_sum, factor):
         me = lax.axis_index("resp")
         for shift in range(self.members):
-            part = lax.rem(me + shift, self.members) * self.part_rows
-            at = pl.ds(pl.multiple_of(part, self.part_rows), self.part_rows)
-            dcaches[shift][...] = (factor * dk_sum[at, :]).astype(BF16)
-            at = pl.ds(shift * self.part_rows, self.part_rows)
+            part = pl.multiple_of(lax.rem(me + shift, self.members) * self.part_rows, self.part_rows)
+            key_at, value_at = pl.ds(part, self.part_rows), pl.ds(part, self.share)
+            dcaches[shift][: self.part_rows, :] = (factor * dk_sum[key_at, :]).astype(BF16)
+            dcaches[shift][self.part_rows :, :] = dv_sum[value_at, :].astype(BF16)
+            at = pl.ds(shift * self.part_rows + self.share, self.part_rows - self.share)
             dcaches[self.members][shift] = dv_sum[at, :].astype(BF16)
 
 
@@ -396,10 +380,6 @@
             pltpu.VMEM((total_rows, rows), BF16),
             pltpu.VMEM((total_rows, rows), BF16),
             pltpu.VMEM((total_rows, rows), BF16),
-            pltpu.VMEM((rows, rows), F32),
-            pltpu.VMEM((rows, rows), F32),
-            pltpu.VMEM((rows, rows), F32),
-            pltpu.VMEM((rows, rows), F32),
             pltpu.VMEM((2, stats, rows), F32),
             pltpu.VMEM((2, 8, rows), F32),
             pltpu.VMEM((total_rows, HD), F32),
@@ -533,9 +513,10 @@
             arrived = [dcaches[0]] + [
                 send(dcaches[shift], members, shift) for shift in range(1, members)
             ]
-            dkey = sum(block.astype(F32) for block in arrived).astype(BF16)
-            dvalue = lax.psum_scatter(dcaches[members], "resp", scatter_dimension=0)
-            totals.append(jnp.stack([dkey, dvalue]))
+            both = sum(block.astype(F32) for block in arrived).astype(BF16)
+            rest = lax.psum_scatter(dcaches[members], "resp", scatter_dimension=0)
+            both = jnp.concatenate([both, rest], axis=0)
+            totals.append(both.reshape(2, ranks * own_rows, HD))
     blocks = [block for total in totals for block in swap(cut_rows(total, ranks))]
     key_grad, value_grad = place(blocks, pairs, columns)
     return (*(a[None] for a in earlier), key_grad, value_grad)

time: 164 us -> 160 us (0.976)
  Pallas kernels: 81.5 us -> 77.6 us
    pallas_call x2, Pallas kernels: 77.5 us -> 73.5 us  [attend(): pl.pallas_call(functools.partial(attention_kernel, layout, heads_per, len...]
    ppermute x6, waiting for transfers between devices: 21.1 us -> 24.9 us  [send(): lax.ppermute(block, 'resp', [(m, (m + shift) % members) for m in range(me...]
    reduce_scatter x1, waiting for transfers between devices: 7.58 us -> 4.57 us  [per_device(): rest = lax.psum_scatter(dcaches[members], 'resp', scatter_dimension=0)]
    another operation x2 -> x0, other arithmetic: 2.43 us -> none  [per_device(): totals.append(jnp.stack([dkey, dvalue]))]
  transfers between devices with their start and end apart: 21 -> 21, of which waited for: 10 -> 11; matrix products, arithmetic and copies ran while one was open for 3% -> 4% of each run, Pallas kernels for 47% -> 46%
where the time goes in v12:
time: 160 us
  Pallas kernels  77.6 us (48%)
  waiting for transfers between devices  40.7 us (25%)
  starting transfers between devices  19.6 us (12%)
  between operations  14.6 us (9%)
  other arithmetic  4.32 us (3%)
  local copies, waits for them, and re-layouts  2.88 us (2%)
    pallas_call x2, Pallas kernels, attend(): pl.pallas_call(functools.partial(attention_kernel, layout, heads_per, len...  73.5 us
    ppermute x6, waiting for transfers between devices, send(): lax.ppermute(block, 'resp', [(m, (m + shift) % members) for m in range(me...  24.9 us
    ppermute x12, waiting for transfers between devices, swap(): lax.ppermute(blocks[i], 'tensor', [(j, j ^ i) for j in range(count)])  11.2 us
    ppermute x6, starting transfers between devices, send(): lax.ppermute(block, 'resp', [(m, (m + shift) % members) for m in range(me...  10.5 us
    ppermute x12, starting transfers between devices, swap(): lax.ppermute(blocks[i], 'tensor', [(j, j ^ i) for j in range(count)])  9.04 us
    reduce_scatter x1, waiting for transfers between devices, per_device(): rest = lax.psum_scatter(dcaches[members], 'resp', scatter_dimension=0)  4.57 us
  transfers between devices with their start and end apart: 21, of which 11 were waited for; matrix products, arithmetic and copies ran while one was open for 4% of the time, Pallas kernels for 46%

profile of v12, /device:TPU:0, one launch (start us, length us, event | category | flops | bytes accessed | tf_op | source)
XLA Modules:
  0.0 159.7 jit_solution(6321898004847977611)
XLA Ops:
  7.2 0.0 all-gather.3.cloned.1.call-start
  7.2 1.9 %cut.1 = (bf16[2,128,128]{2,1,0:T(8,128)(2,1)}, bf16[2,128,128]{2,1,0:T(8,128)(2,1)}, bf16[2,128,128]{2,1,0:T(8,128)(2,1)}, bf16[2,128,128]{2,1,0:T(8,128)(2,1)}...) custom-call(bf16[128,1024]{1,0:T(8,128)(2,1)} %k_ref.1, ...), custom_call_target="tpu_custom_call" | custom-call | tf_op jit(solution)/shard_map/cut/pallas_call | solution.py:420
  9.2 0.5 collective-permute-start
  9.6 2.5 %collective-permute-start.1 = (bf16[2,128,128]{2,1,0:T(8,128)(2,1)}, bf16[2,128,128]{2,1,0:T(8,128)(2,1)S(1)}, u32[]{:S(2)}, u32[]{:S(2)}) collective-permute-start(bf16[2,128,128]{2,1,0:T(8,128)(2,1)} %get-tuple-element.48), channel_id=1, source_target_pairs={{0,2},{1,3},{2,0},{3,1},{4,6},{5,7},{6,4},{7,5},{8,10},{9,11},{10,... | collective-permute-start | bytes 196616 | tf_op jit(solution)/shard_map/ppermute | solution.py:456
  12.1 0.1 collective-permute-start.2
  12.2 0.0 collective-permute-done
  12.2 2.8 %collective-permute-done.1 = bf16[2,128,128]{2,1,0:T(8,128)(2,1)S(1)} collective-permute-done((bf16[2,128,128]{2,1,0:T(8,128)(2,1)}, bf16[2,128,128]{2,1,0:T(8,128)(2,1)S(1)}, u32[]{:S(2)}, u32[]{:S(2)}) %collective-permute-start.1) | collective-permute-done | bytes 65568 | tf_op jit(solution)/shard_map/ppermute | solution.py:456
  15.1 1.4 collective-permute-done.2
  16.5 0.9 pad_maximum_fusion.rest_0_
  17.3 0.0 copy-start
  17.3 3.7 %collective-permute-start.8 = (bf16[2,512,128]{2,1,0:T(8,128)(2,1)S(1)}, bf16[2,512,128]{2,1,0:T(8,128)(2,1)S(1)}, u32[]{:S(2)}, u32[]{:S(2)}) collective-permute-start(bf16[2,512,128]{2,1,0:T(8,128)(2,1)S(1)} %pad_maximum_fusion.rest_0_), channel_id=1, source_target_pairs={{0,12},{4,0},{8,4},{12,8},{1,13},{5,1},{9,5},{13,9},{2,14},{6,2},{... | collective-permute-start | bytes 786440 | tf_op jit(solution)/shard_map/ppermute | solution.py:462
  21.0 0.0 collective-permute-start.7
  21.0 1.0 collective-permute-start.6
  22.0 0.0 collective-permute-start.3
  22.0 1.3 collective-permute-start.4
  23.3 0.1 collective-permute-done.3
  23.5 1.1 collective-permute-start.5
  24.6 2.2 %collective-permute-done.4 = bf16[2,128,128]{2,1,0:T(8,128)(2,1)S(1)} collective-permute-done((bf16[2,128,128]{2,1,0:T(8,128)(2,1)}, bf16[2,128,128]{2,1,0:T(8,128)(2,1)S(1)}, u32[]{:S(2)}, u32[]{:S(2)}) %collective-permute-start.4) | collective-permute-done | bytes 65568 | tf_op jit(solution)/shard_map/ppermute | solution.py:456
  26.8 1.1 collective-permute-done.5
  27.8 1.6 pad_maximum_fusion.1
  29.4 0.0 collective-permute-done.8.rest_3_
  29.4 14.2 %collective-permute-done.7.rest_2_ = bf16[2,512,128]{2,1,0:T(8,128)(2,1)S(1)} collective-permute-done((bf16[2,512,128]{2,1,0:T(8,128)(2,1)S(1)}, bf16[2,512,128]{2,1,0:T(8,128)(2,1)S(1)}, u32[]{:S(2)}, u32[]{:S(2)}) %collective-permute-start.7) | collective-permute-done | bytes 262176 | tf_op jit(solution)/shard_map/ppermute | solution.py:462
  43.6 0.0 collective-permute-done.6.rest_1_
  43.6 0.0 all-gather.3.cloned.1.call-update
  43.6 0.0 reduce-scatter.3.cloned.1.call-start
  44.3 0.0 copy-done
  44.4 0.0 copy-done.7
  44.4 0.0 copy-done.8
  44.4 0.0 copy-done.9
  44.4 36.5 %attend_pair_0.1 = (bf16[512,2048]{1,0:T(8,128)(2,1)}, bf16[512,2048]{1,0:T(8,128)(2,1)}, bf16[512,256]{1,0:T(8,128)(2,1)}, bf16[512,256]{1,0:T(8,128)(2,1)}, bf16[4,2,512,128]{3,2,1,0:T(8,128)(2,1)}) custom-call(s32[1]{0:T(128)S(6)} %copy.21.len_ref, bf16[512,2048]{1,0:T(8,128)(2,1)} %bitcast.15, bf16[512,2048]{1,0:T(8,128)(2,1)} %bitcast.17, ...), custom_call_target="tpu_custom_call" | custom-call | flops 16106127360 | bytes 4194304 | tf_op jit(solution)/shard_map/attend_pair_0/pallas_call | solution.py:357
  80.9 0.0 reduce-scatter.3.cloned.1.call-update
  81.0 0.0 reduce-scatter.5.cloned.1.call-start
  81.0 0.0 all-gather.3.cloned.1.call-done
  81.0 37.0 %attend_pair_1.1 = (bf16[512,2048]{1,0:T(8,128)(2,1)}, bf16[512,2048]{1,0:T(8,128)(2,1)}, bf16[512,256]{1,0:T(8,128)(2,1)}, bf16[512,256]{1,0:T(8,128)(2,1)}, bf...) custom-call(s32[1]{0:T(128)S(6)} %copy.21.len_ref, ...), custom_call_target="tpu_custom_call", output_to_operand_aliasing={{0}: (6, {}), {1}: (7, {}), {2}: (8, {}), {3}: (9, {})} | custom-call | flops 16106127360 | bytes 4194304 | tf_op jit(solution)/shard_map/attend_pair_1/pallas_call | solution.py:357
  118.0 0.0 reduce-scatter.3.cloned.1.call-done
  118.1 0.0 reduce-scatter.5.cloned.1.call-update
  118.1 0.9 collective-permute-start.12
  119.0 2.0 %collective-permute-start.13 = (bf16[768,128]{1,0:T(8,128)(2,1)}, bf16[768,128]{1,0:T(8,128)(2,1)S(1)}, u32[]{:S(2)}, u32[]{:S(2)}) collective-permute-start(bf16[768,128]{1,0:T(8,128)(2,1)} %get-tuple-element.81), channel_id=1, source_target_pairs={{0,8},{4,12},{8,0},{12,4},{1,9},{5,13},{9,1},{13,5},{2,10},{6,14},... | collective-permute-start | bytes 589832 | tf_op jit(solution)/shard_map/ppermute | solution.py:462
  121.0 2.8 %collective-permute-start.14 = (bf16[768,128]{1,0:T(8,128)(2,1)}, bf16[768,128]{1,0:T(8,128)(2,1)S(1)}, u32[]{:S(2)}, u32[]{:S(2)}) collective-permute-start(bf16[768,128]{1,0:T(8,128)(2,1)} %get-tuple-element.82), channel_id=1, source_target_pairs={{0,12},{4,0},{8,4},{12,8},{1,13},{5,1},{9,5},{13,9},{2,14},{6,2},{... | collective-permute-start | bytes 589832 | tf_op jit(solution)/shard_map/ppermute | solution.py:462
  123.9 1.6 fusion.1
  125.5 0.0 collective-permute-start.11
  125.5 1.5 collective-permute-start.10
  127.0 1.1 collective-permute-done.12
  128.1 0.0 collective-permute-start.9
  128.1 9.6 %collective-permute-done.13 = bf16[768,128]{1,0:T(8,128)(2,1)S(1)} collective-permute-done((bf16[768,128]{1,0:T(8,128)(2,1)}, bf16[768,128]{1,0:T(8,128)(2,1)S(1)}, u32[]{:S(2)}, u32[]{:S(2)}) %collective-permute-start.13) | collective-permute-done | bytes 196640 | tf_op jit(solution)/shard_map/ppermute | solution.py:462
  137.7 0.0 collective-permute-done.14
  137.7 1.0 add_convert_fusion
  138.7 4.6 %reduce-scatter.5.cloned.1.call-done = bf16[1,256,128]{2,1,0:T(8,128)(2,1)} async-done(((bf16[4,256,128]{2,1,0:T(8,128)(2,1)}), bf16[1,256,128]{2,1,0:T(8,128)(2,1)}) %reduce-scatter.5.cloned.1.call-update) | async-done | bytes 65552 | tf_op jit(solution)/shard_map/reduce_scatter | solution.py:517
  143.3 0.9 pad_maximum_fusion.2
  144.2 0.6 fusion
  144.8 0.0 collective-permute-start.17
  144.8 1.9 %collective-permute-start.16 = (bf16[2,128,128]{2,1,0:T(8,128)(2,1)S(1)}, bf16[2,128,128]{2,1,0:T(8,128)(2,1)S(1)}, u32[]{:S(2)}, u32[]{:S(2)}) collective-permute-start(bf16[2,128,128]{2,1,0:T(8,128)(2,1)S(1)} %get-tuple-element.87), channel_id=1, source_target_pairs={{0,2},{1,3},{2,0},{3,1},{4,6},{5,7},{6,4},{7,5},{8,10},{9,11},{10,... | collective-permute-start | bytes 196616 | tf_op jit(solution)/shard_map/ppermute | solution.py:456
  146.7 0.0 collective-permute-done.11.refs_3_
  146.7 0.2 collective-permute-start.15
  146.9 0.0 collective-permute-done.10.refs_2_
  146.9 0.0 collective-permute-done.9.refs_1_
  146.9 0.0 copy-start.3
  146.9 2.0 %collective-permute-done.17.refs_7_ = bf16[2,128,128]{2,1,0:T(8,128)(2,1)S(1)} collective-permute-done((bf16[2,128,128]{2,1,0:T(8,128)(2,1)S(1)}, bf16[2,128,128]{2,1,0:T(8,128)(2,1)S(1)}, u32[]{:S(2)}, u32[]{:S(2)}) %collective-permute-start.17) | collective-permute-done | bytes 65568 | tf_op jit(solution)/shard_map/ppermute | solution.py:456
  148.9 1.5 collective-permute-done.16.refs_6_
  150.4 0.0 collective-permute-done.15.refs_5_
  150.4 0.0 copy-done.1
  150.5 0.6 copy-done.5
  151.0 0.0 copy-done.6
  151.1 2.1 %place.1 = (f32[128,1024]{1,0:T(8,128)}, f32[128,1024]{1,0:T(8,128)}) custom-call(bf16[2,128,128]{2,1,0:T(8,128)(2,1)} %get-tuple-element.93.refs_0_, bf16[2,128,128]{2,1,0:T(8,128)(2,1)} %copy-done.3, bf16[2,128,128]{2,1,0:T(8,128)(2,1)} %copy-done.2, bf16[2,128,128]{2,1,0:T(8,128)(2,1)} %copy-done.1, bf16[2,128,128]{2,1,0:T(8,128)(2,1)} %get-tuple-element.89.refs_4_, ...), custom_call_target="tpu_custom_call" | custom-call | tf_op jit(solution)/shard_map/place/pallas_call | solution.py:444
  (11 shorter events, 0.0 us)
Async XLA Ops:
  7.2 73.9 %all-gather.3.cloned.1.call-start = ((), (), s32[]{:S(2)}) async-start(), calls=%async_computation.4 | async-start | bytes 1310720 | tf_op jit(solution)/shard_map/all_gather | solution.py:491
  9.2 3.1 %collective-permute-start = (bf16[2,128,128]{2,1,0:T(8,128)(2,1)}, bf16[2,128,128]{2,1,0:T(8,128)(2,1)S(1)}, u32[]{:S(2)}, u32[]{:S(2)}) collective-permute-start(bf16[2,128,128]{2,1,0:T(8,128)(2,1)} %get-tuple-element.47), channel_id=1, source_target_pairs={{0,1},{1,0},{2,3},{3,2},{4,5},{5,4},{6,7},{7,6},{8,9},{9,8},{10,11... | collective-permute-start | bytes 196616 | tf_op jit(solution)/shard_map/ppermute | solution.py:456
  9.6 5.5 %collective-permute-start.1 = (bf16[2,128,128]{2,1,0:T(8,128)(2,1)}, bf16[2,128,128]{2,1,0:T(8,128)(2,1)S(1)}, u32[]{:S(2)}, u32[]{:S(2)}) collective-permute-start(bf16[2,128,128]{2,1,0:T(8,128)(2,1)} %get-tuple-element.48), channel_id=1, source_target_pairs={{0,2},{1,3},{2,0},{3,1},{4,6},{5,7},{6,4},{7,5},{8,10},{9,11},{10,... | collective-permute-start | bytes 196616 | tf_op jit(solution)/shard_map/ppermute | solution.py:456
  12.1 4.3 %collective-permute-start.2 = (bf16[2,128,128]{2,1,0:T(8,128)(2,1)}, bf16[2,128,128]{2,1,0:T(8,128)(2,1)S(1)}, u32[]{:S(2)}, u32[]{:S(2)}) collective-permute-start(bf16[2,128,128]{2,1,0:T(8,128)(2,1)} %get-tuple-element.49), channel_id=1, source_target_pairs={{0,3},{1,2},{2,1},{3,0},{4,7},{5,6},{6,5},{7,4},{8,11},{9,10},{10,... | collective-permute-start | bytes 196616 | tf_op jit(solution)/shard_map/ppermute | solution.py:456
  17.3 27.0 %copy-start = (bf16[2,512,128]{2,1,0:T(8,128)(2,1)}, bf16[2,512,128]{2,1,0:T(8,128)(2,1)S(1)}, u32[]{:S(2)}) copy-start(bf16[2,512,128]{2,1,0:T(8,128)(2,1)S(1)} %pad_maximum_fusion.rest_0_) | copy-start | bytes 786436
  17.3 12.1 %collective-permute-start.8 = (bf16[2,512,128]{2,1,0:T(8,128)(2,1)S(1)}, bf16[2,512,128]{2,1,0:T(8,128)(2,1)S(1)}, u32[]{:S(2)}, u32[]{:S(2)}) collective-permute-start(bf16[2,512,128]{2,1,0:T(8,128)(2,1)S(1)} %pad_maximum_fusion.rest_0_), channel_id=1, source_target_pairs={{0,12},{4,0},{8,4},{12,8},{1,13},{5,1},{9,5},{13,9},{2,14},{6,2},{... | collective-permute-start | bytes 786440 | tf_op jit(solution)/shard_map/ppermute | solution.py:462
  21.0 22.6 %collective-permute-start.7 = (bf16[2,512,128]{2,1,0:T(8,128)(2,1)S(1)}, bf16[2,512,128]{2,1,0:T(8,128)(2,1)S(1)}, u32[]{:S(2)}, u32[]{:S(2)}) collective-permute-start(bf16[2,512,128]{2,1,0:T(8,128)(2,1)S(1)} %pad_maximum_fusion.rest_0_), channel_id=1, source_target_pairs={{0,8},{4,12},{8,0},{12,4},{1,9},{5,13},{9,1},{13,5},{2,10},{6,14},... | collective-permute-start | bytes 786440 | tf_op jit(solution)/shard_map/ppermute | solution.py:462
  21.0 22.6 %collective-permute-start.6 = (bf16[2,512,128]{2,1,0:T(8,128)(2,1)S(1)}, bf16[2,512,128]{2,1,0:T(8,128)(2,1)S(1)}, u32[]{:S(2)}, u32[]{:S(2)}) collective-permute-start(bf16[2,512,128]{2,1,0:T(8,128)(2,1)S(1)} %pad_maximum_fusion.rest_0_), channel_id=1, source_target_pairs={{0,4},{4,8},{8,12},{12,0},{1,5},{5,9},{9,13},{13,1},{2,6},{6,10},{... | collective-permute-start | bytes 786440 | tf_op jit(solution)/shard_map/ppermute | solution.py:462
  22.0 1.5 collective-permute-start.3
  22.0 4.8 %collective-permute-start.4 = (bf16[2,128,128]{2,1,0:T(8,128)(2,1)}, bf16[2,128,128]{2,1,0:T(8,128)(2,1)S(1)}, u32[]{:S(2)}, u32[]{:S(2)}) collective-permute-start(bf16[2,128,128]{2,1,0:T(8,128)(2,1)} %get-tuple-element.56), channel_id=1, source_target_pairs={{0,2},{1,3},{2,0},{3,1},{4,6},{5,7},{6,4},{7,5},{8,10},{9,11},{10,... | collective-permute-start | bytes 196616 | tf_op jit(solution)/shard_map/ppermute | solution.py:456
  23.5 4.4 %collective-permute-start.5 = (bf16[2,128,128]{2,1,0:T(8,128)(2,1)}, bf16[2,128,128]{2,1,0:T(8,128)(2,1)S(1)}, u32[]{:S(2)}, u32[]{:S(2)}) collective-permute-start(bf16[2,128,128]{2,1,0:T(8,128)(2,1)} %get-tuple-element.57), channel_id=1, source_target_pairs={{0,3},{1,2},{2,1},{3,0},{4,7},{5,6},{6,5},{7,4},{8,11},{9,10},{10,... | collective-permute-start | bytes 196616 | tf_op jit(solution)/shard_map/ppermute | solution.py:456
  29.4 15.0 %copy-start.7 = (bf16[2,512,128]{2,1,0:T(8,128)(2,1)}, bf16[2,512,128]{2,1,0:T(8,128)(2,1)S(1)}, u32[]{:S(2)}) copy-start(bf16[2,512,128]{2,1,0:T(8,128)(2,1)S(1)} %collective-permute-done.8.rest_3_) | copy-start | bytes 786436
  43.6 0.8 copy-start.8
  43.6 0.8 copy-start.9
  43.6 74.4 %reduce-scatter.3.cloned.1.call-start = ((), (), s32[]{:S(2)}) async-start(), calls=%async_computation.2 | async-start | bytes 1310720 | tf_op jit(solution)/shard_map/reduce_scatter | solution.py:511
  81.0 62.4 %reduce-scatter.5.cloned.1.call-start = ((), (), s32[]{:S(2)}) async-start(), calls=%async_computation.3 | async-start | bytes 327680 | tf_op jit(solution)/shard_map/reduce_scatter | solution.py:517
  118.1 10.0 %collective-permute-start.12 = (bf16[768,128]{1,0:T(8,128)(2,1)}, bf16[768,128]{1,0:T(8,128)(2,1)S(1)}, u32[]{:S(2)}, u32[]{:S(2)}) collective-permute-start(bf16[768,128]{1,0:T(8,128)(2,1)} %get-tuple-element.80), channel_id=1, source_target_pairs={{0,4},{4,8},{8,12},{12,0},{1,5},{5,9},{9,13},{13,1},{2,6},{6,10},{... | collective-permute-start | bytes 589832 | tf_op jit(solution)/shard_map/ppermute | solution.py:462
  119.0 18.6 %collective-permute-start.13 = (bf16[768,128]{1,0:T(8,128)(2,1)}, bf16[768,128]{1,0:T(8,128)(2,1)S(1)}, u32[]{:S(2)}, u32[]{:S(2)}) collective-permute-start(bf16[768,128]{1,0:T(8,128)(2,1)} %get-tuple-element.81), channel_id=1, source_target_pairs={{0,8},{4,12},{8,0},{12,4},{1,9},{5,13},{9,1},{13,5},{2,10},{6,14},... | collective-permute-start | bytes 589832 | tf_op jit(solution)/shard_map/ppermute | solution.py:462
  121.0 16.7 %collective-permute-start.14 = (bf16[768,128]{1,0:T(8,128)(2,1)}, bf16[768,128]{1,0:T(8,128)(2,1)S(1)}, u32[]{:S(2)}, u32[]{:S(2)}) collective-permute-start(bf16[768,128]{1,0:T(8,128)(2,1)} %get-tuple-element.82), channel_id=1, source_target_pairs={{0,12},{4,0},{8,4},{12,8},{1,13},{5,1},{9,5},{13,9},{2,14},{6,2},{... | collective-permute-start | bytes 589832 | tf_op jit(solution)/shard_map/ppermute | solution.py:462
  125.5 21.2 %collective-permute-start.11 = (bf16[2,128,128]{2,1,0:T(8,128)(2,1)S(1)}, bf16[2,128,128]{2,1,0:T(8,128)(2,1)S(1)}, u32[]{:S(2)}, u32[]{:S(2)}) collective-permute-start(bf16[2,128,128]{2,1,0:T(8,128)(2,1)S(1)} %get-tuple-element.90), channel_id=1, source_target_pairs={{0,3},{1,2},{2,1},{3,0},{4,7},{5,6},{6,5},{7,4},{8,11},{9,10},{10,... | collective-permute-start | bytes 196616 | tf_op jit(solution)/shard_map/ppermute | solution.py:456
  125.5 21.4 %collective-permute-start.10 = (bf16[2,128,128]{2,1,0:T(8,128)(2,1)S(1)}, bf16[2,128,128]{2,1,0:T(8,128)(2,1)S(1)}, u32[]{:S(2)}, u32[]{:S(2)}) collective-permute-start(bf16[2,128,128]{2,1,0:T(8,128)(2,1)S(1)} %get-tuple-element.91), channel_id=1, source_target_pairs={{0,2},{1,3},{2,0},{3,1},{4,6},{5,7},{6,4},{7,5},{8,10},{9,11},{10,... | collective-permute-start | bytes 196616 | tf_op jit(solution)/shard_map/ppermute | solution.py:456
  128.1 18.8 %collective-permute-start.9 = (bf16[2,128,128]{2,1,0:T(8,128)(2,1)S(1)}, bf16[2,128,128]{2,1,0:T(8,128)(2,1)S(1)}, u32[]{:S(2)}, u32[]{:S(2)}) collective-permute-start(bf16[2,128,128]{2,1,0:T(8,128)(2,1)S(1)} %get-tuple-element.92), channel_id=1, source_target_pairs={{0,1},{1,0},{2,3},{3,2},{4,5},{5,4},{6,7},{7,6},{8,9},{9,8},{10,11... | collective-permute-start | bytes 196616 | tf_op jit(solution)/shard_map/ppermute | solution.py:456
  144.8 4.1 %collective-permute-start.17 = (bf16[2,128,128]{2,1,0:T(8,128)(2,1)S(1)}, bf16[2,128,128]{2,1,0:T(8,128)(2,1)S(1)}, u32[]{:S(2)}, u32[]{:S(2)}) collective-permute-start(bf16[2,128,128]{2,1,0:T(8,128)(2,1)S(1)} %get-tuple-element.86), channel_id=1, source_target_pairs={{0,3},{1,2},{2,1},{3,0},{4,7},{5,6},{6,5},{7,4},{8,11},{9,10},{10,... | collective-permute-start | bytes 196616 | tf_op jit(solution)/shard_map/ppermute | solution.py:456
  144.8 5.6 %collective-permute-start.16 = (bf16[2,128,128]{2,1,0:T(8,128)(2,1)S(1)}, bf16[2,128,128]{2,1,0:T(8,128)(2,1)S(1)}, u32[]{:S(2)}, u32[]{:S(2)}) collective-permute-start(bf16[2,128,128]{2,1,0:T(8,128)(2,1)S(1)} %get-tuple-element.87), channel_id=1, source_target_pairs={{0,2},{1,3},{2,0},{3,1},{4,6},{5,7},{6,4},{7,5},{8,10},{9,11},{10,... | collective-permute-start | bytes 196616 | tf_op jit(solution)/shard_map/ppermute | solution.py:456
  146.7 3.7 %copy-start.1 = (bf16[2,128,128]{2,1,0:T(8,128)(2,1)}, bf16[2,128,128]{2,1,0:T(8,128)(2,1)S(1)}, u32[]{:S(2)}) copy-start(bf16[2,128,128]{2,1,0:T(8,128)(2,1)S(1)} %collective-permute-done.11.refs_3_) | copy-start | bytes 196612
  146.7 3.7 %collective-permute-start.15 = (bf16[2,128,128]{2,1,0:T(8,128)(2,1)S(1)}, bf16[2,128,128]{2,1,0:T(8,128)(2,1)S(1)}, u32[]{:S(2)}, u32[]{:S(2)}) collective-permute-start(bf16[2,128,128]{2,1,0:T(8,128)(2,1)S(1)} %get-tuple-element.88), channel_id=1, source_target_pairs={{0,1},{1,0},{2,3},{3,2},{4,5},{5,4},{6,7},{7,6},{8,9},{9,8},{10,11... | collective-permute-start | bytes 196616 | tf_op jit(solution)/shard_map/ppermute | solution.py:456
  146.9 3.6 %copy-start.2 = (bf16[2,128,128]{2,1,0:T(8,128)(2,1)}, bf16[2,128,128]{2,1,0:T(8,128)(2,1)S(1)}, u32[]{:S(2)}) copy-start(bf16[2,128,128]{2,1,0:T(8,128)(2,1)S(1)} %collective-permute-done.10.refs_2_) | copy-start | bytes 196612
  146.9 3.6 %copy-start.3 = (bf16[2,128,128]{2,1,0:T(8,128)(2,1)}, bf16[2,128,128]{2,1,0:T(8,128)(2,1)S(1)}, u32[]{:S(2)}) copy-start(bf16[2,128,128]{2,1,0:T(8,128)(2,1)S(1)} %collective-permute-done.9.refs_1_) | copy-start | bytes 196612
  148.9 1.6 copy-start.4
  150.4 0.6 copy-start.5
  150.4 0.6 copy-start.6
Sparse Core Ops, SparseCore 0:
  43.7 28.3 all-gather.2
  81.1 27.5 reduce-scatter.2
  118.2 25.0 reduce-scatter.4

commit v13 on v12

--- a/solution.py
+++ b/solution.py
@@ -105,18 +105,18 @@
 
     def units(piece):
         at, size, row = pieces[piece]
-        return [(u, r) for r in range(row, rows, WIDE) for u in range(at, at + size, WIDE)]
-
-    def inner(u, r):
-        for du in range(0, WIDE, SUB):
+        return [(at, size, r) for r in range(row, rows, WIDE)]
+
+    def inner(u, size, r):
+        for du in range(0, size, SUB):
             for dr in range(0, WIDE, SUB):
                 block = (slice(du, du + SUB), slice(dr, dr + SUB))
                 yield block, slice(u + du, u + du + SUB), slice(r + dr, r + dr + SUB)
 
     def score_chains(now, piece):
-        def chain(u, r):
-            score = dot(keys[u : u + WIDE, :], query_t[now, :, r : r + WIDE])
-            for at, key_at, row_at in inner(u, r):
+        def chain(u, size, r):
+            score = dot(keys[u : u + size, :], query_t[now, :, r : r + WIDE])
+            for at, key_at, row_at in inner(u, size, r):
                 block = score[at]
                 if key_at.start >= prompt_rows:
                     j = lax.broadcasted_iota(jnp.int32, (SUB, SUB), 0) + key_at.start - prompt_rows
@@ -135,9 +135,9 @@
         return tiled(exps[slot][key_at, row_at]) * fracs[slot, stat(key_at), row_at][None]
 
     def grad_chains(before, piece):
-        def chain(u, r):
-            dprob = dot(values[u : u + WIDE, :], grad_t[before, :, r : r + WIDE])
-            for at, key_at, row_at in inner(u, r):
+        def chain(u, size, r):
+            dprob = dot(values[u : u + size, :], grad_t[before, :, r : r + WIDE])
+            for at, key_at, row_at in inner(u, size, r):
                 sgrad = tiled(dprob[at]) - deltas[before, :, row_at][None]
                 sgrad = frac(before, key_at, row_at) * sgrad
                 sgrads[key_at, row_at] = sgrad.reshape(SUB, SUB).astype(BF16)
@@ -515,9 +515,16 @@
             ]
             both = sum(block.astype(F32) for block in arrived).astype(BF16)
             rest = lax.psum_scatter(dcaches[members], "resp", scatter_dimension=0)
-            both = jnp.concatenate([both, rest], axis=0)
-            totals.append(both.reshape(2, ranks * own_rows, HD))
-    blocks = [block for total in totals for block in swap(cut_rows(total, ranks))]
+            parts = ranks * own_rows
+            keys, both = both[:parts], both[parts:]
+            split = both.shape[0] // own_rows
+            values = [both[i * own_rows : (i + 1) * own_rows] for i in range(split)]
+            values += [rest[i * own_rows : (i + 1) * own_rows] for i in range(ranks - split)]
+            pieces = [keys[i * own_rows : (i + 1) * own_rows] for i in range(ranks)]
+            totals.append([jnp.stack(both) for both in zip(pieces, values)])
+    blocks = []
+    for total in totals:
+        blocks += swap(total if isinstance(total, list) else cut_rows(total, ranks))
     key_grad, value_grad = place(blocks, pairs, columns)
     return (*(a[None] for a in earlier), key_grad, value_grad)
 

time: 160 us -> 161 us (level)
  Pallas kernels: 77.6 us -> 79.5 us
    pallas_call x2, Pallas kernels: 73.5 us -> 75.4 us  [attend(): pl.pallas_call(functools.partial(attention_kernel, layout, heads_per, len...]
  transfers between devices with their start and end apart: 21 -> 21, of which waited for: 11 -> 11; matrix products, arithmetic and copies ran while one was open for 4% -> 4% of each run, Pallas kernels for 46% -> 47%
where the time goes in v13:
time: 161 us
  Pallas kernels  79.5 us (49%)
  waiting for transfers between devices  40.2 us (25%)
  starting transfers between devices  19.6 us (12%)
  between operations  14.6 us (9%)
  other arithmetic  4.12 us (3%)
  local copies, waits for them, and re-layouts  3.03 us (2%)
    pallas_call x2, Pallas kernels, attend(): pl.pallas_call(functools.partial(attention_kernel, layout, heads_per, len...  75.4 us
    ppermute x6, waiting for transfers between devices, send(): lax.ppermute(block, 'resp', [(m, (m + shift) % members) for m in range(me...  24.9 us
    ppermute x12, waiting for transfers between devices, swap(): lax.ppermute(blocks[i], 'tensor', [(j, j ^ i) for j in range(count)])  10.7 us
    ppermute x6, starting transfers between devices, send(): lax.ppermute(block, 'resp', [(m, (m + shift) % members) for m in range(me...  10.5 us
    ppermute x12, starting transfers between devices, swap(): lax.ppermute(blocks[i], 'tensor', [(j, j ^ i) for j in range(count)])  8.99 us
    reduce_scatter x1, waiting for transfers between devices, per_device(): rest = lax.psum_scatter(dcaches[members], 'resp', scatter_dimension=0)  4.45 us
  transfers between devices with their start and end apart: 21, of which 11 were waited for; matrix products, arithmetic and copies ran while one was open for 4% of the time, Pallas kernels for 47%

profile of v13, /device:TPU:0, one launch (start us, length us, event | category | flops | bytes accessed | tf_op | source)
XLA Modules:
  0.0 161.0 jit_solution(2669613117499389007)
XLA Ops:
  7.2 0.0 all-gather.3.cloned.1.call-start
  7.2 1.9 %cut.1 = (bf16[2,128,128]{2,1,0:T(8,128)(2,1)}, bf16[2,128,128]{2,1,0:T(8,128)(2,1)}, bf16[2,128,128]{2,1,0:T(8,128)(2,1)}, bf16[2,128,128]{2,1,0:T(8,128)(2,1)}...) custom-call(bf16[128,1024]{1,0:T(8,128)(2,1)} %k_ref.1, ...), custom_call_target="tpu_custom_call" | custom-call | tf_op jit(solution)/shard_map/cut/pallas_call | solution.py:420
  9.2 0.5 collective-permute-start
  9.6 2.5 %collective-permute-start.1 = (bf16[2,128,128]{2,1,0:T(8,128)(2,1)}, bf16[2,128,128]{2,1,0:T(8,128)(2,1)S(1)}, u32[]{:S(2)}, u32[]{:S(2)}) collective-permute-start(bf16[2,128,128]{2,1,0:T(8,128)(2,1)} %get-tuple-element.48), channel_id=1, source_target_pairs={{0,2},{1,3},{2,0},{3,1},{4,6},{5,7},{6,4},{7,5},{8,10},{9,11},{10,... | collective-permute-start | bytes 196616 | tf_op jit(solution)/shard_map/ppermute | solution.py:456
  12.1 0.1 collective-permute-start.2
  12.2 0.0 collective-permute-done
  12.2 2.8 %collective-permute-done.1 = bf16[2,128,128]{2,1,0:T(8,128)(2,1)S(1)} collective-permute-done((bf16[2,128,128]{2,1,0:T(8,128)(2,1)}, bf16[2,128,128]{2,1,0:T(8,128)(2,1)S(1)}, u32[]{:S(2)}, u32[]{:S(2)}) %collective-permute-start.1) | collective-permute-done | bytes 65568 | tf_op jit(solution)/shard_map/ppermute | solution.py:456
  15.1 1.4 collective-permute-done.2
  16.5 0.9 pad_maximum_fusion.rest_0_
  17.3 0.0 copy-start
  17.3 3.7 %collective-permute-start.8 = (bf16[2,512,128]{2,1,0:T(8,128)(2,1)S(1)}, bf16[2,512,128]{2,1,0:T(8,128)(2,1)S(1)}, u32[]{:S(2)}, u32[]{:S(2)}) collective-permute-start(bf16[2,512,128]{2,1,0:T(8,128)(2,1)S(1)} %pad_maximum_fusion.rest_0_), channel_id=1, source_target_pairs={{0,12},{4,0},{8,4},{12,8},{1,13},{5,1},{9,5},{13,9},{2,14},{6,2},{... | collective-permute-start | bytes 786440 | tf_op jit(solution)/shard_map/ppermute | solution.py:462
  21.0 0.0 collective-permute-start.7
  21.0 1.0 collective-permute-start.6
  22.0 0.0 collective-permute-start.3
  22.0 1.3 collective-permute-start.4
  23.3 0.2 collective-permute-done.3
  23.5 1.1 collective-permute-start.5
  24.5 2.2 %collective-permute-done.4 = bf16[2,128,128]{2,1,0:T(8,128)(2,1)S(1)} collective-permute-done((bf16[2,128,128]{2,1,0:T(8,128)(2,1)}, bf16[2,128,128]{2,1,0:T(8,128)(2,1)S(1)}, u32[]{:S(2)}, u32[]{:S(2)}) %collective-permute-start.4) | collective-permute-done | bytes 65568 | tf_op jit(solution)/shard_map/ppermute | solution.py:456
  26.8 1.1 collective-permute-done.5
  27.8 1.6 pad_maximum_fusion.1
  29.4 0.0 collective-permute-done.8.rest_3_
  29.4 14.2 %collective-permute-done.7.rest_2_ = bf16[2,512,128]{2,1,0:T(8,128)(2,1)S(1)} collective-permute-done((bf16[2,512,128]{2,1,0:T(8,128)(2,1)S(1)}, bf16[2,512,128]{2,1,0:T(8,128)(2,1)S(1)}, u32[]{:S(2)}, u32[]{:S(2)}) %collective-permute-start.7) | collective-permute-done | bytes 262176 | tf_op jit(solution)/shard_map/ppermute | solution.py:462
  43.6 0.0 collective-permute-done.6.rest_1_
  43.6 0.0 all-gather.3.cloned.1.call-update
  43.6 0.0 reduce-scatter.3.cloned.1.call-start
  44.4 0.0 copy-done
  44.4 0.0 copy-done.7
  44.4 0.0 copy-done.8
  44.4 0.0 copy-done.9
  44.4 37.5 %attend_pair_0.1 = (bf16[512,2048]{1,0:T(8,128)(2,1)}, bf16[512,2048]{1,0:T(8,128)(2,1)}, bf16[512,256]{1,0:T(8,128)(2,1)}, bf16[512,256]{1,0:T(8,128)(2,1)}, bf16[4,2,512,128]{3,2,1,0:T(8,128)(2,1)}) custom-call(s32[1]{0:T(128)S(6)} %copy.21.len_ref, bf16[512,2048]{1,0:T(8,128)(2,1)} %bitcast.23, bf16[512,2048]{1,0:T(8,128)(2,1)} %bitcast.25, ...), custom_call_target="tpu_custom_call" | custom-call | flops 16106127360 | bytes 4194304 | tf_op jit(solution)/shard_map/attend_pair_0/pallas_call | solution.py:357
  81.9 0.0 reduce-scatter.3.cloned.1.call-update
  81.9 0.0 reduce-scatter.5.cloned.1.call-start
  82.0 0.0 all-gather.3.cloned.1.call-done
  82.0 37.9 %attend_pair_1.1 = (bf16[512,2048]{1,0:T(8,128)(2,1)}, bf16[512,2048]{1,0:T(8,128)(2,1)}, bf16[512,256]{1,0:T(8,128)(2,1)}, bf16[512,256]{1,0:T(8,128)(2,1)}, bf...) custom-call(s32[1]{0:T(128)S(6)} %copy.21.len_ref, ...), custom_call_target="tpu_custom_call", output_to_operand_aliasing={{0}: (6, {}), {1}: (7, {}), {2}: (8, {}), {3}: (9, {})} | custom-call | flops 16106127360 | bytes 4194304 | tf_op jit(solution)/shard_map/attend_pair_1/pallas_call | solution.py:357
  119.9 0.0 reduce-scatter.3.cloned.1.call-done
  119.9 0.0 reduce-scatter.5.cloned.1.call-update
  120.0 0.9 collective-permute-start.12
  120.9 2.0 %collective-permute-start.13 = (bf16[768,128]{1,0:T(8,128)(2,1)}, bf16[768,128]{1,0:T(8,128)(2,1)S(1)}, u32[]{:S(2)}, u32[]{:S(2)}) collective-permute-start(bf16[768,128]{1,0:T(8,128)(2,1)} %get-tuple-element.81), channel_id=1, source_target_pairs={{0,8},{4,12},{8,0},{12,4},{1,9},{5,13},{9,1},{13,5},{2,10},{6,14},... | collective-permute-start | bytes 589832 | tf_op jit(solution)/shard_map/ppermute | solution.py:462
  122.9 2.8 %collective-permute-start.14 = (bf16[768,128]{1,0:T(8,128)(2,1)}, bf16[768,128]{1,0:T(8,128)(2,1)S(1)}, u32[]{:S(2)}, u32[]{:S(2)}) collective-permute-start(bf16[768,128]{1,0:T(8,128)(2,1)} %get-tuple-element.82), channel_id=1, source_target_pairs={{0,12},{4,0},{8,4},{12,8},{1,13},{5,1},{9,5},{13,9},{2,14},{6,2},{... | collective-permute-start | bytes 589832 | tf_op jit(solution)/shard_map/ppermute | solution.py:462
  125.8 1.6 fusion
  127.3 0.0 collective-permute-start.11
  127.3 1.5 collective-permute-start.10
  128.8 1.1 collective-permute-done.12
  130.0 0.0 collective-permute-start.9
  130.0 9.6 %collective-permute-done.13 = bf16[768,128]{1,0:T(8,128)(2,1)S(1)} collective-permute-done((bf16[768,128]{1,0:T(8,128)(2,1)}, bf16[768,128]{1,0:T(8,128)(2,1)S(1)}, u32[]{:S(2)}, u32[]{:S(2)}) %collective-permute-start.13) | collective-permute-done | bytes 196640 | tf_op jit(solution)/shard_map/ppermute | solution.py:462
  139.5 0.0 collective-permute-done.14
  139.5 1.0 add_convert_fusion
  140.6 0.1 collective-permute-start.15
  140.7 4.5 %reduce-scatter.5.cloned.1.call-done = bf16[1,256,128]{2,1,0:T(8,128)(2,1)} async-done(((bf16[4,256,128]{2,1,0:T(8,128)(2,1)}), bf16[1,256,128]{2,1,0:T(8,128)(2,1)}) %reduce-scatter.5.cloned.1.call-update) | async-done | bytes 65552 | tf_op jit(solution)/shard_map/reduce_scatter | solution.py:517
  145.2 0.8 fusion.1
  146.0 1.9 %collective-permute-start.16 = (bf16[2,128,128]{2,1,0:T(8,128)(2,1)S(1)}, bf16[2,128,128]{2,1,0:T(8,128)(2,1)S(1)}, u32[]{:S(2)}, u32[]{:S(2)}) collective-permute-start(bf16[2,128,128]{2,1,0:T(8,128)(2,1)S(1)} %pad_maximum_fusion.4), channel_id=1, source_target_pairs={{0,2},{1,3},{2,0},{3,1},{4,6},{5,7},{6,4},{7,5},{8,10},{9,11},{10,... | collective-permute-start | bytes 196616 | tf_op jit(solution)/shard_map/ppermute | solution.py:456
  147.9 0.0 collective-permute-done.11.refs_3_
  147.9 0.0 copy-start.1
  147.9 0.1 collective-permute-start.17
  148.0 0.6 pad_maximum_fusion.2.refs_4_
  148.6 0.0 collective-permute-done.10.refs_2_
  148.6 0.0 collective-permute-done.9.refs_1_
  148.6 0.0 copy-start.3
  148.6 0.0 collective-permute-done.15.refs_5_
  148.6 1.7 %collective-permute-done.16.refs_6_ = bf16[2,128,128]{2,1,0:T(8,128)(2,1)S(1)} collective-permute-done((bf16[2,128,128]{2,1,0:T(8,128)(2,1)S(1)}, bf16[2,128,128]{2,1,0:T(8,128)(2,1)S(1)}, u32[]{:S(2)}, u32[]{:S(2)}) %collective-permute-start.16) | collective-permute-done | bytes 65568 | tf_op jit(solution)/shard_map/ppermute | solution.py:456
  150.3 1.4 collective-permute-done.17.refs_7_
  151.7 0.0 copy-done.3
  151.7 0.6 copy-done.6
  152.3 2.1 %place.1 = (f32[128,1024]{1,0:T(8,128)}, f32[128,1024]{1,0:T(8,128)}) custom-call(bf16[2,128,128]{2,1,0:T(8,128)(2,1)} %get-tuple-element.89.refs_0_, bf16[2,128,128]{2,1,0:T(8,128)(2,1)} %copy-done.3, bf16[2,128,128]{2,1,0:T(8,128)(2,1)} %copy-done.2, bf16[2,128,128]{2,1,0:T(8,128)(2,1)} %copy-done.1, bf16[2,128,128]{2,1,0:T(8,128)(2,1)} %pad_maximum_fusion.2.refs_4_, ...), custom_call_target="tpu_custom_call" | custom-call | tf_op jit(solution)/shard_map/place/pallas_call | solution.py:444
  (15 shorter events, 0.1 us)
Async XLA Ops:
  7.2 74.8 %all-gather.3.cloned.1.call-start = ((), (), s32[]{:S(2)}) async-start(), calls=%async_computation.4 | async-start | bytes 1310720 | tf_op jit(solution)/shard_map/all_gather | solution.py:491
  9.2 3.1 %collective-permute-start = (bf16[2,128,128]{2,1,0:T(8,128)(2,1)}, bf16[2,128,128]{2,1,0:T(8,128)(2,1)S(1)}, u32[]{:S(2)}, u32[]{:S(2)}) collective-permute-start(bf16[2,128,128]{2,1,0:T(8,128)(2,1)} %get-tuple-element.47), channel_id=1, source_target_pairs={{0,1},{1,0},{2,3},{3,2},{4,5},{5,4},{6,7},{7,6},{8,9},{9,8},{10,11... | collective-permute-start | bytes 196616 | tf_op jit(solution)/shard_map/ppermute | solution.py:456
  9.6 5.5 %collective-permute-start.1 = (bf16[2,128,128]{2,1,0:T(8,128)(2,1)}, bf16[2,128,128]{2,1,0:T(8,128)(2,1)S(1)}, u32[]{:S(2)}, u32[]{:S(2)}) collective-permute-start(bf16[2,128,128]{2,1,0:T(8,128)(2,1)} %get-tuple-element.48), channel_id=1, source_target_pairs={{0,2},{1,3},{2,0},{3,1},{4,6},{5,7},{6,4},{7,5},{8,10},{9,11},{10,... | collective-permute-start | bytes 196616 | tf_op jit(solution)/shard_map/ppermute | solution.py:456
  12.1 4.3 %collective-permute-start.2 = (bf16[2,128,128]{2,1,0:T(8,128)(2,1)}, bf16[2,128,128]{2,1,0:T(8,128)(2,1)S(1)}, u32[]{:S(2)}, u32[]{:S(2)}) collective-permute-start(bf16[2,128,128]{2,1,0:T(8,128)(2,1)} %get-tuple-element.49), channel_id=1, source_target_pairs={{0,3},{1,2},{2,1},{3,0},{4,7},{5,6},{6,5},{7,4},{8,11},{9,10},{10,... | collective-permute-start | bytes 196616 | tf_op jit(solution)/shard_map/ppermute | solution.py:456
  17.3 27.0 %copy-start = (bf16[2,512,128]{2,1,0:T(8,128)(2,1)}, bf16[2,512,128]{2,1,0:T(8,128)(2,1)S(1)}, u32[]{:S(2)}) copy-start(bf16[2,512,128]{2,1,0:T(8,128)(2,1)S(1)} %pad_maximum_fusion.rest_0_) | copy-start | bytes 786436
  17.3 12.1 %collective-permute-start.8 = (bf16[2,512,128]{2,1,0:T(8,128)(2,1)S(1)}, bf16[2,512,128]{2,1,0:T(8,128)(2,1)S(1)}, u32[]{:S(2)}, u32[]{:S(2)}) collective-permute-start(bf16[2,512,128]{2,1,0:T(8,128)(2,1)S(1)} %pad_maximum_fusion.rest_0_), channel_id=1, source_target_pairs={{0,12},{4,0},{8,4},{12,8},{1,13},{5,1},{9,5},{13,9},{2,14},{6,2},{... | collective-permute-start | bytes 786440 | tf_op jit(solution)/shard_map/ppermute | solution.py:462
  21.0 22.6 %collective-permute-start.7 = (bf16[2,512,128]{2,1,0:T(8,128)(2,1)S(1)}, bf16[2,512,128]{2,1,0:T(8,128)(2,1)S(1)}, u32[]{:S(2)}, u32[]{:S(2)}) collective-permute-start(bf16[2,512,128]{2,1,0:T(8,128)(2,1)S(1)} %pad_maximum_fusion.rest_0_), channel_id=1, source_target_pairs={{0,8},{4,12},{8,0},{12,4},{1,9},{5,13},{9,1},{13,5},{2,10},{6,14},... | collective-permute-start | bytes 786440 | tf_op jit(solution)/shard_map/ppermute | solution.py:462
  21.0 22.6 %collective-permute-start.6 = (bf16[2,512,128]{2,1,0:T(8,128)(2,1)S(1)}, bf16[2,512,128]{2,1,0:T(8,128)(2,1)S(1)}, u32[]{:S(2)}, u32[]{:S(2)}) collective-permute-start(bf16[2,512,128]{2,1,0:T(8,128)(2,1)S(1)} %pad_maximum_fusion.rest_0_), channel_id=1, source_target_pairs={{0,4},{4,8},{8,12},{12,0},{1,5},{5,9},{9,13},{13,1},{2,6},{6,10},{... | collective-permute-start | bytes 786440 | tf_op jit(solution)/shard_map/ppermute | solution.py:462
  22.0 1.5 collective-permute-start.3
  22.0 4.8 %collective-permute-start.4 = (bf16[2,128,128]{2,1,0:T(8,128)(2,1)}, bf16[2,128,128]{2,1,0:T(8,128)(2,1)S(1)}, u32[]{:S(2)}, u32[]{:S(2)}) collective-permute-start(bf16[2,128,128]{2,1,0:T(8,128)(2,1)} %get-tuple-element.56), channel_id=1, source_target_pairs={{0,2},{1,3},{2,0},{3,1},{4,6},{5,7},{6,4},{7,5},{8,10},{9,11},{10,... | collective-permute-start | bytes 196616 | tf_op jit(solution)/shard_map/ppermute | solution.py:456
  23.5 4.4 %collective-permute-start.5 = (bf16[2,128,128]{2,1,0:T(8,128)(2,1)}, bf16[2,128,128]{2,1,0:T(8,128)(2,1)S(1)}, u32[]{:S(2)}, u32[]{:S(2)}) collective-permute-start(bf16[2,128,128]{2,1,0:T(8,128)(2,1)} %get-tuple-element.57), channel_id=1, source_target_pairs={{0,3},{1,2},{2,1},{3,0},{4,7},{5,6},{6,5},{7,4},{8,11},{9,10},{10,... | collective-permute-start | bytes 196616 | tf_op jit(solution)/shard_map/ppermute | solution.py:456
  29.4 15.0 %copy-start.7 = (bf16[2,512,128]{2,1,0:T(8,128)(2,1)}, bf16[2,512,128]{2,1,0:T(8,128)(2,1)S(1)}, u32[]{:S(2)}) copy-start(bf16[2,512,128]{2,1,0:T(8,128)(2,1)S(1)} %collective-permute-done.8.rest_3_) | copy-start | bytes 786436
  43.6 0.8 copy-start.8
  43.6 0.8 copy-start.9
  43.6 76.3 %reduce-scatter.3.cloned.1.call-start = ((), (), s32[]{:S(2)}) async-start(), calls=%async_computation.2 | async-start | bytes 1310720 | tf_op jit(solution)/shard_map/reduce_scatter | solution.py:511
  81.9 63.3 %reduce-scatter.5.cloned.1.call-start = ((), (), s32[]{:S(2)}) async-start(), calls=%async_computation.3 | async-start | bytes 327680 | tf_op jit(solution)/shard_map/reduce_scatter | solution.py:517
  120.0 10.0 %collective-permute-start.12 = (bf16[768,128]{1,0:T(8,128)(2,1)}, bf16[768,128]{1,0:T(8,128)(2,1)S(1)}, u32[]{:S(2)}, u32[]{:S(2)}) collective-permute-start(bf16[768,128]{1,0:T(8,128)(2,1)} %get-tuple-element.80), channel_id=1, source_target_pairs={{0,4},{4,8},{8,12},{12,0},{1,5},{5,9},{9,13},{13,1},{2,6},{6,10},{... | collective-permute-start | bytes 589832 | tf_op jit(solution)/shard_map/ppermute | solution.py:462
  120.9 18.6 %collective-permute-start.13 = (bf16[768,128]{1,0:T(8,128)(2,1)}, bf16[768,128]{1,0:T(8,128)(2,1)S(1)}, u32[]{:S(2)}, u32[]{:S(2)}) collective-permute-start(bf16[768,128]{1,0:T(8,128)(2,1)} %get-tuple-element.81), channel_id=1, source_target_pairs={{0,8},{4,12},{8,0},{12,4},{1,9},{5,13},{9,1},{13,5},{2,10},{6,14},... | collective-permute-start | bytes 589832 | tf_op jit(solution)/shard_map/ppermute | solution.py:462
  122.9 16.6 %collective-permute-start.14 = (bf16[768,128]{1,0:T(8,128)(2,1)}, bf16[768,128]{1,0:T(8,128)(2,1)S(1)}, u32[]{:S(2)}, u32[]{:S(2)}) collective-permute-start(bf16[768,128]{1,0:T(8,128)(2,1)} %get-tuple-element.82), channel_id=1, source_target_pairs={{0,12},{4,0},{8,4},{12,8},{1,13},{5,1},{9,5},{13,9},{2,14},{6,2},{... | collective-permute-start | bytes 589832 | tf_op jit(solution)/shard_map/ppermute | solution.py:462
  127.3 20.5 %collective-permute-start.11 = (bf16[2,128,128]{2,1,0:T(8,128)(2,1)S(1)}, bf16[2,128,128]{2,1,0:T(8,128)(2,1)S(1)}, u32[]{:S(2)}, u32[]{:S(2)}) collective-permute-start(bf16[2,128,128]{2,1,0:T(8,128)(2,1)S(1)} %get-tuple-element.86), channel_id=1, source_target_pairs={{0,3},{1,2},{2,1},{3,0},{4,7},{5,6},{6,5},{7,4},{8,11},{9,10},{10,... | collective-permute-start | bytes 196616 | tf_op jit(solution)/shard_map/ppermute | solution.py:456
  127.3 21.3 %collective-permute-start.10 = (bf16[2,128,128]{2,1,0:T(8,128)(2,1)S(1)}, bf16[2,128,128]{2,1,0:T(8,128)(2,1)S(1)}, u32[]{:S(2)}, u32[]{:S(2)}) collective-permute-start(bf16[2,128,128]{2,1,0:T(8,128)(2,1)S(1)} %get-tuple-element.87), channel_id=1, source_target_pairs={{0,2},{1,3},{2,0},{3,1},{4,6},{5,7},{6,4},{7,5},{8,10},{9,11},{10,... | collective-permute-start | bytes 196616 | tf_op jit(solution)/shard_map/ppermute | solution.py:456
  130.0 18.7 %collective-permute-start.9 = (bf16[2,128,128]{2,1,0:T(8,128)(2,1)S(1)}, bf16[2,128,128]{2,1,0:T(8,128)(2,1)S(1)}, u32[]{:S(2)}, u32[]{:S(2)}) collective-permute-start(bf16[2,128,128]{2,1,0:T(8,128)(2,1)S(1)} %get-tuple-element.88), channel_id=1, source_target_pairs={{0,1},{1,0},{2,3},{3,2},{4,5},{5,4},{6,7},{7,6},{8,9},{9,8},{10,11... | collective-permute-start | bytes 196616 | tf_op jit(solution)/shard_map/ppermute | solution.py:456
  140.6 8.0 %collective-permute-start.15 = (bf16[2,128,128]{2,1,0:T(8,128)(2,1)S(1)}, bf16[2,128,128]{2,1,0:T(8,128)(2,1)S(1)}, u32[]{:S(2)}, u32[]{:S(2)}) collective-permute-start(bf16[2,128,128]{2,1,0:T(8,128)(2,1)S(1)} %pad_maximum_fusion.3), channel_id=1, source_target_pairs={{0,1},{1,0},{2,3},{3,2},{4,5},{5,4},{6,7},{7,6},{8,9},{9,8},{10,11... | collective-permute-start | bytes 196616 | tf_op jit(solution)/shard_map/ppermute | solution.py:456
  146.0 4.3 %collective-permute-start.16 = (bf16[2,128,128]{2,1,0:T(8,128)(2,1)S(1)}, bf16[2,128,128]{2,1,0:T(8,128)(2,1)S(1)}, u32[]{:S(2)}, u32[]{:S(2)}) collective-permute-start(bf16[2,128,128]{2,1,0:T(8,128)(2,1)S(1)} %pad_maximum_fusion.4), channel_id=1, source_target_pairs={{0,2},{1,3},{2,0},{3,1},{4,6},{5,7},{6,4},{7,5},{8,10},{9,11},{10,... | collective-permute-start | bytes 196616 | tf_op jit(solution)/shard_map/ppermute | solution.py:456
  147.9 3.8 %copy-start.1 = (bf16[2,128,128]{2,1,0:T(8,128)(2,1)}, bf16[2,128,128]{2,1,0:T(8,128)(2,1)S(1)}, u32[]{:S(2)}) copy-start(bf16[2,128,128]{2,1,0:T(8,128)(2,1)S(1)} %collective-permute-done.11.refs_3_) | copy-start | bytes 196612
  147.9 3.8 %collective-permute-start.17 = (bf16[2,128,128]{2,1,0:T(8,128)(2,1)S(1)}, bf16[2,128,128]{2,1,0:T(8,128)(2,1)S(1)}, u32[]{:S(2)}, u32[]{:S(2)}) collective-permute-start(bf16[2,128,128]{2,1,0:T(8,128)(2,1)S(1)} %pad_maximum_fusion.5), channel_id=1, source_target_pairs={{0,3},{1,2},{2,1},{3,0},{4,7},{5,6},{6,5},{7,4},{8,11},{9,10},{10,... | collective-permute-start | bytes 196616 | tf_op jit(solution)/shard_map/ppermute | solution.py:456
  148.6 3.1 %copy-start.2 = (bf16[2,128,128]{2,1,0:T(8,128)(2,1)}, bf16[2,128,128]{2,1,0:T(8,128)(2,1)S(1)}, u32[]{:S(2)}) copy-start(bf16[2,128,128]{2,1,0:T(8,128)(2,1)S(1)} %collective-permute-done.10.refs_2_) | copy-start | bytes 196612
  148.6 3.1 %copy-start.3 = (bf16[2,128,128]{2,1,0:T(8,128)(2,1)}, bf16[2,128,128]{2,1,0:T(8,128)(2,1)S(1)}, u32[]{:S(2)}) copy-start(bf16[2,128,128]{2,1,0:T(8,128)(2,1)S(1)} %collective-permute-done.9.refs_1_) | copy-start | bytes 196612
  148.6 3.1 %copy-start.4 = (bf16[2,128,128]{2,1,0:T(8,128)(2,1)}, bf16[2,128,128]{2,1,0:T(8,128)(2,1)S(1)}, u32[]{:S(2)}) copy-start(bf16[2,128,128]{2,1,0:T(8,128)(2,1)S(1)} %collective-permute-done.15.refs_5_) | copy-start | bytes 196612
  150.3 1.4 copy-start.5
  151.7 0.6 copy-start.6
Sparse Core Ops, SparseCore 0:
  43.7 28.3 all-gather.2
  82.0 27.5 reduce-scatter.2
  120.1 25.0 reduce-scatter.4

commit v14 on v12

--- a/solution.py
+++ b/solution.py
@@ -154,19 +154,15 @@
     def grad_products(before, piece):
         at, size, row = pieces[piece]
 
-        def value_product(u):
-            at = slice(u, u + WIDE)
-            dv_sum[at, :] += dot(weights[before][at, row:], grad[before, row:, :])
-
-        def key_product(u):
-            at = slice(u, u + WIDE)
-            dk_sum[at, :] += dot(sgrads[at, row:], query[before, row:, :])
-
-        return [
-            functools.partial(product, u)
-            for u in range(at, at + size, WIDE)
-            for product in (value_product, key_product)
-        ]
+        key_at = slice(at, at + size)
+
+        def value_product():
+            dv_sum[key_at, :] += dot(weights[before][key_at, row:], grad[before, row:, :])
+
+        def key_product():
+            dk_sum[key_at, :] += dot(sgrads[key_at, row:], query[before, row:, :])
+
+        return [value_product, key_product]
 
     def query_products(before):
         def product(r):
@@ -515,9 +511,16 @@
             ]
             both = sum(block.astype(F32) for block in arrived).astype(BF16)
             rest = lax.psum_scatter(dcaches[members], "resp", scatter_dimension=0)
-            both = jnp.concatenate([both, rest], axis=0)
-            totals.append(both.reshape(2, ranks * own_rows, HD))
-    blocks = [block for total in totals for block in swap(cut_rows(total, ranks))]
+            parts = ranks * own_rows
+            keys, both = both[:parts], both[parts:]
+            split = both.shape[0] // own_rows
+            values = [both[i * own_rows : (i + 1) * own_rows] for i in range(split)]
+            values += [rest[i * own_rows : (i + 1) * own_rows] for i in range(ranks - split)]
+            pieces = [keys[i * own_rows : (i + 1) * own_rows] for i in range(ranks)]
+            totals.append([jnp.stack(both) for both in zip(pieces, values)])
+    blocks = []
+    for total in totals:
+        blocks += swap(total if isinstance(total, list) else cut_rows(total, ranks))
     key_grad, value_grad = place(blocks, pairs, columns)
     return (*(a[None] for a in earlier), key_grad, value_grad)
 

time: 160 us -> 161 us (level)
  transfers between devices with their start and end apart: 21 -> 21, of which waited for: 11 -> 11; matrix products, arithmetic and copies ran while one was open for 4% -> 4% of each run, Pallas kernels for 46% -> 47%
where the time goes in v14:
time: 161 us
  Pallas kernels  79.1 us (49%)
  waiting for transfers between devices  40.2 us (25%)
  starting transfers between devices  19.6 us (12%)
  between operations  14.6 us (9%)
  other arithmetic  4.12 us (3%)
  local copies, waits for them, and re-layouts  3.02 us (2%)
    pallas_call x2, Pallas kernels, attend(): pl.pallas_call(functools.partial(attention_kernel, layout, heads_per, len...  75.1 us
    ppermute x6, waiting for transfers between devices, send(): lax.ppermute(block, 'resp', [(m, (m + shift) % members) for m in range(me...  24.9 us
    ppermute x12, waiting for transfers between devices, swap(): lax.ppermute(blocks[i], 'tensor', [(j, j ^ i) for j in range(count)])  10.7 us
    ppermute x6, starting transfers between devices, send(): lax.ppermute(block, 'resp', [(m, (m + shift) % members) for m in range(me...  10.5 us
    ppermute x12, starting transfers between devices, swap(): lax.ppermute(blocks[i], 'tensor', [(j, j ^ i) for j in range(count)])  9.01 us
    reduce_scatter x1, waiting for transfers between devices, per_device(): rest = lax.psum_scatter(dcaches[members], 'resp', scatter_dimension=0)  4.45 us
  transfers between devices with their start and end apart: 21, of which 11 were waited for; matrix products, arithmetic and copies ran while one was open for 4% of the time, Pallas kernels for 47%

profile of v14, /device:TPU:0, one launch (start us, length us, event | category | flops | bytes accessed | tf_op | source)
XLA Modules:
  0.0 160.6 jit_solution(5711968568703684890)
XLA Ops:
  7.2 0.0 all-gather.3.cloned.1.call-start
  7.2 1.9 %cut.1 = (bf16[2,128,128]{2,1,0:T(8,128)(2,1)}, bf16[2,128,128]{2,1,0:T(8,128)(2,1)}, bf16[2,128,128]{2,1,0:T(8,128)(2,1)}, bf16[2,128,128]{2,1,0:T(8,128)(2,1)}...) custom-call(bf16[128,1024]{1,0:T(8,128)(2,1)} %k_ref.1, ...), custom_call_target="tpu_custom_call" | custom-call | tf_op jit(solution)/shard_map/cut/pallas_call | solution.py:416
  9.2 0.5 collective-permute-start
  9.6 2.5 %collective-permute-start.1 = (bf16[2,128,128]{2,1,0:T(8,128)(2,1)}, bf16[2,128,128]{2,1,0:T(8,128)(2,1)S(1)}, u32[]{:S(2)}, u32[]{:S(2)}) collective-permute-start(bf16[2,128,128]{2,1,0:T(8,128)(2,1)} %get-tuple-element.48), channel_id=1, source_target_pairs={{0,2},{1,3},{2,0},{3,1},{4,6},{5,7},{6,4},{7,5},{8,10},{9,11},{10,... | collective-permute-start | bytes 196616 | tf_op jit(solution)/shard_map/ppermute | solution.py:452
  12.1 0.1 collective-permute-start.2
  12.2 0.0 collective-permute-done
  12.2 2.8 %collective-permute-done.1 = bf16[2,128,128]{2,1,0:T(8,128)(2,1)S(1)} collective-permute-done((bf16[2,128,128]{2,1,0:T(8,128)(2,1)}, bf16[2,128,128]{2,1,0:T(8,128)(2,1)S(1)}, u32[]{:S(2)}, u32[]{:S(2)}) %collective-permute-start.1) | collective-permute-done | bytes 65568 | tf_op jit(solution)/shard_map/ppermute | solution.py:452
  15.1 1.4 collective-permute-done.2
  16.5 0.9 pad_maximum_fusion.rest_0_
  17.3 0.0 copy-start
  17.3 3.7 %collective-permute-start.8 = (bf16[2,512,128]{2,1,0:T(8,128)(2,1)S(1)}, bf16[2,512,128]{2,1,0:T(8,128)(2,1)S(1)}, u32[]{:S(2)}, u32[]{:S(2)}) collective-permute-start(bf16[2,512,128]{2,1,0:T(8,128)(2,1)S(1)} %pad_maximum_fusion.rest_0_), channel_id=1, source_target_pairs={{0,12},{4,0},{8,4},{12,8},{1,13},{5,1},{9,5},{13,9},{2,14},{6,2},{... | collective-permute-start | bytes 786440 | tf_op jit(solution)/shard_map/ppermute | solution.py:458
  21.0 0.0 collective-permute-start.7
  21.0 1.0 collective-permute-start.6
  22.0 0.0 collective-permute-start.3
  22.0 1.3 collective-permute-start.4
  23.3 0.2 collective-permute-done.3
  23.5 1.1 collective-permute-start.5
  24.5 2.2 %collective-permute-done.4 = bf16[2,128,128]{2,1,0:T(8,128)(2,1)S(1)} collective-permute-done((bf16[2,128,128]{2,1,0:T(8,128)(2,1)}, bf16[2,128,128]{2,1,0:T(8,128)(2,1)S(1)}, u32[]{:S(2)}, u32[]{:S(2)}) %collective-permute-start.4) | collective-permute-done | bytes 65568 | tf_op jit(solution)/shard_map/ppermute | solution.py:452
  26.8 1.1 collective-permute-done.5
  27.8 1.6 pad_maximum_fusion.1
  29.4 0.0 collective-permute-done.8.rest_3_
  29.4 14.2 %collective-permute-done.7.rest_2_ = bf16[2,512,128]{2,1,0:T(8,128)(2,1)S(1)} collective-permute-done((bf16[2,512,128]{2,1,0:T(8,128)(2,1)S(1)}, bf16[2,512,128]{2,1,0:T(8,128)(2,1)S(1)}, u32[]{:S(2)}, u32[]{:S(2)}) %collective-permute-start.7) | collective-permute-done | bytes 262176 | tf_op jit(solution)/shard_map/ppermute | solution.py:458
  43.6 0.0 collective-permute-done.6.rest_1_
  43.6 0.0 all-gather.3.cloned.1.call-update
  43.6 0.0 reduce-scatter.3.cloned.1.call-start
  44.4 0.0 copy-done
  44.4 0.0 copy-done.7
  44.4 0.0 copy-done.8
  44.4 0.0 copy-done.9
  44.4 37.3 %attend_pair_0.1 = (bf16[512,2048]{1,0:T(8,128)(2,1)}, bf16[512,2048]{1,0:T(8,128)(2,1)}, bf16[512,256]{1,0:T(8,128)(2,1)}, bf16[512,256]{1,0:T(8,128)(2,1)}, bf16[4,2,512,128]{3,2,1,0:T(8,128)(2,1)}) custom-call(s32[1]{0:T(128)S(6)} %copy.21.len_ref, bf16[512,2048]{1,0:T(8,128)(2,1)} %bitcast.23, bf16[512,2048]{1,0:T(8,128)(2,1)} %bitcast.25, ...), custom_call_target="tpu_custom_call" | custom-call | flops 16106127360 | bytes 4194304 | tf_op jit(solution)/shard_map/attend_pair_0/pallas_call | solution.py:353
  81.7 0.0 reduce-scatter.3.cloned.1.call-update
  81.7 0.0 reduce-scatter.5.cloned.1.call-start
  81.8 0.0 all-gather.3.cloned.1.call-done
  81.8 37.7 %attend_pair_1.1 = (bf16[512,2048]{1,0:T(8,128)(2,1)}, bf16[512,2048]{1,0:T(8,128)(2,1)}, bf16[512,256]{1,0:T(8,128)(2,1)}, bf16[512,256]{1,0:T(8,128)(2,1)}, bf...) custom-call(s32[1]{0:T(128)S(6)} %copy.21.len_ref, ...), custom_call_target="tpu_custom_call", output_to_operand_aliasing={{0}: (6, {}), {1}: (7, {}), {2}: (8, {}), {3}: (9, {})} | custom-call | flops 16106127360 | bytes 4194304 | tf_op jit(solution)/shard_map/attend_pair_1/pallas_call | solution.py:353
  119.6 0.0 reduce-scatter.3.cloned.1.call-done
  119.6 0.0 reduce-scatter.5.cloned.1.call-update
  119.6 0.9 collective-permute-start.12
  120.5 2.0 %collective-permute-start.13 = (bf16[768,128]{1,0:T(8,128)(2,1)}, bf16[768,128]{1,0:T(8,128)(2,1)S(1)}, u32[]{:S(2)}, u32[]{:S(2)}) collective-permute-start(bf16[768,128]{1,0:T(8,128)(2,1)} %get-tuple-element.81), channel_id=1, source_target_pairs={{0,8},{4,12},{8,0},{12,4},{1,9},{5,13},{9,1},{13,5},{2,10},{6,14},... | collective-permute-start | bytes 589832 | tf_op jit(solution)/shard_map/ppermute | solution.py:458
  122.6 2.8 %collective-permute-start.14 = (bf16[768,128]{1,0:T(8,128)(2,1)}, bf16[768,128]{1,0:T(8,128)(2,1)S(1)}, u32[]{:S(2)}, u32[]{:S(2)}) collective-permute-start(bf16[768,128]{1,0:T(8,128)(2,1)} %get-tuple-element.82), channel_id=1, source_target_pairs={{0,12},{4,0},{8,4},{12,8},{1,13},{5,1},{9,5},{13,9},{2,14},{6,2},{... | collective-permute-start | bytes 589832 | tf_op jit(solution)/shard_map/ppermute | solution.py:458
  125.4 1.6 fusion
  127.0 0.0 collective-permute-start.11
  127.0 1.5 collective-permute-start.10
  128.5 1.1 collective-permute-done.12
  129.6 0.0 collective-permute-start.9
  129.6 9.6 %collective-permute-done.13 = bf16[768,128]{1,0:T(8,128)(2,1)S(1)} collective-permute-done((bf16[768,128]{1,0:T(8,128)(2,1)}, bf16[768,128]{1,0:T(8,128)(2,1)S(1)}, u32[]{:S(2)}, u32[]{:S(2)}) %collective-permute-start.13) | collective-permute-done | bytes 196640 | tf_op jit(solution)/shard_map/ppermute | solution.py:458
  139.2 0.0 collective-permute-done.14
  139.2 1.0 add_convert_fusion
  140.3 0.1 collective-permute-start.15
  140.4 4.5 %reduce-scatter.5.cloned.1.call-done = bf16[1,256,128]{2,1,0:T(8,128)(2,1)} async-done(((bf16[4,256,128]{2,1,0:T(8,128)(2,1)}), bf16[1,256,128]{2,1,0:T(8,128)(2,1)}) %reduce-scatter.5.cloned.1.call-update) | async-done | bytes 65552 | tf_op jit(solution)/shard_map/reduce_scatter | solution.py:513
  144.8 0.8 fusion.1
  145.6 1.9 %collective-permute-start.16 = (bf16[2,128,128]{2,1,0:T(8,128)(2,1)S(1)}, bf16[2,128,128]{2,1,0:T(8,128)(2,1)S(1)}, u32[]{:S(2)}, u32[]{:S(2)}) collective-permute-start(bf16[2,128,128]{2,1,0:T(8,128)(2,1)S(1)} %pad_maximum_fusion.4), channel_id=1, source_target_pairs={{0,2},{1,3},{2,0},{3,1},{4,6},{5,7},{6,4},{7,5},{8,10},{9,11},{10,... | collective-permute-start | bytes 196616 | tf_op jit(solution)/shard_map/ppermute | solution.py:452
  147.6 0.0 collective-permute-done.11.refs_3_
  147.6 0.0 copy-start.1
  147.6 0.1 collective-permute-start.17
  147.6 0.6 pad_maximum_fusion.2.refs_4_
  148.3 0.0 collective-permute-done.10.refs_2_
  148.3 0.0 collective-permute-done.9.refs_1_
  148.3 0.0 copy-start.3
  148.3 0.0 collective-permute-done.15.refs_5_
  148.3 1.6 %collective-permute-done.16.refs_6_ = bf16[2,128,128]{2,1,0:T(8,128)(2,1)S(1)} collective-permute-done((bf16[2,128,128]{2,1,0:T(8,128)(2,1)S(1)}, bf16[2,128,128]{2,1,0:T(8,128)(2,1)S(1)}, u32[]{:S(2)}, u32[]{:S(2)}) %collective-permute-start.16) | collective-permute-done | bytes 65568 | tf_op jit(solution)/shard_map/ppermute | solution.py:452
  150.0 1.4 collective-permute-done.17.refs_7_
  151.4 0.0 copy-done.3
  151.4 0.6 copy-done.6
  152.0 2.1 %place.1 = (f32[128,1024]{1,0:T(8,128)}, f32[128,1024]{1,0:T(8,128)}) custom-call(bf16[2,128,128]{2,1,0:T(8,128)(2,1)} %get-tuple-element.89.refs_0_, bf16[2,128,128]{2,1,0:T(8,128)(2,1)} %copy-done.3, bf16[2,128,128]{2,1,0:T(8,128)(2,1)} %copy-done.2, bf16[2,128,128]{2,1,0:T(8,128)(2,1)} %copy-done.1, bf16[2,128,128]{2,1,0:T(8,128)(2,1)} %pad_maximum_fusion.2.refs_4_, ...), custom_call_target="tpu_custom_call" | custom-call | tf_op jit(solution)/shard_map/place/pallas_call | solution.py:440
  (15 shorter events, 0.1 us)
Async XLA Ops:
  7.2 74.6 %all-gather.3.cloned.1.call-start = ((), (), s32[]{:S(2)}) async-start(), calls=%async_computation.4 | async-start | bytes 1310720 | tf_op jit(solution)/shard_map/all_gather | solution.py:487
  9.2 3.1 %collective-permute-start = (bf16[2,128,128]{2,1,0:T(8,128)(2,1)}, bf16[2,128,128]{2,1,0:T(8,128)(2,1)S(1)}, u32[]{:S(2)}, u32[]{:S(2)}) collective-permute-start(bf16[2,128,128]{2,1,0:T(8,128)(2,1)} %get-tuple-element.47), channel_id=1, source_target_pairs={{0,1},{1,0},{2,3},{3,2},{4,5},{5,4},{6,7},{7,6},{8,9},{9,8},{10,11... | collective-permute-start | bytes 196616 | tf_op jit(solution)/shard_map/ppermute | solution.py:452
  9.6 5.5 %collective-permute-start.1 = (bf16[2,128,128]{2,1,0:T(8,128)(2,1)}, bf16[2,128,128]{2,1,0:T(8,128)(2,1)S(1)}, u32[]{:S(2)}, u32[]{:S(2)}) collective-permute-start(bf16[2,128,128]{2,1,0:T(8,128)(2,1)} %get-tuple-element.48), channel_id=1, source_target_pairs={{0,2},{1,3},{2,0},{3,1},{4,6},{5,7},{6,4},{7,5},{8,10},{9,11},{10,... | collective-permute-start | bytes 196616 | tf_op jit(solution)/shard_map/ppermute | solution.py:452
  12.1 4.3 %collective-permute-start.2 = (bf16[2,128,128]{2,1,0:T(8,128)(2,1)}, bf16[2,128,128]{2,1,0:T(8,128)(2,1)S(1)}, u32[]{:S(2)}, u32[]{:S(2)}) collective-permute-start(bf16[2,128,128]{2,1,0:T(8,128)(2,1)} %get-tuple-element.49), channel_id=1, source_target_pairs={{0,3},{1,2},{2,1},{3,0},{4,7},{5,6},{6,5},{7,4},{8,11},{9,10},{10,... | collective-permute-start | bytes 196616 | tf_op jit(solution)/shard_map/ppermute | solution.py:452
  17.3 27.0 %copy-start = (bf16[2,512,128]{2,1,0:T(8,128)(2,1)}, bf16[2,512,128]{2,1,0:T(8,128)(2,1)S(1)}, u32[]{:S(2)}) copy-start(bf16[2,512,128]{2,1,0:T(8,128)(2,1)S(1)} %pad_maximum_fusion.rest_0_) | copy-start | bytes 786436
  17.3 12.1 %collective-permute-start.8 = (bf16[2,512,128]{2,1,0:T(8,128)(2,1)S(1)}, bf16[2,512,128]{2,1,0:T(8,128)(2,1)S(1)}, u32[]{:S(2)}, u32[]{:S(2)}) collective-permute-start(bf16[2,512,128]{2,1,0:T(8,128)(2,1)S(1)} %pad_maximum_fusion.rest_0_), channel_id=1, source_target_pairs={{0,12},{4,0},{8,4},{12,8},{1,13},{5,1},{9,5},{13,9},{2,14},{6,2},{... | collective-permute-start | bytes 786440 | tf_op jit(solution)/shard_map/ppermute | solution.py:458
  21.0 22.6 %collective-permute-start.7 = (bf16[2,512,128]{2,1,0:T(8,128)(2,1)S(1)}, bf16[2,512,128]{2,1,0:T(8,128)(2,1)S(1)}, u32[]{:S(2)}, u32[]{:S(2)}) collective-permute-start(bf16[2,512,128]{2,1,0:T(8,128)(2,1)S(1)} %pad_maximum_fusion.rest_0_), channel_id=1, source_target_pairs={{0,8},{4,12},{8,0},{12,4},{1,9},{5,13},{9,1},{13,5},{2,10},{6,14},... | collective-permute-start | bytes 786440 | tf_op jit(solution)/shard_map/ppermute | solution.py:458
  21.0 22.6 %collective-permute-start.6 = (bf16[2,512,128]{2,1,0:T(8,128)(2,1)S(1)}, bf16[2,512,128]{2,1,0:T(8,128)(2,1)S(1)}, u32[]{:S(2)}, u32[]{:S(2)}) collective-permute-start(bf16[2,512,128]{2,1,0:T(8,128)(2,1)S(1)} %pad_maximum_fusion.rest_0_), channel_id=1, source_target_pairs={{0,4},{4,8},{8,12},{12,0},{1,5},{5,9},{9,13},{13,1},{2,6},{6,10},{... | collective-permute-start | bytes 786440 | tf_op jit(solution)/shard_map/ppermute | solution.py:458
  22.0 1.5 collective-permute-start.3
  22.0 4.8 %collective-permute-start.4 = (bf16[2,128,128]{2,1,0:T(8,128)(2,1)}, bf16[2,128,128]{2,1,0:T(8,128)(2,1)S(1)}, u32[]{:S(2)}, u32[]{:S(2)}) collective-permute-start(bf16[2,128,128]{2,1,0:T(8,128)(2,1)} %get-tuple-element.56), channel_id=1, source_target_pairs={{0,2},{1,3},{2,0},{3,1},{4,6},{5,7},{6,4},{7,5},{8,10},{9,11},{10,... | collective-permute-start | bytes 196616 | tf_op jit(solution)/shard_map/ppermute | solution.py:452
  23.5 4.4 %collective-permute-start.5 = (bf16[2,128,128]{2,1,0:T(8,128)(2,1)}, bf16[2,128,128]{2,1,0:T(8,128)(2,1)S(1)}, u32[]{:S(2)}, u32[]{:S(2)}) collective-permute-start(bf16[2,128,128]{2,1,0:T(8,128)(2,1)} %get-tuple-element.57), channel_id=1, source_target_pairs={{0,3},{1,2},{2,1},{3,0},{4,7},{5,6},{6,5},{7,4},{8,11},{9,10},{10,... | collective-permute-start | bytes 196616 | tf_op jit(solution)/shard_map/ppermute | solution.py:452
  29.4 15.0 %copy-start.7 = (bf16[2,512,128]{2,1,0:T(8,128)(2,1)}, bf16[2,512,128]{2,1,0:T(8,128)(2,1)S(1)}, u32[]{:S(2)}) copy-start(bf16[2,512,128]{2,1,0:T(8,128)(2,1)S(1)} %collective-permute-done.8.rest_3_) | copy-start | bytes 786436
  43.6 0.8 copy-start.8
  43.6 0.8 copy-start.9
  43.6 76.0 %reduce-scatter.3.cloned.1.call-start = ((), (), s32[]{:S(2)}) async-start(), calls=%async_computation.2 | async-start | bytes 1310720 | tf_op jit(solution)/shard_map/reduce_scatter | solution.py:507
  81.7 63.1 %reduce-scatter.5.cloned.1.call-start = ((), (), s32[]{:S(2)}) async-start(), calls=%async_computation.3 | async-start | bytes 327680 | tf_op jit(solution)/shard_map/reduce_scatter | solution.py:513
  119.6 10.0 %collective-permute-start.12 = (bf16[768,128]{1,0:T(8,128)(2,1)}, bf16[768,128]{1,0:T(8,128)(2,1)S(1)}, u32[]{:S(2)}, u32[]{:S(2)}) collective-permute-start(bf16[768,128]{1,0:T(8,128)(2,1)} %get-tuple-element.80), channel_id=1, source_target_pairs={{0,4},{4,8},{8,12},{12,0},{1,5},{5,9},{9,13},{13,1},{2,6},{6,10},{... | collective-permute-start | bytes 589832 | tf_op jit(solution)/shard_map/ppermute | solution.py:458
  120.5 18.7 %collective-permute-start.13 = (bf16[768,128]{1,0:T(8,128)(2,1)}, bf16[768,128]{1,0:T(8,128)(2,1)S(1)}, u32[]{:S(2)}, u32[]{:S(2)}) collective-permute-start(bf16[768,128]{1,0:T(8,128)(2,1)} %get-tuple-element.81), channel_id=1, source_target_pairs={{0,8},{4,12},{8,0},{12,4},{1,9},{5,13},{9,1},{13,5},{2,10},{6,14},... | collective-permute-start | bytes 589832 | tf_op jit(solution)/shard_map/ppermute | solution.py:458
  122.6 16.6 %collective-permute-start.14 = (bf16[768,128]{1,0:T(8,128)(2,1)}, bf16[768,128]{1,0:T(8,128)(2,1)S(1)}, u32[]{:S(2)}, u32[]{:S(2)}) collective-permute-start(bf16[768,128]{1,0:T(8,128)(2,1)} %get-tuple-element.82), channel_id=1, source_target_pairs={{0,12},{4,0},{8,4},{12,8},{1,13},{5,1},{9,5},{13,9},{2,14},{6,2},{... | collective-permute-start | bytes 589832 | tf_op jit(solution)/shard_map/ppermute | solution.py:458
  127.0 20.6 %collective-permute-start.11 = (bf16[2,128,128]{2,1,0:T(8,128)(2,1)S(1)}, bf16[2,128,128]{2,1,0:T(8,128)(2,1)S(1)}, u32[]{:S(2)}, u32[]{:S(2)}) collective-permute-start(bf16[2,128,128]{2,1,0:T(8,128)(2,1)S(1)} %get-tuple-element.86), channel_id=1, source_target_pairs={{0,3},{1,2},{2,1},{3,0},{4,7},{5,6},{6,5},{7,4},{8,11},{9,10},{10,... | collective-permute-start | bytes 196616 | tf_op jit(solution)/shard_map/ppermute | solution.py:452
  127.0 21.3 %collective-permute-start.10 = (bf16[2,128,128]{2,1,0:T(8,128)(2,1)S(1)}, bf16[2,128,128]{2,1,0:T(8,128)(2,1)S(1)}, u32[]{:S(2)}, u32[]{:S(2)}) collective-permute-start(bf16[2,128,128]{2,1,0:T(8,128)(2,1)S(1)} %get-tuple-element.87), channel_id=1, source_target_pairs={{0,2},{1,3},{2,0},{3,1},{4,6},{5,7},{6,4},{7,5},{8,10},{9,11},{10,... | collective-permute-start | bytes 196616 | tf_op jit(solution)/shard_map/ppermute | solution.py:452
  129.6 18.7 %collective-permute-start.9 = (bf16[2,128,128]{2,1,0:T(8,128)(2,1)S(1)}, bf16[2,128,128]{2,1,0:T(8,128)(2,1)S(1)}, u32[]{:S(2)}, u32[]{:S(2)}) collective-permute-start(bf16[2,128,128]{2,1,0:T(8,128)(2,1)S(1)} %get-tuple-element.88), channel_id=1, source_target_pairs={{0,1},{1,0},{2,3},{3,2},{4,5},{5,4},{6,7},{7,6},{8,9},{9,8},{10,11... | collective-permute-start | bytes 196616 | tf_op jit(solution)/shard_map/ppermute | solution.py:452
  140.3 8.0 %collective-permute-start.15 = (bf16[2,128,128]{2,1,0:T(8,128)(2,1)S(1)}, bf16[2,128,128]{2,1,0:T(8,128)(2,1)S(1)}, u32[]{:S(2)}, u32[]{:S(2)}) collective-permute-start(bf16[2,128,128]{2,1,0:T(8,128)(2,1)S(1)} %pad_maximum_fusion.3), channel_id=1, source_target_pairs={{0,1},{1,0},{2,3},{3,2},{4,5},{5,4},{6,7},{7,6},{8,9},{9,8},{10,11... | collective-permute-start | bytes 196616 | tf_op jit(solution)/shard_map/ppermute | solution.py:452
  145.6 4.3 %collective-permute-start.16 = (bf16[2,128,128]{2,1,0:T(8,128)(2,1)S(1)}, bf16[2,128,128]{2,1,0:T(8,128)(2,1)S(1)}, u32[]{:S(2)}, u32[]{:S(2)}) collective-permute-start(bf16[2,128,128]{2,1,0:T(8,128)(2,1)S(1)} %pad_maximum_fusion.4), channel_id=1, source_target_pairs={{0,2},{1,3},{2,0},{3,1},{4,6},{5,7},{6,4},{7,5},{8,10},{9,11},{10,... | collective-permute-start | bytes 196616 | tf_op jit(solution)/shard_map/ppermute | solution.py:452
  147.6 3.8 %copy-start.1 = (bf16[2,128,128]{2,1,0:T(8,128)(2,1)}, bf16[2,128,128]{2,1,0:T(8,128)(2,1)S(1)}, u32[]{:S(2)}) copy-start(bf16[2,128,128]{2,1,0:T(8,128)(2,1)S(1)} %collective-permute-done.11.refs_3_) | copy-start | bytes 196612
  147.6 3.8 %collective-permute-start.17 = (bf16[2,128,128]{2,1,0:T(8,128)(2,1)S(1)}, bf16[2,128,128]{2,1,0:T(8,128)(2,1)S(1)}, u32[]{:S(2)}, u32[]{:S(2)}) collective-permute-start(bf16[2,128,128]{2,1,0:T(8,128)(2,1)S(1)} %pad_maximum_fusion.5), channel_id=1, source_target_pairs={{0,3},{1,2},{2,1},{3,0},{4,7},{5,6},{6,5},{7,4},{8,11},{9,10},{10,... | collective-permute-start | bytes 196616 | tf_op jit(solution)/shard_map/ppermute | solution.py:452
  148.3 3.1 %copy-start.2 = (bf16[2,128,128]{2,1,0:T(8,128)(2,1)}, bf16[2,128,128]{2,1,0:T(8,128)(2,1)S(1)}, u32[]{:S(2)}) copy-start(bf16[2,128,128]{2,1,0:T(8,128)(2,1)S(1)} %collective-permute-done.10.refs_2_) | copy-start | bytes 196612
  148.3 3.1 %copy-start.3 = (bf16[2,128,128]{2,1,0:T(8,128)(2,1)}, bf16[2,128,128]{2,1,0:T(8,128)(2,1)S(1)}, u32[]{:S(2)}) copy-start(bf16[2,128,128]{2,1,0:T(8,128)(2,1)S(1)} %collective-permute-done.9.refs_1_) | copy-start | bytes 196612
  148.3 3.1 %copy-start.4 = (bf16[2,128,128]{2,1,0:T(8,128)(2,1)}, bf16[2,128,128]{2,1,0:T(8,128)(2,1)S(1)}, u32[]{:S(2)}) copy-start(bf16[2,128,128]{2,1,0:T(8,128)(2,1)S(1)} %collective-permute-done.15.refs_5_) | copy-start | bytes 196612
  150.0 1.4 copy-start.5
  151.4 0.6 copy-start.6
Sparse Core Ops, SparseCore 0:
  43.7 28.3 all-gather.2
  81.9 27.5 reduce-scatter.2
  119.7 25.0 reduce-scatter.4
